TPU v7x, 128 devices: a whole 4x4x4 slice. The times are simulated.
128 devices in a mesh: tm: 8 (over x_lo, z), space: 16 (over y, x_hi, core).
Axes of the slice: x: 4 (x_hi: 2, x_lo: 2; x = x_hi * 2 + x_lo), y: 4, z: 4, core: 2. Of those that a mesh axis runs over, the one named last changes fastest.
Arguments:
- fine_nodes: float32 [8, 3, 53, 256, 256], P('tm', None, None, 'space'), may hold values from -6 to 6
- fine_rates: float32 [53, 53], replicated, may hold values from -3 to 3
- fine_pairs: float32 [53, 53], replicated, may hold values from -0.4 to 0.4
- fine_diff: float32 [53], replicated, may hold values from 0.1 to 0.8
- coarse_rates: float32 [21, 21], replicated, may hold values from -4 to 4
- coarse_pairs: float32 [21, 21], replicated, may hold values from -0.8 to 0.8
- coarse_diff: float32 [21], replicated, may hold values from 0.1 to 0.8
- species_map: int32 [53, 1], replicated, may hold values from 0 to 20
Outputs:
- new_nodes: float32 [8, 3, 53, 256, 256], P('tm', None, None, 'space')
Inputs may be any that keep to these rules, and one draw needn't show every extreme that they name: `species_map`: every one of the 21 lumped species is named by at least one detailed species.
All inputs are finite; a program needn't handle non-finite values.
Results may differ from a plain program's by a relative error of at most 0.00011.
Values sent between devices are 32-bit elements; how exact they have to be, the bound alone decides.
No kernel may reach another device: no remote copies, remote signals or barrier semaphores. Data moves between devices by JAX's collectives and lax.ppermute only.
A program may use at most 128 MiB of HBM per device.

v0:
```python
import functools

import jax
import jax.numpy as jnp
from jax import lax
from jax.experimental import pallas as pl
from jax.experimental.pallas import tpu as pltpu
from jax.sharding import PartitionSpec as P

SPECIES, COARSE = 53, 21
SP, CP = 56, 24
ROWS, COLS = 16, 256
SLICES, SLABS = 8, 16
STEP, HALF, RELAX = 0.1, 0.05, 3.0
W0 = (5.0 / 24.0, 1.0 / 3.0, -1.0 / 24.0)
W1 = (-1.0 / 24.0, 1.0 / 3.0, 5.0 / 24.0)
F32, BF16 = jnp.float32, jnp.bfloat16
VMEM_LIMIT = 48 * 1024 * 1024


def split(x):
    hi = x.astype(BF16)
    lo = (x - hi.astype(F32)).astype(BF16)
    return jnp.concatenate([hi, lo], axis=0)


def thirds(x):
    hi = x.astype(BF16)
    rest = x - hi.astype(F32)
    mid = rest.astype(BF16)
    return jnp.concatenate([hi, mid, (rest - mid.astype(F32)).astype(BF16)], axis=0)


def zeros(rows):
    return jnp.zeros((rows, COLS), F32)


def dot(w, x):
    return jnp.dot(w, x, preferred_element_type=F32)


def stacked(x, squares):
    return split(jnp.concatenate([x, squares, zeros(16)], axis=0))


def lap_y(x):
    near = pltpu.roll(x, 1, 1) + pltpu.roll(x, COLS - 1, 1)
    far = pltpu.roll(x, 2, 1) + pltpu.roll(x, COLS - 2, 1)
    return 16.0 * near - far - 60.0 * x


def lap_x(row, x, low, high):
    total = None
    for offset, factor in ((-1, 16.0), (1, 16.0), (-2, -1.0), (2, -1.0)):
        if low <= x + offset < high:
            term = factor * row(x + offset)
            total = term if total is None else total + term
    return total


def beside(near, far):
    return 16.0 * near - far, -near


def prep_kernel(rates, pairs, diff, crates, cpairs, cdiff, smap, wf, wr, wfr, lv, wc, pro, d12, dc12, share, a, mi):
    row = lax.broadcasted_iota(jnp.int32, (SP, 128), 0)
    lane = lax.broadcasted_iota(jnp.int32, (SP, 128), 1)

    def framed(ref, rows, columns, height):
        a[...] = jnp.zeros((SP, 128), F32)
        a[:rows, :columns] = ref[...]
        return a[:height, :]

    def halves(x):
        hi = x.astype(BF16).astype(F32)
        return hi, (x - hi).astype(BF16).astype(F32)

    def column(values, height):
        return jnp.sum(jnp.where(row == lane, values, 0.0), axis=1, keepdims=True)[:height]

    eye = jnp.where(row == lane, RELAX, 0.0)
    fine = framed(rates, SPECIES, SPECIES, SP) - jnp.where(row < SPECIES, eye, 0.0)
    fine = fine + pltpu.roll(framed(pairs, SPECIES, SPECIES, SP), SP, 1)
    coarse = framed(crates, COARSE, COARSE, CP) - jnp.where(row < COARSE, eye, 0.0)[:CP]
    coarse = coarse + pltpu.roll(framed(cpairs, COARSE, COARSE, CP), CP, 1)
    diff_row = framed(diff, 1, SPECIES, 8)[0:1]
    d12[...] = jnp.broadcast_to(column(diff_row, SP) / 12.0, (SP, COLS))
    dc12[...] = jnp.broadcast_to(column(framed(cdiff, 1, COARSE, 8)[0:1], CP) / 12.0, (CP, COLS))
    mi[...] = jnp.full((SP, 128), -1, jnp.int32)
    mi[:SPECIES, 0:1] = smap[...]
    map_column = mi[:, 0:1]
    map_row = jnp.sum(jnp.where(row == lane, map_column, 0), axis=0, keepdims=True)
    lum = jnp.where((map_row == row[:CP]) & (lane[:CP] < SPECIES), 1.0, 0.0)
    counts = jnp.sum(lum, axis=1, keepdims=True)
    share[...] = jnp.broadcast_to(1.0 / jnp.maximum(counts, 1.0), (CP, COLS))
    lumped = jnp.dot(lum[:, :SP], fine, precision=lax.Precision.HIGHEST, preferred_element_type=F32)
    fh, fl = halves(fine)
    rh, rl = halves(lumped)
    dh, dl = halves(lum * diff_row)
    ch, cl = halves(coarse)
    f = jnp.concatenate([fh, fl], axis=0).astype(BF16)
    r = jnp.concatenate([rh, rl, lum, dh, dl, jnp.zeros((8, 128), F32)], axis=0).astype(BF16)
    for at in (0, 128):
        wf[:, at : at + 128] = f
        wr[:, at : at + 128] = r
        wfr[: 2 * SP, at : at + 128] = f
        wfr[2 * SP :, at : at + 128] = r
    v = jnp.concatenate([lum, dh, dl, jnp.zeros((8, 128), F32)], axis=0)
    lv[...] = (v + pltpu.roll(v, 64, 1)).astype(BF16)
    c = jnp.concatenate([ch, cl], axis=0)
    wc[...] = (c + pltpu.roll(c, 64, 1)).astype(BF16)
    lane96 = lax.broadcasted_iota(jnp.int32, (SP, 96), 1)
    pro[...] = jnp.where(map_column == lane96 % 32, 1.0, 0.0).astype(BF16)


def first_kernel(info, u, outer, inner):
    at_top = info[0] == 0
    for m in range(3):
        for r in range(2):
            first, last = u[m, :, r, :], u[m, :, ROWS - 2 + r, :]
            for out, value in ((outer, jnp.where(at_top, first, last)), (inner, jnp.where(at_top, last, first))):
                out[m, r, SP - 8 :, :] = zeros(8)
                out[m, r, :SPECIES, :] = value


def restricted(y):
    return y[0:24] + y[24:48], y[48:72], y[72:96] + y[96:120]


MIX0 = [STEP * w for w in W0]
MIXS = [STEP * W1[0], STEP * W1[1] - HALF, STEP * W1[2]]


def mixed(factors, values):
    return factors[0] * values[0] + factors[1] * values[1] + factors[2] * values[2]


def old_kernel(u, wf, wr, wc, d12, dc12, n1, s, r0, e0, c0, ut, p0s, pss, v0s):
    for x in range(ROWS):
        for m in range(3):
            ut[x, m, SP - 8 :, :] = zeros(8)
            ut[x, m, :SPECIES, :] = u[m, :, x, :]
        us = [ut[x, m] for m in range(3)]
        qs = [v * v for v in us]
        p0, ps = mixed(MIX0, us), mixed(MIXS, us)
        y = dot(wf[...], stacked(p0, mixed(MIX0, qs)))
        n1[x] = us[0] + (y[:SP] + y[SP:]) + d12[...] * lap_y(p0)
        y = dot(wf[...], stacked(ps, mixed(MIXS, qs)))
        s[x] = (y[:SP] + y[SP:]) + d12[...] * lap_y(ps)
        r, c, v = restricted(dot(wr[...], stacked(us[0], qs[0])))
        r0[x] = r + lap_y(v) * (1.0 / 12.0)
        y = dot(wc[...], stacked(c, c * c))
        e0[x] = (y[:CP] + y[CP:]) + dc12[...] * lap_y(c)
        p0s[x], pss[x], v0s[x], c0[x] = p0, ps, v, c
    for x in range(ROWS):
        n1[x] += d12[...] * lap_x(lambda i: p0s[i], x, 0, ROWS)
        s[x] += d12[...] * lap_x(lambda i: pss[i], x, 0, ROWS)
        r0[x] += lap_x(lambda i: v0s[i], x, 0, ROWS) * (1.0 / 12.0)
        e0[x] += dc12[...] * lap_x(lambda i: c0[i], x, 0, ROWS)


def lumped_halo(lv, row):
    y = dot(lv[...], split(jnp.concatenate([row, zeros(8)], axis=0)))
    return y[0:24], y[24:48] + y[48:72]


SIDES = (((0, 1), (1, 0)), ((ROWS - 1, ROWS - 2), (0, 1)))


def pick_halo(info, side, outer, inner):
    take = info[0] == side
    return lambda *at: jnp.where(take, outer[at], inner[at])


def send(info, outer, inner, tops, bottoms):
    at_top = info[0] == 0
    for r, (top, bottom) in enumerate(zip(tops, bottoms)):
        outer[r] = jnp.where(at_top, top, bottom)
        inner[r] = jnp.where(at_top, bottom, top)


def old_edge_kernel(info, uo, ui, lv, d12, dc12, n1i, si, r0i, e0i, n1, s, r0, e0, outer, inner):
    for side, (rows, order) in enumerate(SIDES):
        halo = pick_halo(info, side, uo, ui)
        us = [[halo(m, r) for m in range(3)] for r in order]
        p0 = beside(*[mixed(MIX0, v) for v in us])
        ps = beside(*[mixed(MIXS, v) for v in us])
        lumped = [lumped_halo(lv, v[0]) for v in us]
        c = beside(lumped[0][0], lumped[1][0])
        v = beside(lumped[0][1], lumped[1][1])
        for i, x in enumerate(rows):
            n1[x] = n1i[x] + d12[...] * p0[i]
            s[x] = si[x] + d12[...] * ps[i]
            r0[x] = r0i[x] + v[i] * (1.0 / 12.0)
            e0[x] = e0i[x] + dc12[...] * c[i]
    send(info, outer, inner, [n1[0], n1[1]], [n1[ROWS - 2], n1[ROWS - 1]])


def mid_kernel(n1, s, wfr, wc, d12, dc12, n2, r1, e1, c1, v1s):
    for x in range(ROWS):
        n = n1[x]
        y = dot(wfr[...], stacked(n, n * n))
        lap = lap_y(n) + lap_x(lambda i: n1[i], x, 0, ROWS)
        n2[x] = n + HALF * ((y[:SP] + y[SP : 2 * SP]) + d12[...] * lap) + s[x]
        r, c, v = restricted(y[2 * SP :])
        r1[x] = r + lap_y(v) * (1.0 / 12.0)
        y = dot(wc[...], stacked(c, c * c))
        e1[x] = (y[:CP] + y[CP:]) + dc12[...] * lap_y(c)
        v1s[x], c1[x] = v, c
    for x in range(ROWS):
        r1[x] += lap_x(lambda i: v1s[i], x, 0, ROWS) * (1.0 / 12.0)
        e1[x] += dc12[...] * lap_x(lambda i: c1[i], x, 0, ROWS)


def lumped_old(first, c0, e0):
    return jnp.where(first, c0, -HALF * e0)


def piece_a(first, x, g2, r0, r1, e0, c0):
    return mixed(MIX0, (r0[x], r1[x], g2)) + lumped_old(first, c0[x], e0[x])


def mid_edge_kernel(info, no, ni, lv, wr, d12, dc12, r0, e0, c0, n2i, r1i, e1i, n2, r1, e1, outer, inner):
    first = info[1] == 0
    messages = []
    for side, (rows, order) in enumerate(SIDES):
        halo = pick_halo(info, side, no, ni)
        ns = [halo(r) for r in order]
        lumped = [lumped_halo(lv, v) for v in ns]
        c = beside(lumped[0][0], lumped[1][0])
        v = beside(lumped[0][1], lumped[1][1])
        n = beside(*ns)
        for i, x in enumerate(rows):
            n2[x] = n2i[x] + (HALF * d12[...]) * n[i]
            r1[x] = r1i[x] + v[i] * (1.0 / 12.0)
            e1[x] = e1i[x] + dc12[...] * c[i]
        step = 1 if side == 0 else -1
        near = [rows[0] + step * i for i in range(4)]
        terms = [restricted(dot(wr[...], stacked(n2[x], n2[x] * n2[x]))) for x in near[:2]]
        terms += [restricted(dot(wr[...], stacked(n2i[x], n2i[x] * n2i[x]))) for x in near[2:]]
        vs = [t[2] for t in terms]
        laps = [16.0 * vs[1] - vs[2], 16.0 * (vs[0] + vs[2]) - vs[3]]
        pieces = [
            piece_a(first, x, terms[i][0] + (lap_y(vs[i]) + laps[i]) * (1.0 / 12.0), r0, r1, e0, c0)
            for i, x in enumerate(rows)
        ]
        messages.append(pieces[::step] + vs[:2][::step])
    send(info, outer, inner, *messages)


def row_a(x):
    return x + 2


def row_b(x):
    return x + 4 + ROWS


def last_kernel(info, n2, wr, r0, r1, e0, e1, c0, ab, c2, v2s):
    first = info[1] == 0
    gs = []
    for x in range(ROWS):
        r, c, v = restricted(dot(wr[...], stacked(n2[x], n2[x] * n2[x])))
        gs.append(r + lap_y(v) * (1.0 / 12.0))
        v2s[x], c2[x] = v, c
    for x in range(ROWS):
        g2 = gs[x] + lap_x(lambda i: v2s[i], x, 0, ROWS) * (1.0 / 12.0)
        ab[row_a(x)] = piece_a(first, x, g2, r0, r1, e0, c0)
        ab[row_b(x)] = (
            (STEP * W1[0]) * r0[x] + (STEP * W1[1]) * r1[x] + (STEP * W1[2]) * g2 - HALF * e1[x]
        )


def last_edge_kernel(info, mo, mi, ho, hi, abi, ab, outer, inner):
    ka, kb = STEP * W0[2] / 12.0, STEP * W1[2] / 12.0
    for side, (rows, order) in enumerate(SIDES):
        inside = info[2] > 0 if side == 0 else info[2] < SLABS - 1
        own, halo = pick_halo(info, side, mo, mi), pick_halo(info, side, ho, hi)
        fix = beside(*[halo(2 + r) for r in order])
        theirs = beside(*[own(2 + r) for r in order[::-1]])
        step = 1 if side == 0 else -1
        for i, x in enumerate(rows):
            ab[row_a(x)] = abi[row_a(x)] + ka * fix[i]
            ab[row_b(x)] = abi[row_b(x)] + kb * fix[i]
            ab[row_a(rows[0] - step * (i + 1))] = jnp.where(inside, halo(order[i]) + ka * theirs[i], 0.0)
    tops = [abi[row_a(x)] for x in range(2, 6)] + [ab[row_b(x)] for x in (0, 1)] + [abi[row_b(x)] for x in (2, 3)]
    bottoms = [abi[row_a(x)] for x in range(10, 14)] + [abi[row_b(x)] for x in (12, 13)]
    bottoms += [ab[row_b(x)] for x in (14, 15)]
    send(info, outer, inner, tops, bottoms)


AB_ROWS, EXT_ROWS = 2 * ROWS + 4, 2 * ROWS + 20


def extend_kernel(info, ab, eo, ei, ext):
    for x in range(AB_ROWS):
        ext[x] = ab[x]
    for side in range(2):
        halo = pick_halo(info, side, eo, ei)
        for r in range(8):
            ext[AB_ROWS + 8 * side + r] = halo(r)


def ext_a(ext, x):
    if -2 <= x < ROWS + 2:
        return ext[row_a(x)]
    return ext[AB_ROWS + x + 6] if x < 0 else ext[AB_ROWS + 8 + x - (ROWS + 2)]


def ext_b(ext, x):
    if 0 <= x < ROWS:
        return ext[row_b(x)]
    return ext[AB_ROWS + 4 + x + 4] if x < 0 else ext[AB_ROWS + 12 + x - ROWS]


def swept(info, z, x, reach, add, wc, dc12):
    value = z(x)
    y = dot(wc[...], stacked(value, value * value))
    lap = lap_y(value) + lap_x(z, x, -reach, ROWS + reach)
    value = value + HALF * ((y[:CP] + y[CP:]) + dc12[...] * lap) + add
    if x < 0:
        value = jnp.where(info[2] > 0, value, 0.0)
    elif x >= ROWS:
        value = jnp.where(info[2] < SLABS - 1, value, 0.0)
    return value


def begin(info, z0, zo, zi, depth):
    top, bottom = pick_halo(info, 0, zo, zi), pick_halo(info, 1, zo, zi)

    def row(x):
        if x < 0:
            return top(x + depth)
        return bottom(x - ROWS) if x >= ROWS else z0[x]

    return row


def from_scratch(ref, reach):
    return lambda x: ref[x + reach]


def give(info, depth, message, outer, inner, value):
    for x in range(ROWS):
        message[x] = value(x)
    send(info, outer, inner, [value(x) for x in range(depth)], [value(x) for x in range(ROWS - depth, ROWS)])


def start_kernel(info, ab, wc, dc12, result, message, outer, inner):
    @pl.when(info[1] == 0)
    def _():
        z1 = lambda x: ab[row_a(x)]
        for x in range(ROWS):
            result[x] = zeros(CP)
            result[ROWS + x] = z1(x)
            result[2 * ROWS + x] = swept(info, z1, x, 2, ab[row_b(x)], wc, dc12)
        give(info, 8, message, outer, inner, lambda x: result[2 * ROWS + x])


def pair_kernel(at, depth, info, z0, zo, zi, exta, abb, wc, dc12, ra, rb, message, outer, inner, za, zb, zc):
    @pl.when(info[1] == at)
    def _():
        z = begin(info, z0, zo, zi, 8)
        for x in range(-6, ROWS + 6):
            za[x + 6] = swept(info, z, x, 8, ext_a(exta, x), wc, dc12)
        z = from_scratch(za, 6)
        for x in range(-4, ROWS + 4):
            zb[x + 4] = swept(info, z, x, 6, ext_b(exta, x), wc, dc12)
        z = from_scratch(zb, 4)
        for x in range(-2, ROWS + 2):
            zc[x + 2] = swept(info, z, x, 4, abb[row_a(x)], wc, dc12)
        z = from_scratch(zc, 2)
        for x in range(ROWS):
            ra[x], ra[ROWS + x], ra[2 * ROWS + x] = z0[x], za[x + 6], zb[x + 4]
            rb[x], rb[ROWS + x] = zb[x + 4], zc[x + 2]
            rb[2 * ROWS + x] = swept(info, z, x, 2, abb[row_b(x)], wc, dc12)
        give(info, depth, message, outer, inner, lambda x: rb[2 * ROWS + x])


def single_kernel(at, info, z0, zo, zi, ab, wc, dc12, result, za):
    @pl.when(info[1] == at)
    def _():
        z = begin(info, z0, zo, zi, 4)
        for x in range(-2, ROWS + 2):
            za[x + 2] = swept(info, z, x, 4, ab[row_a(x)], wc, dc12)
        z = from_scratch(za, 2)
        for x in range(ROWS):
            result[x], result[ROWS + x] = z0[x], za[x + 2]
            result[2 * ROWS + x] = swept(info, z, x, 2, ab[row_b(x)], wc, dc12)


def base_kernel(n1, n2, c1, c2, pro, share, b1, b2):
    for x in range(ROWS):
        for n, c, b in ((n1, c1, b1), (n2, c2, b2)):
            value = thirds(jnp.concatenate([share[...] * c[x], zeros(8)], axis=0))
            b[:, x, :] = (n[x] - dot(pro[...], value))[:SPECIES]


def out_kernel(info, where, u, b0, b1, b2, share, *refs):
    results, (out, z, spread, sem) = refs[:SLICES], refs[SLICES:]
    for p in range(SLICES):

        @pl.when(info[1] == p)
        def _():
            copy = pltpu.make_async_copy(results[p], z, sem)
            copy.start()
            copy.wait()

    for m in range(3):
        for x in range(ROWS):
            spread[m, :, x, :] = share[...] * z[m * ROWS + x]
    first = info[1] == 0
    for s in range(SPECIES):
        to = where[s]
        out[0, s] = jnp.where(first, u[0, s], b0[s]) + spread[0, to]
        out[1, s] = b1[s] + spread[1, to]
        out[2, s] = b2[s] + spread[2, to]


def field(*shape):
    return jax.ShapeDtypeStruct(shape + (COLS,), F32)


SMEM = pl.BlockSpec(memory_space=pltpu.SMEM)
VMEM = pl.BlockSpec(memory_space=pltpu.VMEM)
ANY = pl.BlockSpec(memory_space=pl.ANY)


def call(kernel, name, outs, *args, specs=None, scratch=(), alias=None):
    specs = specs or [SMEM if a.dtype == jnp.int32 and a.ndim == 1 else VMEM for a in args]
    return pl.pallas_call(
        kernel,
        out_shape=outs,
        in_specs=specs,
        scratch_shapes=[pltpu.VMEM(f.shape, f.dtype) if isinstance(f, jax.ShapeDtypeStruct) else f for f in scratch],
        input_output_aliases=alias or {},
        compiler_params=pltpu.CompilerParams(vmem_limit_bytes=VMEM_LIMIT),
        name=name,
    )(*args)


AXES = ("tm", "space")
OUTER = [(s, s + 1) for s in range(1, SLABS - 1, 2)] + [(s + 1, s) for s in range(1, SLABS - 1, 2)]
INNER = [(s, s ^ 1) for s in range(SLABS)]
SAME = [(s, s) for s in range(SLABS)]


def moved(value, slices, slabs):
    route = [(p * SLABS + s, q * SLABS + t) for p, q in slices for s, t in slabs]
    return lax.ppermute(value, AXES, route)


def swap(outer, inner, slices=tuple(range(SLICES))):
    pairs = [(p, p) for p in slices]
    got_inner = moved(inner, pairs, INNER)
    got_outer = moved(outer, pairs, OUTER)
    return got_outer, got_inner


def hop(message, outer, inner, p, q):
    return moved(message, [(p, q)], SAME), moved(outer, [(p, q)], OUTER), moved(inner, [(p, q)], INNER)


def after(value, other):
    return lax.optimization_barrier((value, other))[0]


def local(fine_nodes, fine_rates, fine_pairs, fine_diff, coarse_rates, coarse_pairs, coarse_diff, species_map):
    slice_at, slab = lax.axis_index("tm"), lax.axis_index("space")
    info = jnp.stack([slab % 2, slice_at, slab]).astype(jnp.int32)
    nodes = fine_nodes[0]
    fine, coarse = field(ROWS, SP), field(ROWS, CP)
    message = field(3, 2, SP)
    outer, inner = call(first_kernel, "first", [message, message], info, nodes)
    uo, ui = swap(outer, inner)

    def bf16(*shape):
        return jax.ShapeDtypeStruct(shape, BF16)

    wf, wr, wfr, lv, wc, pro, d12, dc12, share = call(
        prep_kernel,
        "prep",
        [bf16(2 * SP, 256), bf16(128, 256), bf16(2 * SP + 128, 256), bf16(80, 128), bf16(2 * CP, 128), bf16(SP, 96)]
        + [field(SP), field(CP), field(CP)],
        fine_rates,
        fine_pairs,
        fine_diff.reshape(1, SPECIES),
        coarse_rates,
        coarse_pairs,
        coarse_diff.reshape(1, COARSE),
        species_map,
        scratch=[pltpu.VMEM((SP, 128), F32), pltpu.VMEM((SP, 128), jnp.int32)],
    )
    n1, s, r0, e0, c0 = call(
        old_kernel,
        "old",
        [fine, fine, coarse, coarse, coarse],
        *(nodes, wf, wr, wc, d12, dc12),
        scratch=[field(ROWS, 3, SP), fine, fine, coarse],
    )
    two, four, eight = field(2, SP), field(4, CP), field(8, CP)
    n1, s, r0, e0, outer, inner = call(
        old_edge_kernel,
        "old_edge",
        [fine, fine, coarse, coarse, two, two],
        *(info, uo, ui, lv, d12, dc12, n1, s, r0, e0),
        alias={6: 0, 7: 1, 8: 2, 9: 3},
    )
    no, ni = swap(outer, inner)
    n2, r1, e1, c1 = call(
        mid_kernel, "mid", [fine, coarse, coarse, coarse], n1, s, wfr, wc, d12, dc12, scratch=[coarse]
    )
    n2, r1, e1, outer, inner = call(
        mid_edge_kernel,
        "mid_edge",
        [fine, coarse, coarse, four, four],
        *(info, no, ni, lv, wr, d12, dc12, r0, e0, c0, n2, r1, e1),
        alias={10: 0, 11: 1, 12: 2},
    )
    ho, hi = swap(outer, inner)
    pieces, extended = field(AB_ROWS, CP), field(EXT_ROWS, CP)
    ab, c2 = call(
        last_kernel, "last", [pieces, coarse], *(info, n2, wr, r0, r1, e0, e1, c0), scratch=[coarse]
    )
    ab, ext_outer, ext_inner = call(
        last_edge_kernel, "last_edge", [pieces, eight, eight], info, outer, inner, ho, hi, ab, alias={5: 0}
    )

    result = field(3 * ROWS, CP)
    result0, *sent = call(start_kernel, "start", [result, coarse, eight, eight], info, ab, wc, dc12)
    z = hop(*sent, 0, 1)
    ext_outer, ext_inner = after(ext_outer, sent[0]), after(ext_inner, sent[0])
    eo, ei = swap(ext_outer, ext_inner, (1, 3, 5))
    ext = call(extend_kernel, "extend", extended, info, ab, eo, ei)
    ab_two = moved(after(ab, sent[0]), [(2, 1)], SAME)
    ext_odd = moved(ext, [(3, 4), (5, 6)], SAME)

    def pair(at, depth, z, exta, abb):
        return call(
            functools.partial(pair_kernel, at, depth),
            "pair",
            [result, result, coarse, field(depth, CP), field(depth, CP)],
            *(info, *z, exta, abb, wc, dc12),
            scratch=[field(ROWS + 12, CP), field(ROWS + 8, CP), field(ROWS + 4, CP)],
        )

    result1, rb, *sent = pair(1, 8, z, ext, ab_two)
    z = hop(*sent, 1, 4)
    result2 = moved(rb, [(1, 2)], SAME)
    b1, b2 = call(base_kernel, "base", [field(SPECIES, ROWS)] * 2, after(n1, result0), n2, c1, c2, pro, share)
    b0 = moved(b2, [(p, p + 1) for p in range(SLICES - 1)], SAME)
    ra, result4, *sent = pair(4, 8, z, ext_odd, ab)
    z = hop(*sent, 4, 6)
    result3 = moved(ra, [(4, 3)], SAME)
    ra, result6, *sent = pair(6, 4, z, ext_odd, ab)
    z = hop(*sent, 6, 7)
    result5 = moved(ra, [(6, 5)], SAME)
    result7 = call(
        functools.partial(single_kernel, 7),
        "single",
        result,
        *(info, *z, ab, wc, dc12),
        scratch=[field(ROWS + 4, CP)],
    )
    results = [result0, result1, result2, result3, result4, result5, result6, result7]
    out = call(
        out_kernel,
        "out",
        field(3, SPECIES, ROWS),
        *(info, species_map[:, 0], nodes, b0, b1, b2, share, *results),
        specs=[SMEM, SMEM] + [VMEM] * 5 + [ANY] * SLICES,
        scratch=[result, field(3, CP, ROWS), pltpu.SemaphoreType.DMA],
    )
    return out[None]


def solution(mesh):
    in_specs = (P("tm", None, None, "space", None), P(), P(), P(), P(), P(), P(), P())
    out_specs = P("tm", None, None, "space", None)
    return jax.shard_map(local, mesh=mesh, in_specs=in_specs, out_specs=out_specs, check_vma=False)
```

profile of v0, /device:TPU:114, one launch (start us, length us, event | category | flops | bytes accessed | tf_op | source)
XLA Modules:
  0.0 170.9 jit_solution(5109809880170062790)
XLA Ops:
  0.1 1.7 %copy-done = f32[1,3,53,16,256]{4,3,2,1,0:T(8,128)S(1)} copy-done((f32[1,3,53,16,256]{4,3,2,1,0:T(8,128)S(1)}, f32[1,3,53,16,256]{4,3,2,1,0:T(8,128)}, u32[]{:S(2)}) %copy-start) | copy-done | bytes 2605080
  1.8 1.8 %first.1 = (f32[3,2,56,256]{3,2,1,0:T(8,128)}, f32[3,2,56,256]{3,2,1,0:T(8,128)}) custom-call(s32[3]{0:T(128)S(1)} %pad_add_fusion.info, f32[3,53,16,256]{3,2,1,0:T(8,128)S(1)} %bitcast.9), custom_call_target="tpu_custom_call" | custom-call | tf_op jit(solution)/shard_map/first/pallas_call | solution.py:431
  3.6 3.3 %collective-permute-start = (f32[3,2,56,256]{3,2,1,0:T(8,128)}, f32[3,2,56,256]{3,2,1,0:T(8,128)S(1)}, u32[]{:S(2)}, u32[]{:S(2)}) collective-permute-start(f32[3,2,56,256]{3,2,1,0:T(8,128)} %get-tuple-element.66), channel_id=1, source_target_pairs={{1,2},{3,4},{5,6},{7,8},{9,10},{11,12},{13,14},{2,1},{4,3},{6,5},{... | collective-permute-start | bytes 1032200 | tf_op jit(solution)/shard_map/ppermute | solution.py:450
  7.0 0.9 collective-permute-start.1
  8.0 0.7 copy-done.6
  9.0 5.4 %old.1 = (f32[16,56,256]{2,1,0:T(8,128)S(1)}, f32[16,56,256]{2,1,0:T(8,128)S(1)}, f32[16,24,256]{2,1,0:T(8,128)S(1)}, f32[16,24,256]{2,1,0:T(8,128)S(1)}, f32[16,24,256]{2,1,0:T(8,128)S(1)}) custom-call(f32[3,53,16,256]{3,2,1,0:T(8,128)S(1)} %bitcast.10, bf16[112,256]{1,0:T(8,128)(2,1)S(1)} %get-tuple-element.71.wf, ...), custom_call_target="tpu_custom_call" | custom-call | tf_op jit(solution)/shard_map/old/pallas_call | solution.py:431
  14.4 3.0 %collective-permute-done.uo = f32[3,2,56,256]{3,2,1,0:T(8,128)S(1)} collective-permute-done((f32[3,2,56,256]{3,2,1,0:T(8,128)}, f32[3,2,56,256]{3,2,1,0:T(8,128)S(1)}, u32[]{:S(2)}, u32[]{:S(2)}) %collective-permute-start) | collective-permute-done | bytes 344096 | tf_op jit(solution)/shard_map/ppermute | solution.py:450
  17.5 0.9 old_edge.1
  18.4 4.3 %collective-permute-start.2 = (f32[2,56,256]{2,1,0:T(8,128)S(1)}, f32[2,56,256]{2,1,0:T(8,128)S(1)}, u32[]{:S(2)}, u32[]{:S(2)}) collective-permute-start(f32[2,56,256]{2,1,0:T(8,128)S(1)} %get-tuple-element.79), channel_id=1, source_target_pairs={{1,2},{3,4},{5,6},{7,8},{9,10},{11,12},{13,14},{2,1},{4,3},{6,5},{... | collective-permute-start | bytes 344072 | tf_op jit(solution)/shard_map/ppermute | solution.py:450
  22.7 2.7 %mid.1 = (f32[16,56,256]{2,1,0:T(8,128)S(1)}, f32[16,24,256]{2,1,0:T(8,128)S(1)}, f32[16,24,256]{2,1,0:T(8,128)S(1)}, f32[16,24,256]{2,1,0:T(8,128)S(1)}) custom-call(f32[16,56,256]{2,1,0:T(8,128)S(1)} %get-tuple-element.97.n1, f32[16,56,256]{2,1,0:T(8,128)S(1)} %get-tuple-element.84.s, bf16[240,256]{1,0:T(8,128)(2,1)S(1)} %get-tuple-element.85.wfr, ...), custom_call_target="tpu_custom_call" | custom-call | tf_op jit(solution)/shard_map/mid/pallas_call | solution.py:431
  25.4 1.5 collective-permute-done.2.no
  26.9 1.1 mid_edge.1
  28.0 4.7 %collective-permute-start.4 = (f32[4,24,256]{2,1,0:T(8,128)S(1)}, f32[4,24,256]{2,1,0:T(8,128)S(1)}, u32[]{:S(2)}, u32[]{:S(2)}) collective-permute-start(f32[4,24,256]{2,1,0:T(8,128)S(1)} %get-tuple-element.89.mo), channel_id=1, source_target_pairs={{1,2},{3,4},{5,6},{7,8},{9,10},{11,12},{13,14},{2,1},{4,3},{6,5},{... | collective-permute-start | bytes 294920 | tf_op jit(solution)/shard_map/ppermute | solution.py:450
  32.8 1.4 last.1
  34.3 2.1 %collective-permute-done.4.ho = f32[4,24,256]{2,1,0:T(8,128)S(1)} collective-permute-done((f32[4,24,256]{2,1,0:T(8,128)S(1)}, f32[4,24,256]{2,1,0:T(8,128)S(1)}, u32[]{:S(2)}, u32[]{:S(2)}) %collective-permute-start.4) | collective-permute-done | bytes 98336 | tf_op jit(solution)/shard_map/ppermute | solution.py:450
  36.4 0.6 last_edge.1
  37.6 0.9 collective-permute-start.10
  38.5 0.7 collective-permute-start.11
  39.1 0.7 collective-permute-start.12
  39.9 0.6 extend.1.exta
  40.5 0.7 collective-permute-start.17
  41.3 0.7 collective-permute-start.7
  42.0 0.7 collective-permute-start.8
  42.6 0.7 collective-permute-start.9
  43.4 0.6 pair.3
  43.9 0.7 collective-permute-start.14
  44.6 0.7 collective-permute-start.15
  45.3 0.7 collective-permute-start.16
  46.0 1.6 pair.4
  47.6 1.0 copy-done.3
  48.6 0.7 collective-permute-start.19
  49.3 0.7 collective-permute-start.20
  50.0 0.7 collective-permute-start.21
  50.7 0.7 collective-permute-start.13
  51.4 1.7 %collective-permute-start.18 = (f32[48,24,256]{2,1,0:T(8,128)}, f32[48,24,256]{2,1,0:T(8,128)}, u32[]{:S(2)}, u32[]{:S(2)}) collective-permute-start(f32[48,24,256]{2,1,0:T(8,128)} %get-tuple-element.117), channel_id=1, source_target_pairs={{64,48},{65,49},{66,50},{67,51},{68,52},{69,53},{70,54},{71,55},{7... | collective-permute-start | bytes 3538952 | tf_op jit(solution)/shard_map/ppermute | solution.py:450
  53.7 1.0 copy-done.4
  54.7 1.7 collective-permute-start.22
  56.4 1.0 base.1
  57.4 1.3 collective-permute-start.6
  58.7 1.3 collective-permute-start.24
  60.0 67.7 %collective-permute-done.24.zo = f32[4,24,256]{2,1,0:T(8,128)S(1)} collective-permute-done((f32[4,24,256]{2,1,0:T(8,128)S(1)}, f32[4,24,256]{2,1,0:T(8,128)S(1)}, u32[]{:S(2)}, u32[]{:S(2)}) %collective-permute-start.24) | collective-permute-done | bytes 98336 | tf_op jit(solution)/shard_map/ppermute | solution.py:450
  127.7 1.3 collective-permute-start.25
  129.0 20.2 %collective-permute-done.25.zi = f32[4,24,256]{2,1,0:T(8,128)S(1)} collective-permute-done((f32[4,24,256]{2,1,0:T(8,128)S(1)}, f32[4,24,256]{2,1,0:T(8,128)S(1)}, u32[]{:S(2)}, u32[]{:S(2)}) %collective-permute-start.25) | collective-permute-done | bytes 98336 | tf_op jit(solution)/shard_map/ppermute | solution.py:450
  149.2 1.3 collective-permute-start.23
  150.5 11.9 %collective-permute-done.23.z0 = f32[16,24,256]{2,1,0:T(8,128)S(1)} collective-permute-done((f32[16,24,256]{2,1,0:T(8,128)S(1)}, f32[16,24,256]{2,1,0:T(8,128)S(1)}, u32[]{:S(2)}, u32[]{:S(2)}) %collective-permute-start.23) | collective-permute-done | bytes 393248 | tf_op jit(solution)/shard_map/ppermute | solution.py:450
  162.5 1.7 %single.1.refs_7_ = f32[48,24,256]{2,1,0:T(8,128)S(1)} custom-call(s32[3]{0:T(128)S(1)} %pad_add_fusion.info, f32[16,24,256]{2,1,0:T(8,128)S(1)} %collective-permute-done.23.z0, f32[4,24,256]{2,1,0:T(8,128)S(1)} %collective-permute-done.24.zo, f32[4,24,256]{2,1,0:T(8,128)S(1)} %collective-permute-done.25.zi, f32[36,24,256]{2,1,0:T(8,128)S(1)} %get-tuple-element.111.ab.abb, ...), custom_call_target="tpu_custom_call" | custom-call | tf_op jit(solution)/shard_map/single/pallas_call | solution.py:431
  164.2 1.0 copy-done.2
  165.3 5.5 %out.1 = f32[3,53,16,256]{3,2,1,0:T(8,128)} custom-call(s32[3]{0:T(128)S(1)} %pad_add_fusion.info, s32[53]{0:T(128)S(1)} %bitcast.11, f32[3,53,16,256]{3,2,1,0:T(8,128)} %bitcast.8, f32[53,16,256]{2,1,0:T(8,128)S(1)} %collective-permute-done.6.b0, f32[53,16,256]{2,1,0:T(8,128)S(1)} %get-tuple-element.103.b1, f32[53,16,256]{2,1,0:T(8,128)S(1)} %get-tuple-element.102.b2, ...), custom_call_target="tpu_custom_call" | custom-call | tf_op jit(solution)/shard_map/out/pallas_call | solution.py:431
  (46 shorter events, 1.8 us)
Async XLA Ops:
  0.0 7.8 %copy-start.9 = (s32[53,1]{0,1:T(1,128)S(1)}, s32[53,1]{0,1:T(1,128)}, u32[]{:S(2)}) copy-start(s32[53,1]{0,1:T(1,128)} %param.15) | copy-start | bytes 640
  0.0 7.9 %copy-start.7 = (f32[21,21]{1,0:T(8,128)S(1)}, f32[21,21]{1,0:T(8,128)}, u32[]{:S(2)}) copy-start(f32[21,21]{1,0:T(8,128)} %crates.1) | copy-start | bytes 5296
  0.0 7.9 %copy-start.8 = (f32[21,21]{1,0:T(8,128)S(1)}, f32[21,21]{1,0:T(8,128)}, u32[]{:S(2)}) copy-start(f32[21,21]{1,0:T(8,128)} %cpairs.1) | copy-start | bytes 5296
  0.1 1.7 %copy-start = (f32[1,3,53,16,256]{4,3,2,1,0:T(8,128)S(1)}, f32[1,3,53,16,256]{4,3,2,1,0:T(8,128)}, u32[]{:S(2)}) copy-start(f32[1,3,53,16,256]{4,3,2,1,0:T(8,128)} %param.8) | copy-start | bytes 7815172
  1.8 6.1 %copy-start.5 = (f32[53,53]{1,0:T(8,128)S(1)}, f32[53,53]{1,0:T(8,128)}, u32[]{:S(2)}) copy-start(f32[53,53]{1,0:T(8,128)} %rates.1) | copy-start | bytes 33712
  1.8 6.1 %copy-start.10 = (f32[53]{0:T(128)S(1)}, f32[53]{0:T(128)}, u32[]{:S(2)}) copy-start(f32[53]{0:T(128)} %param.11) | copy-start | bytes 640
  1.8 6.1 %copy-start.11 = (f32[21]{0:T(128)S(1)}, f32[21]{0:T(128)}, u32[]{:S(2)}) copy-start(f32[21]{0:T(128)} %param.14) | copy-start | bytes 256
  1.8 7.1 %copy-start.1 = (f32[1,3,53,16,256]{4,3,2,1,0:T(8,128)S(1)}, f32[1,3,53,16,256]{4,3,2,1,0:T(8,128)}, u32[]{:S(2)}) copy-start(f32[1,3,53,16,256]{4,3,2,1,0:T(8,128)} %param.8) | copy-start | bytes 7815172
  3.6 13.9 %collective-permute-start = (f32[3,2,56,256]{3,2,1,0:T(8,128)}, f32[3,2,56,256]{3,2,1,0:T(8,128)S(1)}, u32[]{:S(2)}, u32[]{:S(2)}) collective-permute-start(f32[3,2,56,256]{3,2,1,0:T(8,128)} %get-tuple-element.66), channel_id=1, source_target_pairs={{1,2},{3,4},{5,6},{7,8},{9,10},{11,12},{13,14},{2,1},{4,3},{6,5},{... | collective-permute-start | bytes 1032200 | tf_op jit(solution)/shard_map/ppermute | solution.py:450
  7.0 10.5 %collective-permute-start.1 = (f32[3,2,56,256]{3,2,1,0:T(8,128)}, f32[3,2,56,256]{3,2,1,0:T(8,128)S(1)}, u32[]{:S(2)}, u32[]{:S(2)}) collective-permute-start(f32[3,2,56,256]{3,2,1,0:T(8,128)} %get-tuple-element.67), channel_id=1, source_target_pairs={{0,1},{1,0},{2,3},{3,2},{4,5},{5,4},{6,7},{7,6},{8,9},{9,8},{10,11... | collective-permute-start | bytes 1032200 | tf_op jit(solution)/shard_map/ppermute | solution.py:450
  8.0 0.8 copy-start.6
  18.4 8.5 %collective-permute-start.2 = (f32[2,56,256]{2,1,0:T(8,128)S(1)}, f32[2,56,256]{2,1,0:T(8,128)S(1)}, u32[]{:S(2)}, u32[]{:S(2)}) collective-permute-start(f32[2,56,256]{2,1,0:T(8,128)S(1)} %get-tuple-element.79), channel_id=1, source_target_pairs={{1,2},{3,4},{5,6},{7,8},{9,10},{11,12},{13,14},{2,1},{4,3},{6,5},{... | collective-permute-start | bytes 344072 | tf_op jit(solution)/shard_map/ppermute | solution.py:450
  22.7 4.3 %collective-permute-start.3 = (f32[2,56,256]{2,1,0:T(8,128)S(1)}, f32[2,56,256]{2,1,0:T(8,128)S(1)}, u32[]{:S(2)}, u32[]{:S(2)}) collective-permute-start(f32[2,56,256]{2,1,0:T(8,128)S(1)} %get-tuple-element.80), channel_id=1, source_target_pairs={{0,1},{1,0},{2,3},{3,2},{4,5},{5,4},{6,7},{7,6},{8,9},{9,8},{10,11... | collective-permute-start | bytes 344072 | tf_op jit(solution)/shard_map/ppermute | solution.py:450
  28.0 8.3 %collective-permute-start.4 = (f32[4,24,256]{2,1,0:T(8,128)S(1)}, f32[4,24,256]{2,1,0:T(8,128)S(1)}, u32[]{:S(2)}, u32[]{:S(2)}) collective-permute-start(f32[4,24,256]{2,1,0:T(8,128)S(1)} %get-tuple-element.89.mo), channel_id=1, source_target_pairs={{1,2},{3,4},{5,6},{7,8},{9,10},{11,12},{13,14},{2,1},{4,3},{6,5},{... | collective-permute-start | bytes 294920 | tf_op jit(solution)/shard_map/ppermute | solution.py:450
  32.7 3.6 %collective-permute-start.5 = (f32[4,24,256]{2,1,0:T(8,128)S(1)}, f32[4,24,256]{2,1,0:T(8,128)S(1)}, u32[]{:S(2)}, u32[]{:S(2)}) collective-permute-start(f32[4,24,256]{2,1,0:T(8,128)S(1)} %get-tuple-element.90.mi), channel_id=1, source_target_pairs={{0,1},{1,0},{2,3},{3,2},{4,5},{5,4},{6,7},{7,6},{8,9},{9,8},{10,11... | collective-permute-start | bytes 294920 | tf_op jit(solution)/shard_map/ppermute | solution.py:450
  37.6 2.3 %collective-permute-start.10 = (f32[8,24,256]{2,1,0:T(8,128)S(1)}, f32[8,24,256]{2,1,0:T(8,128)S(1)}, u32[]{:S(2)}, u32[]{:S(2)}) collective-permute-start(f32[8,24,256]{2,1,0:T(8,128)S(1)} %get-tuple-element.108), channel_id=1, source_target_pairs={{17,18},{19,20},{21,22},{23,24},{25,26},{27,28},{29,30},{18,17},{2... | collective-permute-start | bytes 589832 | tf_op jit(solution)/shard_map/ppermute | solution.py:450
  38.5 1.4 collective-permute-start.11
  39.1 4.2 %collective-permute-start.12 = (f32[36,24,256]{2,1,0:T(8,128)S(1)}, f32[36,24,256]{2,1,0:T(8,128)S(1)}, u32[]{:S(2)}, u32[]{:S(2)}) collective-permute-start(f32[36,24,256]{2,1,0:T(8,128)S(1)} %get-tuple-element.111.ab.abb), channel_id=1, source_target_pairs={{32,16},{33,17},{34,18},{35,19},{36,20},{37,21},{38,22},{39,23},{4... | collective-permute-start | bytes 2654216 | tf_op jit(solution)/shard_map/ppermute | solution.py:450
  40.5 5.5 %collective-permute-start.17 = (f32[52,24,256]{2,1,0:T(8,128)S(1)}, f32[52,24,256]{2,1,0:T(8,128)S(1)}, u32[]{:S(2)}, u32[]{:S(2)}) collective-permute-start(f32[52,24,256]{2,1,0:T(8,128)S(1)} %extend.1.exta), channel_id=1, source_target_pairs={{48,64},{49,65},{50,66},{51,67},{52,68},{53,69},{54,70},{55,71},{5... | collective-permute-start | bytes 3833864 | tf_op jit(solution)/shard_map/ppermute | solution.py:450
  41.3 2.1 %collective-permute-start.7 = (f32[16,24,256]{2,1,0:T(8,128)S(1)}, f32[16,24,256]{2,1,0:T(8,128)S(1)}, u32[]{:S(2)}, u32[]{:S(2)}) collective-permute-start(f32[16,24,256]{2,1,0:T(8,128)S(1)} %get-tuple-element.104), channel_id=1, source_target_pairs={{0,16},{1,17},{2,18},{3,19},{4,20},{5,21},{6,22},{7,23},{8,24},{9,... | collective-permute-start | bytes 1179656 | tf_op jit(solution)/shard_map/ppermute | solution.py:450
  42.0 1.4 collective-permute-start.8
  42.6 0.7 collective-permute-start.9
  43.9 2.1 %collective-permute-start.14 = (f32[16,24,256]{2,1,0:T(8,128)S(1)}, f32[16,24,256]{2,1,0:T(8,128)S(1)}, u32[]{:S(2)}, u32[]{:S(2)}) collective-permute-start(f32[16,24,256]{2,1,0:T(8,128)S(1)} %get-tuple-element.114), channel_id=1, source_target_pairs={{16,64},{17,65},{18,66},{19,67},{20,68},{21,69},{22,70},{23,71},{2... | collective-permute-start | bytes 1179656 | tf_op jit(solution)/shard_map/ppermute | solution.py:450
  44.6 1.4 collective-permute-start.15
  45.3 0.7 collective-permute-start.16
  47.6 1.0 copy-start.3
  48.6 4.5 %collective-permute-start.19 = (f32[16,24,256]{2,1,0:T(8,128)S(1)}, f32[16,24,256]{2,1,0:T(8,128)S(1)}, u32[]{:S(2)}, u32[]{:S(2)}) collective-permute-start(f32[16,24,256]{2,1,0:T(8,128)S(1)} %get-tuple-element.119), channel_id=1, source_target_pairs={{64,96},{65,97},{66,98},{67,99},{68,100},{69,101},{70,102},{71,103... | collective-permute-start | bytes 1179656 | tf_op jit(solution)/shard_map/ppermute | solution.py:450
  49.3 3.8 %collective-permute-start.20 = (f32[8,24,256]{2,1,0:T(8,128)S(1)}, f32[8,24,256]{2,1,0:T(8,128)S(1)}, u32[]{:S(2)}, u32[]{:S(2)}) collective-permute-start(f32[8,24,256]{2,1,0:T(8,128)S(1)} %get-tuple-element.120), channel_id=1, source_target_pairs={{65,98},{67,100},{69,102},{71,104},{73,106},{75,108},{77,110},{66,... | collective-permute-start | bytes 589832 | tf_op jit(solution)/shard_map/ppermute | solution.py:450
  50.0 3.2 %collective-permute-start.21 = (f32[8,24,256]{2,1,0:T(8,128)S(1)}, f32[8,24,256]{2,1,0:T(8,128)S(1)}, u32[]{:S(2)}, u32[]{:S(2)}) collective-permute-start(f32[8,24,256]{2,1,0:T(8,128)S(1)} %get-tuple-element.121), channel_id=1, source_target_pairs={{64,97},{65,96},{66,99},{67,98},{68,101},{69,100},{70,103},{71,102... | collective-permute-start | bytes 589832 | tf_op jit(solution)/shard_map/ppermute | solution.py:450
  50.7 114.6 %collective-permute-start.13 = (f32[48,24,256]{2,1,0:T(8,128)S(1)}, f32[48,24,256]{2,1,0:T(8,128)S(1)}, u32[]{:S(2)}, u32[]{:S(2)}) collective-permute-start(f32[48,24,256]{2,1,0:T(8,128)S(1)} %get-tuple-element.113), channel_id=1, source_target_pairs={{16,32},{17,33},{18,34},{19,35},{20,36},{21,37},{22,38},{23,39},{2... | collective-permute-start | bytes 3538952 | tf_op jit(solution)/shard_map/ppermute | solution.py:450
  51.4 113.8 %collective-permute-start.18 = (f32[48,24,256]{2,1,0:T(8,128)}, f32[48,24,256]{2,1,0:T(8,128)}, u32[]{:S(2)}, u32[]{:S(2)}) collective-permute-start(f32[48,24,256]{2,1,0:T(8,128)} %get-tuple-element.117), channel_id=1, source_target_pairs={{64,48},{65,49},{66,50},{67,51},{68,52},{69,53},{70,54},{71,55},{7... | collective-permute-start | bytes 3538952 | tf_op jit(solution)/shard_map/ppermute | solution.py:450
  53.7 1.0 copy-start.4
  54.7 110.5 %collective-permute-start.22 = (f32[48,24,256]{2,1,0:T(8,128)S(1)}, f32[48,24,256]{2,1,0:T(8,128)}, u32[]{:S(2)}, u32[]{:S(2)}) collective-permute-start(f32[48,24,256]{2,1,0:T(8,128)S(1)} %get-tuple-element.122), channel_id=1, source_target_pairs={{96,80},{97,81},{98,82},{99,83},{100,84},{101,85},{102,86},{103,87... | collective-permute-start | bytes 3538952 | tf_op jit(solution)/shard_map/ppermute | solution.py:450
  57.4 107.8 %collective-permute-start.6 = (f32[53,16,256]{2,1,0:T(8,128)S(1)}, f32[53,16,256]{2,1,0:T(8,128)S(1)}, u32[]{:S(2)}, u32[]{:S(2)}) collective-permute-start(f32[53,16,256]{2,1,0:T(8,128)S(1)} %get-tuple-element.102.b2), channel_id=1, source_target_pairs={{0,16},{1,17},{2,18},{3,19},{4,20},{5,21},{6,22},{7,23},{8,24},{9,... | collective-permute-start | bytes 2605064 | tf_op jit(solution)/shard_map/ppermute | solution.py:450
  58.7 69.0 %collective-permute-start.24 = (f32[4,24,256]{2,1,0:T(8,128)S(1)}, f32[4,24,256]{2,1,0:T(8,128)S(1)}, u32[]{:S(2)}, u32[]{:S(2)}) collective-permute-start(f32[4,24,256]{2,1,0:T(8,128)S(1)} %get-tuple-element.125), channel_id=1, source_target_pairs={{97,114},{99,116},{101,118},{103,120},{105,122},{107,124},{109,126... | collective-permute-start | bytes 294920 | tf_op jit(solution)/shard_map/ppermute | solution.py:450
  127.7 21.5 %collective-permute-start.25 = (f32[4,24,256]{2,1,0:T(8,128)S(1)}, f32[4,24,256]{2,1,0:T(8,128)S(1)}, u32[]{:S(2)}, u32[]{:S(2)}) collective-permute-start(f32[4,24,256]{2,1,0:T(8,128)S(1)} %get-tuple-element.126), channel_id=1, source_target_pairs={{96,113},{97,112},{98,115},{99,114},{100,117},{101,116},{102,119},... | collective-permute-start | bytes 294920 | tf_op jit(solution)/shard_map/ppermute | solution.py:450
  149.2 13.2 %collective-permute-start.23 = (f32[16,24,256]{2,1,0:T(8,128)S(1)}, f32[16,24,256]{2,1,0:T(8,128)S(1)}, u32[]{:S(2)}, u32[]{:S(2)}) collective-permute-start(f32[16,24,256]{2,1,0:T(8,128)S(1)} %get-tuple-element.124), channel_id=1, source_target_pairs={{96,112},{97,113},{98,114},{99,115},{100,116},{101,117},{102,118},... | collective-permute-start | bytes 1179656 | tf_op jit(solution)/shard_map/ppermute | solution.py:450
  164.2 1.0 copy-start.2
where the time goes:
time: 172 us; the launch traced here: 171 us
  waiting for transfers between devices  107 us (62%)
  starting transfers between devices  31.7 us (18%)
  Pallas kernels  26.3 us (15%)
  local copies, waits for them, and re-layouts  5.7 us (3%)
    ppermute x26, waiting for transfers between devices, moved(): return lax.ppermute(value, AXES, route)  107 us
    ppermute x26, starting transfers between devices, moved(): return lax.ppermute(value, AXES, route)  31.7 us
    pallas_call x16, Pallas kernels, call(): pl.pallas_call(kernel, out_shape=outs, in_specs=specs, scratch_shapes=[pl...  26.3 us
    unnamed x25, local copies, waits for them, and re-layouts  5.7 us
  transfers between devices with their start and end apart: 26, of which 6 were waited for; matrix products, arithmetic and copies ran while one was open for 0% of the time, Pallas kernels for 8%

commit v1 on v0

--- a/solution.py
+++ b/solution.py
@@ -216,13 +216,31 @@
     return jnp.where(first, c0, -HALF * e0)
 
 
-def piece_a(first, x, g2, r0, r1, e0, c0):
-    return mixed(MIX0, (r0[x], r1[x], g2)) + lumped_old(first, c0[x], e0[x])
-
-
-def mid_edge_kernel(info, no, ni, lv, wr, d12, dc12, r0, e0, c0, n2i, r1i, e1i, n2, r1, e1, outer, inner):
+def row_a(x):
+    return x + 2
+
+
+def row_b(x):
+    return x + 4 + ROWS
+
+
+AB_ROWS, EXT_ROWS = 2 * ROWS + 4, 2 * ROWS + 20
+
+
+def ext_a(x):
+    if -2 <= x < ROWS + 2:
+        return row_a(x)
+    return AB_ROWS + x + 6 if x < 0 else AB_ROWS + 8 + x - (ROWS + 2)
+
+
+def ext_b(x):
+    if 0 <= x < ROWS:
+        return row_b(x)
+    return AB_ROWS + 4 + x + 4 if x < 0 else AB_ROWS + 12 + x - ROWS
+
+
+def mid_edge_kernel(info, no, ni, lv, wr, d12, dc12, r0, e0, c0, n2i, r1i, e1i, n2, r1, e1, ab, c2, outer, inner, v2s):
     first = info[1] == 0
-    messages = []
     for side, (rows, order) in enumerate(SIDES):
         halo = pick_halo(info, side, no, ni)
         ns = [halo(r) for r in order]
@@ -234,83 +252,44 @@
             n2[x] = n2i[x] + (HALF * d12[...]) * n[i]
             r1[x] = r1i[x] + v[i] * (1.0 / 12.0)
             e1[x] = e1i[x] + dc12[...] * c[i]
-        step = 1 if side == 0 else -1
-        near = [rows[0] + step * i for i in range(4)]
-        terms = [restricted(dot(wr[...], stacked(n2[x], n2[x] * n2[x]))) for x in near[:2]]
-        terms += [restricted(dot(wr[...], stacked(n2i[x], n2i[x] * n2i[x]))) for x in near[2:]]
-        vs = [t[2] for t in terms]
-        laps = [16.0 * vs[1] - vs[2], 16.0 * (vs[0] + vs[2]) - vs[3]]
-        pieces = [
-            piece_a(first, x, terms[i][0] + (lap_y(vs[i]) + laps[i]) * (1.0 / 12.0), r0, r1, e0, c0)
-            for i, x in enumerate(rows)
-        ]
-        messages.append(pieces[::step] + vs[:2][::step])
-    send(info, outer, inner, *messages)
-
-
-def row_a(x):
-    return x + 2
-
-
-def row_b(x):
-    return x + 4 + ROWS
-
-
-def last_kernel(info, n2, wr, r0, r1, e0, e1, c0, ab, c2, v2s):
-    first = info[1] == 0
     gs = []
     for x in range(ROWS):
-        r, c, v = restricted(dot(wr[...], stacked(n2[x], n2[x] * n2[x])))
-        gs.append(r + lap_y(v) * (1.0 / 12.0))
-        v2s[x], c2[x] = v, c
-    for x in range(ROWS):
-        g2 = gs[x] + lap_x(lambda i: v2s[i], x, 0, ROWS) * (1.0 / 12.0)
-        ab[row_a(x)] = piece_a(first, x, g2, r0, r1, e0, c0)
-        ab[row_b(x)] = (
-            (STEP * W1[0]) * r0[x] + (STEP * W1[1]) * r1[x] + (STEP * W1[2]) * g2 - HALF * e1[x]
-        )
-
-
-def last_edge_kernel(info, mo, mi, ho, hi, abi, ab, outer, inner):
+        value = n2[x] if x in (0, 1, ROWS - 2, ROWS - 1) else n2i[x]
+        r, c2[x], v2s[x] = restricted(dot(wr[...], stacked(value, value * value)))
+        gs.append(r)
+    for x in range(ROWS):
+        edge = x in (0, 1, ROWS - 2, ROWS - 1)
+        mid, late = (r1[x], e1[x]) if edge else (r1i[x], e1i[x])
+        g2 = gs[x] + (lap_y(v2s[x]) + lap_x(lambda i: v2s[i], x, 0, ROWS)) * (1.0 / 12.0)
+        ab[row_a(x)] = mixed(MIX0, (r0[x], mid, g2)) + lumped_old(first, c0[x], e0[x])
+        ab[row_b(x)] = mixed([STEP * w for w in W1], (r0[x], mid, g2)) - HALF * late
+    top = [ab[row_a(x)] for x in range(6)] + [ab[row_b(x)] for x in range(4)] + [v2s[x] for x in range(2)]
+    bottom = [ab[row_a(x)] for x in range(ROWS - 6, ROWS)] + [ab[row_b(x)] for x in range(ROWS - 4, ROWS)]
+    send(info, outer, inner, top, bottom + [v2s[x] for x in range(ROWS - 2, ROWS)])
+
+
+def last_edge_kernel(info, mo, mi, ho, hi, abi, ab, short):
     ka, kb = STEP * W0[2] / 12.0, STEP * W1[2] / 12.0
+    done = {}
     for side, (rows, order) in enumerate(SIDES):
         inside = info[2] > 0 if side == 0 else info[2] < SLABS - 1
         own, halo = pick_halo(info, side, mo, mi), pick_halo(info, side, ho, hi)
-        fix = beside(*[halo(2 + r) for r in order])
-        theirs = beside(*[own(2 + r) for r in order[::-1]])
-        step = 1 if side == 0 else -1
+        fix = beside(*[halo(10 + r) for r in order])
+        theirs = beside(*[own(10 + r) for r in order[::-1]])
         for i, x in enumerate(rows):
-            ab[row_a(x)] = abi[row_a(x)] + ka * fix[i]
-            ab[row_b(x)] = abi[row_b(x)] + kb * fix[i]
-            ab[row_a(rows[0] - step * (i + 1))] = jnp.where(inside, halo(order[i]) + ka * theirs[i], 0.0)
-    tops = [abi[row_a(x)] for x in range(2, 6)] + [ab[row_b(x)] for x in (0, 1)] + [abi[row_b(x)] for x in (2, 3)]
-    bottoms = [abi[row_a(x)] for x in range(10, 14)] + [abi[row_b(x)] for x in (12, 13)]
-    bottoms += [ab[row_b(x)] for x in (14, 15)]
-    send(info, outer, inner, tops, bottoms)
-
-
-AB_ROWS, EXT_ROWS = 2 * ROWS + 4, 2 * ROWS + 20
-
-
-def extend_kernel(info, ab, eo, ei, ext):
-    for x in range(AB_ROWS):
-        ext[x] = ab[x]
-    for side in range(2):
-        halo = pick_halo(info, side, eo, ei)
-        for r in range(8):
-            ext[AB_ROWS + 8 * side + r] = halo(r)
-
-
-def ext_a(ext, x):
-    if -2 <= x < ROWS + 2:
-        return ext[row_a(x)]
-    return ext[AB_ROWS + x + 6] if x < 0 else ext[AB_ROWS + 8 + x - (ROWS + 2)]
-
-
-def ext_b(ext, x):
-    if 0 <= x < ROWS:
-        return ext[row_b(x)]
-    return ext[AB_ROWS + 4 + x + 4] if x < 0 else ext[AB_ROWS + 12 + x - ROWS]
+            done[row_a(x)] = abi[row_a(x)] + ka * fix[i]
+            done[row_b(x)] = abi[row_b(x)] + kb * fix[i]
+        for depth, at, to, factor in ((6, 0, ext_a, ka), (4, 6, ext_b, kb)):
+            for i in range(depth):
+                x = -1 - i if side == 0 else ROWS + i
+                value = halo(at + (depth - 1 - i if side == 0 else i))
+                if i < 2:
+                    value = value + factor * theirs[i]
+                done[to(x)] = jnp.where(inside, value, 0.0)
+    for at, value in done.items():
+        ab[at] = value
+    for at in range(AB_ROWS):
+        short[at] = done[at] if at in done else abi[at]
 
 
 def swept(info, z, x, reach, add, wc, dc12):
@@ -346,26 +325,31 @@
     send(info, outer, inner, [value(x) for x in range(depth)], [value(x) for x in range(ROWS - depth, ROWS)])
 
 
-def start_kernel(info, ab, wc, dc12, result, message, outer, inner):
-    @pl.when(info[1] == 0)
+def hosting(info, hosts):
+    return info[1] == jnp.where(info[0] == 0, hosts[0], hosts[1])
+
+
+def start_kernel(hosts, info, ab, wc, dc12, rb, message, outer, inner):
+    @pl.when(hosting(info, hosts))
     def _():
         z1 = lambda x: ab[row_a(x)]
         for x in range(ROWS):
-            result[x] = zeros(CP)
-            result[ROWS + x] = z1(x)
-            result[2 * ROWS + x] = swept(info, z1, x, 2, ab[row_b(x)], wc, dc12)
-        give(info, 8, message, outer, inner, lambda x: result[2 * ROWS + x])
-
-
-def pair_kernel(at, depth, info, z0, zo, zi, exta, abb, wc, dc12, ra, rb, message, outer, inner, za, zb, zc):
-    @pl.when(info[1] == at)
-    def _():
+            rb[x] = zeros(CP)
+            rb[ROWS + x] = z1(x)
+            rb[2 * ROWS + x] = swept(info, z1, x, 2, ab[row_b(x)], wc, dc12)
+        give(info, 8, message, outer, inner, lambda x: rb[2 * ROWS + x])
+
+
+def pair_kernel(
+    hosts, depth, info, z0, zo, zi, mine, short, long, wc, dc12, rai, rbi, ra, rb, message, outer, inner, za, zb, zc
+):
+    def sweep(exta, abb):
         z = begin(info, z0, zo, zi, 8)
         for x in range(-6, ROWS + 6):
-            za[x + 6] = swept(info, z, x, 8, ext_a(exta, x), wc, dc12)
+            za[x + 6] = swept(info, z, x, 8, exta[ext_a(x)], wc, dc12)
         z = from_scratch(za, 6)
         for x in range(-4, ROWS + 4):
-            zb[x + 4] = swept(info, z, x, 6, ext_b(exta, x), wc, dc12)
+            zb[x + 4] = swept(info, z, x, 6, exta[ext_b(x)], wc, dc12)
         z = from_scratch(zb, 4)
         for x in range(-2, ROWS + 2):
             zc[x + 2] = swept(info, z, x, 4, abb[row_a(x)], wc, dc12)
@@ -376,17 +360,12 @@
             rb[2 * ROWS + x] = swept(info, z, x, 2, abb[row_b(x)], wc, dc12)
         give(info, depth, message, outer, inner, lambda x: rb[2 * ROWS + x])
 
-
-def single_kernel(at, info, z0, zo, zi, ab, wc, dc12, result, za):
-    @pl.when(info[1] == at)
-    def _():
-        z = begin(info, z0, zo, zi, 4)
-        for x in range(-2, ROWS + 2):
-            za[x + 2] = swept(info, z, x, 4, ab[row_a(x)], wc, dc12)
-        z = from_scratch(za, 2)
-        for x in range(ROWS):
-            result[x], result[ROWS + x] = z0[x], za[x + 2]
-            result[2 * ROWS + x] = swept(info, z, x, 2, ab[row_b(x)], wc, dc12)
+    active, odd = hosting(info, hosts), info[1] % 2 == 1
+    if hosts[0] % 2 or hosts[1] % 2:
+        pl.when(active & odd)(lambda: sweep(mine, short))
+    if not (hosts[0] % 2 and hosts[1] % 2):
+
+        pl.when(active & (info[1] % 2 == 0))(lambda: sweep(long, mine))
 
 
 def base_kernel(n1, n2, c1, c2, pro, share, b1, b2):
@@ -396,25 +375,47 @@
             b[:, x, :] = (n[x] - dot(pro[...], value))[:SPECIES]
 
 
-def out_kernel(info, where, u, b0, b1, b2, share, *refs):
-    results, (out, z, spread, sem) = refs[:SLICES], refs[SLICES:]
-    for p in range(SLICES):
-
-        @pl.when(info[1] == p)
+def out_kernel(
+    info, where, u, b0, b1, b2, share, z0, zo, zi, ab, wc, dc12, ra, rb, out, z, za, spread, node, sem
+):
+    last = info[1] == SLICES - 1
+    for parity, result in enumerate((rb, ra)):
+
+        @pl.when((info[1] % 2 == parity) & (info[1] < SLICES - 1))
         def _():
-            copy = pltpu.make_async_copy(results[p], z, sem)
-            copy.start()
-            copy.wait()
-
-    for m in range(3):
+            for x in range(3 * ROWS):
+                z[x] = result[x]
+
+    @pl.when(last)
+    def _():
+        for x in range(ROWS):
+            z[x] = z0[x]
+
+    def finish(m, base):
         for x in range(ROWS):
             spread[m, :, x, :] = share[...] * z[m * ROWS + x]
+        for s in range(SPECIES):
+            node[m, s] = base(s) + spread[m, where[s]]
+        copy = pltpu.make_async_copy(node.at[m], out.at[m], sem.at[m])
+        copy.start()
+        return copy
+
     first = info[1] == 0
-    for s in range(SPECIES):
-        to = where[s]
-        out[0, s] = jnp.where(first, u[0, s], b0[s]) + spread[0, to]
-        out[1, s] = b1[s] + spread[1, to]
-        out[2, s] = b2[s] + spread[2, to]
+    copies = [finish(0, lambda s: jnp.where(first, u[0, s], b0[s]))]
+
+    @pl.when(last)
+    def _():
+        row = begin(info, z0, zo, zi, 4)
+        for x in range(-2, ROWS + 2):
+            za[x + 2] = swept(info, row, x, 4, ab[row_a(x)], wc, dc12)
+        row = from_scratch(za, 2)
+        for x in range(ROWS):
+            z[ROWS + x] = za[x + 2]
+            z[2 * ROWS + x] = swept(info, row, x, 2, ab[row_b(x)], wc, dc12)
+
+    copies += [finish(1, lambda s: b1[s]), finish(2, lambda s: b2[s])]
+    for copy in copies:
+        copy.wait()
 
 
 def field(*shape):
@@ -426,12 +427,13 @@
 ANY = pl.BlockSpec(memory_space=pl.ANY)
 
 
-def call(kernel, name, outs, *args, specs=None, scratch=(), alias=None):
-    specs = specs or [SMEM if a.dtype == jnp.int32 and a.ndim == 1 else VMEM for a in args]
+def call(kernel, name, outs, *args, scratch=(), alias=None, out_specs=None):
+    specs = [SMEM if a.dtype == jnp.int32 and a.ndim == 1 else VMEM for a in args]
     return pl.pallas_call(
         kernel,
         out_shape=outs,
         in_specs=specs,
+        **({"out_specs": out_specs} if out_specs else {}),
         scratch_shapes=[pltpu.VMEM(f.shape, f.dtype) if isinstance(f, jax.ShapeDtypeStruct) else f for f in scratch],
         input_output_aliases=alias or {},
         compiler_params=pltpu.CompilerParams(vmem_limit_bytes=VMEM_LIMIT),
@@ -443,22 +445,28 @@
 OUTER = [(s, s + 1) for s in range(1, SLABS - 1, 2)] + [(s + 1, s) for s in range(1, SLABS - 1, 2)]
 INNER = [(s, s ^ 1) for s in range(SLABS)]
 SAME = [(s, s) for s in range(SLABS)]
-
-
-def moved(value, slices, slabs):
-    route = [(p * SLABS + s, q * SLABS + t) for p, q in slices for s, t in slabs]
-    return lax.ppermute(value, AXES, route)
-
-
-def swap(outer, inner, slices=tuple(range(SLICES))):
-    pairs = [(p, p) for p in slices]
-    got_inner = moved(inner, pairs, INNER)
-    got_outer = moved(outer, pairs, OUTER)
+GROUPS = (((0,), (0, 0)), ((1, 2), (1, 1)), ((3, 4), (3, 4)), ((5, 6), (6, 5)), ((7,), (7, 7)))
+
+
+def moved(value, *routes):
+    pairs = [
+        (source[s % 2] * SLABS + s, target[t % 2] * SLABS + t) for source, target, slabs in routes for s, t in slabs
+    ]
+    return lax.ppermute(value, AXES, pairs)
+
+
+def both(p):
+    return (p, p)
+
+
+def swap(outer, inner):
+    got_inner = moved(inner, *[(both(p), both(p), INNER) for p in range(SLICES)])
+    got_outer = moved(outer, *[(both(p), both(p), OUTER) for p in range(SLICES)])
     return got_outer, got_inner
 
 
-def hop(message, outer, inner, p, q):
-    return moved(message, [(p, q)], SAME), moved(outer, [(p, q)], OUTER), moved(inner, [(p, q)], INNER)
+def hop(message, outer, inner, source, target):
+    return [moved(value, (source, target, slabs)) for value, slabs in ((message, SAME), (outer, OUTER), (inner, INNER))]
 
 
 def after(value, other):
@@ -498,7 +506,7 @@
         *(nodes, wf, wr, wc, d12, dc12),
         scratch=[field(ROWS, 3, SP), fine, fine, coarse],
     )
-    two, four, eight = field(2, SP), field(4, CP), field(8, CP)
+    two, twelve, eight = field(2, SP), field(12, CP), field(8, CP)
     n1, s, r0, e0, outer, inner = call(
         old_edge_kernel,
         "old_edge",
@@ -510,66 +518,66 @@
     n2, r1, e1, c1 = call(
         mid_kernel, "mid", [fine, coarse, coarse, coarse], n1, s, wfr, wc, d12, dc12, scratch=[coarse]
     )
-    n2, r1, e1, outer, inner = call(
+    extended, short = field(EXT_ROWS, CP), field(AB_ROWS, CP)
+    n2, r1, e1, abx, c2, outer, inner = call(
         mid_edge_kernel,
         "mid_edge",
-        [fine, coarse, coarse, four, four],
+        [fine, coarse, coarse, extended, coarse, twelve, twelve],
         *(info, no, ni, lv, wr, d12, dc12, r0, e0, c0, n2, r1, e1),
         alias={10: 0, 11: 1, 12: 2},
+        scratch=[coarse],
     )
     ho, hi = swap(outer, inner)
-    pieces, extended = field(AB_ROWS, CP), field(EXT_ROWS, CP)
-    ab, c2 = call(
-        last_kernel, "last", [pieces, coarse], *(info, n2, wr, r0, r1, e0, e1, c0), scratch=[coarse]
-    )
-    ab, ext_outer, ext_inner = call(
-        last_edge_kernel, "last_edge", [pieces, eight, eight], info, outer, inner, ho, hi, ab, alias={5: 0}
-    )
-
+    b1, b2 = call(base_kernel, "base", [field(SPECIES, ROWS)] * 2, n1, n2, c1, c2, pro, share)
+    abx, ab = call(last_edge_kernel, "last_edge", [extended, short], info, outer, inner, ho, hi, abx, alias={5: 0})
+
+    ab, abx = after(ab, b1), after(abx, b1)
     result = field(3 * ROWS, CP)
-    result0, *sent = call(start_kernel, "start", [result, coarse, eight, eight], info, ab, wc, dc12)
-    z = hop(*sent, 0, 1)
-    ext_outer, ext_inner = after(ext_outer, sent[0]), after(ext_inner, sent[0])
-    eo, ei = swap(ext_outer, ext_inner, (1, 3, 5))
-    ext = call(extend_kernel, "extend", extended, info, ab, eo, ei)
-    ab_two = moved(after(ab, sent[0]), [(2, 1)], SAME)
-    ext_odd = moved(ext, [(3, 4), (5, 6)], SAME)
-
-    def pair(at, depth, z, exta, abb):
-        return call(
-            functools.partial(pair_kernel, at, depth),
-            "pair",
-            [result, result, coarse, field(depth, CP), field(depth, CP)],
-            *(info, *z, exta, abb, wc, dc12),
-            scratch=[field(ROWS + 12, CP), field(ROWS + 8, CP), field(ROWS + 4, CP)],
-        )
-
-    result1, rb, *sent = pair(1, 8, z, ext, ab_two)
-    z = hop(*sent, 1, 4)
-    result2 = moved(rb, [(1, 2)], SAME)
-    b1, b2 = call(base_kernel, "base", [field(SPECIES, ROWS)] * 2, after(n1, result0), n2, c1, c2, pro, share)
-    b0 = moved(b2, [(p, p + 1) for p in range(SLICES - 1)], SAME)
-    ra, result4, *sent = pair(4, 8, z, ext_odd, ab)
-    z = hop(*sent, 4, 6)
-    result3 = moved(ra, [(4, 3)], SAME)
-    ra, result6, *sent = pair(6, 4, z, ext_odd, ab)
-    z = hop(*sent, 6, 7)
-    result5 = moved(ra, [(6, 5)], SAME)
-    result7 = call(
-        functools.partial(single_kernel, 7),
-        "single",
-        result,
-        *(info, *z, ab, wc, dc12),
-        scratch=[field(ROWS + 4, CP)],
-    )
-    results = [result0, result1, result2, result3, result4, result5, result6, result7]
+    pairs = [(slices, hosts) for slices, hosts in GROUPS if len(slices) == 2]
+    short, long = [], []
+    for slices, hosts in pairs:
+        for core, host in enumerate(hosts):
+            slabs = [(t, t) for t in range(core, SLABS, 2)]
+            if host == slices[0]:
+                short.append((both(slices[1]), both(host), slabs))
+            else:
+                long.append((both(slices[0]), both(host), slabs))
+    short, long = moved(ab, *short), moved(abx, *long)
+    rb, *sent = call(
+        functools.partial(start_kernel, GROUPS[0][1]), "start", [result, coarse, eight, eight], info, ab, wc, dc12
+    )
+    ra = rb
+    for at, (slices, hosts) in enumerate(GROUPS[1:], 1):
+        z = hop(*sent, GROUPS[at - 1][1], hosts)
+        if at == 1:
+            *z, short, long = lax.optimization_barrier((*z, short, long))
+            b0 = moved(after(b2, z[0]), *[(both(p), both(p + 1), SAME) for p in range(3, SLICES - 1)])
+        elif at == 2:
+            *z, b0 = lax.optimization_barrier((*z, b0))
+            late = moved(after(b2, z[0]), *[(both(p), both(p + 1), SAME) for p in range(3)])
+        elif at == 3:
+            *z, late = lax.optimization_barrier((*z, late))
+        else:
+            ra = moved(ra, *[(hosts, both(slices[0]), SAME) for slices, hosts in pairs])
+            rb = moved(rb, (both(0), both(0), SAME), *[(hosts, both(slices[1]), SAME) for slices, hosts in pairs])
+            *z, ra, rb = lax.optimization_barrier((*z, ra, rb))
+        if len(slices) == 2:
+            depth = 4 * len(GROUPS[at + 1][0])
+            ra, rb, *sent = call(
+                functools.partial(pair_kernel, hosts, depth),
+                "pair",
+                [result, result, coarse, field(depth, CP), field(depth, CP)],
+                *(info, *z, abx, short, long, wc, dc12, ra, rb),
+                scratch=[field(ROWS + 12, CP), field(ROWS + 8, CP), field(ROWS + 4, CP)],
+                alias={9: 0, 10: 1},
+            )
     out = call(
         out_kernel,
         "out",
         field(3, SPECIES, ROWS),
-        *(info, species_map[:, 0], nodes, b0, b1, b2, share, *results),
-        specs=[SMEM, SMEM] + [VMEM] * 5 + [ANY] * SLICES,
-        scratch=[result, field(3, CP, ROWS), pltpu.SemaphoreType.DMA],
+        *(info, species_map[:, 0], nodes, b0 + late, b1, b2, share, *z, ab, wc, dc12, ra, rb),
+        out_specs=ANY,
+        scratch=[result, field(ROWS + 4, CP), field(3, CP, ROWS), field(3, SPECIES, ROWS), pltpu.SemaphoreType.DMA((3,))],
     )
     return out[None]
 

time: 172 us -> 141 us (0.82)
  the two profiles are of different devices: /device:TPU:114 before, /device:TPU:80 now
where the time goes in v1:
time: 141 us
  waiting for transfers between devices  61.4 us (44%)
  starting transfers between devices  50.8 us (36%)
  Pallas kernels  23.6 us (17%)
  local copies, waits for them, and re-layouts  3.97 us (3%)
    ppermute x24, waiting for transfers between devices, moved(): return lax.ppermute(value, AXES, pairs)  61.4 us
    ppermute x24, starting transfers between devices, moved(): return lax.ppermute(value, AXES, pairs)  50.8 us
    pallas_call x13, Pallas kernels, call(): pl.pallas_call(kernel, out_shape=outs, in_specs=specs, **{'out_specs': ou...  23.6 us
    unnamed x24, local copies, waits for them, and re-layouts  3.97 us
  transfers between devices with their start and end apart: 24, of which 6 were waited for; matrix products, arithmetic and copies ran while one was open for 0% of the time, Pallas kernels for 9%

profile of v1, /device:TPU:80, one launch (start us, length us, event | category | flops | bytes accessed | tf_op | source)
XLA Modules:
  0.0 140.6 jit_solution(14656316197133215130)
XLA Ops:
  0.1 1.7 %copy-done = f32[1,3,53,16,256]{4,3,2,1,0:T(8,128)S(1)} copy-done((f32[1,3,53,16,256]{4,3,2,1,0:T(8,128)S(1)}, f32[1,3,53,16,256]{4,3,2,1,0:T(8,128)}, u32[]{:S(2)}) %copy-start) | copy-done | bytes 2605080
  1.8 1.8 %first.1 = (f32[3,2,56,256]{3,2,1,0:T(8,128)}, f32[3,2,56,256]{3,2,1,0:T(8,128)}) custom-call(s32[3]{0:T(128)S(1)} %pad_add_fusion.info, f32[3,53,16,256]{3,2,1,0:T(8,128)S(1)} %bitcast.9), custom_call_target="tpu_custom_call" | custom-call | tf_op jit(solution)/shard_map/first/pallas_call | solution.py:432
  3.6 4.2 %collective-permute-start = (f32[3,2,56,256]{3,2,1,0:T(8,128)}, f32[3,2,56,256]{3,2,1,0:T(8,128)S(1)}, u32[]{:S(2)}, u32[]{:S(2)}) collective-permute-start(f32[3,2,56,256]{3,2,1,0:T(8,128)} %get-tuple-element.81), channel_id=1, source_target_pairs={{1,2},{3,4},{5,6},{7,8},{9,10},{11,12},{13,14},{2,1},{4,3},{6,5},{... | collective-permute-start | bytes 1032200 | tf_op jit(solution)/shard_map/ppermute | solution.py:455
  7.8 0.9 collective-permute-start.1
  8.7 0.1 copy.23.smap
  8.9 0.7 copy-done.3
  9.6 0.2 prep.1
  9.9 5.6 %old.1 = (f32[16,56,256]{2,1,0:T(8,128)S(1)}, f32[16,56,256]{2,1,0:T(8,128)S(1)}, f32[16,24,256]{2,1,0:T(8,128)S(1)}, f32[16,24,256]{2,1,0:T(8,128)S(1)}, f32[16,24,256]{2,1,0:T(8,128)S(1)}) custom-call(f32[3,53,16,256]{3,2,1,0:T(8,128)S(1)} %bitcast.10, bf16[112,256]{1,0:T(8,128)(2,1)S(1)} %get-tuple-element.86.wf, ...), custom_call_target="tpu_custom_call" | custom-call | tf_op jit(solution)/shard_map/old/pallas_call | solution.py:432
  15.4 2.1 %collective-permute-done.uo = f32[3,2,56,256]{3,2,1,0:T(8,128)S(1)} collective-permute-done((f32[3,2,56,256]{3,2,1,0:T(8,128)}, f32[3,2,56,256]{3,2,1,0:T(8,128)S(1)}, u32[]{:S(2)}, u32[]{:S(2)}) %collective-permute-start) | collective-permute-done | bytes 344096 | tf_op jit(solution)/shard_map/ppermute | solution.py:455
  17.5 0.9 old_edge.1
  18.5 5.1 %collective-permute-start.2 = (f32[2,56,256]{2,1,0:T(8,128)S(1)}, f32[2,56,256]{2,1,0:T(8,128)S(1)}, u32[]{:S(2)}, u32[]{:S(2)}) collective-permute-start(f32[2,56,256]{2,1,0:T(8,128)S(1)} %get-tuple-element.93), channel_id=1, source_target_pairs={{1,2},{3,4},{5,6},{7,8},{9,10},{11,12},{13,14},{2,1},{4,3},{6,5},{... | collective-permute-start | bytes 344072 | tf_op jit(solution)/shard_map/ppermute | solution.py:455
  23.6 2.7 %mid.1 = (f32[16,56,256]{2,1,0:T(8,128)S(1)}, f32[16,24,256]{2,1,0:T(8,128)S(1)}, f32[16,24,256]{2,1,0:T(8,128)S(1)}, f32[16,24,256]{2,1,0:T(8,128)S(1)}) custom-call(f32[16,56,256]{2,1,0:T(8,128)S(1)} %get-tuple-element.98.n1, f32[16,56,256]{2,1,0:T(8,128)S(1)} %get-tuple-element.99.s, bf16[240,256]{1,0:T(8,128)(2,1)S(1)} %get-tuple-element.100.wfr, ...), custom_call_target="tpu_custom_call" | custom-call | tf_op jit(solution)/shard_map/mid/pallas_call | solution.py:432
  26.3 0.9 collective-permute-done.2.no
  27.2 1.7 %mid_edge.1 = (f32[16,56,256]{2,1,0:T(8,128)S(1)}, f32[16,24,256]{2,1,0:T(8,128)S(1)}, f32[16,24,256]{2,1,0:T(8,128)S(1)}, f32[52,24,256]{2,1,0:T(8,128)S(1)}, f...) custom-call(s32[3]{0:T(128)S(1)} %pad_add_fusion.info, ...), custom_call_target="tpu_custom_call", output_to_operand_aliasing={{0}: (10, {}), {1}: (11, {}), {2}: (12, {})} | custom-call | tf_op jit(solution)/shard_map/mid_edge/pallas_call | solution.py:432
  28.9 5.3 %collective-permute-start.4 = (f32[12,24,256]{2,1,0:T(8,128)S(1)}, f32[12,24,256]{2,1,0:T(8,128)S(1)}, u32[]{:S(2)}, u32[]{:S(2)}) collective-permute-start(f32[12,24,256]{2,1,0:T(8,128)S(1)} %get-tuple-element.104.mo), channel_id=1, source_target_pairs={{1,2},{3,4},{5,6},{7,8},{9,10},{11,12},{13,14},{2,1},{4,3},{6,5},{... | collective-permute-start | bytes 884744 | tf_op jit(solution)/shard_map/ppermute | solution.py:455
  34.2 0.3 collective-permute-start.5
  34.4 1.3 base.1
  35.7 5.6 %collective-permute-done.4.ho = f32[12,24,256]{2,1,0:T(8,128)S(1)} collective-permute-done((f32[12,24,256]{2,1,0:T(8,128)S(1)}, f32[12,24,256]{2,1,0:T(8,128)S(1)}, u32[]{:S(2)}, u32[]{:S(2)}) %collective-permute-start.4) | collective-permute-done | bytes 294944 | tf_op jit(solution)/shard_map/ppermute | solution.py:455
  41.3 0.7 last_edge.1
  42.0 0.7 collective-permute-start.10
  42.8 2.1 %collective-permute-start.9 = (f32[36,24,256]{2,1,0:T(8,128)S(1)}, f32[36,24,256]{2,1,0:T(8,128)S(1)}, u32[]{:S(2)}, u32[]{:S(2)}) collective-permute-start(f32[36,24,256]{2,1,0:T(8,128)S(1)} %get-tuple-element.114.ab), channel_id=1, source_target_pairs={{32,16},{34,18},{36,20},{38,22},{40,24},{42,26},{44,28},{46,30},{3... | collective-permute-start | bytes 2654216 | tf_op jit(solution)/shard_map/ppermute | solution.py:455
  44.9 0.6 start.1
  45.4 0.7 collective-permute-start.6
  46.1 0.7 collective-permute-start.7
  46.8 0.7 collective-permute-start.8
  47.5 15.4 %collective-permute-done.9.short = f32[36,24,256]{2,1,0:T(8,128)S(1)} collective-permute-done((f32[36,24,256]{2,1,0:T(8,128)S(1)}, f32[36,24,256]{2,1,0:T(8,128)S(1)}, u32[]{:S(2)}, u32[]{:S(2)}) %collective-permute-start.9) | collective-permute-done | bytes 884768 | tf_op jit(solution)/shard_map/ppermute | solution.py:455
  62.9 0.7 collective-permute-start.14
  63.7 0.2 copy-done.9
  63.9 1.3 pair.3
  65.3 0.7 collective-permute-start.11
  66.0 0.7 collective-permute-start.12
  66.6 0.7 collective-permute-start.13
  67.4 21.3 %collective-permute-start.18 = (f32[53,16,256]{2,1,0:T(8,128)S(1)}, f32[53,16,256]{2,1,0:T(8,128)S(1)}, u32[]{:S(2)}, u32[]{:S(2)}) collective-permute-start(f32[53,16,256]{2,1,0:T(8,128)S(1)} %get-tuple-element.140.b2), channel_id=1, source_target_pairs={{0,16},{1,17},{2,18},{3,19},{4,20},{5,21},{6,22},{7,23},{8,24},{9,... | collective-permute-start | bytes 2605064 | tf_op jit(solution)/shard_map/ppermute | solution.py:455
  88.6 1.3 pair.4
  90.0 0.7 collective-permute-start.15
  90.7 0.7 collective-permute-start.16
  91.4 0.7 collective-permute-start.17
  92.1 11.2 %collective-permute-done.18 = f32[53,16,256]{2,1,0:T(8,128)S(1)} collective-permute-done((f32[53,16,256]{2,1,0:T(8,128)S(1)}, f32[53,16,256]{2,1,0:T(8,128)S(1)}, u32[]{:S(2)}, u32[]{:S(2)}) %collective-permute-start.18) | collective-permute-done | bytes 868384 | tf_op jit(solution)/shard_map/ppermute | solution.py:455
  103.3 1.6 %pair.5 = (f32[48,24,256]{2,1,0:T(8,128)S(1)}, f32[48,24,256]{2,1,0:T(8,128)S(1)}, f32[16,24,256]{2,1,0:T(8,128)S(1)}, f32[4,24,256]{2,1,0:T(8,128)S(1)}, f32[4,24,256]{2,1,0:T(8,128)S(1)}) custom-call(s32[3]{0:T(128)S(1)} %pad_add_fusion.info, f32[16,24,256]{2,1,0:T(8,128)S(1)} %collective-permute-done.15.z0, ...), custom_call_target="tpu_custom_call", output_to_operand_aliasing={{0}: (9, {}), {1}: (10, {})} | custom-call | tf_op jit(solution)/shard_map/pair/pallas_call | solution.py:432
  104.9 0.7 collective-permute-start.22
  105.6 1.3 collective-permute-start.23
  106.9 0.7 collective-permute-start.19
  107.6 0.7 collective-permute-start.20
  108.3 0.7 collective-permute-start.21
  108.9 0.2 add.8.b0
  109.2 26.2 %collective-permute-done.23.rb = f32[48,24,256]{2,1,0:T(8,128)S(1)} collective-permute-done((f32[48,24,256]{2,1,0:T(8,128)S(1)}, f32[48,24,256]{2,1,0:T(8,128)S(1)}, u32[]{:S(2)}, u32[]{:S(2)}) %collective-permute-start.23) | collective-permute-done | bytes 1179680 | tf_op jit(solution)/shard_map/ppermute | solution.py:455
  135.4 1.0 copy-done.10
  136.4 4.1 %out.1 = f32[3,53,16,256]{3,2,1,0:T(8,128)} custom-call(s32[3]{0:T(128)S(1)} %pad_add_fusion.info, s32[53]{0:T(128)S(1)} %bitcast.11, f32[3,53,16,256]{3,2,1,0:T(8,128)} %bitcast.8, f32[53,16,256]{2,1,0:T(8,128)S(1)} %add.8.b0, f32[53,16,256]{2,1,0:T(8,128)S(1)} %get-tuple-element.113.b1, f32[53,16,256]{2,1,0:T(8,128)S(1)} %get-tuple-element.140.b2, ...), custom_call_target="tpu_custom_call" | custom-call | tf_op jit(solution)/shard_map/out/pallas_call | solution.py:432
  (39 shorter events, 0.3 us)
Async XLA Ops:
  0.0 8.7 %copy-start.6 = (s32[53,1]{0,1:T(1,128)S(1)}, s32[53,1]{0,1:T(1,128)}, u32[]{:S(2)}) copy-start(s32[53,1]{0,1:T(1,128)} %param.15) | copy-start | bytes 640
  0.0 8.8 %copy-start.4 = (f32[21,21]{1,0:T(8,128)S(1)}, f32[21,21]{1,0:T(8,128)}, u32[]{:S(2)}) copy-start(f32[21,21]{1,0:T(8,128)} %crates.1) | copy-start | bytes 5296
  0.0 8.8 %copy-start.5 = (f32[21,21]{1,0:T(8,128)S(1)}, f32[21,21]{1,0:T(8,128)}, u32[]{:S(2)}) copy-start(f32[21,21]{1,0:T(8,128)} %cpairs.1) | copy-start | bytes 5296
  0.1 1.7 %copy-start = (f32[1,3,53,16,256]{4,3,2,1,0:T(8,128)S(1)}, f32[1,3,53,16,256]{4,3,2,1,0:T(8,128)}, u32[]{:S(2)}) copy-start(f32[1,3,53,16,256]{4,3,2,1,0:T(8,128)} %param.8) | copy-start | bytes 7815172
  1.8 7.0 %copy-start.2 = (f32[53,53]{1,0:T(8,128)S(1)}, f32[53,53]{1,0:T(8,128)}, u32[]{:S(2)}) copy-start(f32[53,53]{1,0:T(8,128)} %rates.1) | copy-start | bytes 33712
  1.8 7.0 %copy-start.7 = (f32[53]{0:T(128)S(1)}, f32[53]{0:T(128)}, u32[]{:S(2)}) copy-start(f32[53]{0:T(128)} %param.11) | copy-start | bytes 640
  1.8 7.0 %copy-start.8 = (f32[21]{0:T(128)S(1)}, f32[21]{0:T(128)}, u32[]{:S(2)}) copy-start(f32[21]{0:T(128)} %param.14) | copy-start | bytes 256
  1.8 8.0 %copy-start.1 = (f32[1,3,53,16,256]{4,3,2,1,0:T(8,128)S(1)}, f32[1,3,53,16,256]{4,3,2,1,0:T(8,128)}, u32[]{:S(2)}) copy-start(f32[1,3,53,16,256]{4,3,2,1,0:T(8,128)} %param.8) | copy-start | bytes 7815172
  3.6 13.9 %collective-permute-start = (f32[3,2,56,256]{3,2,1,0:T(8,128)}, f32[3,2,56,256]{3,2,1,0:T(8,128)S(1)}, u32[]{:S(2)}, u32[]{:S(2)}) collective-permute-start(f32[3,2,56,256]{3,2,1,0:T(8,128)} %get-tuple-element.81), channel_id=1, source_target_pairs={{1,2},{3,4},{5,6},{7,8},{9,10},{11,12},{13,14},{2,1},{4,3},{6,5},{... | collective-permute-start | bytes 1032200 | tf_op jit(solution)/shard_map/ppermute | solution.py:455
  7.8 9.7 %collective-permute-start.1 = (f32[3,2,56,256]{3,2,1,0:T(8,128)}, f32[3,2,56,256]{3,2,1,0:T(8,128)S(1)}, u32[]{:S(2)}, u32[]{:S(2)}) collective-permute-start(f32[3,2,56,256]{3,2,1,0:T(8,128)} %get-tuple-element.82), channel_id=1, source_target_pairs={{0,1},{1,0},{2,3},{3,2},{4,5},{5,4},{6,7},{7,6},{8,9},{9,8},{10,11... | collective-permute-start | bytes 1032200 | tf_op jit(solution)/shard_map/ppermute | solution.py:455
  8.9 0.8 copy-start.3
  18.5 8.7 %collective-permute-start.2 = (f32[2,56,256]{2,1,0:T(8,128)S(1)}, f32[2,56,256]{2,1,0:T(8,128)S(1)}, u32[]{:S(2)}, u32[]{:S(2)}) collective-permute-start(f32[2,56,256]{2,1,0:T(8,128)S(1)} %get-tuple-element.93), channel_id=1, source_target_pairs={{1,2},{3,4},{5,6},{7,8},{9,10},{11,12},{13,14},{2,1},{4,3},{6,5},{... | collective-permute-start | bytes 344072 | tf_op jit(solution)/shard_map/ppermute | solution.py:455
  23.5 3.7 %collective-permute-start.3 = (f32[2,56,256]{2,1,0:T(8,128)S(1)}, f32[2,56,256]{2,1,0:T(8,128)S(1)}, u32[]{:S(2)}, u32[]{:S(2)}) collective-permute-start(f32[2,56,256]{2,1,0:T(8,128)S(1)} %get-tuple-element.94), channel_id=1, source_target_pairs={{0,1},{1,0},{2,3},{3,2},{4,5},{5,4},{6,7},{7,6},{8,9},{9,8},{10,11... | collective-permute-start | bytes 344072 | tf_op jit(solution)/shard_map/ppermute | solution.py:455
  28.9 12.4 %collective-permute-start.4 = (f32[12,24,256]{2,1,0:T(8,128)S(1)}, f32[12,24,256]{2,1,0:T(8,128)S(1)}, u32[]{:S(2)}, u32[]{:S(2)}) collective-permute-start(f32[12,24,256]{2,1,0:T(8,128)S(1)} %get-tuple-element.104.mo), channel_id=1, source_target_pairs={{1,2},{3,4},{5,6},{7,8},{9,10},{11,12},{13,14},{2,1},{4,3},{6,5},{... | collective-permute-start | bytes 884744 | tf_op jit(solution)/shard_map/ppermute | solution.py:455
  34.2 7.1 %collective-permute-start.5 = (f32[12,24,256]{2,1,0:T(8,128)S(1)}, f32[12,24,256]{2,1,0:T(8,128)S(1)}, u32[]{:S(2)}, u32[]{:S(2)}) collective-permute-start(f32[12,24,256]{2,1,0:T(8,128)S(1)} %get-tuple-element.105.mi), channel_id=1, source_target_pairs={{0,1},{1,0},{2,3},{3,2},{4,5},{5,4},{6,7},{7,6},{8,9},{9,8},{10,11... | collective-permute-start | bytes 884744 | tf_op jit(solution)/shard_map/ppermute | solution.py:455
  42.0 20.9 %collective-permute-start.10 = (f32[52,24,256]{2,1,0:T(8,128)S(1)}, f32[52,24,256]{2,1,0:T(8,128)S(1)}, u32[]{:S(2)}, u32[]{:S(2)}) collective-permute-start(f32[52,24,256]{2,1,0:T(8,128)S(1)} %get-tuple-element.119.mine), channel_id=1, source_target_pairs={{49,65},{51,67},{53,69},{55,71},{57,73},{59,75},{61,77},{63,79},{8... | collective-permute-start | bytes 3833864 | tf_op jit(solution)/shard_map/ppermute | solution.py:455
  42.8 20.1 %collective-permute-start.9 = (f32[36,24,256]{2,1,0:T(8,128)S(1)}, f32[36,24,256]{2,1,0:T(8,128)S(1)}, u32[]{:S(2)}, u32[]{:S(2)}) collective-permute-start(f32[36,24,256]{2,1,0:T(8,128)S(1)} %get-tuple-element.114.ab), channel_id=1, source_target_pairs={{32,16},{34,18},{36,20},{38,22},{40,24},{42,26},{44,28},{46,30},{3... | collective-permute-start | bytes 2654216 | tf_op jit(solution)/shard_map/ppermute | solution.py:455
  45.4 2.1 %collective-permute-start.6 = (f32[16,24,256]{2,1,0:T(8,128)S(1)}, f32[16,24,256]{2,1,0:T(8,128)S(1)}, u32[]{:S(2)}, u32[]{:S(2)}) collective-permute-start(f32[16,24,256]{2,1,0:T(8,128)S(1)} %get-tuple-element.115), channel_id=1, source_target_pairs={{0,16},{1,17},{2,18},{3,19},{4,20},{5,21},{6,22},{7,23},{8,24},{9,... | collective-permute-start | bytes 1179656 | tf_op jit(solution)/shard_map/ppermute | solution.py:455
  46.1 1.4 collective-permute-start.7
  46.8 0.7 collective-permute-start.8
  62.9 1.0 copy-start.9
  62.9 4.5 %collective-permute-start.14 = (f32[53,16,256]{2,1,0:T(8,128)S(1)}, f32[53,16,256]{2,1,0:T(8,128)S(1)}, u32[]{:S(2)}, u32[]{:S(2)}) collective-permute-start(f32[53,16,256]{2,1,0:T(8,128)S(1)} %get-tuple-element.140.b2), channel_id=1, source_target_pairs={{48,64},{49,65},{50,66},{51,67},{52,68},{53,69},{54,70},{55,71},{5... | collective-permute-start | bytes 2605064 | tf_op jit(solution)/shard_map/ppermute | solution.py:455
  65.3 2.1 %collective-permute-start.11 = (f32[16,24,256]{2,1,0:T(8,128)S(1)}, f32[16,24,256]{2,1,0:T(8,128)S(1)}, u32[]{:S(2)}, u32[]{:S(2)}) collective-permute-start(f32[16,24,256]{2,1,0:T(8,128)S(1)} %get-tuple-element.126), channel_id=1, source_target_pairs={{16,48},{17,65},{18,50},{19,67},{20,52},{21,69},{22,54},{23,71},{2... | collective-permute-start | bytes 1179656 | tf_op jit(solution)/shard_map/ppermute | solution.py:455
  66.0 1.4 collective-permute-start.12
  66.6 0.7 collective-permute-start.13
  67.4 35.9 %collective-permute-start.18 = (f32[53,16,256]{2,1,0:T(8,128)S(1)}, f32[53,16,256]{2,1,0:T(8,128)S(1)}, u32[]{:S(2)}, u32[]{:S(2)}) collective-permute-start(f32[53,16,256]{2,1,0:T(8,128)S(1)} %get-tuple-element.140.b2), channel_id=1, source_target_pairs={{0,16},{1,17},{2,18},{3,19},{4,20},{5,21},{6,22},{7,23},{8,24},{9,... | collective-permute-start | bytes 2605064 | tf_op jit(solution)/shard_map/ppermute | solution.py:455
  90.0 2.1 %collective-permute-start.15 = (f32[16,24,256]{2,1,0:T(8,128)S(1)}, f32[16,24,256]{2,1,0:T(8,128)S(1)}, u32[]{:S(2)}, u32[]{:S(2)}) collective-permute-start(f32[16,24,256]{2,1,0:T(8,128)S(1)} %get-tuple-element.137), channel_id=1, source_target_pairs={{48,96},{65,81},{50,98},{67,83},{52,100},{69,85},{54,102},{71,87},... | collective-permute-start | bytes 1179656 | tf_op jit(solution)/shard_map/ppermute | solution.py:455
  90.7 1.4 collective-permute-start.16
  91.4 0.7 collective-permute-start.17
  104.9 4.3 %collective-permute-start.22 = (f32[48,24,256]{2,1,0:T(8,128)S(1)}, f32[48,24,256]{2,1,0:T(8,128)S(1)}, u32[]{:S(2)}, u32[]{:S(2)}) collective-permute-start(f32[48,24,256]{2,1,0:T(8,128)S(1)} %get-tuple-element.150), channel_id=1, source_target_pairs={{16,16},{17,17},{18,18},{19,19},{20,20},{21,21},{22,22},{23,23},{2... | collective-permute-start | bytes 3538952 | tf_op jit(solution)/shard_map/ppermute | solution.py:455
  105.6 29.8 %collective-permute-start.23 = (f32[48,24,256]{2,1,0:T(8,128)S(1)}, f32[48,24,256]{2,1,0:T(8,128)S(1)}, u32[]{:S(2)}, u32[]{:S(2)}) collective-permute-start(f32[48,24,256]{2,1,0:T(8,128)S(1)} %get-tuple-element.151), channel_id=1, source_target_pairs={{0,0},{1,1},{2,2},{3,3},{4,4},{5,5},{6,6},{7,7},{8,8},{9,9},{10,10... | collective-permute-start | bytes 3538952 | tf_op jit(solution)/shard_map/ppermute | solution.py:455
  106.9 2.2 %collective-permute-start.19 = (f32[16,24,256]{2,1,0:T(8,128)S(1)}, f32[16,24,256]{2,1,0:T(8,128)S(1)}, u32[]{:S(2)}, u32[]{:S(2)}) collective-permute-start(f32[16,24,256]{2,1,0:T(8,128)S(1)} %get-tuple-element.147), channel_id=1, source_target_pairs={{96,112},{81,113},{98,114},{83,115},{100,116},{85,117},{102,118},{... | collective-permute-start | bytes 1179656 | tf_op jit(solution)/shard_map/ppermute | solution.py:455
  107.6 1.5 %collective-permute-start.20 = (f32[4,24,256]{2,1,0:T(8,128)S(1)}, f32[4,24,256]{2,1,0:T(8,128)S(1)}, u32[]{:S(2)}, u32[]{:S(2)}) collective-permute-start(f32[4,24,256]{2,1,0:T(8,128)S(1)} %get-tuple-element.148), channel_id=1, source_target_pairs={{81,114},{83,116},{85,118},{87,120},{89,122},{91,124},{93,126},{98... | collective-permute-start | bytes 294920 | tf_op jit(solution)/shard_map/ppermute | solution.py:455
  108.3 0.9 collective-permute-start.21
  135.4 1.0 copy-start.10

commit v2 on v1

--- a/solution.py
+++ b/solution.py
@@ -15,7 +15,8 @@
 W0 = (5.0 / 24.0, 1.0 / 3.0, -1.0 / 24.0)
 W1 = (-1.0 / 24.0, 1.0 / 3.0, 5.0 / 24.0)
 F32, BF16 = jnp.float32, jnp.bfloat16
-VMEM_LIMIT = 48 * 1024 * 1024
+GROUPS = (((0,), (0, 0)), ((1, 2), (1, 1)), ((3, 4), (3, 4)), ((5, 6), (6, 5)), ((7,), (7, 7)))
+VMEM_LIMIT = 24 * 1024 * 1024
 
 
 def split(x):
@@ -319,9 +320,7 @@
     return lambda x: ref[x + reach]
 
 
-def give(info, depth, message, outer, inner, value):
-    for x in range(ROWS):
-        message[x] = value(x)
+def give(info, depth, outer, inner, value):
     send(info, outer, inner, [value(x) for x in range(depth)], [value(x) for x in range(ROWS - depth, ROWS)])
 
 
@@ -336,12 +335,13 @@
         for x in range(ROWS):
             rb[x] = zeros(CP)
             rb[ROWS + x] = z1(x)
-            rb[2 * ROWS + x] = swept(info, z1, x, 2, ab[row_b(x)], wc, dc12)
-        give(info, 8, message, outer, inner, lambda x: rb[2 * ROWS + x])
+            message[x] = swept(info, z1, x, 2, ab[row_b(x)], wc, dc12)
+            rb[2 * ROWS + x] = message[x]
+        give(info, 8, outer, inner, lambda x: message[x])
 
 
 def pair_kernel(
-    hosts, depth, info, z0, zo, zi, mine, short, long, wc, dc12, rai, rbi, ra, rb, message, outer, inner, za, zb, zc
+    hosts, depth, info, z0, zo, zi, mine, short, long, wc, dc12, message, outer, inner, za, zb, zc
 ):
     def sweep(exta, abb):
         z = begin(info, z0, zo, zi, 8)
@@ -355,10 +355,8 @@
             zc[x + 2] = swept(info, z, x, 4, abb[row_a(x)], wc, dc12)
         z = from_scratch(zc, 2)
         for x in range(ROWS):
-            ra[x], ra[ROWS + x], ra[2 * ROWS + x] = z0[x], za[x + 6], zb[x + 4]
-            rb[x], rb[ROWS + x] = zb[x + 4], zc[x + 2]
-            rb[2 * ROWS + x] = swept(info, z, x, 2, abb[row_b(x)], wc, dc12)
-        give(info, depth, message, outer, inner, lambda x: rb[2 * ROWS + x])
+            message[x] = swept(info, z, x, 2, abb[row_b(x)], wc, dc12)
+        give(info, depth, outer, inner, lambda x: message[x])
 
     active, odd = hosting(info, hosts), info[1] % 2 == 1
     if hosts[0] % 2 or hosts[1] % 2:
@@ -366,6 +364,17 @@
     if not (hosts[0] % 2 and hosts[1] % 2):
 
         pl.when(active & (info[1] % 2 == 0))(lambda: sweep(long, mine))
+
+
+def gather_kernel(hosts, info, z0, za, zb, zc, z2, home_in, away_in, home, away):
+    def fill(one, two):
+        for x in range(ROWS):
+            one[x], one[ROWS + x], one[2 * ROWS + x] = z0[x], za[x + 6], zb[x + 4]
+            two[x], two[ROWS + x], two[2 * ROWS + x] = zb[x + 4], zc[x + 2], z2[x]
+
+    active, odd = hosting(info, hosts), info[1] % 2 == 1
+    pl.when(active & odd)(lambda: fill(home, away))
+    pl.when(active & ~odd)(lambda: fill(away, home))
 
 
 def base_kernel(n1, n2, c1, c2, pro, share, b1, b2):
@@ -376,12 +385,16 @@
 
 
 def out_kernel(
-    info, where, u, b0, b1, b2, share, z0, zo, zi, ab, wc, dc12, ra, rb, out, z, za, spread, node, sem
+    info, where, u, b0, b1, b2, share, z0, zo, zi, ab, wc, dc12, home, early, other, out, z, za, spread, node, sem
 ):
     last = info[1] == SLICES - 1
-    for parity, result in enumerate((rb, ra)):
-
-        @pl.when((info[1] % 2 == parity) & (info[1] < SLICES - 1))
+    hosts = hosting(info, GROUPS[0][1])
+    for slices, at in GROUPS[1:]:
+        hosts = hosts | (hosting(info, at) & ~last)
+    second = info[1] == GROUPS[1][0][1]
+    for here, result in ((hosts, home), (second, early), (~hosts & ~second & ~last, other)):
+
+        @pl.when(here)
         def _():
             for x in range(3 * ROWS):
                 z[x] = result[x]
@@ -445,7 +458,6 @@
 OUTER = [(s, s + 1) for s in range(1, SLABS - 1, 2)] + [(s + 1, s) for s in range(1, SLABS - 1, 2)]
 INNER = [(s, s ^ 1) for s in range(SLABS)]
 SAME = [(s, s) for s in range(SLABS)]
-GROUPS = (((0,), (0, 0)), ((1, 2), (1, 1)), ((3, 4), (3, 4)), ((5, 6), (6, 5)), ((7,), (7, 7)))
 
 
 def moved(value, *routes):
@@ -534,48 +546,54 @@
     ab, abx = after(ab, b1), after(abx, b1)
     result = field(3 * ROWS, CP)
     pairs = [(slices, hosts) for slices, hosts in GROUPS if len(slices) == 2]
-    short, long = [], []
+    short, long, back = [], [], []
     for slices, hosts in pairs:
         for core, host in enumerate(hosts):
             slabs = [(t, t) for t in range(core, SLABS, 2)]
-            if host == slices[0]:
-                short.append((both(slices[1]), both(host), slabs))
-            else:
-                long.append((both(slices[0]), both(host), slabs))
-    short, long = moved(ab, *short), moved(abx, *long)
-    rb, *sent = call(
+            other = slices[1] if host == slices[0] else slices[0]
+            (short if host == slices[0] else long).append((both(other), both(host), slabs))
+            back.append((both(host), both(other), slabs))
+    short = moved(ab, *short)
+    forward = [(both(p), both(p + 1), SAME) for p in range(SLICES - 1)]
+    b0 = moved(after(b2, ab), *forward[1:])
+    home, *sent = call(
         functools.partial(start_kernel, GROUPS[0][1]), "start", [result, coarse, eight, eight], info, ab, wc, dc12
     )
-    ra = rb
+    away = home
     for at, (slices, hosts) in enumerate(GROUPS[1:], 1):
         z = hop(*sent, GROUPS[at - 1][1], hosts)
         if at == 1:
-            *z, short, long = lax.optimization_barrier((*z, short, long))
-            b0 = moved(after(b2, z[0]), *[(both(p), both(p + 1), SAME) for p in range(3, SLICES - 1)])
+            *z, short, b0 = lax.optimization_barrier((*z, short, b0))
+            long = moved(after(abx, z[0]), *long)
         elif at == 2:
-            *z, b0 = lax.optimization_barrier((*z, b0))
-            late = moved(after(b2, z[0]), *[(both(p), both(p + 1), SAME) for p in range(3)])
+            *z, long = lax.optimization_barrier((*z, long))
+            late = moved(after(b2, z[0]), forward[0])
+            early = moved(after(away, z[0]), *back[:2])
         elif at == 3:
-            *z, late = lax.optimization_barrier((*z, late))
+            *z, late, early, home, away = lax.optimization_barrier((*z, late, early, home, away))
         else:
-            ra = moved(ra, *[(hosts, both(slices[0]), SAME) for slices, hosts in pairs])
-            rb = moved(rb, (both(0), both(0), SAME), *[(hosts, both(slices[1]), SAME) for slices, hosts in pairs])
-            *z, ra, rb = lax.optimization_barrier((*z, ra, rb))
+            other = moved(away, *back[2:])
+            *z, other, home = lax.optimization_barrier((*z, other, home))
         if len(slices) == 2:
             depth = 4 * len(GROUPS[at + 1][0])
-            ra, rb, *sent = call(
+            *sent, za, zb, zc = call(
                 functools.partial(pair_kernel, hosts, depth),
                 "pair",
-                [result, result, coarse, field(depth, CP), field(depth, CP)],
-                *(info, *z, abx, short, long, wc, dc12, ra, rb),
-                scratch=[field(ROWS + 12, CP), field(ROWS + 8, CP), field(ROWS + 4, CP)],
-                alias={9: 0, 10: 1},
+                [coarse, field(depth, CP), field(depth, CP), field(ROWS + 12, CP), field(ROWS + 8, CP), field(ROWS + 4, CP)],
+                *(info, *z, abx, short, long, wc, dc12),
+            )
+            home, away = call(
+                functools.partial(gather_kernel, hosts),
+                "gather",
+                [result, result],
+                *(info, z[0], za, zb, zc, sent[0], home, away),
+                alias={6: 0, 7: 1},
             )
     out = call(
         out_kernel,
         "out",
         field(3, SPECIES, ROWS),
-        *(info, species_map[:, 0], nodes, b0 + late, b1, b2, share, *z, ab, wc, dc12, ra, rb),
+        *(info, species_map[:, 0], nodes, b0 + late, b1, b2, share, *z, ab, wc, dc12, home, early, other),
         out_specs=ANY,
         scratch=[result, field(ROWS + 4, CP), field(3, CP, ROWS), field(3, SPECIES, ROWS), pltpu.SemaphoreType.DMA((3,))],
     )

time: 141 us -> 143 us (1.014)
  the two profiles are of different devices: /device:TPU:80 before, /device:TPU:75 now
where the time goes in v2:
time: 143 us
  waiting for transfers between devices  85.6 us (60%)
  starting transfers between devices  32 us (22%)
  Pallas kernels  21.4 us (15%)
  local copies, waits for them, and re-layouts  2.69 us (2%)
    ppermute x24, waiting for transfers between devices, moved(): return lax.ppermute(value, AXES, pairs)  85.6 us
    ppermute x24, starting transfers between devices, moved(): return lax.ppermute(value, AXES, pairs)  32 us
    pallas_call x16, Pallas kernels, call(): pl.pallas_call(kernel, out_shape=outs, in_specs=specs, **{'out_specs': ou...  21.4 us
  transfers between devices with their start and end apart: 24, of which 4 were waited for; matrix products, arithmetic and copies ran while one was open for 0% of the time, Pallas kernels for 9%

profile of v2, /device:TPU:75, one launch (start us, length us, event | category | flops | bytes accessed | tf_op | source)
XLA Modules:
  0.0 142.7 jit_solution(2792918233149685442)
XLA Ops:
  0.1 1.7 %copy-done = f32[1,3,53,16,256]{4,3,2,1,0:T(8,128)S(1)} copy-done((f32[1,3,53,16,256]{4,3,2,1,0:T(8,128)S(1)}, f32[1,3,53,16,256]{4,3,2,1,0:T(8,128)}, u32[]{:S(2)}) %copy-start) | copy-done | bytes 2605080
  1.8 1.8 %first.1 = (f32[3,2,56,256]{3,2,1,0:T(8,128)}, f32[3,2,56,256]{3,2,1,0:T(8,128)}) custom-call(s32[3]{0:T(128)S(1)} %pad_add_fusion.info, f32[3,53,16,256]{3,2,1,0:T(8,128)S(1)} %bitcast.8), custom_call_target="tpu_custom_call" | custom-call | tf_op jit(solution)/shard_map/first/pallas_call | solution.py:445
  3.6 4.3 %collective-permute-start = (f32[3,2,56,256]{3,2,1,0:T(8,128)}, f32[3,2,56,256]{3,2,1,0:T(8,128)S(1)}, u32[]{:S(2)}, u32[]{:S(2)}) collective-permute-start(f32[3,2,56,256]{3,2,1,0:T(8,128)} %get-tuple-element.95), channel_id=1, source_target_pairs={{1,2},{3,4},{5,6},{7,8},{9,10},{11,12},{13,14},{2,1},{4,3},{6,5},{... | collective-permute-start | bytes 1032200 | tf_op jit(solution)/shard_map/ppermute | solution.py:467
  7.9 0.1 collective-permute-start.1
  8.0 0.1 copy.23.smap
  8.2 0.7 copy-done.3
  8.9 0.2 prep.1
  9.2 5.6 %old.1 = (f32[16,56,256]{2,1,0:T(8,128)S(1)}, f32[16,56,256]{2,1,0:T(8,128)S(1)}, f32[16,24,256]{2,1,0:T(8,128)S(1)}, f32[16,24,256]{2,1,0:T(8,128)S(1)}, f32[16,24,256]{2,1,0:T(8,128)S(1)}) custom-call(f32[3,53,16,256]{3,2,1,0:T(8,128)S(1)} %bitcast.9, bf16[112,256]{1,0:T(8,128)(2,1)S(1)} %get-tuple-element.100.wf, ...), custom_call_target="tpu_custom_call" | custom-call | tf_op jit(solution)/shard_map/old/pallas_call | solution.py:445
  14.7 2.1 %collective-permute-done.uo = f32[3,2,56,256]{3,2,1,0:T(8,128)S(1)} collective-permute-done((f32[3,2,56,256]{3,2,1,0:T(8,128)}, f32[3,2,56,256]{3,2,1,0:T(8,128)S(1)}, u32[]{:S(2)}, u32[]{:S(2)}) %collective-permute-start) | collective-permute-done | bytes 344096 | tf_op jit(solution)/shard_map/ppermute | solution.py:467
  16.9 0.9 old_edge.1
  17.8 4.9 %collective-permute-start.2 = (f32[2,56,256]{2,1,0:T(8,128)S(1)}, f32[2,56,256]{2,1,0:T(8,128)S(1)}, u32[]{:S(2)}, u32[]{:S(2)}) collective-permute-start(f32[2,56,256]{2,1,0:T(8,128)S(1)} %get-tuple-element.107), channel_id=1, source_target_pairs={{1,2},{3,4},{5,6},{7,8},{9,10},{11,12},{13,14},{2,1},{4,3},{6,5},{... | collective-permute-start | bytes 344072 | tf_op jit(solution)/shard_map/ppermute | solution.py:467
  22.7 0.7 collective-permute-start.3
  23.4 2.6 %mid.1 = (f32[16,56,256]{2,1,0:T(8,128)S(1)}, f32[16,24,256]{2,1,0:T(8,128)S(1)}, f32[16,24,256]{2,1,0:T(8,128)S(1)}, f32[16,24,256]{2,1,0:T(8,128)S(1)}) custom-call(f32[16,56,256]{2,1,0:T(8,128)S(1)} %get-tuple-element.112.n1, f32[16,56,256]{2,1,0:T(8,128)S(1)} %get-tuple-element.113.s, bf16[240,256]{1,0:T(8,128)(2,1)S(1)} %get-tuple-element.114.wfr, ...), custom_call_target="tpu_custom_call" | custom-call | tf_op jit(solution)/shard_map/mid/pallas_call | solution.py:445
  26.1 1.7 %mid_edge.1 = (f32[16,56,256]{2,1,0:T(8,128)S(1)}, f32[16,24,256]{2,1,0:T(8,128)S(1)}, f32[16,24,256]{2,1,0:T(8,128)S(1)}, f32[52,24,256]{2,1,0:T(8,128)S(1)}, f...) custom-call(s32[3]{0:T(128)S(1)} %pad_add_fusion.info, ...), custom_call_target="tpu_custom_call", output_to_operand_aliasing={{0}: (10, {}), {1}: (11, {}), {2}: (12, {})} | custom-call | tf_op jit(solution)/shard_map/mid_edge/pallas_call | solution.py:445
  27.7 4.7 %collective-permute-start.4 = (f32[12,24,256]{2,1,0:T(8,128)S(1)}, f32[12,24,256]{2,1,0:T(8,128)S(1)}, u32[]{:S(2)}, u32[]{:S(2)}) collective-permute-start(f32[12,24,256]{2,1,0:T(8,128)S(1)} %get-tuple-element.118.mo), channel_id=1, source_target_pairs={{1,2},{3,4},{5,6},{7,8},{9,10},{11,12},{13,14},{2,1},{4,3},{6,5},{... | collective-permute-start | bytes 884744 | tf_op jit(solution)/shard_map/ppermute | solution.py:467
  32.5 1.7 %collective-permute-start.5 = (f32[12,24,256]{2,1,0:T(8,128)S(1)}, f32[12,24,256]{2,1,0:T(8,128)S(1)}, u32[]{:S(2)}, u32[]{:S(2)}) collective-permute-start(f32[12,24,256]{2,1,0:T(8,128)S(1)} %get-tuple-element.119.mi), channel_id=1, source_target_pairs={{0,1},{1,0},{2,3},{3,2},{4,5},{5,4},{6,7},{7,6},{8,9},{9,8},{10,11... | collective-permute-start | bytes 884744 | tf_op jit(solution)/shard_map/ppermute | solution.py:467
  34.2 1.3 base.1
  35.5 3.3 %collective-permute-done.4.ho = f32[12,24,256]{2,1,0:T(8,128)S(1)} collective-permute-done((f32[12,24,256]{2,1,0:T(8,128)S(1)}, f32[12,24,256]{2,1,0:T(8,128)S(1)}, u32[]{:S(2)}, u32[]{:S(2)}) %collective-permute-start.4) | collective-permute-done | bytes 294944 | tf_op jit(solution)/shard_map/ppermute | solution.py:467
  38.8 0.7 last_edge.1
  39.5 1.8 %collective-permute-start.9 = (f32[36,24,256]{2,1,0:T(8,128)S(1)}, f32[36,24,256]{2,1,0:T(8,128)S(1)}, u32[]{:S(2)}, u32[]{:S(2)}) collective-permute-start(f32[36,24,256]{2,1,0:T(8,128)S(1)} %get-tuple-element.128.ab), channel_id=1, source_target_pairs={{32,16},{34,18},{36,20},{38,22},{40,24},{42,26},{44,28},{46,30},{3... | collective-permute-start | bytes 2654216 | tf_op jit(solution)/shard_map/ppermute | solution.py:467
  41.4 2.2 %collective-permute-start.10 = (f32[53,16,256]{2,1,0:T(8,128)S(1)}, f32[53,16,256]{2,1,0:T(8,128)S(1)}, u32[]{:S(2)}, u32[]{:S(2)}) collective-permute-start(f32[53,16,256]{2,1,0:T(8,128)S(1)} %get-tuple-element.152.b2), channel_id=1, source_target_pairs={{16,32},{17,33},{18,34},{19,35},{20,36},{21,37},{22,38},{23,39},{2... | collective-permute-start | bytes 2605064 | tf_op jit(solution)/shard_map/ppermute | solution.py:467
  43.5 0.6 start.1
  44.1 0.7 collective-permute-start.6
  44.8 0.7 collective-permute-start.7
  45.5 0.7 collective-permute-start.8
  46.2 17.8 %collective-permute-done.10 = f32[53,16,256]{2,1,0:T(8,128)S(1)} collective-permute-done((f32[53,16,256]{2,1,0:T(8,128)S(1)}, f32[53,16,256]{2,1,0:T(8,128)S(1)}, u32[]{:S(2)}, u32[]{:S(2)}) %collective-permute-start.10) | collective-permute-done | bytes 868384 | tf_op jit(solution)/shard_map/ppermute | solution.py:467
  64.0 0.7 collective-permute-start.11
  64.7 0.6 pair.3
  65.3 0.7 collective-permute-start.12
  66.0 0.7 collective-permute-start.13
  66.7 0.7 collective-permute-start.14
  67.5 0.6 gather.3
  68.1 0.7 collective-permute-start.19
  68.8 0.7 collective-permute-start.18
  69.5 0.6 pair.4
  70.1 0.7 collective-permute-start.15
  70.8 0.7 collective-permute-start.16
  71.5 0.7 collective-permute-start.17
  72.2 0.8 gather.4
  73.0 0.6 pair.5
  73.6 0.6 gather.5
  74.2 1.3 collective-permute-start.23
  75.5 0.7 collective-permute-start.20
  76.1 0.7 collective-permute-start.21
  76.8 0.7 collective-permute-start.22
  77.5 0.2 add.8.b0
  77.7 62.3 %collective-permute-done.23.other = f32[48,24,256]{2,1,0:T(8,128)S(1)} collective-permute-done((f32[48,24,256]{2,1,0:T(8,128)S(1)}, f32[48,24,256]{2,1,0:T(8,128)S(1)}, u32[]{:S(2)}, u32[]{:S(2)}) %collective-permute-start.23) | collective-permute-done | bytes 1179680 | tf_op jit(solution)/shard_map/ppermute | solution.py:467
  140.0 2.5 %out.1 = f32[3,53,16,256]{3,2,1,0:T(8,128)} custom-call(s32[3]{0:T(128)S(1)} %pad_add_fusion.info, s32[53]{0:T(128)S(1)} %bitcast.11, f32[3,53,16,256]{3,2,1,0:T(8,128)S(1)} %bitcast.10, f32[53,16,256]{2,1,0:T(8,128)S(1)} %add.8.b0, f32[53,16,256]{2,1,0:T(8,128)S(1)} %get-tuple-element.127.b1, f32[53,16,256]{2,1,0:T(8,128)S(1)} %get-tuple-element.152.b2, ...), custom_call_target="tpu_custom_call" | custom-call | tf_op jit(solution)/shard_map/out/pallas_call | solution.py:445
  (38 shorter events, 0.2 us)
Async XLA Ops:
  0.0 8.0 %copy-start.6 = (s32[53,1]{0,1:T(1,128)S(1)}, s32[53,1]{0,1:T(1,128)}, u32[]{:S(2)}) copy-start(s32[53,1]{0,1:T(1,128)} %param.15) | copy-start | bytes 640
  0.0 8.1 %copy-start.4 = (f32[21,21]{1,0:T(8,128)S(1)}, f32[21,21]{1,0:T(8,128)}, u32[]{:S(2)}) copy-start(f32[21,21]{1,0:T(8,128)} %crates.1) | copy-start | bytes 5296
  0.0 8.1 %copy-start.5 = (f32[21,21]{1,0:T(8,128)S(1)}, f32[21,21]{1,0:T(8,128)}, u32[]{:S(2)}) copy-start(f32[21,21]{1,0:T(8,128)} %cpairs.1) | copy-start | bytes 5296
  0.1 1.7 %copy-start = (f32[1,3,53,16,256]{4,3,2,1,0:T(8,128)S(1)}, f32[1,3,53,16,256]{4,3,2,1,0:T(8,128)}, u32[]{:S(2)}) copy-start(f32[1,3,53,16,256]{4,3,2,1,0:T(8,128)} %param.8) | copy-start | bytes 7815172
  1.8 6.3 %copy-start.2 = (f32[53,53]{1,0:T(8,128)S(1)}, f32[53,53]{1,0:T(8,128)}, u32[]{:S(2)}) copy-start(f32[53,53]{1,0:T(8,128)} %rates.1) | copy-start | bytes 33712
  1.8 6.3 %copy-start.7 = (f32[53]{0:T(128)S(1)}, f32[53]{0:T(128)}, u32[]{:S(2)}) copy-start(f32[53]{0:T(128)} %param.11) | copy-start | bytes 640
  1.8 6.3 %copy-start.8 = (f32[21]{0:T(128)S(1)}, f32[21]{0:T(128)}, u32[]{:S(2)}) copy-start(f32[21]{0:T(128)} %param.14) | copy-start | bytes 256
  1.8 7.3 %copy-start.1 = (f32[1,3,53,16,256]{4,3,2,1,0:T(8,128)S(1)}, f32[1,3,53,16,256]{4,3,2,1,0:T(8,128)}, u32[]{:S(2)}) copy-start(f32[1,3,53,16,256]{4,3,2,1,0:T(8,128)} %param.8) | copy-start | bytes 7815172
  3.6 13.2 %collective-permute-start = (f32[3,2,56,256]{3,2,1,0:T(8,128)}, f32[3,2,56,256]{3,2,1,0:T(8,128)S(1)}, u32[]{:S(2)}, u32[]{:S(2)}) collective-permute-start(f32[3,2,56,256]{3,2,1,0:T(8,128)} %get-tuple-element.95), channel_id=1, source_target_pairs={{1,2},{3,4},{5,6},{7,8},{9,10},{11,12},{13,14},{2,1},{4,3},{6,5},{... | collective-permute-start | bytes 1032200 | tf_op jit(solution)/shard_map/ppermute | solution.py:467
  7.9 8.9 %collective-permute-start.1 = (f32[3,2,56,256]{3,2,1,0:T(8,128)}, f32[3,2,56,256]{3,2,1,0:T(8,128)S(1)}, u32[]{:S(2)}, u32[]{:S(2)}) collective-permute-start(f32[3,2,56,256]{3,2,1,0:T(8,128)} %get-tuple-element.96), channel_id=1, source_target_pairs={{0,1},{1,0},{2,3},{3,2},{4,5},{5,4},{6,7},{7,6},{8,9},{9,8},{10,11... | collective-permute-start | bytes 1032200 | tf_op jit(solution)/shard_map/ppermute | solution.py:467
  8.2 0.8 copy-start.3
  17.8 8.3 %collective-permute-start.2 = (f32[2,56,256]{2,1,0:T(8,128)S(1)}, f32[2,56,256]{2,1,0:T(8,128)S(1)}, u32[]{:S(2)}, u32[]{:S(2)}) collective-permute-start(f32[2,56,256]{2,1,0:T(8,128)S(1)} %get-tuple-element.107), channel_id=1, source_target_pairs={{1,2},{3,4},{5,6},{7,8},{9,10},{11,12},{13,14},{2,1},{4,3},{6,5},{... | collective-permute-start | bytes 344072 | tf_op jit(solution)/shard_map/ppermute | solution.py:467
  22.7 3.3 %collective-permute-start.3 = (f32[2,56,256]{2,1,0:T(8,128)S(1)}, f32[2,56,256]{2,1,0:T(8,128)S(1)}, u32[]{:S(2)}, u32[]{:S(2)}) collective-permute-start(f32[2,56,256]{2,1,0:T(8,128)S(1)} %get-tuple-element.108), channel_id=1, source_target_pairs={{0,1},{1,0},{2,3},{3,2},{4,5},{5,4},{6,7},{7,6},{8,9},{9,8},{10,11... | collective-permute-start | bytes 344072 | tf_op jit(solution)/shard_map/ppermute | solution.py:467
  27.7 11.1 %collective-permute-start.4 = (f32[12,24,256]{2,1,0:T(8,128)S(1)}, f32[12,24,256]{2,1,0:T(8,128)S(1)}, u32[]{:S(2)}, u32[]{:S(2)}) collective-permute-start(f32[12,24,256]{2,1,0:T(8,128)S(1)} %get-tuple-element.118.mo), channel_id=1, source_target_pairs={{1,2},{3,4},{5,6},{7,8},{9,10},{11,12},{13,14},{2,1},{4,3},{6,5},{... | collective-permute-start | bytes 884744 | tf_op jit(solution)/shard_map/ppermute | solution.py:467
  32.5 6.4 %collective-permute-start.5 = (f32[12,24,256]{2,1,0:T(8,128)S(1)}, f32[12,24,256]{2,1,0:T(8,128)S(1)}, u32[]{:S(2)}, u32[]{:S(2)}) collective-permute-start(f32[12,24,256]{2,1,0:T(8,128)S(1)} %get-tuple-element.119.mi), channel_id=1, source_target_pairs={{0,1},{1,0},{2,3},{3,2},{4,5},{5,4},{6,7},{7,6},{8,9},{9,8},{10,11... | collective-permute-start | bytes 884744 | tf_op jit(solution)/shard_map/ppermute | solution.py:467
  39.5 24.4 %collective-permute-start.9 = (f32[36,24,256]{2,1,0:T(8,128)S(1)}, f32[36,24,256]{2,1,0:T(8,128)S(1)}, u32[]{:S(2)}, u32[]{:S(2)}) collective-permute-start(f32[36,24,256]{2,1,0:T(8,128)S(1)} %get-tuple-element.128.ab), channel_id=1, source_target_pairs={{32,16},{34,18},{36,20},{38,22},{40,24},{42,26},{44,28},{46,30},{3... | collective-permute-start | bytes 2654216 | tf_op jit(solution)/shard_map/ppermute | solution.py:467
  41.4 22.6 %collective-permute-start.10 = (f32[53,16,256]{2,1,0:T(8,128)S(1)}, f32[53,16,256]{2,1,0:T(8,128)S(1)}, u32[]{:S(2)}, u32[]{:S(2)}) collective-permute-start(f32[53,16,256]{2,1,0:T(8,128)S(1)} %get-tuple-element.152.b2), channel_id=1, source_target_pairs={{16,32},{17,33},{18,34},{19,35},{20,36},{21,37},{22,38},{23,39},{2... | collective-permute-start | bytes 2605064 | tf_op jit(solution)/shard_map/ppermute | solution.py:467
  44.1 2.1 %collective-permute-start.6 = (f32[16,24,256]{2,1,0:T(8,128)S(1)}, f32[16,24,256]{2,1,0:T(8,128)S(1)}, u32[]{:S(2)}, u32[]{:S(2)}) collective-permute-start(f32[16,24,256]{2,1,0:T(8,128)S(1)} %get-tuple-element.129), channel_id=1, source_target_pairs={{0,16},{1,17},{2,18},{3,19},{4,20},{5,21},{6,22},{7,23},{8,24},{9,... | collective-permute-start | bytes 1179656 | tf_op jit(solution)/shard_map/ppermute | solution.py:467
  44.8 1.4 collective-permute-start.7
  45.5 0.7 collective-permute-start.8
  64.0 0.7 collective-permute-start.11
  65.3 2.7 %collective-permute-start.12 = (f32[16,24,256]{2,1,0:T(8,128)S(1)}, f32[16,24,256]{2,1,0:T(8,128)S(1)}, u32[]{:S(2)}, u32[]{:S(2)}) collective-permute-start(f32[16,24,256]{2,1,0:T(8,128)S(1)} %get-tuple-element.142.z2), channel_id=1, source_target_pairs={{16,48},{17,65},{18,50},{19,67},{20,52},{21,69},{22,54},{23,71},{2... | collective-permute-start | bytes 1179656 | tf_op jit(solution)/shard_map/ppermute | solution.py:467
  66.0 2.0 %collective-permute-start.13 = (f32[8,24,256]{2,1,0:T(8,128)S(1)}, f32[8,24,256]{2,1,0:T(8,128)S(1)}, u32[]{:S(2)}, u32[]{:S(2)}) collective-permute-start(f32[8,24,256]{2,1,0:T(8,128)S(1)} %get-tuple-element.143), channel_id=1, source_target_pairs={{17,50},{19,52},{21,54},{23,56},{25,58},{27,60},{29,62},{18,65},{2... | collective-permute-start | bytes 589832 | tf_op jit(solution)/shard_map/ppermute | solution.py:467
  66.7 1.3 collective-permute-start.14
  68.1 4.1 %collective-permute-start.19 = (f32[48,24,256]{2,1,0:T(8,128)S(1)}, f32[48,24,256]{2,1,0:T(8,128)S(1)}, u32[]{:S(2)}, u32[]{:S(2)}) collective-permute-start(f32[48,24,256]{2,1,0:T(8,128)S(1)} %get-tuple-element.158.away_in), channel_id=1, source_target_pairs={{16,32},{18,34},{20,36},{22,38},{24,40},{26,42},{28,44},{30,46},{1... | collective-permute-start | bytes 3538952 | tf_op jit(solution)/shard_map/ppermute | solution.py:467
  68.8 4.2 %collective-permute-start.18 = (f32[53,16,256]{2,1,0:T(8,128)S(1)}, f32[53,16,256]{2,1,0:T(8,128)S(1)}, u32[]{:S(2)}, u32[]{:S(2)}) collective-permute-start(f32[53,16,256]{2,1,0:T(8,128)S(1)} %get-tuple-element.152.b2), channel_id=1, source_target_pairs={{0,16},{1,17},{2,18},{3,19},{4,20},{5,21},{6,22},{7,23},{8,24},{9,... | collective-permute-start | bytes 2605064 | tf_op jit(solution)/shard_map/ppermute | solution.py:467
  70.1 2.9 %collective-permute-start.15 = (f32[16,24,256]{2,1,0:T(8,128)S(1)}, f32[16,24,256]{2,1,0:T(8,128)S(1)}, u32[]{:S(2)}, u32[]{:S(2)}) collective-permute-start(f32[16,24,256]{2,1,0:T(8,128)S(1)} %get-tuple-element.149.z2), channel_id=1, source_target_pairs={{48,96},{65,81},{50,98},{67,83},{52,100},{69,85},{54,102},{71,87},... | collective-permute-start | bytes 1179656 | tf_op jit(solution)/shard_map/ppermute | solution.py:467
  70.8 2.2 %collective-permute-start.16 = (f32[8,24,256]{2,1,0:T(8,128)S(1)}, f32[8,24,256]{2,1,0:T(8,128)S(1)}, u32[]{:S(2)}, u32[]{:S(2)}) collective-permute-start(f32[8,24,256]{2,1,0:T(8,128)S(1)} %get-tuple-element.150), channel_id=1, source_target_pairs={{65,98},{67,100},{69,102},{71,104},{73,106},{75,108},{77,110},{50,... | collective-permute-start | bytes 589832 | tf_op jit(solution)/shard_map/ppermute | solution.py:467
  71.5 1.5 %collective-permute-start.17 = (f32[8,24,256]{2,1,0:T(8,128)S(1)}, f32[8,24,256]{2,1,0:T(8,128)S(1)}, u32[]{:S(2)}, u32[]{:S(2)}) collective-permute-start(f32[8,24,256]{2,1,0:T(8,128)S(1)} %get-tuple-element.151), channel_id=1, source_target_pairs={{48,81},{65,96},{50,83},{67,98},{52,85},{69,100},{54,87},{71,102},... | collective-permute-start | bytes 589832 | tf_op jit(solution)/shard_map/ppermute | solution.py:467
  74.2 65.8 %collective-permute-start.23 = (f32[48,24,256]{2,1,0:T(8,128)S(1)}, f32[48,24,256]{2,1,0:T(8,128)S(1)}, u32[]{:S(2)}, u32[]{:S(2)}) collective-permute-start(f32[48,24,256]{2,1,0:T(8,128)S(1)} %get-tuple-element.177), channel_id=1, source_target_pairs={{48,64},{50,66},{52,68},{54,70},{56,72},{58,74},{60,76},{62,78},{6... | collective-permute-start | bytes 3538952 | tf_op jit(solution)/shard_map/ppermute | solution.py:467
  75.5 2.2 %collective-permute-start.20 = (f32[16,24,256]{2,1,0:T(8,128)S(1)}, f32[16,24,256]{2,1,0:T(8,128)S(1)}, u32[]{:S(2)}, u32[]{:S(2)}) collective-permute-start(f32[16,24,256]{2,1,0:T(8,128)S(1)} %get-tuple-element.169.z2), channel_id=1, source_target_pairs={{96,112},{81,113},{98,114},{83,115},{100,116},{85,117},{102,118},{... | collective-permute-start | bytes 1179656 | tf_op jit(solution)/shard_map/ppermute | solution.py:467
  76.1 1.5 %collective-permute-start.21 = (f32[4,24,256]{2,1,0:T(8,128)S(1)}, f32[4,24,256]{2,1,0:T(8,128)S(1)}, u32[]{:S(2)}, u32[]{:S(2)}) collective-permute-start(f32[4,24,256]{2,1,0:T(8,128)S(1)} %get-tuple-element.170), channel_id=1, source_target_pairs={{81,114},{83,116},{85,118},{87,120},{89,122},{91,124},{93,126},{98... | collective-permute-start | bytes 294920 | tf_op jit(solution)/shard_map/ppermute | solution.py:467
  76.8 0.9 collective-permute-start.22

commit v3 on v2

v3 whole, which is shorter than its diff:
```python
import functools

import jax
import jax.numpy as jnp
from jax import lax
from jax.experimental import pallas as pl
from jax.experimental.pallas import tpu as pltpu
from jax.sharding import PartitionSpec as P

SPECIES, COARSE = 53, 21
SP, CP = 56, 24
ROWS, COLS = 16, 256
SLICES, SLABS = 8, 16
STEP, HALF, RELAX = 0.1, 0.05, 3.0
W0 = (5.0 / 24.0, 1.0 / 3.0, -1.0 / 24.0)
W1 = (-1.0 / 24.0, 1.0 / 3.0, 5.0 / 24.0)
F32, BF16 = jnp.float32, jnp.bfloat16
GROUPS = (((0,), (0, 0)), ((1, 2), (1, 5)), ((3, 4), (3, 4)), ((5, 6), (5, 6)), ((7,), (7, 7)))
VMEM_LIMIT = 24 * 1024 * 1024


def split(x):
    hi = x.astype(BF16)
    lo = (x - hi.astype(F32)).astype(BF16)
    return jnp.concatenate([hi, lo], axis=0)


def thirds(x):
    hi = x.astype(BF16)
    rest = x - hi.astype(F32)
    mid = rest.astype(BF16)
    return jnp.concatenate([hi, mid, (rest - mid.astype(F32)).astype(BF16)], axis=0)


def zeros(rows):
    return jnp.zeros((rows, COLS), F32)


def dot(w, x):
    return jnp.dot(w, x, preferred_element_type=F32)


def stacked(x, squares):
    return split(jnp.concatenate([x, squares, zeros(16)], axis=0))


def lap_y(x):
    near = pltpu.roll(x, 1, 1) + pltpu.roll(x, COLS - 1, 1)
    far = pltpu.roll(x, 2, 1) + pltpu.roll(x, COLS - 2, 1)
    return 16.0 * near - far - 60.0 * x


def lap_rows(ref, x):
    return 16.0 * (ref[x - 1] + ref[x + 1]) - (ref[x - 2] + ref[x + 2])


def beside(near, far):
    return 16.0 * near - far, -near


def prep_kernel(rates, pairs, diff, crates, cpairs, cdiff, smap, wf, wr, wfr, lv, wc, pro, d12, dc12, share, a, mi):
    row = lax.broadcasted_iota(jnp.int32, (SP, 128), 0)
    lane = lax.broadcasted_iota(jnp.int32, (SP, 128), 1)

    def framed(ref, rows, columns, height):
        a[...] = jnp.zeros((SP, 128), F32)
        a[:rows, :columns] = ref[...]
        return a[:height, :]

    def halves(x):
        hi = x.astype(BF16).astype(F32)
        return hi, (x - hi).astype(BF16).astype(F32)

    def column(values, height):
        return jnp.sum(jnp.where(row == lane, values, 0.0), axis=1, keepdims=True)[:height]

    eye = jnp.where(row == lane, RELAX, 0.0)
    fine = framed(rates, SPECIES, SPECIES, SP) - jnp.where(row < SPECIES, eye, 0.0)
    fine = fine + pltpu.roll(framed(pairs, SPECIES, SPECIES, SP), SP, 1)
    coarse = framed(crates, COARSE, COARSE, CP) - jnp.where(row < COARSE, eye, 0.0)[:CP]
    coarse = coarse + pltpu.roll(framed(cpairs, COARSE, COARSE, CP), CP, 1)
    diff_row = framed(diff, 1, SPECIES, 8)[0:1]
    d12[...] = jnp.broadcast_to(column(diff_row, SP) / 12.0, (SP, COLS))
    dc12[...] = jnp.broadcast_to(column(framed(cdiff, 1, COARSE, 8)[0:1], CP) / 12.0, (CP, COLS))
    mi[...] = jnp.full((SP, 128), -1, jnp.int32)
    mi[:SPECIES, 0:1] = smap[...]
    map_column = mi[:, 0:1]
    map_row = jnp.sum(jnp.where(row == lane, map_column, 0), axis=0, keepdims=True)
    lum = jnp.where((map_row == row[:CP]) & (lane[:CP] < SPECIES), 1.0, 0.0)
    counts = jnp.sum(lum, axis=1, keepdims=True)
    share[...] = jnp.broadcast_to(1.0 / jnp.maximum(counts, 1.0), (CP, COLS))
    lumped = jnp.dot(lum[:, :SP], fine, precision=lax.Precision.HIGHEST, preferred_element_type=F32)
    fh, fl = halves(fine)
    rh, rl = halves(lumped)
    dh, dl = halves(lum * diff_row)
    ch, cl = halves(coarse)
    f = jnp.concatenate([fh, fl], axis=0).astype(BF16)
    r = jnp.concatenate([rh, rl, lum, dh, dl, jnp.zeros((8, 128), F32)], axis=0).astype(BF16)
    for at in (0, 128):
        wf[:, at : at + 128] = f
        wr[:, at : at + 128] = r
        wfr[: 2 * SP, at : at + 128] = f
        wfr[2 * SP :, at : at + 128] = r
    v = jnp.concatenate([lum, dh, dl, jnp.zeros((8, 128), F32)], axis=0)
    lv[...] = (v + pltpu.roll(v, 64, 1)).astype(BF16)
    c = jnp.concatenate([ch, cl], axis=0)
    wc[...] = (c + pltpu.roll(c, 64, 1)).astype(BF16)
    lane96 = lax.broadcasted_iota(jnp.int32, (SP, 96), 1)
    pro[...] = jnp.where(map_column == lane96 % 32, 1.0, 0.0).astype(BF16)


class Position:
    def __init__(self):
        self.slice_at, self.slab = lax.axis_index("tm"), lax.axis_index("space")

    def __getitem__(self, at):
        return (self.slab % 2, self.slice_at, self.slab)[at]


def blocks(rows, body):
    @pl.loop(0, rows // 4)
    def _(i):
        body(4 * i)


def first_kernel(u, outer, inner):
    info = Position()
    at_top = info[0] == 0
    for m in range(3):
        for r in range(2):
            first, last = u[m, :, r, :], u[m, :, ROWS - 2 + r, :]
            for out, value in ((outer, jnp.where(at_top, first, last)), (inner, jnp.where(at_top, last, first))):
                out[m, r, SP - 8 :, :] = zeros(8)
                out[m, r, :SPECIES, :] = value


def restricted(y):
    return y[0:24] + y[24:48], y[48:72], y[72:96] + y[96:120]


MIX0 = [STEP * w for w in W0]
MIXS = [STEP * W1[0], STEP * W1[1] - HALF, STEP * W1[2]]


def mixed(factors, values):
    return factors[0] * values[0] + factors[1] * values[1] + factors[2] * values[2]


def old_kernel(u, wf, wr, wc, d12, dc12, n1, s, r0, e0, c0, ut, p0s, pss, v0s, c0s):
    for k in range(4):
        for m in range(3):
            ut[k, m, SP - 8 :, :] = zeros(8)
    for x in (0, 1, ROWS + 2, ROWS + 3):
        p0s[x], pss[x], v0s[x], c0s[x] = zeros(SP), zeros(SP), zeros(CP), zeros(CP)

    def terms(x0):
        for k in range(4):
            for m in range(3):
                ut[k, m, :SPECIES, :] = u[m, :, x0 + k, :]
        for k in range(4):
            x = x0 + k
            us = [ut[k, m] for m in range(3)]
            qs = [v * v for v in us]
            p0, ps = mixed(MIX0, us), mixed(MIXS, us)
            y = dot(wf[...], stacked(p0, mixed(MIX0, qs)))
            n1[x] = us[0] + (y[:SP] + y[SP:]) + d12[...] * lap_y(p0)
            y = dot(wf[...], stacked(ps, mixed(MIXS, qs)))
            s[x] = (y[:SP] + y[SP:]) + d12[...] * lap_y(ps)
            r, c, v = restricted(dot(wr[...], stacked(us[0], qs[0])))
            r0[x] = r + lap_y(v) * (1.0 / 12.0)
            y = dot(wc[...], stacked(c, c * c))
            e0[x] = (y[:CP] + y[CP:]) + dc12[...] * lap_y(c)
            p0s[x + 2], pss[x + 2], v0s[x + 2], c0s[x + 2], c0[x] = p0, ps, v, c, c

    blocks(ROWS, terms)

    def laps(x0):
        for k in range(4):
            x = x0 + k
            n1[x] += d12[...] * lap_rows(p0s, x + 2)
            s[x] += d12[...] * lap_rows(pss, x + 2)
            r0[x] += lap_rows(v0s, x + 2) * (1.0 / 12.0)
            e0[x] += dc12[...] * lap_rows(c0s, x + 2)

    blocks(ROWS, laps)


def lumped_halo(lv, row):
    y = dot(lv[...], split(jnp.concatenate([row, zeros(8)], axis=0)))
    return y[0:24], y[24:48] + y[48:72]


SIDES = (((0, 1), (1, 0)), ((ROWS - 1, ROWS - 2), (0, 1)))


def pick_halo(info, side, outer, inner):
    take = info[0] == side
    return lambda *at: jnp.where(take, outer[at], inner[at])


def send(info, outer, inner, tops, bottoms):
    at_top = info[0] == 0
    for r, (top, bottom) in enumerate(zip(tops, bottoms)):
        outer[r] = jnp.where(at_top, top, bottom)
        inner[r] = jnp.where(at_top, bottom, top)


def old_edge_kernel(uo, ui, lv, d12, dc12, n1i, si, r0i, e0i, n1, s, r0, e0, outer, inner):
    info = Position()
    for side, (rows, order) in enumerate(SIDES):
        halo = pick_halo(info, side, uo, ui)
        us = [[halo(m, r) for m in range(3)] for r in order]
        p0 = beside(*[mixed(MIX0, v) for v in us])
        ps = beside(*[mixed(MIXS, v) for v in us])
        lumped = [lumped_halo(lv, v[0]) for v in us]
        c = beside(lumped[0][0], lumped[1][0])
        v = beside(lumped[0][1], lumped[1][1])
        for i, x in enumerate(rows):
            n1[x] = n1i[x] + d12[...] * p0[i]
            s[x] = si[x] + d12[...] * ps[i]
            r0[x] = r0i[x] + v[i] * (1.0 / 12.0)
            e0[x] = e0i[x] + dc12[...] * c[i]
    send(info, outer, inner, [n1[0], n1[1]], [n1[ROWS - 2], n1[ROWS - 1]])


def mid_kernel(n1, s, wfr, wc, d12, dc12, n2, r1, e1, c1, n1s, v1s, c1s):
    for x in (0, 1, ROWS + 2, ROWS + 3):
        n1s[x], v1s[x], c1s[x] = zeros(SP), zeros(CP), zeros(CP)

    def terms(x0):
        for k in range(4):
            x = x0 + k
            n = n1[x]
            y = dot(wfr[...], stacked(n, n * n))
            n2[x] = n + HALF * ((y[:SP] + y[SP : 2 * SP]) + d12[...] * lap_y(n)) + s[x]
            r, c, v = restricted(y[2 * SP :])
            r1[x] = r + lap_y(v) * (1.0 / 12.0)
            y = dot(wc[...], stacked(c, c * c))
            e1[x] = (y[:CP] + y[CP:]) + dc12[...] * lap_y(c)
            n1s[x + 2], v1s[x + 2], c1s[x + 2], c1[x] = n, v, c, c

    blocks(ROWS, terms)

    def laps(x0):
        for k in range(4):
            x = x0 + k
            n2[x] += (HALF * d12[...]) * lap_rows(n1s, x + 2)
            r1[x] += lap_rows(v1s, x + 2) * (1.0 / 12.0)
            e1[x] += dc12[...] * lap_rows(c1s, x + 2)

    blocks(ROWS, laps)


def lumped_old(first, c0, e0):
    return jnp.where(first, c0, -HALF * e0)


AB_ROWS, EXT_ROWS = 2 * ROWS + 4, 2 * ROWS + 20
A0, B0 = 2, ROWS + 4
XA0, XB0 = 6, ROWS + 16


def mid_edge_kernel(no, ni, lv, wr, d12, dc12, r0, e0, c0, n2i, r1i, e1i, n2, r1, e1, ab, c2, outer, inner, v2s, gs):
    info = Position()
    first = info[1] == 0
    for side, (rows, order) in enumerate(SIDES):
        halo = pick_halo(info, side, no, ni)
        ns = [halo(r) for r in order]
        lumped = [lumped_halo(lv, v) for v in ns]
        c = beside(lumped[0][0], lumped[1][0])
        v = beside(lumped[0][1], lumped[1][1])
        n = beside(*ns)
        for i, x in enumerate(rows):
            n2[x] = n2i[x] + (HALF * d12[...]) * n[i]
            r1[x] = r1i[x] + v[i] * (1.0 / 12.0)
            e1[x] = e1i[x] + dc12[...] * c[i]
    for x in (0, 1, ROWS + 2, ROWS + 3):
        v2s[x] = zeros(CP)

    def lumped(x, value):
        gs[x], c2[x], v2s[x + 2] = restricted(dot(wr[...], stacked(value, value * value)))

    def pieces(x, mid, late):
        v = v2s[x + 2]
        g2 = gs[x] + (lap_y(v) + lap_rows(v2s, x + 2)) * (1.0 / 12.0)
        ab[x + XA0] = mixed(MIX0, (r0[x], mid, g2)) + lumped_old(first, c0[x], e0[x])
        ab[x + XB0] = mixed([STEP * w for w in W1], (r0[x], mid, g2)) - HALF * late

    edges = (0, 1, ROWS - 2, ROWS - 1)
    for x in edges:
        lumped(x, n2[x])
    blocks(ROWS - 4, lambda x0: [lumped(x, n2i[x]) for x in (x0 + 2, x0 + 3, x0 + 4, x0 + 5)])
    for x in edges:
        pieces(x, r1[x], e1[x])
    blocks(ROWS - 4, lambda x0: [pieces(x, r1i[x], e1i[x]) for x in (x0 + 2, x0 + 3, x0 + 4, x0 + 5)])
    top = [ab[x + XA0] for x in range(6)] + [ab[x + XB0] for x in range(4)] + [v2s[x + 2] for x in range(2)]
    bottom = [ab[x + XA0] for x in range(ROWS - 6, ROWS)] + [ab[x + XB0] for x in range(ROWS - 4, ROWS)]
    send(info, outer, inner, top, bottom + [v2s[x] for x in range(ROWS, ROWS + 2)])


def last_edge_kernel(mo, mi, ho, hi, abi, ab, short):
    info = Position()
    ka, kb = STEP * W0[2] / 12.0, STEP * W1[2] / 12.0
    done = {}
    for side, (rows, order) in enumerate(SIDES):
        inside = info[2] > 0 if side == 0 else info[2] < SLABS - 1
        own, halo = pick_halo(info, side, mo, mi), pick_halo(info, side, ho, hi)
        fix = beside(*[halo(10 + r) for r in order])
        theirs = beside(*[own(10 + r) for r in order[::-1]])
        for i, x in enumerate(rows):
            done[x + XA0] = abi[x + XA0] + ka * fix[i]
            done[x + XB0] = abi[x + XB0] + kb * fix[i]
        for depth, at, to, factor in ((6, 0, XA0, ka), (4, 6, XB0, kb)):
            for i in range(depth):
                x = -1 - i if side == 0 else ROWS + i
                value = halo(at + (depth - 1 - i if side == 0 else i))
                if i < 2:
                    value = value + factor * theirs[i]
                done[x + to] = jnp.where(inside, value, 0.0)
    for at, value in done.items():
        ab[at] = value
    for x in range(-2, ROWS + 2):
        short[x + A0] = done[x + XA0] if x + XA0 in done else abi[x + XA0]
    for x in range(ROWS):
        short[x + B0] = done[x + XB0] if x + XB0 in done else abi[x + XB0]


def sweep(info, z, z0, add, add0, out, out0, low, rows, wc, dc12):
    def body(i):
        x0 = i + low
        z8 = [z[x0 + z0 + k] for k in range(-2, 6)]
        for k in range(4):
            x, value = x0 + k, z8[k + 2]
            y = dot(wc[...], stacked(value, value * value))
            lap = lap_y(value) + 16.0 * (z8[k + 1] + z8[k + 3]) - (z8[k] + z8[k + 4])
            value = value + HALF * ((y[:CP] + y[CP:]) + dc12[...] * lap) + add[x + add0]
            if low < 0:
                inside = ((x >= 0) | (info[2] > 0)) & ((x < ROWS) | (info[2] < SLABS - 1))
                value = jnp.where(inside, value, 0.0)
            out[x + out0] = value

    blocks(rows, body)


def begin(info, z0, zo, zi, depth, zs):
    top, bottom = pick_halo(info, 0, zo, zi), pick_halo(info, 1, zo, zi)
    for r in range(depth):
        zs[r], zs[depth + ROWS + r] = top(r), bottom(r)

    def body(x):
        for k in range(4):
            zs[depth + x + k] = z0[x + k]

    blocks(ROWS, body)


def give(info, depth, outer, inner, value):
    send(info, outer, inner, [value(x) for x in range(depth)], [value(x) for x in range(ROWS - depth, ROWS)])


def hosting(info, hosts):
    return info[1] == jnp.where(info[0] == 0, hosts[0], hosts[1])


def start_kernel(hosts, ab, wc, dc12, result, message, outer, inner):
    info = Position()

    @pl.when(hosting(info, hosts))
    def _():
        sweep(info, ab, A0, ab, B0, message, 0, 0, ROWS, wc, dc12)
        give(info, 8, outer, inner, lambda x: message[x])

        def body(x0):
            for x in (x0, x0 + 1, x0 + 2, x0 + 3):
                result[x], result[ROWS + x], result[2 * ROWS + x] = zeros(CP), ab[x + A0], message[x]

        blocks(ROWS, body)


def pair_kernel(
    slices, hosts, depth, z0, zo, zi, mine, short, long, wc, dc12, message, outer, inner, za, zb, zc, zs
):
    info = Position()

    def sweeps(one, two):
        begin(info, z0, zo, zi, 8, zs)
        sweep(info, zs, 8, one, XA0, za, 6, -6, ROWS + 12, wc, dc12)
        sweep(info, za, 6, one, XB0, zb, 4, -4, ROWS + 8, wc, dc12)
        if two is mine:
            sweep(info, zb, 4, two, XA0, zc, 2, -2, ROWS + 4, wc, dc12)
            sweep(info, zc, 2, two, XB0, message, 0, 0, ROWS, wc, dc12)
        else:
            sweep(info, zb, 4, two, A0, zc, 2, -2, ROWS + 4, wc, dc12)
            sweep(info, zc, 2, two, B0, message, 0, 0, ROWS, wc, dc12)
        give(info, depth, outer, inner, lambda x: message[x])

    for host in sorted(set(hosts)):
        one = mine if host == slices[0] else long
        two = mine if host == slices[1] else short
        pl.when(hosting(info, hosts) & (info[1] == host))(functools.partial(sweeps, one, two))


def gather(z0, za, zb, zc, z2, one, two):
    def body(x0):
        for x in (x0, x0 + 1, x0 + 2, x0 + 3):
            one[x], one[ROWS + x], one[2 * ROWS + x] = z0[x], za[x + 6], zb[x + 4]
            two[x], two[ROWS + x], two[2 * ROWS + x] = zb[x + 4], zc[x + 2], z2[x]

    blocks(ROWS, body)


def gather_kernel(slices, hosts, z0, za, zb, zc, z2, home_in, away_in, home, away):
    info = Position()
    active, second = hosting(info, hosts), info[1] == slices[1]
    pl.when(active & ~second)(lambda: gather(z0, za, zb, zc, z2, home, away))
    pl.when(active & second)(lambda: gather(z0, za, zb, zc, z2, away, home))


def base_kernel(n1, n2, c1, c2, pro, share, b1, b2):
    def body(x0):
        for x in (x0, x0 + 1, x0 + 2, x0 + 3):
            for n, c, b in ((n1, c1, b1), (n2, c2, b2)):
                value = thirds(jnp.concatenate([share[...] * c[x], zeros(8)], axis=0))
                b[:, x, :] = (n[x] - dot(pro[...], value))[:SPECIES]

    blocks(ROWS, body)


def out_kernel(
    where, u, b0, b1, b2, share, z0, zo, zi, ab, wc, dc12, home, one, other, out, z, za, zs, spread, node, sem
):
    info = Position()
    last = info[1] == SLICES - 1
    at_home = hosting(info, GROUPS[0][1])
    for slices, hosts in GROUPS[1:-1]:
        at_home = at_home | (hosting(info, hosts) & ((info[1] == slices[0]) | (info[1] == slices[1])))
    first = info[1] == GROUPS[1][0][0]
    for here, result in ((at_home, home), (first & ~at_home, one), (~at_home & ~first & ~last, other)):

        @pl.when(here)
        def _():

            def body(x0):
                for x in (x0, x0 + 1, x0 + 2, x0 + 3):
                    z[x] = result[x]

            blocks(3 * ROWS, body)

    @pl.when(last)
    def _():
        begin(info, z0, zo, zi, 4, zs)

        def body(x0):
            for x in (x0, x0 + 1, x0 + 2, x0 + 3):
                z[x] = z0[x]

        blocks(ROWS, body)

    def finish(m, base):
        def body(x0):
            for x in (x0, x0 + 1, x0 + 2, x0 + 3):
                spread[m, :, x, :] = share[...] * z[m * ROWS + x]

        blocks(ROWS, body)

        def add(s):
            node[m, s] = base(s) + spread[m, where[s]]

        blocks(SPECIES, lambda s: [add(s + k) for k in range(4)])
        for s in range(SPECIES - SPECIES % 4, SPECIES):
            add(s)
        copy = pltpu.make_async_copy(node.at[m], out.at[m], sem.at[m])
        copy.start()
        return copy

    first = info[1] == 0
    copies = [finish(0, lambda s: jnp.where(first, u[0, s], b0[s]))]

    @pl.when(last)
    def _():
        sweep(info, zs, 4, ab, A0, za, 2, -2, ROWS + 4, wc, dc12)
        sweep(info, za, 2, ab, B0, z.at[pl.ds(2 * ROWS, ROWS)], 0, 0, ROWS, wc, dc12)

        def body(x0):
            for x in (x0, x0 + 1, x0 + 2, x0 + 3):
                z[ROWS + x] = za[x + 2]

        blocks(ROWS, body)

    copies += [finish(1, lambda s: b1[s]), finish(2, lambda s: b2[s])]
    for copy in copies:
        copy.wait()


def field(*shape):
    return jax.ShapeDtypeStruct(shape + (COLS,), F32)


SMEM = pl.BlockSpec(memory_space=pltpu.SMEM)
VMEM = pl.BlockSpec(memory_space=pltpu.VMEM)
ANY = pl.BlockSpec(memory_space=pl.ANY)


def call(kernel, name, outs, *args, scratch=(), alias=None, out_specs=None):
    specs = [SMEM if a.dtype == jnp.int32 and a.ndim == 1 else VMEM for a in args]
    return pl.pallas_call(
        kernel,
        out_shape=outs,
        in_specs=specs,
        **({"out_specs": out_specs} if out_specs else {}),
        scratch_shapes=[pltpu.VMEM(f.shape, f.dtype) if isinstance(f, jax.ShapeDtypeStruct) else f for f in scratch],
        input_output_aliases=alias or {},
        compiler_params=pltpu.CompilerParams(vmem_limit_bytes=VMEM_LIMIT),
        name=name,
    )(*args)


AXES = ("tm", "space")
OUTER = [(s, s + 1) for s in range(1, SLABS - 1, 2)] + [(s + 1, s) for s in range(1, SLABS - 1, 2)]
INNER = [(s, s ^ 1) for s in range(SLABS)]
SAME = [(s, s) for s in range(SLABS)]


def moved(value, *routes):
    pairs = [
        (source[s % 2] * SLABS + s, target[t % 2] * SLABS + t) for source, target, slabs in routes for s, t in slabs
    ]
    return lax.ppermute(value, AXES, pairs)


def both(p):
    return (p, p)


def swap(outer, inner):
    got_inner = moved(inner, *[(both(p), both(p), INNER) for p in range(SLICES)])
    got_outer = moved(outer, *[(both(p), both(p), OUTER) for p in range(SLICES)])
    return got_outer, got_inner


def hop(message, outer, inner, source, target):
    parts = ((outer, OUTER), (inner, INNER), (message, SAME))
    zo, zi, z = [moved(value, (source, target, slabs)) for value, slabs in parts]
    return [z, zo, zi]


def after(value, other):
    return lax.optimization_barrier((value, other))[0]


def local(fine_nodes, fine_rates, fine_pairs, fine_diff, coarse_rates, coarse_pairs, coarse_diff, species_map):
    nodes = fine_nodes[0]
    fine, coarse = field(ROWS, SP), field(ROWS, CP)
    message = field(3, 2, SP)
    outer, inner = call(first_kernel, "first", [message, message], nodes)
    uo, ui = swap(outer, inner)

    def bf16(*shape):
        return jax.ShapeDtypeStruct(shape, BF16)

    wf, wr, wfr, lv, wc, pro, d12, dc12, share = call(
        prep_kernel,
        "prep",
        [bf16(2 * SP, 256), bf16(128, 256), bf16(2 * SP + 128, 256), bf16(80, 128), bf16(2 * CP, 128), bf16(SP, 96)]
        + [field(SP), field(CP), field(CP)],
        fine_rates,
        fine_pairs,
        fine_diff.reshape(1, SPECIES),
        coarse_rates,
        coarse_pairs,
        coarse_diff.reshape(1, COARSE),
        species_map,
        scratch=[pltpu.VMEM((SP, 128), F32), pltpu.VMEM((SP, 128), jnp.int32)],
    )
    n1, s, r0, e0, c0 = call(
        old_kernel,
        "old",
        [fine, fine, coarse, coarse, coarse],
        *(nodes, wf, wr, wc, d12, dc12),
        scratch=[field(4, 3, SP), field(ROWS + 4, SP), field(ROWS + 4, SP), field(ROWS + 4, CP), field(ROWS + 4, CP)],
    )
    two, twelve, eight = field(2, SP), field(12, CP), field(8, CP)
    n1, s, r0, e0, outer, inner = call(
        old_edge_kernel,
        "old_edge",
        [fine, fine, coarse, coarse, two, two],
        *(uo, ui, lv, d12, dc12, n1, s, r0, e0),
        alias={5: 0, 6: 1, 7: 2, 8: 3},
    )
    no, ni = swap(outer, inner)
    n2, r1, e1, c1 = call(
        mid_kernel, "mid", [fine, coarse, coarse, coarse], n1, s, wfr, wc, d12, dc12, scratch=[field(ROWS + 4, SP), field(ROWS + 4, CP), field(ROWS + 4, CP)]
    )
    extended, short = field(EXT_ROWS, CP), field(AB_ROWS, CP)
    n2, r1, e1, abx, c2, outer, inner = call(
        mid_edge_kernel,
        "mid_edge",
        [fine, coarse, coarse, extended, coarse, twelve, twelve],
        *(no, ni, lv, wr, d12, dc12, r0, e0, c0, n2, r1, e1),
        alias={9: 0, 10: 1, 11: 2},
        scratch=[field(ROWS + 4, CP), coarse],
    )
    ho, hi = swap(outer, inner)
    b1, b2 = call(base_kernel, "base", [field(SPECIES, ROWS)] * 2, n1, n2, c1, c2, pro, share)
    abx, ab = call(last_edge_kernel, "last_edge", [extended, short], outer, inner, ho, hi, abx, alias={4: 0})

    ab, abx = after(ab, b1), after(abx, b1)
    result = field(3 * ROWS, CP)
    pairs = [(slices, hosts) for slices, hosts in GROUPS if len(slices) == 2]
    short, long, back, first = [], [], [], []
    for slices, hosts in pairs:
        for core, host in enumerate(hosts):
            slabs = [(t, t) for t in range(core, SLABS, 2)]
            if host != slices[0]:
                long.append((both(slices[0]), both(host), slabs))
            if host != slices[1]:
                short.append((both(slices[1]), both(host), slabs))
            back.append((both(host), both(slices[0] if host == slices[1] else slices[1]), slabs))
            if host not in slices:
                first.append((both(host), both(slices[0]), slabs))
    short, long = moved(ab, *short), moved(abx, *long)
    forward = [(both(p), both(p + 1), SAME) for p in range(SLICES - 1)]
    home, *sent = call(
        functools.partial(start_kernel, GROUPS[0][1]), "start", [result, coarse, eight, eight], ab, wc, dc12
    )
    away = home
    for at, (slices, hosts) in enumerate(GROUPS[1:], 1):
        z = hop(*sent, GROUPS[at - 1][1], hosts)
        if at == 1:
            *z, short, long = lax.optimization_barrier((*z, short, long))
            b0 = moved(after(b2, z[0]), *forward)
        elif at == 2:
            *z, b0 = lax.optimization_barrier((*z, b0))
            one = moved(after(home, z[0]), *first)
        elif at == 3:
            *z, one, home, away = lax.optimization_barrier((*z, one, home, away))
        else:
            other = moved(away, *back)
            *z, other, home = lax.optimization_barrier((*z, other, home))
        if len(slices) == 2:
            depth = 4 * len(GROUPS[at + 1][0])
            *sent, za, zb, zc = call(
                functools.partial(pair_kernel, slices, hosts, depth),
                "pair",
                [coarse, field(depth, CP), field(depth, CP), field(ROWS + 12, CP), field(ROWS + 8, CP), field(ROWS + 4, CP)],
                *(*z, abx, short, long, wc, dc12),
                scratch=[field(ROWS + 16, CP)],
            )
            home, away = call(
                functools.partial(gather_kernel, slices, hosts),
                "gather",
                [result, result],
                *(z[0], za, zb, zc, sent[0], home, away),
                alias={5: 0, 6: 1},
            )
    out = call(
        out_kernel,
        "out",
        field(3, SPECIES, ROWS),
        *(species_map[:, 0], nodes, b0, b1, b2, share, *z, ab, wc, dc12, home, one, other),
        out_specs=ANY,
        scratch=[result, field(ROWS + 4, CP), field(ROWS + 8, CP), field(3, CP, ROWS), field(3, SPECIES, ROWS), pltpu.SemaphoreType.DMA((3,))],
    )
    return out[None]


def solution(mesh):
    in_specs = (P("tm", None, None, "space", None), P(), P(), P(), P(), P(), P(), P())
    out_specs = P("tm", None, None, "space", None)
    return jax.shard_map(local, mesh=mesh, in_specs=in_specs, out_specs=out_specs, check_vma=False)
```

time: 143 us -> 125 us (0.87)
  the two profiles are of different devices: /device:TPU:75 before, /device:TPU:51 now
where the time goes in v3:
time: 125 us; the launch traced here: 123 us
  waiting for transfers between devices  57.7 us (46%)
  starting transfers between devices  37.1 us (30%)
  Pallas kernels  23.3 us (19%)
  local copies, waits for them, and re-layouts  4.75 us (4%)
    ppermute x23, waiting for transfers between devices, moved(): return lax.ppermute(value, AXES, pairs)  57.7 us
    ppermute x23, starting transfers between devices, moved(): return lax.ppermute(value, AXES, pairs)  37.1 us
    pallas_call x16, Pallas kernels, call(): pl.pallas_call(kernel, out_shape=outs, in_specs=specs, **{'out_specs': ou...  23.3 us
    unnamed x20, local copies, waits for them, and re-layouts  4.75 us
  transfers between devices with their start and end apart: 23, of which 9 were waited for; matrix products, arithmetic and copies ran while one was open for 1% of the time, Pallas kernels for 14%

profile of v3, /device:TPU:51, one launch (start us, length us, event | category | flops | bytes accessed | tf_op | source)
XLA Modules:
  0.0 123.3 jit_solution(3196680053046071509)
XLA Ops:
  0.0 1.7 %copy-done = f32[1,3,53,16,256]{4,3,2,1,0:T(8,128)S(1)} copy-done((f32[1,3,53,16,256]{4,3,2,1,0:T(8,128)S(1)}, f32[1,3,53,16,256]{4,3,2,1,0:T(8,128)}, u32[]{:S(2)}) %copy-start) | copy-done | bytes 2605080
  1.7 1.2 first.1
  3.0 4.3 %collective-permute-start = (f32[3,2,56,256]{3,2,1,0:T(8,128)}, f32[3,2,56,256]{3,2,1,0:T(8,128)S(1)}, u32[]{:S(2)}, u32[]{:S(2)}) collective-permute-start(f32[3,2,56,256]{3,2,1,0:T(8,128)} %get-tuple-element.92), channel_id=1, source_target_pairs={{1,2},{3,4},{5,6},{7,8},{9,10},{11,12},{13,14},{2,1},{4,3},{6,5},{... | collective-permute-start | bytes 1032200 | tf_op jit(solution)/shard_map/ppermute | solution.py:528
  7.3 0.1 collective-permute-start.1
  7.4 0.8 copy.23.smap
  8.1 0.7 copy-done.3
  8.9 0.7 copy-done.4
  9.6 0.7 copy-done.5
  10.3 0.2 prep.1
  10.6 6.4 %old.1 = (f32[16,56,256]{2,1,0:T(8,128)S(1)}, f32[16,56,256]{2,1,0:T(8,128)S(1)}, f32[16,24,256]{2,1,0:T(8,128)S(1)}, f32[16,24,256]{2,1,0:T(8,128)S(1)}, f32[16,24,256]{2,1,0:T(8,128)S(1)}) custom-call(f32[3,53,16,256]{3,2,1,0:T(8,128)S(1)} %bitcast.6, bf16[112,256]{1,0:T(8,128)(2,1)S(1)} %get-tuple-element.97.wf, ...), custom_call_target="tpu_custom_call" | custom-call | tf_op jit(solution)/shard_map/old/pallas_call | solution.py:506
  17.0 0.4 old_edge.1
  17.4 4.2 %collective-permute-start.2 = (f32[2,56,256]{2,1,0:T(8,128)S(1)}, f32[2,56,256]{2,1,0:T(8,128)S(1)}, u32[]{:S(2)}, u32[]{:S(2)}) collective-permute-start(f32[2,56,256]{2,1,0:T(8,128)S(1)} %get-tuple-element.104), channel_id=1, source_target_pairs={{1,2},{3,4},{5,6},{7,8},{9,10},{11,12},{13,14},{2,1},{4,3},{6,5},{... | collective-permute-start | bytes 344072 | tf_op jit(solution)/shard_map/ppermute | solution.py:528
  21.5 0.7 collective-permute-start.3
  22.2 3.7 %mid.1 = (f32[16,56,256]{2,1,0:T(8,128)S(1)}, f32[16,24,256]{2,1,0:T(8,128)S(1)}, f32[16,24,256]{2,1,0:T(8,128)S(1)}, f32[16,24,256]{2,1,0:T(8,128)S(1)}) custom-call(f32[16,56,256]{2,1,0:T(8,128)S(1)} %get-tuple-element.109.n1, f32[16,56,256]{2,1,0:T(8,128)S(1)} %get-tuple-element.110.s, bf16[240,256]{1,0:T(8,128)(2,1)S(1)} %get-tuple-element.111.wfr, ...), custom_call_target="tpu_custom_call" | custom-call | tf_op jit(solution)/shard_map/mid/pallas_call | solution.py:506
  25.9 1.9 %mid_edge.1 = (f32[16,56,256]{2,1,0:T(8,128)S(1)}, f32[16,24,256]{2,1,0:T(8,128)S(1)}, f32[16,24,256]{2,1,0:T(8,128)S(1)}, f32[52,24,256]{2,1,0:T(8,128)S(1)}, f...) custom-call(f32[2,56,256]{2,1,0:T(8,128)S(1)} %collective-permute-do, ...), custom_call_target="tpu_custom_call", output_to_operand_aliasing={{0}: (9, {}), {1}: (10, {}), {2}: (11, {})} | custom-call | tf_op jit(solution)/shard_map/mid_edge/pallas_call | solution.py:506
  27.9 3.8 %collective-permute-start.4 = (f32[12,24,256]{2,1,0:T(8,128)S(1)}, f32[12,24,256]{2,1,0:T(8,128)S(1)}, u32[]{:S(2)}, u32[]{:S(2)}) collective-permute-start(f32[12,24,256]{2,1,0:T(8,128)S(1)} %get-tuple-element.115.mo), channel_id=1, source_target_pairs={{1,2},{3,4},{5,6},{7,8},{9,10},{11,12},{13,14},{2,1},{4,3},{6,5},{... | collective-permute-start | bytes 884744 | tf_op jit(solution)/shard_map/ppermute | solution.py:528
  31.7 1.4 %collective-permute-start.5 = (f32[12,24,256]{2,1,0:T(8,128)S(1)}, f32[12,24,256]{2,1,0:T(8,128)S(1)}, u32[]{:S(2)}, u32[]{:S(2)}) collective-permute-start(f32[12,24,256]{2,1,0:T(8,128)S(1)} %get-tuple-element.116.mi), channel_id=1, source_target_pairs={{0,1},{1,0},{2,3},{3,2},{4,5},{5,4},{6,7},{7,6},{8,9},{9,8},{10,11... | collective-permute-start | bytes 884744 | tf_op jit(solution)/shard_map/ppermute | solution.py:528
  33.1 1.5 %base.1 = (f32[53,16,256]{2,1,0:T(8,128)S(1)}, f32[53,16,256]{2,1,0:T(8,128)S(1)}) custom-call(f32[16,56,256]{2,1,0:T(8,128)S(1)} %get-tuple-element.109.n1, f32[16,56,256]{2,1,0:T(8,128)S(1)} %get-tuple-element.119.n2, f32[16,24,256]{2,1,0:T(8,128)S(1)} %get-tuple-element.120.c1, f32[16,24,256]{2,1,0:T(8,128)S(1)} %get-tuple-element.121.c2, ...), custom_call_target="tpu_custom_call" | custom-call | tf_op jit(solution)/shard_map/base/pallas_call | solution.py:506
  34.6 5.1 %collective-permute-done.4.ho = f32[12,24,256]{2,1,0:T(8,128)S(1)} collective-permute-done((f32[12,24,256]{2,1,0:T(8,128)S(1)}, f32[12,24,256]{2,1,0:T(8,128)S(1)}, u32[]{:S(2)}, u32[]{:S(2)}) %collective-permute-start.4) | collective-permute-done | bytes 294944 | tf_op jit(solution)/shard_map/ppermute | solution.py:528
  39.7 0.2 last_edge.1
  39.9 3.6 %collective-permute-start.10 = (f32[52,24,256]{2,1,0:T(8,128)S(1)}, f32[52,24,256]{2,1,0:T(8,128)S(1)}, u32[]{:S(2)}, u32[]{:S(2)}) collective-permute-start(f32[52,24,256]{2,1,0:T(8,128)S(1)} %get-tuple-element.130.mine), channel_id=1, source_target_pairs={{17,81},{19,83},{21,85},{23,87},{25,89},{27,91},{29,93},{31,95},{4... | collective-permute-start | bytes 3833864 | tf_op jit(solution)/shard_map/ppermute | solution.py:528
  43.4 1.3 %collective-permute-start.9 = (f32[36,24,256]{2,1,0:T(8,128)S(1)}, f32[36,24,256]{2,1,0:T(8,128)S(1)}, u32[]{:S(2)}, u32[]{:S(2)}) collective-permute-start(f32[36,24,256]{2,1,0:T(8,128)S(1)} %get-tuple-element.125.ab), channel_id=1, source_target_pairs={{32,16},{34,18},{36,20},{38,22},{40,24},{42,26},{44,28},{46,30},{3... | collective-permute-start | bytes 2654216 | tf_op jit(solution)/shard_map/ppermute | solution.py:528
  44.8 1.3 %collective-permute-start.6 = (f32[16,24,256]{2,1,0:T(8,128)S(1)}, f32[16,24,256]{2,1,0:T(8,128)S(1)}, u32[]{:S(2)}, u32[]{:S(2)}) collective-permute-start(f32[16,24,256]{2,1,0:T(8,128)S(1)} %get-tuple-element.126), channel_id=1, source_target_pairs={{0,16},{1,81},{2,18},{3,83},{4,20},{5,85},{6,22},{7,87},{8,24},{9,... | collective-permute-start | bytes 1179656 | tf_op jit(solution)/shard_map/ppermute | solution.py:528
  46.1 1.3 %collective-permute-start.7 = (f32[8,24,256]{2,1,0:T(8,128)S(1)}, f32[8,24,256]{2,1,0:T(8,128)S(1)}, u32[]{:S(2)}, u32[]{:S(2)}) collective-permute-start(f32[8,24,256]{2,1,0:T(8,128)S(1)} %get-tuple-element.127), channel_id=1, source_target_pairs={{1,18},{3,20},{5,22},{7,24},{9,26},{11,28},{13,30},{2,81},{4,83},{... | collective-permute-start | bytes 589832 | tf_op jit(solution)/shard_map/ppermute | solution.py:528
  47.4 1.3 %collective-permute-start.8 = (f32[8,24,256]{2,1,0:T(8,128)S(1)}, f32[8,24,256]{2,1,0:T(8,128)S(1)}, u32[]{:S(2)}, u32[]{:S(2)}) collective-permute-start(f32[8,24,256]{2,1,0:T(8,128)S(1)} %get-tuple-element.128), channel_id=1, source_target_pairs={{0,81},{1,16},{2,83},{3,18},{4,85},{5,20},{6,87},{7,22},{8,89},{9,... | collective-permute-start | bytes 589832 | tf_op jit(solution)/shard_map/ppermute | solution.py:528
  48.7 7.4 %collective-permute-done.7.zo = f32[8,24,256]{2,1,0:T(8,128)S(1)} collective-permute-done((f32[8,24,256]{2,1,0:T(8,128)S(1)}, f32[8,24,256]{2,1,0:T(8,128)S(1)}, u32[]{:S(2)}, u32[]{:S(2)}) %collective-permute-start.7) | collective-permute-done | bytes 196640 | tf_op jit(solution)/shard_map/ppermute | solution.py:528
  56.0 3.7 %collective-permute-done.8.zi = f32[8,24,256]{2,1,0:T(8,128)S(1)} collective-permute-done((f32[8,24,256]{2,1,0:T(8,128)S(1)}, f32[8,24,256]{2,1,0:T(8,128)S(1)}, u32[]{:S(2)}, u32[]{:S(2)}) %collective-permute-start.8) | collective-permute-done | bytes 196640 | tf_op jit(solution)/shard_map/ppermute | solution.py:528
  59.7 1.9 %collective-permute-start.14 = (f32[53,16,256]{2,1,0:T(8,128)S(1)}, f32[53,16,256]{2,1,0:T(8,128)S(1)}, u32[]{:S(2)}, u32[]{:S(2)}) collective-permute-start(f32[53,16,256]{2,1,0:T(8,128)S(1)} %get-tuple-element.140.b2), channel_id=1, source_target_pairs={{0,16},{1,17},{2,18},{3,19},{4,20},{5,21},{6,22},{7,23},{8,24},{9,... | collective-permute-start | bytes 2605064 | tf_op jit(solution)/shard_map/ppermute | solution.py:528
  61.7 4.7 %pair.3 = (f32[16,24,256]{2,1,0:T(8,128)S(1)}, f32[8,24,256]{2,1,0:T(8,128)S(1)}, f32[8,24,256]{2,1,0:T(8,128)S(1)}, f32[28,24,256]{2,1,0:T(8,128)S(1)}, f32[24,...) custom-call(f32[16,24,256]{2,1,0:T(8,128)S(1)} %collective-permute-done.6.z0, ...), custom_call_target="tpu_custom_call" | custom-call | tf_op jit(solution)/shard_map/pair/pallas_call | solution.py:506
  66.4 1.3 %collective-permute-start.11 = (f32[16,24,256]{2,1,0:T(8,128)S(1)}, f32[16,24,256]{2,1,0:T(8,128)S(1)}, u32[]{:S(2)}, u32[]{:S(2)}) collective-permute-start(f32[16,24,256]{2,1,0:T(8,128)S(1)} %get-tuple-element.136.z2), channel_id=1, source_target_pairs={{16,48},{81,65},{18,50},{83,67},{20,52},{85,69},{22,54},{87,71},{2... | collective-permute-start | bytes 1179656 | tf_op jit(solution)/shard_map/ppermute | solution.py:528
  67.7 1.3 %collective-permute-start.12 = (f32[8,24,256]{2,1,0:T(8,128)S(1)}, f32[8,24,256]{2,1,0:T(8,128)S(1)}, u32[]{:S(2)}, u32[]{:S(2)}) collective-permute-start(f32[8,24,256]{2,1,0:T(8,128)S(1)} %get-tuple-element.137), channel_id=1, source_target_pairs={{81,50},{83,52},{85,54},{87,56},{89,58},{91,60},{93,62},{18,65},{2... | collective-permute-start | bytes 589832 | tf_op jit(solution)/shard_map/ppermute | solution.py:528
  69.0 1.3 %collective-permute-start.13 = (f32[8,24,256]{2,1,0:T(8,128)S(1)}, f32[8,24,256]{2,1,0:T(8,128)S(1)}, u32[]{:S(2)}, u32[]{:S(2)}) collective-permute-start(f32[8,24,256]{2,1,0:T(8,128)S(1)} %get-tuple-element.138), channel_id=1, source_target_pairs={{16,65},{81,48},{18,67},{83,50},{20,69},{85,52},{22,71},{87,54},{2... | collective-permute-start | bytes 589832 | tf_op jit(solution)/shard_map/ppermute | solution.py:528
  70.4 0.2 gather.3
  70.6 1.0 collective-permute-done.12.zo
  71.6 1.3 %collective-permute-done.13.zi = f32[8,24,256]{2,1,0:T(8,128)S(1)} collective-permute-done((f32[8,24,256]{2,1,0:T(8,128)S(1)}, f32[8,24,256]{2,1,0:T(8,128)S(1)}, u32[]{:S(2)}, u32[]{:S(2)}) %collective-permute-start.13) | collective-permute-done | bytes 196640 | tf_op jit(solution)/shard_map/ppermute | solution.py:528
  73.0 1.5 %collective-permute-done.11.z0 = f32[16,24,256]{2,1,0:T(8,128)S(1)} collective-permute-done((f32[16,24,256]{2,1,0:T(8,128)S(1)}, f32[16,24,256]{2,1,0:T(8,128)S(1)}, u32[]{:S(2)}, u32[]{:S(2)}) %collective-permute-start.11) | collective-permute-done | bytes 393248 | tf_op jit(solution)/shard_map/ppermute | solution.py:528
  74.5 1.1 collective-permute-done.14.b0
  75.6 2.1 %collective-permute-start.18 = (f32[48,24,256]{2,1,0:T(8,128)S(1)}, f32[48,24,256]{2,1,0:T(8,128)S(1)}, u32[]{:S(2)}, u32[]{:S(2)}) collective-permute-start(f32[48,24,256]{2,1,0:T(8,128)S(1)} %get-tuple-element.153.home_in), channel_id=1, source_target_pairs={{81,17},{83,19},{85,21},{87,23},{89,25},{91,27},{93,29},{95,31}} | collective-permute-start | bytes 3538952 | tf_op jit(solution)/shard_map/ppermute | solution.py:528
  77.7 0.7 collective-permute-start.15
  78.4 0.7 collective-permute-start.16
  79.1 0.7 collective-permute-start.17
  79.8 11.0 %collective-permute-done.18.one = f32[48,24,256]{2,1,0:T(8,128)S(1)} collective-permute-done((f32[48,24,256]{2,1,0:T(8,128)S(1)}, f32[48,24,256]{2,1,0:T(8,128)S(1)}, u32[]{:S(2)}, u32[]{:S(2)}) %collective-permute-start.18) | collective-permute-done | bytes 1179680 | tf_op jit(solution)/shard_map/ppermute | solution.py:528
  90.9 1.9 %collective-permute-start.22 = (f32[48,24,256]{2,1,0:T(8,128)S(1)}, f32[48,24,256]{2,1,0:T(8,128)S(1)}, u32[]{:S(2)}, u32[]{:S(2)}) collective-permute-start(f32[48,24,256]{2,1,0:T(8,128)S(1)} %get-tuple-element.171), channel_id=1, source_target_pairs={{16,32},{18,34},{20,36},{22,38},{24,40},{26,42},{28,44},{30,46},{8... | collective-permute-start | bytes 3538952 | tf_op jit(solution)/shard_map/ppermute | solution.py:528
  92.8 0.7 collective-permute-start.19
  93.5 0.7 collective-permute-start.20
  94.2 0.7 collective-permute-start.21
  94.9 25.6 %collective-permute-done.22.other = f32[48,24,256]{2,1,0:T(8,128)S(1)} collective-permute-done((f32[48,24,256]{2,1,0:T(8,128)S(1)}, f32[48,24,256]{2,1,0:T(8,128)S(1)}, u32[]{:S(2)}, u32[]{:S(2)}) %collective-permute-start.22) | collective-permute-done | bytes 1179680 | tf_op jit(solution)/shard_map/ppermute | solution.py:528
  120.4 2.8 %out.1 = f32[3,53,16,256]{3,2,1,0:T(8,128)} custom-call(s32[53]{0:T(128)S(1)} %bitcast.8, f32[3,53,16,256]{3,2,1,0:T(8,128)S(1)} %bitcast.7, f32[53,16,256]{2,1,0:T(8,128)S(1)} %collective-permute-done.14.b0, f32[53,16,256]{2,1,0:T(8,128)S(1)} %get-tuple-element.124.b1, f32[53,16,256]{2,1,0:T(8,128)S(1)} %get-tuple-element.140.b2, ...), custom_call_target="tpu_custom_call" | custom-call | tf_op jit(solution)/shard_map/out/pallas_call | solution.py:506
  (34 shorter events, 0.2 us)
Async XLA Ops:
  0.0 1.7 %copy-start = (f32[1,3,53,16,256]{4,3,2,1,0:T(8,128)S(1)}, f32[1,3,53,16,256]{4,3,2,1,0:T(8,128)}, u32[]{:S(2)}) copy-start(f32[1,3,53,16,256]{4,3,2,1,0:T(8,128)} %param.8) | copy-start | bytes 7815172
  1.7 6.4 %copy-start.2 = (f32[53,53]{1,0:T(8,128)S(1)}, f32[53,53]{1,0:T(8,128)}, u32[]{:S(2)}) copy-start(f32[53,53]{1,0:T(8,128)} %rates.1) | copy-start | bytes 33712
  1.7 6.4 %copy-start.7 = (f32[53]{0:T(128)S(1)}, f32[53]{0:T(128)}, u32[]{:S(2)}) copy-start(f32[53]{0:T(128)} %param.11) | copy-start | bytes 640
  1.7 6.4 %copy-start.8 = (f32[21]{0:T(128)S(1)}, f32[21]{0:T(128)}, u32[]{:S(2)}) copy-start(f32[21]{0:T(128)} %param.14) | copy-start | bytes 256
  1.7 8.8 %copy-start.1 = (f32[1,3,53,16,256]{4,3,2,1,0:T(8,128)S(1)}, f32[1,3,53,16,256]{4,3,2,1,0:T(8,128)}, u32[]{:S(2)}) copy-start(f32[1,3,53,16,256]{4,3,2,1,0:T(8,128)} %param.8) | copy-start | bytes 7815172
  3.0 14.0 %collective-permute-start = (f32[3,2,56,256]{3,2,1,0:T(8,128)}, f32[3,2,56,256]{3,2,1,0:T(8,128)S(1)}, u32[]{:S(2)}, u32[]{:S(2)}) collective-permute-start(f32[3,2,56,256]{3,2,1,0:T(8,128)} %get-tuple-element.92), channel_id=1, source_target_pairs={{1,2},{3,4},{5,6},{7,8},{9,10},{11,12},{13,14},{2,1},{4,3},{6,5},{... | collective-permute-start | bytes 1032200 | tf_op jit(solution)/shard_map/ppermute | solution.py:528
  7.3 9.7 %collective-permute-start.1 = (f32[3,2,56,256]{3,2,1,0:T(8,128)}, f32[3,2,56,256]{3,2,1,0:T(8,128)S(1)}, u32[]{:S(2)}, u32[]{:S(2)}) collective-permute-start(f32[3,2,56,256]{3,2,1,0:T(8,128)} %get-tuple-element.93), channel_id=1, source_target_pairs={{0,1},{1,0},{2,3},{3,2},{4,5},{5,4},{6,7},{7,6},{8,9},{9,8},{10,11... | collective-permute-start | bytes 1032200 | tf_op jit(solution)/shard_map/ppermute | solution.py:528
  8.1 0.8 copy-start.3
  8.9 0.7 copy-start.4
  9.6 0.7 copy-start.5
  17.4 8.5 %collective-permute-start.2 = (f32[2,56,256]{2,1,0:T(8,128)S(1)}, f32[2,56,256]{2,1,0:T(8,128)S(1)}, u32[]{:S(2)}, u32[]{:S(2)}) collective-permute-start(f32[2,56,256]{2,1,0:T(8,128)S(1)} %get-tuple-element.104), channel_id=1, source_target_pairs={{1,2},{3,4},{5,6},{7,8},{9,10},{11,12},{13,14},{2,1},{4,3},{6,5},{... | collective-permute-start | bytes 344072 | tf_op jit(solution)/shard_map/ppermute | solution.py:528
  21.5 4.4 %collective-permute-start.3 = (f32[2,56,256]{2,1,0:T(8,128)S(1)}, f32[2,56,256]{2,1,0:T(8,128)S(1)}, u32[]{:S(2)}, u32[]{:S(2)}) collective-permute-start(f32[2,56,256]{2,1,0:T(8,128)S(1)} %get-tuple-element.105), channel_id=1, source_target_pairs={{0,1},{1,0},{2,3},{3,2},{4,5},{5,4},{6,7},{7,6},{8,9},{9,8},{10,11... | collective-permute-start | bytes 344072 | tf_op jit(solution)/shard_map/ppermute | solution.py:528
  27.9 11.8 %collective-permute-start.4 = (f32[12,24,256]{2,1,0:T(8,128)S(1)}, f32[12,24,256]{2,1,0:T(8,128)S(1)}, u32[]{:S(2)}, u32[]{:S(2)}) collective-permute-start(f32[12,24,256]{2,1,0:T(8,128)S(1)} %get-tuple-element.115.mo), channel_id=1, source_target_pairs={{1,2},{3,4},{5,6},{7,8},{9,10},{11,12},{13,14},{2,1},{4,3},{6,5},{... | collective-permute-start | bytes 884744 | tf_op jit(solution)/shard_map/ppermute | solution.py:528
  31.7 8.0 %collective-permute-start.5 = (f32[12,24,256]{2,1,0:T(8,128)S(1)}, f32[12,24,256]{2,1,0:T(8,128)S(1)}, u32[]{:S(2)}, u32[]{:S(2)}) collective-permute-start(f32[12,24,256]{2,1,0:T(8,128)S(1)} %get-tuple-element.116.mi), channel_id=1, source_target_pairs={{0,1},{1,0},{2,3},{3,2},{4,5},{5,4},{6,7},{7,6},{8,9},{9,8},{10,11... | collective-permute-start | bytes 884744 | tf_op jit(solution)/shard_map/ppermute | solution.py:528
  39.9 19.9 %collective-permute-start.10 = (f32[52,24,256]{2,1,0:T(8,128)S(1)}, f32[52,24,256]{2,1,0:T(8,128)S(1)}, u32[]{:S(2)}, u32[]{:S(2)}) collective-permute-start(f32[52,24,256]{2,1,0:T(8,128)S(1)} %get-tuple-element.130.mine), channel_id=1, source_target_pairs={{17,81},{19,83},{21,85},{23,87},{25,89},{27,91},{29,93},{31,95},{4... | collective-permute-start | bytes 3833864 | tf_op jit(solution)/shard_map/ppermute | solution.py:528
  43.4 16.3 %collective-permute-start.9 = (f32[36,24,256]{2,1,0:T(8,128)S(1)}, f32[36,24,256]{2,1,0:T(8,128)S(1)}, u32[]{:S(2)}, u32[]{:S(2)}) collective-permute-start(f32[36,24,256]{2,1,0:T(8,128)S(1)} %get-tuple-element.125.ab), channel_id=1, source_target_pairs={{32,16},{34,18},{36,20},{38,22},{40,24},{42,26},{44,28},{46,30},{3... | collective-permute-start | bytes 2654216 | tf_op jit(solution)/shard_map/ppermute | solution.py:528
  44.8 15.0 %collective-permute-start.6 = (f32[16,24,256]{2,1,0:T(8,128)S(1)}, f32[16,24,256]{2,1,0:T(8,128)S(1)}, u32[]{:S(2)}, u32[]{:S(2)}) collective-permute-start(f32[16,24,256]{2,1,0:T(8,128)S(1)} %get-tuple-element.126), channel_id=1, source_target_pairs={{0,16},{1,81},{2,18},{3,83},{4,20},{5,85},{6,22},{7,87},{8,24},{9,... | collective-permute-start | bytes 1179656 | tf_op jit(solution)/shard_map/ppermute | solution.py:528
  46.1 10.0 %collective-permute-start.7 = (f32[8,24,256]{2,1,0:T(8,128)S(1)}, f32[8,24,256]{2,1,0:T(8,128)S(1)}, u32[]{:S(2)}, u32[]{:S(2)}) collective-permute-start(f32[8,24,256]{2,1,0:T(8,128)S(1)} %get-tuple-element.127), channel_id=1, source_target_pairs={{1,18},{3,20},{5,22},{7,24},{9,26},{11,28},{13,30},{2,81},{4,83},{... | collective-permute-start | bytes 589832 | tf_op jit(solution)/shard_map/ppermute | solution.py:528
  47.4 12.4 %collective-permute-start.8 = (f32[8,24,256]{2,1,0:T(8,128)S(1)}, f32[8,24,256]{2,1,0:T(8,128)S(1)}, u32[]{:S(2)}, u32[]{:S(2)}) collective-permute-start(f32[8,24,256]{2,1,0:T(8,128)S(1)} %get-tuple-element.128), channel_id=1, source_target_pairs={{0,81},{1,16},{2,83},{3,18},{4,85},{5,20},{6,87},{7,22},{8,89},{9,... | collective-permute-start | bytes 589832 | tf_op jit(solution)/shard_map/ppermute | solution.py:528
  59.7 15.9 %collective-permute-start.14 = (f32[53,16,256]{2,1,0:T(8,128)S(1)}, f32[53,16,256]{2,1,0:T(8,128)S(1)}, u32[]{:S(2)}, u32[]{:S(2)}) collective-permute-start(f32[53,16,256]{2,1,0:T(8,128)S(1)} %get-tuple-element.140.b2), channel_id=1, source_target_pairs={{0,16},{1,17},{2,18},{3,19},{4,20},{5,21},{6,22},{7,23},{8,24},{9,... | collective-permute-start | bytes 2605064 | tf_op jit(solution)/shard_map/ppermute | solution.py:528
  66.4 8.1 %collective-permute-start.11 = (f32[16,24,256]{2,1,0:T(8,128)S(1)}, f32[16,24,256]{2,1,0:T(8,128)S(1)}, u32[]{:S(2)}, u32[]{:S(2)}) collective-permute-start(f32[16,24,256]{2,1,0:T(8,128)S(1)} %get-tuple-element.136.z2), channel_id=1, source_target_pairs={{16,48},{81,65},{18,50},{83,67},{20,52},{85,69},{22,54},{87,71},{2... | collective-permute-start | bytes 1179656 | tf_op jit(solution)/shard_map/ppermute | solution.py:528
  67.7 3.9 %collective-permute-start.12 = (f32[8,24,256]{2,1,0:T(8,128)S(1)}, f32[8,24,256]{2,1,0:T(8,128)S(1)}, u32[]{:S(2)}, u32[]{:S(2)}) collective-permute-start(f32[8,24,256]{2,1,0:T(8,128)S(1)} %get-tuple-element.137), channel_id=1, source_target_pairs={{81,50},{83,52},{85,54},{87,56},{89,58},{91,60},{93,62},{18,65},{2... | collective-permute-start | bytes 589832 | tf_op jit(solution)/shard_map/ppermute | solution.py:528
  69.0 3.9 %collective-permute-start.13 = (f32[8,24,256]{2,1,0:T(8,128)S(1)}, f32[8,24,256]{2,1,0:T(8,128)S(1)}, u32[]{:S(2)}, u32[]{:S(2)}) collective-permute-start(f32[8,24,256]{2,1,0:T(8,128)S(1)} %get-tuple-element.138), channel_id=1, source_target_pairs={{16,65},{81,48},{18,67},{83,50},{20,69},{85,52},{22,71},{87,54},{2... | collective-permute-start | bytes 589832 | tf_op jit(solution)/shard_map/ppermute | solution.py:528
  75.6 15.1 %collective-permute-start.18 = (f32[48,24,256]{2,1,0:T(8,128)S(1)}, f32[48,24,256]{2,1,0:T(8,128)S(1)}, u32[]{:S(2)}, u32[]{:S(2)}) collective-permute-start(f32[48,24,256]{2,1,0:T(8,128)S(1)} %get-tuple-element.153.home_in), channel_id=1, source_target_pairs={{81,17},{83,19},{85,21},{87,23},{89,25},{91,27},{93,29},{95,31}} | collective-permute-start | bytes 3538952 | tf_op jit(solution)/shard_map/ppermute | solution.py:528
  77.7 13.0 %collective-permute-start.15 = (f32[16,24,256]{2,1,0:T(8,128)S(1)}, f32[16,24,256]{2,1,0:T(8,128)S(1)}, u32[]{:S(2)}, u32[]{:S(2)}) collective-permute-start(f32[16,24,256]{2,1,0:T(8,128)S(1)} %get-tuple-element.145.z2), channel_id=1, source_target_pairs={{48,80},{65,97},{50,82},{67,99},{52,84},{69,101},{54,86},{71,103},... | collective-permute-start | bytes 1179656 | tf_op jit(solution)/shard_map/ppermute | solution.py:528
  78.4 12.3 %collective-permute-start.16 = (f32[8,24,256]{2,1,0:T(8,128)S(1)}, f32[8,24,256]{2,1,0:T(8,128)S(1)}, u32[]{:S(2)}, u32[]{:S(2)}) collective-permute-start(f32[8,24,256]{2,1,0:T(8,128)S(1)} %get-tuple-element.146), channel_id=1, source_target_pairs={{65,82},{67,84},{69,86},{71,88},{73,90},{75,92},{77,94},{50,97},{5... | collective-permute-start | bytes 589832 | tf_op jit(solution)/shard_map/ppermute | solution.py:528
  79.1 11.7 %collective-permute-start.17 = (f32[8,24,256]{2,1,0:T(8,128)S(1)}, f32[8,24,256]{2,1,0:T(8,128)S(1)}, u32[]{:S(2)}, u32[]{:S(2)}) collective-permute-start(f32[8,24,256]{2,1,0:T(8,128)S(1)} %get-tuple-element.147), channel_id=1, source_target_pairs={{48,97},{65,80},{50,99},{67,82},{52,101},{69,84},{54,103},{71,86},... | collective-permute-start | bytes 589832 | tf_op jit(solution)/shard_map/ppermute | solution.py:528
  90.8 29.6 %copy-start.6 = (s32[53,1]{0,1:T(1,128)S(1)}, s32[53,1]{0,1:T(1,128)}, u32[]{:S(2)}) copy-start(s32[53,1]{0,1:T(1,128)} %param.15) | copy-start | bytes 640
  90.9 29.6 %collective-permute-start.22 = (f32[48,24,256]{2,1,0:T(8,128)S(1)}, f32[48,24,256]{2,1,0:T(8,128)S(1)}, u32[]{:S(2)}, u32[]{:S(2)}) collective-permute-start(f32[48,24,256]{2,1,0:T(8,128)S(1)} %get-tuple-element.171), channel_id=1, source_target_pairs={{16,32},{18,34},{20,36},{22,38},{24,40},{26,42},{28,44},{30,46},{8... | collective-permute-start | bytes 3538952 | tf_op jit(solution)/shard_map/ppermute | solution.py:528
  92.8 2.1 %collective-permute-start.19 = (f32[16,24,256]{2,1,0:T(8,128)S(1)}, f32[16,24,256]{2,1,0:T(8,128)S(1)}, u32[]{:S(2)}, u32[]{:S(2)}) collective-permute-start(f32[16,24,256]{2,1,0:T(8,128)S(1)} %get-tuple-element.163.z2), channel_id=1, source_target_pairs={{80,112},{97,113},{82,114},{99,115},{84,116},{101,117},{86,118},{1... | collective-permute-start | bytes 1179656 | tf_op jit(solution)/shard_map/ppermute | solution.py:528
  93.5 1.4 %collective-permute-start.20 = (f32[4,24,256]{2,1,0:T(8,128)S(1)}, f32[4,24,256]{2,1,0:T(8,128)S(1)}, u32[]{:S(2)}, u32[]{:S(2)}) collective-permute-start(f32[4,24,256]{2,1,0:T(8,128)S(1)} %get-tuple-element.164), channel_id=1, source_target_pairs={{97,114},{99,116},{101,118},{103,120},{105,122},{107,124},{109,126... | collective-permute-start | bytes 294920 | tf_op jit(solution)/shard_map/ppermute | solution.py:528
  94.2 0.7 collective-permute-start.21

commit v4 on v3

--- a/solution.py
+++ b/solution.py
@@ -58,14 +58,12 @@
     return 16.0 * near - far, -near
 
 
-def prep_kernel(rates, pairs, diff, crates, cpairs, cdiff, smap, wf, wr, wfr, lv, wc, pro, d12, dc12, share, a, mi):
+RATES, PAIRS, CRATES, CPAIRS, DIFF, CDIFF, MAP, RAW = 0, 56, 112, 136, 160, 161, 162, 168
+
+
+def prep_kernel(raw, wf, wr, wfr, lv, wc, pro, d12, dc12, share):
     row = lax.broadcasted_iota(jnp.int32, (SP, 128), 0)
     lane = lax.broadcasted_iota(jnp.int32, (SP, 128), 1)
-
-    def framed(ref, rows, columns, height):
-        a[...] = jnp.zeros((SP, 128), F32)
-        a[:rows, :columns] = ref[...]
-        return a[:height, :]
 
     def halves(x):
         hi = x.astype(BF16).astype(F32)
@@ -75,17 +73,17 @@
         return jnp.sum(jnp.where(row == lane, values, 0.0), axis=1, keepdims=True)[:height]
 
     eye = jnp.where(row == lane, RELAX, 0.0)
-    fine = framed(rates, SPECIES, SPECIES, SP) - jnp.where(row < SPECIES, eye, 0.0)
-    fine = fine + pltpu.roll(framed(pairs, SPECIES, SPECIES, SP), SP, 1)
-    coarse = framed(crates, COARSE, COARSE, CP) - jnp.where(row < COARSE, eye, 0.0)[:CP]
-    coarse = coarse + pltpu.roll(framed(cpairs, COARSE, COARSE, CP), CP, 1)
-    diff_row = framed(diff, 1, SPECIES, 8)[0:1]
+    fine = raw[RATES : RATES + SP, :] - jnp.where(row < SPECIES, eye, 0.0)
+    fine = fine + pltpu.roll(raw[PAIRS : PAIRS + SP, :], SP, 1)
+    coarse = raw[CRATES : CRATES + CP, :] - jnp.where(row < COARSE, eye, 0.0)[:CP]
+    coarse = coarse + pltpu.roll(raw[CPAIRS : CPAIRS + CP, :], CP, 1)
+    vectors = raw[DIFF : DIFF + 8, :]
+    diff_row = vectors[0:1]
     d12[...] = jnp.broadcast_to(column(diff_row, SP) / 12.0, (SP, COLS))
-    dc12[...] = jnp.broadcast_to(column(framed(cdiff, 1, COARSE, 8)[0:1], CP) / 12.0, (CP, COLS))
-    mi[...] = jnp.full((SP, 128), -1, jnp.int32)
-    mi[:SPECIES, 0:1] = smap[...]
-    map_column = mi[:, 0:1]
-    map_row = jnp.sum(jnp.where(row == lane, map_column, 0), axis=0, keepdims=True)
+    dc12[...] = jnp.broadcast_to(column(vectors[1:2], CP) / 12.0, (CP, COLS))
+    map_row = jnp.where(lane[0:1] < SPECIES, vectors[2:3].astype(jnp.int32), -1)
+    map_column = jnp.sum(jnp.where(row == lane, map_row, 0), axis=1, keepdims=True)
+    map_column = jnp.where(row[:, 0:1] < SPECIES, map_column, -1)
     lum = jnp.where((map_row == row[:CP]) & (lane[:CP] < SPECIES), 1.0, 0.0)
     counts = jnp.sum(lum, axis=1, keepdims=True)
     share[...] = jnp.broadcast_to(1.0 / jnp.maximum(counts, 1.0), (CP, COLS))
@@ -117,13 +115,13 @@
         return (self.slab % 2, self.slice_at, self.slab)[at]
 
 
-def blocks(rows, body):
-    @pl.loop(0, rows // 4)
+def blocks(rows, body, size=4):
+    @pl.loop(0, rows // size)
     def _(i):
-        body(4 * i)
-
-
-def first_kernel(u, outer, inner):
+        body([size * i + k for k in range(size)])
+
+
+def first_kernel(u, weights_made, outer, inner):
     info = Position()
     at_top = info[0] == 0
     for m in range(3):
@@ -153,12 +151,11 @@
     for x in (0, 1, ROWS + 2, ROWS + 3):
         p0s[x], pss[x], v0s[x], c0s[x] = zeros(SP), zeros(SP), zeros(CP), zeros(CP)
 
-    def terms(x0):
-        for k in range(4):
+    def terms(xs):
+        for k, x in enumerate(xs):
             for m in range(3):
-                ut[k, m, :SPECIES, :] = u[m, :, x0 + k, :]
-        for k in range(4):
-            x = x0 + k
+                ut[k, m, :SPECIES, :] = u[m, :, x, :]
+        for k, x in enumerate(xs):
             us = [ut[k, m] for m in range(3)]
             qs = [v * v for v in us]
             p0, ps = mixed(MIX0, us), mixed(MIXS, us)
@@ -174,9 +171,8 @@
 
     blocks(ROWS, terms)
 
-    def laps(x0):
-        for k in range(4):
-            x = x0 + k
+    def laps(xs):
+        for x in xs:
             n1[x] += d12[...] * lap_rows(p0s, x + 2)
             s[x] += d12[...] * lap_rows(pss, x + 2)
             r0[x] += lap_rows(v0s, x + 2) * (1.0 / 12.0)
@@ -227,9 +223,8 @@
     for x in (0, 1, ROWS + 2, ROWS + 3):
         n1s[x], v1s[x], c1s[x] = zeros(SP), zeros(CP), zeros(CP)
 
-    def terms(x0):
-        for k in range(4):
-            x = x0 + k
+    def terms(xs):
+        for x in xs:
             n = n1[x]
             y = dot(wfr[...], stacked(n, n * n))
             n2[x] = n + HALF * ((y[:SP] + y[SP : 2 * SP]) + d12[...] * lap_y(n)) + s[x]
@@ -241,9 +236,8 @@
 
     blocks(ROWS, terms)
 
-    def laps(x0):
-        for k in range(4):
-            x = x0 + k
+    def laps(xs):
+        for x in xs:
             n2[x] += (HALF * d12[...]) * lap_rows(n1s, x + 2)
             r1[x] += lap_rows(v1s, x + 2) * (1.0 / 12.0)
             e1[x] += dc12[...] * lap_rows(c1s, x + 2)
@@ -289,10 +283,10 @@
     edges = (0, 1, ROWS - 2, ROWS - 1)
     for x in edges:
         lumped(x, n2[x])
-    blocks(ROWS - 4, lambda x0: [lumped(x, n2i[x]) for x in (x0 + 2, x0 + 3, x0 + 4, x0 + 5)])
+    blocks(ROWS - 4, lambda xs: [lumped(x + 2, n2i[x + 2]) for x in xs], ROWS - 4)
     for x in edges:
         pieces(x, r1[x], e1[x])
-    blocks(ROWS - 4, lambda x0: [pieces(x, r1i[x], e1i[x]) for x in (x0 + 2, x0 + 3, x0 + 4, x0 + 5)])
+    blocks(ROWS - 4, lambda xs: [pieces(x + 2, r1i[x + 2], e1i[x + 2]) for x in xs], ROWS - 4)
     top = [ab[x + XA0] for x in range(6)] + [ab[x + XB0] for x in range(4)] + [v2s[x + 2] for x in range(2)]
     bottom = [ab[x + XA0] for x in range(ROWS - 6, ROWS)] + [ab[x + XB0] for x in range(ROWS - 4, ROWS)]
     send(info, outer, inner, top, bottom + [v2s[x] for x in range(ROWS, ROWS + 2)])
@@ -326,20 +320,21 @@
 
 
 def sweep(info, z, z0, add, add0, out, out0, low, rows, wc, dc12):
-    def body(i):
-        x0 = i + low
-        z8 = [z[x0 + z0 + k] for k in range(-2, 6)]
-        for k in range(4):
-            x, value = x0 + k, z8[k + 2]
+    size = rows // 2
+
+    def body(xs):
+        zr = [z[xs[0] + (low + z0 + k)] for k in range(-2, size + 2)]
+        for k in range(size):
+            x, value = xs[k] + low, zr[k + 2]
             y = dot(wc[...], stacked(value, value * value))
-            lap = lap_y(value) + 16.0 * (z8[k + 1] + z8[k + 3]) - (z8[k] + z8[k + 4])
+            lap = lap_y(value) + 16.0 * (zr[k + 1] + zr[k + 3]) - (zr[k] + zr[k + 4])
             value = value + HALF * ((y[:CP] + y[CP:]) + dc12[...] * lap) + add[x + add0]
             if low < 0:
                 inside = ((x >= 0) | (info[2] > 0)) & ((x < ROWS) | (info[2] < SLABS - 1))
                 value = jnp.where(inside, value, 0.0)
             out[x + out0] = value
 
-    blocks(rows, body)
+    blocks(rows, body, size)
 
 
 def begin(info, z0, zo, zi, depth, zs):
@@ -347,9 +342,9 @@
     for r in range(depth):
         zs[r], zs[depth + ROWS + r] = top(r), bottom(r)
 
-    def body(x):
-        for k in range(4):
-            zs[depth + x + k] = z0[x + k]
+    def body(xs):
+        for x in xs:
+            zs[depth + x] = z0[x]
 
     blocks(ROWS, body)
 
@@ -362,7 +357,7 @@
     return info[1] == jnp.where(info[0] == 0, hosts[0], hosts[1])
 
 
-def start_kernel(hosts, ab, wc, dc12, result, message, outer, inner):
+def start_kernel(hosts, ab, wc, dc12, result, unused, message, outer, inner):
     info = Position()
 
     @pl.when(hosting(info, hosts))
@@ -370,8 +365,8 @@
         sweep(info, ab, A0, ab, B0, message, 0, 0, ROWS, wc, dc12)
         give(info, 8, outer, inner, lambda x: message[x])
 
-        def body(x0):
-            for x in (x0, x0 + 1, x0 + 2, x0 + 3):
+        def body(xs):
+            for x in xs:
                 result[x], result[ROWS + x], result[2 * ROWS + x] = zeros(CP), ab[x + A0], message[x]
 
         blocks(ROWS, body)
@@ -401,8 +396,8 @@
 
 
 def gather(z0, za, zb, zc, z2, one, two):
-    def body(x0):
-        for x in (x0, x0 + 1, x0 + 2, x0 + 3):
+    def body(xs):
+        for x in xs:
             one[x], one[ROWS + x], one[2 * ROWS + x] = z0[x], za[x + 6], zb[x + 4]
             two[x], two[ROWS + x], two[2 * ROWS + x] = zb[x + 4], zc[x + 2], z2[x]
 
@@ -417,8 +412,8 @@
 
 
 def base_kernel(n1, n2, c1, c2, pro, share, b1, b2):
-    def body(x0):
-        for x in (x0, x0 + 1, x0 + 2, x0 + 3):
+    def body(xs):
+        for x in xs:
             for n, c, b in ((n1, c1, b1), (n2, c2, b2)):
                 value = thirds(jnp.concatenate([share[...] * c[x], zeros(8)], axis=0))
                 b[:, x, :] = (n[x] - dot(pro[...], value))[:SPECIES]
@@ -440,8 +435,8 @@
         @pl.when(here)
         def _():
 
-            def body(x0):
-                for x in (x0, x0 + 1, x0 + 2, x0 + 3):
+            def body(xs):
+                for x in xs:
                     z[x] = result[x]
 
             blocks(3 * ROWS, body)
@@ -450,25 +445,24 @@
     def _():
         begin(info, z0, zo, zi, 4, zs)
 
-        def body(x0):
-            for x in (x0, x0 + 1, x0 + 2, x0 + 3):
+        def body(xs):
+            for x in xs:
                 z[x] = z0[x]
 
         blocks(ROWS, body)
 
     def finish(m, base):
-        def body(x0):
-            for x in (x0, x0 + 1, x0 + 2, x0 + 3):
+        def body(xs):
+            for x in xs:
                 spread[m, :, x, :] = share[...] * z[m * ROWS + x]
 
-        blocks(ROWS, body)
+        blocks(ROWS, body, ROWS)
 
         def add(s):
             node[m, s] = base(s) + spread[m, where[s]]
 
-        blocks(SPECIES, lambda s: [add(s + k) for k in range(4)])
-        for s in range(SPECIES - SPECIES % 4, SPECIES):
-            add(s)
+        blocks(SPECIES, lambda at: [add(s) for s in at], 13)
+        add(SPECIES - 1)
         copy = pltpu.make_async_copy(node.at[m], out.at[m], sem.at[m])
         copy.start()
         return copy
@@ -481,8 +475,8 @@
         sweep(info, zs, 4, ab, A0, za, 2, -2, ROWS + 4, wc, dc12)
         sweep(info, za, 2, ab, B0, z.at[pl.ds(2 * ROWS, ROWS)], 0, 0, ROWS, wc, dc12)
 
-        def body(x0):
-            for x in (x0, x0 + 1, x0 + 2, x0 + 3):
+        def body(xs):
+            for x in xs:
                 z[ROWS + x] = za[x + 2]
 
         blocks(ROWS, body)
@@ -501,8 +495,8 @@
 ANY = pl.BlockSpec(memory_space=pl.ANY)
 
 
-def call(kernel, name, outs, *args, scratch=(), alias=None, out_specs=None):
-    specs = [SMEM if a.dtype == jnp.int32 and a.ndim == 1 else VMEM for a in args]
+def call(kernel, name, outs, *args, scratch=(), alias=None, out_specs=None, specs=None):
+    specs = specs or [SMEM if a.dtype == jnp.int32 and a.ndim == 1 else VMEM for a in args]
     return pl.pallas_call(
         kernel,
         out_shape=outs,
@@ -552,26 +546,31 @@
     nodes = fine_nodes[0]
     fine, coarse = field(ROWS, SP), field(ROWS, CP)
     message = field(3, 2, SP)
-    outer, inner = call(first_kernel, "first", [message, message], nodes)
-    uo, ui = swap(outer, inner)
-
     def bf16(*shape):
         return jax.ShapeDtypeStruct(shape, BF16)
 
+    raw = sum(
+        jnp.pad(v.astype(F32), ((at, RAW - at - v.shape[0]), (0, 128 - v.shape[1])))
+        for at, v in (
+            (RATES, fine_rates),
+            (PAIRS, fine_pairs),
+            (CRATES, coarse_rates),
+            (CPAIRS, coarse_pairs),
+            (DIFF, fine_diff.reshape(1, SPECIES)),
+            (CDIFF, coarse_diff.reshape(1, COARSE)),
+            (MAP, species_map.reshape(1, SPECIES)),
+        )
+    )
     wf, wr, wfr, lv, wc, pro, d12, dc12, share = call(
         prep_kernel,
         "prep",
         [bf16(2 * SP, 256), bf16(128, 256), bf16(2 * SP + 128, 256), bf16(80, 128), bf16(2 * CP, 128), bf16(SP, 96)]
         + [field(SP), field(CP), field(CP)],
-        fine_rates,
-        fine_pairs,
-        fine_diff.reshape(1, SPECIES),
-        coarse_rates,
-        coarse_pairs,
-        coarse_diff.reshape(1, COARSE),
-        species_map,
-        scratch=[pltpu.VMEM((SP, 128), F32), pltpu.VMEM((SP, 128), jnp.int32)],
-    )
+        raw,
+    )
+    outer, inner = call(first_kernel, "first", [message, message], nodes, wc)
+    uo, ui = swap(outer, inner)
+
     n1, s, r0, e0, c0 = call(
         old_kernel,
         "old",
@@ -618,32 +617,30 @@
             back.append((both(host), both(slices[0] if host == slices[1] else slices[1]), slabs))
             if host not in slices:
                 first.append((both(host), both(slices[0]), slabs))
-    short, long = moved(ab, *short), moved(abx, *long)
+    short, long, long_last = moved(ab, *short), moved(abx, *long[:-1]), long[-1:]
     forward = [(both(p), both(p + 1), SAME) for p in range(SLICES - 1)]
-    home, *sent = call(
-        functools.partial(start_kernel, GROUPS[0][1]), "start", [result, coarse, eight, eight], ab, wc, dc12
-    )
-    away = home
+    home, away, *sent = call(
+        functools.partial(start_kernel, GROUPS[0][1]), "start", [result, result, coarse, eight, eight], ab, wc, dc12
+    )
     for at, (slices, hosts) in enumerate(GROUPS[1:], 1):
         z = hop(*sent, GROUPS[at - 1][1], hosts)
         if at == 1:
             *z, short, long = lax.optimization_barrier((*z, short, long))
-            b0 = moved(after(b2, z[0]), *forward)
+            b0, long_last = moved(after(b2, z[0]), *forward), moved(after(abx, z[0]), *long_last)
         elif at == 2:
-            *z, b0 = lax.optimization_barrier((*z, b0))
-            one = moved(after(home, z[0]), *first)
+            *z, b0, long_last = lax.optimization_barrier((*z, b0, long_last))
         elif at == 3:
-            *z, one, home, away = lax.optimization_barrier((*z, one, home, away))
+            *z, home, away = lax.optimization_barrier((*z, home, away))
         else:
-            other = moved(away, *back)
-            *z, other, home = lax.optimization_barrier((*z, other, home))
+            other, one = moved(away, *back), moved(home, *first)
+            *z, other, one, home = lax.optimization_barrier((*z, other, one, home))
         if len(slices) == 2:
             depth = 4 * len(GROUPS[at + 1][0])
             *sent, za, zb, zc = call(
                 functools.partial(pair_kernel, slices, hosts, depth),
                 "pair",
                 [coarse, field(depth, CP), field(depth, CP), field(ROWS + 12, CP), field(ROWS + 8, CP), field(ROWS + 4, CP)],
-                *(*z, abx, short, long, wc, dc12),
+                *(*z, abx, short, long_last if at == 3 else long, wc, dc12),
                 scratch=[field(ROWS + 16, CP)],
             )
             home, away = call(

time: 125 us -> 131 us (1.048)
  the two profiles are of different devices: /device:TPU:51 before, /device:TPU:78 now
where the time goes in v4:
time: 131 us; the launch traced here: 130 us
  waiting for transfers between devices  80.6 us (62%)
  starting transfers between devices  29.6 us (23%)
  Pallas kernels  16.5 us (13%)
  local copies, waits for them, and re-layouts  1.74 us (1%)
  other arithmetic  1.5 us (1%)
    ppermute x24, waiting for transfers between devices, moved(): return lax.ppermute(value, AXES, pairs)  80.6 us
    ppermute x24, starting transfers between devices, moved(): return lax.ppermute(value, AXES, pairs)  29.6 us
    pallas_call x16, Pallas kernels, call(): pl.pallas_call(kernel, out_shape=outs, in_specs=specs, **{'out_specs': ou...  16.5 us
  transfers between devices with their start and end apart: 24, of which 5 were waited for; matrix products, arithmetic and copies ran while one was open for 0% of the time, Pallas kernels for 9%

profile of v4, /device:TPU:78, one launch (start us, length us, event | category | flops | bytes accessed | tf_op | source)
XLA Modules:
  0.0 130.4 jit_solution(13688552407607474439)
XLA Ops:
  0.0 0.7 convert_bitcast_fusion
  0.7 0.8 pad_add_fusion.raw
  1.5 0.2 prep.1
  1.7 0.0 copy-start
  1.8 1.7 %copy-done = f32[1,3,53,16,256]{4,3,2,1,0:T(8,128)S(1)} copy-done((f32[1,3,53,16,256]{4,3,2,1,0:T(8,128)S(1)}, f32[1,3,53,16,256]{4,3,2,1,0:T(8,128)}, u32[]{:S(2)}) %copy-start) | copy-done | bytes 2605080
  3.5 0.4 first.1
  3.9 2.9 %collective-permute-start = (f32[3,2,56,256]{3,2,1,0:T(8,128)S(1)}, f32[3,2,56,256]{3,2,1,0:T(8,128)S(1)}, u32[]{:S(2)}, u32[]{:S(2)}) collective-permute-start(f32[3,2,56,256]{3,2,1,0:T(8,128)S(1)} %get-tuple-element.95), channel_id=1, source_target_pairs={{1,2},{3,4},{5,6},{7,8},{9,10},{11,12},{13,14},{2,1},{4,3},{6,5},{... | collective-permute-start | bytes 1032200 | tf_op jit(solution)/shard_map/ppermute | solution.py:522
  6.8 1.8 %collective-permute-start.1 = (f32[3,2,56,256]{3,2,1,0:T(8,128)S(1)}, f32[3,2,56,256]{3,2,1,0:T(8,128)S(1)}, u32[]{:S(2)}, u32[]{:S(2)}) collective-permute-start(f32[3,2,56,256]{3,2,1,0:T(8,128)S(1)} %get-tuple-element.96), channel_id=1, source_target_pairs={{0,1},{1,0},{2,3},{3,2},{4,5},{5,4},{6,7},{7,6},{8,9},{9,8},{10,11... | collective-permute-start | bytes 1032200 | tf_op jit(solution)/shard_map/ppermute | solution.py:522
  8.5 6.3 %old.1 = (f32[16,56,256]{2,1,0:T(8,128)S(1)}, f32[16,56,256]{2,1,0:T(8,128)S(1)}, f32[16,24,256]{2,1,0:T(8,128)S(1)}, f32[16,24,256]{2,1,0:T(8,128)S(1)}, f32[16,24,256]{2,1,0:T(8,128)S(1)}) custom-call(f32[3,53,16,256]{3,2,1,0:T(8,128)S(1)} %bitcast.8, bf16[112,256]{1,0:T(8,128)(2,1)S(1)} %get-tuple-element.100.wf, ...), custom_call_target="tpu_custom_call" | custom-call | tf_op jit(solution)/shard_map/old/pallas_call | solution.py:500
  14.9 2.8 %collective-permute-done.uo = f32[3,2,56,256]{3,2,1,0:T(8,128)S(1)} collective-permute-done((f32[3,2,56,256]{3,2,1,0:T(8,128)S(1)}, f32[3,2,56,256]{3,2,1,0:T(8,128)S(1)}, u32[]{:S(2)}, u32[]{:S(2)}) %collective-permute-start) | collective-permute-done | bytes 344096 | tf_op jit(solution)/shard_map/ppermute | solution.py:522
  17.7 0.4 old_edge.1
  18.1 2.1 %collective-permute-start.2 = (f32[2,56,256]{2,1,0:T(8,128)S(1)}, f32[2,56,256]{2,1,0:T(8,128)S(1)}, u32[]{:S(2)}, u32[]{:S(2)}) collective-permute-start(f32[2,56,256]{2,1,0:T(8,128)S(1)} %get-tuple-element.106), channel_id=1, source_target_pairs={{1,2},{3,4},{5,6},{7,8},{9,10},{11,12},{13,14},{2,1},{4,3},{6,5},{... | collective-permute-start | bytes 344072 | tf_op jit(solution)/shard_map/ppermute | solution.py:522
  20.2 2.4 %collective-permute-start.3 = (f32[2,56,256]{2,1,0:T(8,128)S(1)}, f32[2,56,256]{2,1,0:T(8,128)S(1)}, u32[]{:S(2)}, u32[]{:S(2)}) collective-permute-start(f32[2,56,256]{2,1,0:T(8,128)S(1)} %get-tuple-element.107), channel_id=1, source_target_pairs={{0,1},{1,0},{2,3},{3,2},{4,5},{5,4},{6,7},{7,6},{8,9},{9,8},{10,11... | collective-permute-start | bytes 344072 | tf_op jit(solution)/shard_map/ppermute | solution.py:522
  22.6 3.7 %mid.1 = (f32[16,56,256]{2,1,0:T(8,128)S(1)}, f32[16,24,256]{2,1,0:T(8,128)S(1)}, f32[16,24,256]{2,1,0:T(8,128)S(1)}, f32[16,24,256]{2,1,0:T(8,128)S(1)}) custom-call(f32[16,56,256]{2,1,0:T(8,128)S(1)} %get-tuple-element.111.n1, f32[16,56,256]{2,1,0:T(8,128)S(1)} %get-tuple-element.112.s, bf16[240,256]{1,0:T(8,128)(2,1)S(1)} %get-tuple-element.113.wfr, ...), custom_call_target="tpu_custom_call" | custom-call | tf_op jit(solution)/shard_map/mid/pallas_call | solution.py:500
  26.3 0.0 collective-permute-done.2.no
  26.3 0.0 collective-permute-done.3.ni
  26.3 1.0 mid_edge.1
  27.3 3.2 %collective-permute-start.4 = (f32[12,24,256]{2,1,0:T(8,128)S(1)}, f32[12,24,256]{2,1,0:T(8,128)S(1)}, u32[]{:S(2)}, u32[]{:S(2)}) collective-permute-start(f32[12,24,256]{2,1,0:T(8,128)S(1)} %get-tuple-element.117.mo), channel_id=1, source_target_pairs={{1,2},{3,4},{5,6},{7,8},{9,10},{11,12},{13,14},{2,1},{4,3},{6,5},{... | collective-permute-start | bytes 884744 | tf_op jit(solution)/shard_map/ppermute | solution.py:522
  30.6 1.5 %collective-permute-start.5 = (f32[12,24,256]{2,1,0:T(8,128)S(1)}, f32[12,24,256]{2,1,0:T(8,128)S(1)}, u32[]{:S(2)}, u32[]{:S(2)}) collective-permute-start(f32[12,24,256]{2,1,0:T(8,128)S(1)} %get-tuple-element.118.mi), channel_id=1, source_target_pairs={{0,1},{1,0},{2,3},{3,2},{4,5},{5,4},{6,7},{7,6},{8,9},{9,8},{10,11... | collective-permute-start | bytes 884744 | tf_op jit(solution)/shard_map/ppermute | solution.py:522
  32.1 1.5 %base.1 = (f32[53,16,256]{2,1,0:T(8,128)S(1)}, f32[53,16,256]{2,1,0:T(8,128)S(1)}) custom-call(f32[16,56,256]{2,1,0:T(8,128)S(1)} %get-tuple-element.111.n1, f32[16,56,256]{2,1,0:T(8,128)S(1)} %get-tuple-element.121.n2, f32[16,24,256]{2,1,0:T(8,128)S(1)} %get-tuple-element.122.c1, f32[16,24,256]{2,1,0:T(8,128)S(1)} %get-tuple-element.123.c2, ...), custom_call_target="tpu_custom_call" | custom-call | tf_op jit(solution)/shard_map/base/pallas_call | solution.py:500
  33.6 4.8 %collective-permute-done.4.ho = f32[12,24,256]{2,1,0:T(8,128)S(1)} collective-permute-done((f32[12,24,256]{2,1,0:T(8,128)S(1)}, f32[12,24,256]{2,1,0:T(8,128)S(1)}, u32[]{:S(2)}, u32[]{:S(2)}) %collective-permute-start.4) | collective-permute-done | bytes 294944 | tf_op jit(solution)/shard_map/ppermute | solution.py:522
  38.5 0.0 collective-permute-done.5.hi
  38.5 0.2 last_edge.1
  38.7 0.7 collective-permute-start.10
  39.4 2.1 %collective-permute-start.9 = (f32[36,24,256]{2,1,0:T(8,128)S(1)}, f32[36,24,256]{2,1,0:T(8,128)S(1)}, u32[]{:S(2)}, u32[]{:S(2)}) collective-permute-start(f32[36,24,256]{2,1,0:T(8,128)S(1)} %get-tuple-element.127.ab), channel_id=1, source_target_pairs={{32,16},{34,18},{36,20},{38,22},{40,24},{42,26},{44,28},{46,30},{3... | collective-permute-start | bytes 2654216 | tf_op jit(solution)/shard_map/ppermute | solution.py:522
  41.5 0.7 collective-permute-start.6
  42.2 0.7 collective-permute-start.7
  42.9 0.7 collective-permute-start.8
  43.6 0.0 collective-permute-done.6.z0
  43.6 17.9 %collective-permute-done.9.short = f32[36,24,256]{2,1,0:T(8,128)S(1)} collective-permute-done((f32[36,24,256]{2,1,0:T(8,128)S(1)}, f32[36,24,256]{2,1,0:T(8,128)S(1)}, u32[]{:S(2)}, u32[]{:S(2)}) %collective-permute-start.9) | collective-permute-done | bytes 884768 | tf_op jit(solution)/shard_map/ppermute | solution.py:522
  61.5 0.7 collective-permute-start.15
  62.2 1.9 %collective-permute-start.14 = (f32[53,16,256]{2,1,0:T(8,128)S(1)}, f32[53,16,256]{2,1,0:T(8,128)S(1)}, u32[]{:S(2)}, u32[]{:S(2)}) collective-permute-start(f32[53,16,256]{2,1,0:T(8,128)S(1)} %get-tuple-element.142.b2), channel_id=1, source_target_pairs={{0,16},{1,17},{2,18},{3,19},{4,20},{5,21},{6,22},{7,23},{8,24},{9,... | collective-permute-start | bytes 2605064 | tf_op jit(solution)/shard_map/ppermute | solution.py:522
  64.2 0.7 collective-permute-start.11
  64.9 0.7 collective-permute-start.12
  65.6 0.7 collective-permute-start.13
  66.3 0.0 collective-permute-done.11.z0
  66.3 20.5 %collective-permute-done.14.b0 = f32[53,16,256]{2,1,0:T(8,128)S(1)} collective-permute-done((f32[53,16,256]{2,1,0:T(8,128)S(1)}, f32[53,16,256]{2,1,0:T(8,128)S(1)}, u32[]{:S(2)}, u32[]{:S(2)}) %collective-permute-start.14) | collective-permute-done | bytes 868384 | tf_op jit(solution)/shard_map/ppermute | solution.py:522
  86.8 0.7 collective-permute-start.16
  87.5 0.7 collective-permute-start.17
  88.2 0.7 collective-permute-start.18
  89.0 0.0 copy-start.2
  89.1 1.3 collective-permute-start.22
  90.4 0.7 collective-permute-start.23
  91.1 0.7 collective-permute-start.19
  91.8 0.7 collective-permute-start.20
  92.5 0.7 collective-permute-start.21
  93.2 34.5 %collective-permute-done.22.other = f32[48,24,256]{2,1,0:T(8,128)S(1)} collective-permute-done((f32[48,24,256]{2,1,0:T(8,128)S(1)}, f32[48,24,256]{2,1,0:T(8,128)S(1)}, u32[]{:S(2)}, u32[]{:S(2)}) %collective-permute-start.22) | collective-permute-done | bytes 1179680 | tf_op jit(solution)/shard_map/ppermute | solution.py:522
  127.7 2.6 %out.1 = f32[3,53,16,256]{3,2,1,0:T(8,128)} custom-call(s32[53]{0:T(128)S(1)} %bitcast.10, f32[3,53,16,256]{3,2,1,0:T(8,128)S(1)} %bitcast.9, f32[53,16,256]{2,1,0:T(8,128)S(1)} %collective-permute-done.14.b0, f32[53,16,256]{2,1,0:T(8,128)S(1)} %get-tuple-element.126.b1, f32[53,16,256]{2,1,0:T(8,128)S(1)} %get-tuple-element.142.b2, ...), custom_call_target="tpu_custom_call" | custom-call | tf_op jit(solution)/shard_map/out/pallas_call | solution.py:500
  (24 shorter events, 0.2 us)
Async XLA Ops:
  1.7 1.7 %copy-start = (f32[1,3,53,16,256]{4,3,2,1,0:T(8,128)S(1)}, f32[1,3,53,16,256]{4,3,2,1,0:T(8,128)}, u32[]{:S(2)}) copy-start(f32[1,3,53,16,256]{4,3,2,1,0:T(8,128)} %param.8) | copy-start | bytes 7815172
  3.5 5.1 %copy-start.1 = (f32[1,3,53,16,256]{4,3,2,1,0:T(8,128)S(1)}, f32[1,3,53,16,256]{4,3,2,1,0:T(8,128)}, u32[]{:S(2)}) copy-start(f32[1,3,53,16,256]{4,3,2,1,0:T(8,128)} %param.8) | copy-start | bytes 7815172
  3.9 13.8 %collective-permute-start = (f32[3,2,56,256]{3,2,1,0:T(8,128)S(1)}, f32[3,2,56,256]{3,2,1,0:T(8,128)S(1)}, u32[]{:S(2)}, u32[]{:S(2)}) collective-permute-start(f32[3,2,56,256]{3,2,1,0:T(8,128)S(1)} %get-tuple-element.95), channel_id=1, source_target_pairs={{1,2},{3,4},{5,6},{7,8},{9,10},{11,12},{13,14},{2,1},{4,3},{6,5},{... | collective-permute-start | bytes 1032200 | tf_op jit(solution)/shard_map/ppermute | solution.py:522
  6.8 10.9 %collective-permute-start.1 = (f32[3,2,56,256]{3,2,1,0:T(8,128)S(1)}, f32[3,2,56,256]{3,2,1,0:T(8,128)S(1)}, u32[]{:S(2)}, u32[]{:S(2)}) collective-permute-start(f32[3,2,56,256]{3,2,1,0:T(8,128)S(1)} %get-tuple-element.96), channel_id=1, source_target_pairs={{0,1},{1,0},{2,3},{3,2},{4,5},{5,4},{6,7},{7,6},{8,9},{9,8},{10,11... | collective-permute-start | bytes 1032200 | tf_op jit(solution)/shard_map/ppermute | solution.py:522
  18.1 8.2 %collective-permute-start.2 = (f32[2,56,256]{2,1,0:T(8,128)S(1)}, f32[2,56,256]{2,1,0:T(8,128)S(1)}, u32[]{:S(2)}, u32[]{:S(2)}) collective-permute-start(f32[2,56,256]{2,1,0:T(8,128)S(1)} %get-tuple-element.106), channel_id=1, source_target_pairs={{1,2},{3,4},{5,6},{7,8},{9,10},{11,12},{13,14},{2,1},{4,3},{6,5},{... | collective-permute-start | bytes 344072 | tf_op jit(solution)/shard_map/ppermute | solution.py:522
  20.2 6.1 %collective-permute-start.3 = (f32[2,56,256]{2,1,0:T(8,128)S(1)}, f32[2,56,256]{2,1,0:T(8,128)S(1)}, u32[]{:S(2)}, u32[]{:S(2)}) collective-permute-start(f32[2,56,256]{2,1,0:T(8,128)S(1)} %get-tuple-element.107), channel_id=1, source_target_pairs={{0,1},{1,0},{2,3},{3,2},{4,5},{5,4},{6,7},{7,6},{8,9},{9,8},{10,11... | collective-permute-start | bytes 344072 | tf_op jit(solution)/shard_map/ppermute | solution.py:522
  27.3 11.1 %collective-permute-start.4 = (f32[12,24,256]{2,1,0:T(8,128)S(1)}, f32[12,24,256]{2,1,0:T(8,128)S(1)}, u32[]{:S(2)}, u32[]{:S(2)}) collective-permute-start(f32[12,24,256]{2,1,0:T(8,128)S(1)} %get-tuple-element.117.mo), channel_id=1, source_target_pairs={{1,2},{3,4},{5,6},{7,8},{9,10},{11,12},{13,14},{2,1},{4,3},{6,5},{... | collective-permute-start | bytes 884744 | tf_op jit(solution)/shard_map/ppermute | solution.py:522
  30.6 7.9 %collective-permute-start.5 = (f32[12,24,256]{2,1,0:T(8,128)S(1)}, f32[12,24,256]{2,1,0:T(8,128)S(1)}, u32[]{:S(2)}, u32[]{:S(2)}) collective-permute-start(f32[12,24,256]{2,1,0:T(8,128)S(1)} %get-tuple-element.118.mi), channel_id=1, source_target_pairs={{0,1},{1,0},{2,3},{3,2},{4,5},{5,4},{6,7},{7,6},{8,9},{9,8},{10,11... | collective-permute-start | bytes 884744 | tf_op jit(solution)/shard_map/ppermute | solution.py:522
  38.7 22.8 %collective-permute-start.10 = (f32[52,24,256]{2,1,0:T(8,128)S(1)}, f32[52,24,256]{2,1,0:T(8,128)S(1)}, u32[]{:S(2)}, u32[]{:S(2)}) collective-permute-start(f32[52,24,256]{2,1,0:T(8,128)S(1)} %get-tuple-element.143.mine), channel_id=1, source_target_pairs={{17,81},{19,83},{21,85},{23,87},{25,89},{27,91},{29,93},{31,95},{4... | collective-permute-start | bytes 3833864 | tf_op jit(solution)/shard_map/ppermute | solution.py:522
  39.4 22.1 %collective-permute-start.9 = (f32[36,24,256]{2,1,0:T(8,128)S(1)}, f32[36,24,256]{2,1,0:T(8,128)S(1)}, u32[]{:S(2)}, u32[]{:S(2)}) collective-permute-start(f32[36,24,256]{2,1,0:T(8,128)S(1)} %get-tuple-element.127.ab), channel_id=1, source_target_pairs={{32,16},{34,18},{36,20},{38,22},{40,24},{42,26},{44,28},{46,30},{3... | collective-permute-start | bytes 2654216 | tf_op jit(solution)/shard_map/ppermute | solution.py:522
  41.5 2.1 %collective-permute-start.6 = (f32[16,24,256]{2,1,0:T(8,128)S(1)}, f32[16,24,256]{2,1,0:T(8,128)S(1)}, u32[]{:S(2)}, u32[]{:S(2)}) collective-permute-start(f32[16,24,256]{2,1,0:T(8,128)S(1)} %get-tuple-element.128), channel_id=1, source_target_pairs={{0,16},{1,81},{2,18},{3,83},{4,20},{5,85},{6,22},{7,87},{8,24},{9,... | collective-permute-start | bytes 1179656 | tf_op jit(solution)/shard_map/ppermute | solution.py:522
  42.2 1.4 %collective-permute-start.7 = (f32[8,24,256]{2,1,0:T(8,128)S(1)}, f32[8,24,256]{2,1,0:T(8,128)S(1)}, u32[]{:S(2)}, u32[]{:S(2)}) collective-permute-start(f32[8,24,256]{2,1,0:T(8,128)S(1)} %get-tuple-element.129), channel_id=1, source_target_pairs={{1,18},{3,20},{5,22},{7,24},{9,26},{11,28},{13,30},{2,81},{4,83},{... | collective-permute-start | bytes 589832 | tf_op jit(solution)/shard_map/ppermute | solution.py:522
  42.9 0.7 collective-permute-start.8
  61.5 25.3 %collective-permute-start.15 = (f32[52,24,256]{2,1,0:T(8,128)S(1)}, f32[52,24,256]{2,1,0:T(8,128)S(1)}, u32[]{:S(2)}, u32[]{:S(2)}) collective-permute-start(f32[52,24,256]{2,1,0:T(8,128)S(1)} %get-tuple-element.143.mine), channel_id=1, source_target_pairs={{81,97},{83,99},{85,101},{87,103},{89,105},{91,107},{93,109},{95,1... | collective-permute-start | bytes 3833864 | tf_op jit(solution)/shard_map/ppermute | solution.py:522
  62.2 24.6 %collective-permute-start.14 = (f32[53,16,256]{2,1,0:T(8,128)S(1)}, f32[53,16,256]{2,1,0:T(8,128)S(1)}, u32[]{:S(2)}, u32[]{:S(2)}) collective-permute-start(f32[53,16,256]{2,1,0:T(8,128)S(1)} %get-tuple-element.142.b2), channel_id=1, source_target_pairs={{0,16},{1,17},{2,18},{3,19},{4,20},{5,21},{6,22},{7,23},{8,24},{9,... | collective-permute-start | bytes 2605064 | tf_op jit(solution)/shard_map/ppermute | solution.py:522
  64.2 2.1 %collective-permute-start.11 = (f32[16,24,256]{2,1,0:T(8,128)S(1)}, f32[16,24,256]{2,1,0:T(8,128)S(1)}, u32[]{:S(2)}, u32[]{:S(2)}) collective-permute-start(f32[16,24,256]{2,1,0:T(8,128)S(1)} %get-tuple-element.138.z2), channel_id=1, source_target_pairs={{16,48},{81,65},{18,50},{83,67},{20,52},{85,69},{22,54},{87,71},{2... | collective-permute-start | bytes 1179656 | tf_op jit(solution)/shard_map/ppermute | solution.py:522
  64.9 1.4 %collective-permute-start.12 = (f32[8,24,256]{2,1,0:T(8,128)S(1)}, f32[8,24,256]{2,1,0:T(8,128)S(1)}, u32[]{:S(2)}, u32[]{:S(2)}) collective-permute-start(f32[8,24,256]{2,1,0:T(8,128)S(1)} %get-tuple-element.139), channel_id=1, source_target_pairs={{81,50},{83,52},{85,54},{87,56},{89,58},{91,60},{93,62},{18,65},{2... | collective-permute-start | bytes 589832 | tf_op jit(solution)/shard_map/ppermute | solution.py:522
  65.6 0.7 collective-permute-start.13
  86.8 2.1 %collective-permute-start.16 = (f32[16,24,256]{2,1,0:T(8,128)S(1)}, f32[16,24,256]{2,1,0:T(8,128)S(1)}, u32[]{:S(2)}, u32[]{:S(2)}) collective-permute-start(f32[16,24,256]{2,1,0:T(8,128)S(1)} %get-tuple-element.148.z2), channel_id=1, source_target_pairs={{48,80},{65,97},{50,82},{67,99},{52,84},{69,101},{54,86},{71,103},... | collective-permute-start | bytes 1179656 | tf_op jit(solution)/shard_map/ppermute | solution.py:522
  87.5 1.4 %collective-permute-start.17 = (f32[8,24,256]{2,1,0:T(8,128)S(1)}, f32[8,24,256]{2,1,0:T(8,128)S(1)}, u32[]{:S(2)}, u32[]{:S(2)}) collective-permute-start(f32[8,24,256]{2,1,0:T(8,128)S(1)} %get-tuple-element.149), channel_id=1, source_target_pairs={{65,82},{67,84},{69,86},{71,88},{73,90},{75,92},{77,94},{50,97},{5... | collective-permute-start | bytes 589832 | tf_op jit(solution)/shard_map/ppermute | solution.py:522
  88.2 0.8 collective-permute-start.18
  89.0 38.7 %copy-start.2 = (s32[53,1]{0,1:T(1,128)S(1)}, s32[53,1]{0,1:T(1,128)}, u32[]{:S(2)}) copy-start(s32[53,1]{0,1:T(1,128)} %param.15) | copy-start | bytes 640
  89.1 38.6 %collective-permute-start.22 = (f32[48,24,256]{2,1,0:T(8,128)S(1)}, f32[48,24,256]{2,1,0:T(8,128)S(1)}, u32[]{:S(2)}, u32[]{:S(2)}) collective-permute-start(f32[48,24,256]{2,1,0:T(8,128)S(1)} %get-tuple-element.175), channel_id=1, source_target_pairs={{16,32},{18,34},{20,36},{22,38},{24,40},{26,42},{28,44},{30,46},{8... | collective-permute-start | bytes 3538952 | tf_op jit(solution)/shard_map/ppermute | solution.py:522
  90.4 37.3 %collective-permute-start.23 = (f32[48,24,256]{2,1,0:T(8,128)S(1)}, f32[48,24,256]{2,1,0:T(8,128)S(1)}, u32[]{:S(2)}, u32[]{:S(2)}) collective-permute-start(f32[48,24,256]{2,1,0:T(8,128)S(1)} %get-tuple-element.180.home), channel_id=1, source_target_pairs={{81,17},{83,19},{85,21},{87,23},{89,25},{91,27},{93,29},{95,31}} | collective-permute-start | bytes 3538952 | tf_op jit(solution)/shard_map/ppermute | solution.py:522
  91.1 2.1 %collective-permute-start.19 = (f32[16,24,256]{2,1,0:T(8,128)S(1)}, f32[16,24,256]{2,1,0:T(8,128)S(1)}, u32[]{:S(2)}, u32[]{:S(2)}) collective-permute-start(f32[16,24,256]{2,1,0:T(8,128)S(1)} %get-tuple-element.167.z2), channel_id=1, source_target_pairs={{80,112},{97,113},{82,114},{99,115},{84,116},{101,117},{86,118},{1... | collective-permute-start | bytes 1179656 | tf_op jit(solution)/shard_map/ppermute | solution.py:522
  91.8 1.4 %collective-permute-start.20 = (f32[4,24,256]{2,1,0:T(8,128)S(1)}, f32[4,24,256]{2,1,0:T(8,128)S(1)}, u32[]{:S(2)}, u32[]{:S(2)}) collective-permute-start(f32[4,24,256]{2,1,0:T(8,128)S(1)} %get-tuple-element.168), channel_id=1, source_target_pairs={{97,114},{99,116},{101,118},{103,120},{105,122},{107,124},{109,126... | collective-permute-start | bytes 294920 | tf_op jit(solution)/shard_map/ppermute | solution.py:522
  92.5 0.7 collective-permute-start.21

commit v5 on v4

--- a/solution.py
+++ b/solution.py
@@ -617,7 +617,7 @@
             back.append((both(host), both(slices[0] if host == slices[1] else slices[1]), slabs))
             if host not in slices:
                 first.append((both(host), both(slices[0]), slabs))
-    short, long, long_last = moved(ab, *short), moved(abx, *long[:-1]), long[-1:]
+    short, long = moved(ab, *short), moved(abx, *long)
     forward = [(both(p), both(p + 1), SAME) for p in range(SLICES - 1)]
     home, away, *sent = call(
         functools.partial(start_kernel, GROUPS[0][1]), "start", [result, result, coarse, eight, eight], ab, wc, dc12
@@ -625,10 +625,10 @@
     for at, (slices, hosts) in enumerate(GROUPS[1:], 1):
         z = hop(*sent, GROUPS[at - 1][1], hosts)
         if at == 1:
-            *z, short, long = lax.optimization_barrier((*z, short, long))
-            b0, long_last = moved(after(b2, z[0]), *forward), moved(after(abx, z[0]), *long_last)
+            z = list(lax.optimization_barrier(tuple(z)))
+            b0 = moved(after(b2, z[0]), *forward)
         elif at == 2:
-            *z, b0, long_last = lax.optimization_barrier((*z, b0, long_last))
+            *z, b0 = lax.optimization_barrier((*z, b0))
         elif at == 3:
             *z, home, away = lax.optimization_barrier((*z, home, away))
         else:
@@ -640,7 +640,7 @@
                 functools.partial(pair_kernel, slices, hosts, depth),
                 "pair",
                 [coarse, field(depth, CP), field(depth, CP), field(ROWS + 12, CP), field(ROWS + 8, CP), field(ROWS + 4, CP)],
-                *(*z, abx, short, long_last if at == 3 else long, wc, dc12),
+                *(*z, abx, short, long, wc, dc12),
                 scratch=[field(ROWS + 16, CP)],
             )
             home, away = call(

time: 131 us -> 120 us (0.916)
  the two profiles are of different devices: /device:TPU:78 before, /device:TPU:51 now
where the time goes in v5:
time: 120 us; the launch traced here: 119 us
  waiting for transfers between devices  58.1 us (48%)
  starting transfers between devices  36.9 us (31%)
  Pallas kernels  19.9 us (17%)
  local copies, waits for them, and re-layouts  1.74 us (1%)
  other arithmetic  1.5 us (1%)
    ppermute x23, waiting for transfers between devices, moved(): return lax.ppermute(value, AXES, pairs)  58.1 us
    ppermute x23, starting transfers between devices, moved(): return lax.ppermute(value, AXES, pairs)  36.9 us
    pallas_call x16, Pallas kernels, call(): pl.pallas_call(kernel, out_shape=outs, in_specs=specs, **{'out_specs': ou...  19.9 us
  transfers between devices with their start and end apart: 23, of which 8 were waited for; matrix products, arithmetic and copies ran while one was open for 0% of the time, Pallas kernels for 13%

profile of v5, /device:TPU:51, one launch (start us, length us, event | category | flops | bytes accessed | tf_op | source)
XLA Modules:
  0.0 118.7 jit_solution(6810953803188977196)
XLA Ops:
  0.0 0.7 convert_bitcast_fusion
  0.7 0.8 pad_add_fusion.raw
  1.5 0.2 prep.1
  1.7 0.0 copy-start
  1.8 1.7 %copy-done = f32[1,3,53,16,256]{4,3,2,1,0:T(8,128)S(1)} copy-done((f32[1,3,53,16,256]{4,3,2,1,0:T(8,128)S(1)}, f32[1,3,53,16,256]{4,3,2,1,0:T(8,128)}, u32[]{:S(2)}) %copy-start) | copy-done | bytes 2605080
  3.5 0.4 first.1
  3.9 4.4 %collective-permute-start = (f32[3,2,56,256]{3,2,1,0:T(8,128)S(1)}, f32[3,2,56,256]{3,2,1,0:T(8,128)S(1)}, u32[]{:S(2)}, u32[]{:S(2)}) collective-permute-start(f32[3,2,56,256]{3,2,1,0:T(8,128)S(1)} %get-tuple-element.91), channel_id=1, source_target_pairs={{1,2},{3,4},{5,6},{7,8},{9,10},{11,12},{13,14},{2,1},{4,3},{6,5},{... | collective-permute-start | bytes 1032200 | tf_op jit(solution)/shard_map/ppermute | solution.py:522
  8.3 0.1 collective-permute-start.1
  8.4 6.3 %old.1 = (f32[16,56,256]{2,1,0:T(8,128)S(1)}, f32[16,56,256]{2,1,0:T(8,128)S(1)}, f32[16,24,256]{2,1,0:T(8,128)S(1)}, f32[16,24,256]{2,1,0:T(8,128)S(1)}, f32[16,24,256]{2,1,0:T(8,128)S(1)}) custom-call(f32[3,53,16,256]{3,2,1,0:T(8,128)S(1)} %bitcast.8, bf16[112,256]{1,0:T(8,128)(2,1)S(1)} %get-tuple-element.96.wf, ...), custom_call_target="tpu_custom_call" | custom-call | tf_op jit(solution)/shard_map/old/pallas_call | solution.py:500
  14.8 2.6 %collective-permute-done.uo = f32[3,2,56,256]{3,2,1,0:T(8,128)S(1)} collective-permute-done((f32[3,2,56,256]{3,2,1,0:T(8,128)S(1)}, f32[3,2,56,256]{3,2,1,0:T(8,128)S(1)}, u32[]{:S(2)}, u32[]{:S(2)}) %collective-permute-start) | collective-permute-done | bytes 344096 | tf_op jit(solution)/shard_map/ppermute | solution.py:522
  17.4 0.0 collective-permute-done.1.ui
  17.4 0.4 old_edge.1
  17.8 4.6 %collective-permute-start.2 = (f32[2,56,256]{2,1,0:T(8,128)S(1)}, f32[2,56,256]{2,1,0:T(8,128)S(1)}, u32[]{:S(2)}, u32[]{:S(2)}) collective-permute-start(f32[2,56,256]{2,1,0:T(8,128)S(1)} %get-tuple-element.102), channel_id=1, source_target_pairs={{1,2},{3,4},{5,6},{7,8},{9,10},{11,12},{13,14},{2,1},{4,3},{6,5},{... | collective-permute-start | bytes 344072 | tf_op jit(solution)/shard_map/ppermute | solution.py:522
  22.4 0.7 collective-permute-start.3
  23.1 3.7 %mid.1 = (f32[16,56,256]{2,1,0:T(8,128)S(1)}, f32[16,24,256]{2,1,0:T(8,128)S(1)}, f32[16,24,256]{2,1,0:T(8,128)S(1)}, f32[16,24,256]{2,1,0:T(8,128)S(1)}) custom-call(f32[16,56,256]{2,1,0:T(8,128)S(1)} %get-tuple-element.107.n1, f32[16,56,256]{2,1,0:T(8,128)S(1)} %get-tuple-element.108.s, bf16[240,256]{1,0:T(8,128)(2,1)S(1)} %get-tuple-element.109.wfr, ...), custom_call_target="tpu_custom_call" | custom-call | tf_op jit(solution)/shard_map/mid/pallas_call | solution.py:500
  26.8 1.0 mid_edge.1
  27.8 3.8 %collective-permute-start.4 = (f32[12,24,256]{2,1,0:T(8,128)S(1)}, f32[12,24,256]{2,1,0:T(8,128)S(1)}, u32[]{:S(2)}, u32[]{:S(2)}) collective-permute-start(f32[12,24,256]{2,1,0:T(8,128)S(1)} %get-tuple-element.113.mo), channel_id=1, source_target_pairs={{1,2},{3,4},{5,6},{7,8},{9,10},{11,12},{13,14},{2,1},{4,3},{6,5},{... | collective-permute-start | bytes 884744 | tf_op jit(solution)/shard_map/ppermute | solution.py:522
  31.7 1.4 %collective-permute-start.5 = (f32[12,24,256]{2,1,0:T(8,128)S(1)}, f32[12,24,256]{2,1,0:T(8,128)S(1)}, u32[]{:S(2)}, u32[]{:S(2)}) collective-permute-start(f32[12,24,256]{2,1,0:T(8,128)S(1)} %get-tuple-element.114.mi), channel_id=1, source_target_pairs={{0,1},{1,0},{2,3},{3,2},{4,5},{5,4},{6,7},{7,6},{8,9},{9,8},{10,11... | collective-permute-start | bytes 884744 | tf_op jit(solution)/shard_map/ppermute | solution.py:522
  33.1 1.5 %base.1 = (f32[53,16,256]{2,1,0:T(8,128)S(1)}, f32[53,16,256]{2,1,0:T(8,128)S(1)}) custom-call(f32[16,56,256]{2,1,0:T(8,128)S(1)} %get-tuple-element.107.n1, f32[16,56,256]{2,1,0:T(8,128)S(1)} %get-tuple-element.117.n2, f32[16,24,256]{2,1,0:T(8,128)S(1)} %get-tuple-element.118.c1, f32[16,24,256]{2,1,0:T(8,128)S(1)} %get-tuple-element.119.c2, ...), custom_call_target="tpu_custom_call" | custom-call | tf_op jit(solution)/shard_map/base/pallas_call | solution.py:500
  34.6 5.5 %collective-permute-done.4.ho = f32[12,24,256]{2,1,0:T(8,128)S(1)} collective-permute-done((f32[12,24,256]{2,1,0:T(8,128)S(1)}, f32[12,24,256]{2,1,0:T(8,128)S(1)}, u32[]{:S(2)}, u32[]{:S(2)}) %collective-permute-start.4) | collective-permute-done | bytes 294944 | tf_op jit(solution)/shard_map/ppermute | solution.py:522
  40.1 0.2 last_edge.1
  40.3 3.5 %collective-permute-start.10 = (f32[52,24,256]{2,1,0:T(8,128)S(1)}, f32[52,24,256]{2,1,0:T(8,128)S(1)}, u32[]{:S(2)}, u32[]{:S(2)}) collective-permute-start(f32[52,24,256]{2,1,0:T(8,128)S(1)} %get-tuple-element.131.mine), channel_id=1, source_target_pairs={{17,81},{19,83},{21,85},{23,87},{25,89},{27,91},{29,93},{31,95},{4... | collective-permute-start | bytes 3833864 | tf_op jit(solution)/shard_map/ppermute | solution.py:522
  43.8 1.3 %collective-permute-start.9 = (f32[36,24,256]{2,1,0:T(8,128)S(1)}, f32[36,24,256]{2,1,0:T(8,128)S(1)}, u32[]{:S(2)}, u32[]{:S(2)}) collective-permute-start(f32[36,24,256]{2,1,0:T(8,128)S(1)} %get-tuple-element.123.ab), channel_id=1, source_target_pairs={{32,16},{34,18},{36,20},{38,22},{40,24},{42,26},{44,28},{46,30},{3... | collective-permute-start | bytes 2654216 | tf_op jit(solution)/shard_map/ppermute | solution.py:522
  45.2 1.3 %collective-permute-start.6 = (f32[16,24,256]{2,1,0:T(8,128)S(1)}, f32[16,24,256]{2,1,0:T(8,128)S(1)}, u32[]{:S(2)}, u32[]{:S(2)}) collective-permute-start(f32[16,24,256]{2,1,0:T(8,128)S(1)} %get-tuple-element.124), channel_id=1, source_target_pairs={{0,16},{1,81},{2,18},{3,83},{4,20},{5,85},{6,22},{7,87},{8,24},{9,... | collective-permute-start | bytes 1179656 | tf_op jit(solution)/shard_map/ppermute | solution.py:522
  46.5 1.3 %collective-permute-start.7 = (f32[8,24,256]{2,1,0:T(8,128)S(1)}, f32[8,24,256]{2,1,0:T(8,128)S(1)}, u32[]{:S(2)}, u32[]{:S(2)}) collective-permute-start(f32[8,24,256]{2,1,0:T(8,128)S(1)} %get-tuple-element.125), channel_id=1, source_target_pairs={{1,18},{3,20},{5,22},{7,24},{9,26},{11,28},{13,30},{2,81},{4,83},{... | collective-permute-start | bytes 589832 | tf_op jit(solution)/shard_map/ppermute | solution.py:522
  47.8 1.3 %collective-permute-start.8 = (f32[8,24,256]{2,1,0:T(8,128)S(1)}, f32[8,24,256]{2,1,0:T(8,128)S(1)}, u32[]{:S(2)}, u32[]{:S(2)}) collective-permute-start(f32[8,24,256]{2,1,0:T(8,128)S(1)} %get-tuple-element.126), channel_id=1, source_target_pairs={{0,81},{1,16},{2,83},{3,18},{4,85},{5,20},{6,87},{7,22},{8,89},{9,... | collective-permute-start | bytes 589832 | tf_op jit(solution)/shard_map/ppermute | solution.py:522
  49.1 7.5 %collective-permute-done.7.zo = f32[8,24,256]{2,1,0:T(8,128)S(1)} collective-permute-done((f32[8,24,256]{2,1,0:T(8,128)S(1)}, f32[8,24,256]{2,1,0:T(8,128)S(1)}, u32[]{:S(2)}, u32[]{:S(2)}) %collective-permute-start.7) | collective-permute-done | bytes 196640 | tf_op jit(solution)/shard_map/ppermute | solution.py:522
  56.6 3.7 %collective-permute-done.8.zi = f32[8,24,256]{2,1,0:T(8,128)S(1)} collective-permute-done((f32[8,24,256]{2,1,0:T(8,128)S(1)}, f32[8,24,256]{2,1,0:T(8,128)S(1)}, u32[]{:S(2)}, u32[]{:S(2)}) %collective-permute-start.8) | collective-permute-done | bytes 196640 | tf_op jit(solution)/shard_map/ppermute | solution.py:522
  60.2 1.9 %collective-permute-start.14 = (f32[53,16,256]{2,1,0:T(8,128)S(1)}, f32[53,16,256]{2,1,0:T(8,128)S(1)}, u32[]{:S(2)}, u32[]{:S(2)}) collective-permute-start(f32[53,16,256]{2,1,0:T(8,128)S(1)} %get-tuple-element.136.b2), channel_id=1, source_target_pairs={{0,16},{1,17},{2,18},{3,19},{4,20},{5,21},{6,22},{7,23},{8,24},{9,... | collective-permute-start | bytes 2605064 | tf_op jit(solution)/shard_map/ppermute | solution.py:522
  62.2 3.1 %collective-permute-done.10.long = f32[52,24,256]{2,1,0:T(8,128)S(1)} collective-permute-done((f32[52,24,256]{2,1,0:T(8,128)S(1)}, f32[52,24,256]{2,1,0:T(8,128)S(1)}, u32[]{:S(2)}, u32[]{:S(2)}) %collective-permute-start.10) | collective-permute-done | bytes 1277984 | tf_op jit(solution)/shard_map/ppermute | solution.py:522
  65.2 3.4 %pair.3 = (f32[16,24,256]{2,1,0:T(8,128)S(1)}, f32[8,24,256]{2,1,0:T(8,128)S(1)}, f32[8,24,256]{2,1,0:T(8,128)S(1)}, f32[28,24,256]{2,1,0:T(8,128)S(1)}, f32[24,...) custom-call(f32[16,24,256]{2,1,0:T(8,128)S(1)} %collective-permute-done.6.z0, ...), custom_call_target="tpu_custom_call" | custom-call | tf_op jit(solution)/shard_map/pair/pallas_call | solution.py:500
  68.6 1.3 %collective-permute-start.11 = (f32[16,24,256]{2,1,0:T(8,128)S(1)}, f32[16,24,256]{2,1,0:T(8,128)S(1)}, u32[]{:S(2)}, u32[]{:S(2)}) collective-permute-start(f32[16,24,256]{2,1,0:T(8,128)S(1)} %get-tuple-element.132.z2), channel_id=1, source_target_pairs={{16,48},{81,65},{18,50},{83,67},{20,52},{85,69},{22,54},{87,71},{2... | collective-permute-start | bytes 1179656 | tf_op jit(solution)/shard_map/ppermute | solution.py:522
  69.9 1.3 %collective-permute-start.12 = (f32[8,24,256]{2,1,0:T(8,128)S(1)}, f32[8,24,256]{2,1,0:T(8,128)S(1)}, u32[]{:S(2)}, u32[]{:S(2)}) collective-permute-start(f32[8,24,256]{2,1,0:T(8,128)S(1)} %get-tuple-element.133), channel_id=1, source_target_pairs={{81,50},{83,52},{85,54},{87,56},{89,58},{91,60},{93,62},{18,65},{2... | collective-permute-start | bytes 589832 | tf_op jit(solution)/shard_map/ppermute | solution.py:522
  71.2 1.3 %collective-permute-start.13 = (f32[8,24,256]{2,1,0:T(8,128)S(1)}, f32[8,24,256]{2,1,0:T(8,128)S(1)}, u32[]{:S(2)}, u32[]{:S(2)}) collective-permute-start(f32[8,24,256]{2,1,0:T(8,128)S(1)} %get-tuple-element.134), channel_id=1, source_target_pairs={{16,65},{81,48},{18,67},{83,50},{20,69},{85,52},{22,71},{87,54},{2... | collective-permute-start | bytes 589832 | tf_op jit(solution)/shard_map/ppermute | solution.py:522
  72.5 4.9 %collective-permute-done.14.b0 = f32[53,16,256]{2,1,0:T(8,128)S(1)} collective-permute-done((f32[53,16,256]{2,1,0:T(8,128)S(1)}, f32[53,16,256]{2,1,0:T(8,128)S(1)}, u32[]{:S(2)}, u32[]{:S(2)}) %collective-permute-start.14) | collective-permute-done | bytes 868384 | tf_op jit(solution)/shard_map/ppermute | solution.py:522
  77.4 1.4 %collective-permute-done.11.z0 = f32[16,24,256]{2,1,0:T(8,128)S(1)} collective-permute-done((f32[16,24,256]{2,1,0:T(8,128)S(1)}, f32[16,24,256]{2,1,0:T(8,128)S(1)}, u32[]{:S(2)}, u32[]{:S(2)}) %collective-permute-start.11) | collective-permute-done | bytes 393248 | tf_op jit(solution)/shard_map/ppermute | solution.py:522
  78.8 0.7 collective-permute-start.15
  79.5 0.7 collective-permute-start.16
  80.2 0.7 collective-permute-start.17
  80.9 0.2 gather.3
  81.2 0.0 copy-start.2
  81.2 1.9 %collective-permute-start.21 = (f32[48,24,256]{2,1,0:T(8,128)S(1)}, f32[48,24,256]{2,1,0:T(8,128)S(1)}, u32[]{:S(2)}, u32[]{:S(2)}) collective-permute-start(f32[48,24,256]{2,1,0:T(8,128)S(1)} %get-tuple-element.167), channel_id=1, source_target_pairs={{16,32},{18,34},{20,36},{22,38},{24,40},{26,42},{28,44},{30,46},{8... | collective-permute-start | bytes 3538952 | tf_op jit(solution)/shard_map/ppermute | solution.py:522
  83.1 1.4 %collective-permute-start.22 = (f32[48,24,256]{2,1,0:T(8,128)S(1)}, f32[48,24,256]{2,1,0:T(8,128)S(1)}, u32[]{:S(2)}, u32[]{:S(2)}) collective-permute-start(f32[48,24,256]{2,1,0:T(8,128)S(1)} %get-tuple-element.172.home), channel_id=1, source_target_pairs={{81,17},{83,19},{85,21},{87,23},{89,25},{91,27},{93,29},{95,31}} | collective-permute-start | bytes 3538952 | tf_op jit(solution)/shard_map/ppermute | solution.py:522
  84.5 0.7 collective-permute-start.18
  85.2 0.7 collective-permute-start.19
  85.9 0.7 collective-permute-start.20
  86.6 29.4 %collective-permute-done.21.other = f32[48,24,256]{2,1,0:T(8,128)S(1)} collective-permute-done((f32[48,24,256]{2,1,0:T(8,128)S(1)}, f32[48,24,256]{2,1,0:T(8,128)S(1)}, u32[]{:S(2)}, u32[]{:S(2)}) %collective-permute-start.21) | collective-permute-done | bytes 1179680 | tf_op jit(solution)/shard_map/ppermute | solution.py:522
  115.9 2.6 %out.1 = f32[3,53,16,256]{3,2,1,0:T(8,128)} custom-call(s32[53]{0:T(128)S(1)} %bitcast.10, f32[3,53,16,256]{3,2,1,0:T(8,128)S(1)} %bitcast.9, f32[53,16,256]{2,1,0:T(8,128)S(1)} %collective-permute-done.14.b0, f32[53,16,256]{2,1,0:T(8,128)S(1)} %get-tuple-element.122.b1, f32[53,16,256]{2,1,0:T(8,128)S(1)} %get-tuple-element.136.b2, ...), custom_call_target="tpu_custom_call" | custom-call | tf_op jit(solution)/shard_map/out/pallas_call | solution.py:500
  (22 shorter events, 0.1 us)
Async XLA Ops:
  1.7 1.7 %copy-start = (f32[1,3,53,16,256]{4,3,2,1,0:T(8,128)S(1)}, f32[1,3,53,16,256]{4,3,2,1,0:T(8,128)}, u32[]{:S(2)}) copy-start(f32[1,3,53,16,256]{4,3,2,1,0:T(8,128)} %param.8) | copy-start | bytes 7815172
  3.5 5.0 %copy-start.1 = (f32[1,3,53,16,256]{4,3,2,1,0:T(8,128)S(1)}, f32[1,3,53,16,256]{4,3,2,1,0:T(8,128)}, u32[]{:S(2)}) copy-start(f32[1,3,53,16,256]{4,3,2,1,0:T(8,128)} %param.8) | copy-start | bytes 7815172
  3.9 13.5 %collective-permute-start = (f32[3,2,56,256]{3,2,1,0:T(8,128)S(1)}, f32[3,2,56,256]{3,2,1,0:T(8,128)S(1)}, u32[]{:S(2)}, u32[]{:S(2)}) collective-permute-start(f32[3,2,56,256]{3,2,1,0:T(8,128)S(1)} %get-tuple-element.91), channel_id=1, source_target_pairs={{1,2},{3,4},{5,6},{7,8},{9,10},{11,12},{13,14},{2,1},{4,3},{6,5},{... | collective-permute-start | bytes 1032200 | tf_op jit(solution)/shard_map/ppermute | solution.py:522
  8.3 9.1 %collective-permute-start.1 = (f32[3,2,56,256]{3,2,1,0:T(8,128)S(1)}, f32[3,2,56,256]{3,2,1,0:T(8,128)S(1)}, u32[]{:S(2)}, u32[]{:S(2)}) collective-permute-start(f32[3,2,56,256]{3,2,1,0:T(8,128)S(1)} %get-tuple-element.92), channel_id=1, source_target_pairs={{0,1},{1,0},{2,3},{3,2},{4,5},{5,4},{6,7},{7,6},{8,9},{9,8},{10,11... | collective-permute-start | bytes 1032200 | tf_op jit(solution)/shard_map/ppermute | solution.py:522
  17.8 9.0 %collective-permute-start.2 = (f32[2,56,256]{2,1,0:T(8,128)S(1)}, f32[2,56,256]{2,1,0:T(8,128)S(1)}, u32[]{:S(2)}, u32[]{:S(2)}) collective-permute-start(f32[2,56,256]{2,1,0:T(8,128)S(1)} %get-tuple-element.102), channel_id=1, source_target_pairs={{1,2},{3,4},{5,6},{7,8},{9,10},{11,12},{13,14},{2,1},{4,3},{6,5},{... | collective-permute-start | bytes 344072 | tf_op jit(solution)/shard_map/ppermute | solution.py:522
  22.4 4.4 %collective-permute-start.3 = (f32[2,56,256]{2,1,0:T(8,128)S(1)}, f32[2,56,256]{2,1,0:T(8,128)S(1)}, u32[]{:S(2)}, u32[]{:S(2)}) collective-permute-start(f32[2,56,256]{2,1,0:T(8,128)S(1)} %get-tuple-element.103), channel_id=1, source_target_pairs={{0,1},{1,0},{2,3},{3,2},{4,5},{5,4},{6,7},{7,6},{8,9},{9,8},{10,11... | collective-permute-start | bytes 344072 | tf_op jit(solution)/shard_map/ppermute | solution.py:522
  27.8 12.3 %collective-permute-start.4 = (f32[12,24,256]{2,1,0:T(8,128)S(1)}, f32[12,24,256]{2,1,0:T(8,128)S(1)}, u32[]{:S(2)}, u32[]{:S(2)}) collective-permute-start(f32[12,24,256]{2,1,0:T(8,128)S(1)} %get-tuple-element.113.mo), channel_id=1, source_target_pairs={{1,2},{3,4},{5,6},{7,8},{9,10},{11,12},{13,14},{2,1},{4,3},{6,5},{... | collective-permute-start | bytes 884744 | tf_op jit(solution)/shard_map/ppermute | solution.py:522
  31.7 8.4 %collective-permute-start.5 = (f32[12,24,256]{2,1,0:T(8,128)S(1)}, f32[12,24,256]{2,1,0:T(8,128)S(1)}, u32[]{:S(2)}, u32[]{:S(2)}) collective-permute-start(f32[12,24,256]{2,1,0:T(8,128)S(1)} %get-tuple-element.114.mi), channel_id=1, source_target_pairs={{0,1},{1,0},{2,3},{3,2},{4,5},{5,4},{6,7},{7,6},{8,9},{9,8},{10,11... | collective-permute-start | bytes 884744 | tf_op jit(solution)/shard_map/ppermute | solution.py:522
  40.3 24.9 %collective-permute-start.10 = (f32[52,24,256]{2,1,0:T(8,128)S(1)}, f32[52,24,256]{2,1,0:T(8,128)S(1)}, u32[]{:S(2)}, u32[]{:S(2)}) collective-permute-start(f32[52,24,256]{2,1,0:T(8,128)S(1)} %get-tuple-element.131.mine), channel_id=1, source_target_pairs={{17,81},{19,83},{21,85},{23,87},{25,89},{27,91},{29,93},{31,95},{4... | collective-permute-start | bytes 3833864 | tf_op jit(solution)/shard_map/ppermute | solution.py:522
  43.8 18.3 %collective-permute-start.9 = (f32[36,24,256]{2,1,0:T(8,128)S(1)}, f32[36,24,256]{2,1,0:T(8,128)S(1)}, u32[]{:S(2)}, u32[]{:S(2)}) collective-permute-start(f32[36,24,256]{2,1,0:T(8,128)S(1)} %get-tuple-element.123.ab), channel_id=1, source_target_pairs={{32,16},{34,18},{36,20},{38,22},{40,24},{42,26},{44,28},{46,30},{3... | collective-permute-start | bytes 2654216 | tf_op jit(solution)/shard_map/ppermute | solution.py:522
  45.2 15.1 %collective-permute-start.6 = (f32[16,24,256]{2,1,0:T(8,128)S(1)}, f32[16,24,256]{2,1,0:T(8,128)S(1)}, u32[]{:S(2)}, u32[]{:S(2)}) collective-permute-start(f32[16,24,256]{2,1,0:T(8,128)S(1)} %get-tuple-element.124), channel_id=1, source_target_pairs={{0,16},{1,81},{2,18},{3,83},{4,20},{5,85},{6,22},{7,87},{8,24},{9,... | collective-permute-start | bytes 1179656 | tf_op jit(solution)/shard_map/ppermute | solution.py:522
  46.5 10.1 %collective-permute-start.7 = (f32[8,24,256]{2,1,0:T(8,128)S(1)}, f32[8,24,256]{2,1,0:T(8,128)S(1)}, u32[]{:S(2)}, u32[]{:S(2)}) collective-permute-start(f32[8,24,256]{2,1,0:T(8,128)S(1)} %get-tuple-element.125), channel_id=1, source_target_pairs={{1,18},{3,20},{5,22},{7,24},{9,26},{11,28},{13,30},{2,81},{4,83},{... | collective-permute-start | bytes 589832 | tf_op jit(solution)/shard_map/ppermute | solution.py:522
  47.8 12.5 %collective-permute-start.8 = (f32[8,24,256]{2,1,0:T(8,128)S(1)}, f32[8,24,256]{2,1,0:T(8,128)S(1)}, u32[]{:S(2)}, u32[]{:S(2)}) collective-permute-start(f32[8,24,256]{2,1,0:T(8,128)S(1)} %get-tuple-element.126), channel_id=1, source_target_pairs={{0,81},{1,16},{2,83},{3,18},{4,85},{5,20},{6,87},{7,22},{8,89},{9,... | collective-permute-start | bytes 589832 | tf_op jit(solution)/shard_map/ppermute | solution.py:522
  60.2 17.2 %collective-permute-start.14 = (f32[53,16,256]{2,1,0:T(8,128)S(1)}, f32[53,16,256]{2,1,0:T(8,128)S(1)}, u32[]{:S(2)}, u32[]{:S(2)}) collective-permute-start(f32[53,16,256]{2,1,0:T(8,128)S(1)} %get-tuple-element.136.b2), channel_id=1, source_target_pairs={{0,16},{1,17},{2,18},{3,19},{4,20},{5,21},{6,22},{7,23},{8,24},{9,... | collective-permute-start | bytes 2605064 | tf_op jit(solution)/shard_map/ppermute | solution.py:522
  68.6 10.2 %collective-permute-start.11 = (f32[16,24,256]{2,1,0:T(8,128)S(1)}, f32[16,24,256]{2,1,0:T(8,128)S(1)}, u32[]{:S(2)}, u32[]{:S(2)}) collective-permute-start(f32[16,24,256]{2,1,0:T(8,128)S(1)} %get-tuple-element.132.z2), channel_id=1, source_target_pairs={{16,48},{81,65},{18,50},{83,67},{20,52},{85,69},{22,54},{87,71},{2... | collective-permute-start | bytes 1179656 | tf_op jit(solution)/shard_map/ppermute | solution.py:522
  69.9 7.5 %collective-permute-start.12 = (f32[8,24,256]{2,1,0:T(8,128)S(1)}, f32[8,24,256]{2,1,0:T(8,128)S(1)}, u32[]{:S(2)}, u32[]{:S(2)}) collective-permute-start(f32[8,24,256]{2,1,0:T(8,128)S(1)} %get-tuple-element.133), channel_id=1, source_target_pairs={{81,50},{83,52},{85,54},{87,56},{89,58},{91,60},{93,62},{18,65},{2... | collective-permute-start | bytes 589832 | tf_op jit(solution)/shard_map/ppermute | solution.py:522
  71.2 6.2 %collective-permute-start.13 = (f32[8,24,256]{2,1,0:T(8,128)S(1)}, f32[8,24,256]{2,1,0:T(8,128)S(1)}, u32[]{:S(2)}, u32[]{:S(2)}) collective-permute-start(f32[8,24,256]{2,1,0:T(8,128)S(1)} %get-tuple-element.134), channel_id=1, source_target_pairs={{16,65},{81,48},{18,67},{83,50},{20,69},{85,52},{22,71},{87,54},{2... | collective-permute-start | bytes 589832 | tf_op jit(solution)/shard_map/ppermute | solution.py:522
  78.8 2.3 %collective-permute-start.15 = (f32[16,24,256]{2,1,0:T(8,128)S(1)}, f32[16,24,256]{2,1,0:T(8,128)S(1)}, u32[]{:S(2)}, u32[]{:S(2)}) collective-permute-start(f32[16,24,256]{2,1,0:T(8,128)S(1)} %get-tuple-element.141.z2), channel_id=1, source_target_pairs={{48,80},{65,97},{50,82},{67,99},{52,84},{69,101},{54,86},{71,103},... | collective-permute-start | bytes 1179656 | tf_op jit(solution)/shard_map/ppermute | solution.py:522
  79.5 1.6 %collective-permute-start.16 = (f32[8,24,256]{2,1,0:T(8,128)S(1)}, f32[8,24,256]{2,1,0:T(8,128)S(1)}, u32[]{:S(2)}, u32[]{:S(2)}) collective-permute-start(f32[8,24,256]{2,1,0:T(8,128)S(1)} %get-tuple-element.142), channel_id=1, source_target_pairs={{65,82},{67,84},{69,86},{71,88},{73,90},{75,92},{77,94},{50,97},{5... | collective-permute-start | bytes 589832 | tf_op jit(solution)/shard_map/ppermute | solution.py:522
  80.2 0.9 collective-permute-start.17
  81.2 34.8 %copy-start.2 = (s32[53,1]{0,1:T(1,128)S(1)}, s32[53,1]{0,1:T(1,128)}, u32[]{:S(2)}) copy-start(s32[53,1]{0,1:T(1,128)} %param.15) | copy-start | bytes 640
  81.2 34.7 %collective-permute-start.21 = (f32[48,24,256]{2,1,0:T(8,128)S(1)}, f32[48,24,256]{2,1,0:T(8,128)S(1)}, u32[]{:S(2)}, u32[]{:S(2)}) collective-permute-start(f32[48,24,256]{2,1,0:T(8,128)S(1)} %get-tuple-element.167), channel_id=1, source_target_pairs={{16,32},{18,34},{20,36},{22,38},{24,40},{26,42},{28,44},{30,46},{8... | collective-permute-start | bytes 3538952 | tf_op jit(solution)/shard_map/ppermute | solution.py:522
  83.1 32.8 %collective-permute-start.22 = (f32[48,24,256]{2,1,0:T(8,128)S(1)}, f32[48,24,256]{2,1,0:T(8,128)S(1)}, u32[]{:S(2)}, u32[]{:S(2)}) collective-permute-start(f32[48,24,256]{2,1,0:T(8,128)S(1)} %get-tuple-element.172.home), channel_id=1, source_target_pairs={{81,17},{83,19},{85,21},{87,23},{89,25},{91,27},{93,29},{95,31}} | collective-permute-start | bytes 3538952 | tf_op jit(solution)/shard_map/ppermute | solution.py:522
  84.5 2.1 %collective-permute-start.18 = (f32[16,24,256]{2,1,0:T(8,128)S(1)}, f32[16,24,256]{2,1,0:T(8,128)S(1)}, u32[]{:S(2)}, u32[]{:S(2)}) collective-permute-start(f32[16,24,256]{2,1,0:T(8,128)S(1)} %get-tuple-element.159.z2), channel_id=1, source_target_pairs={{80,112},{97,113},{82,114},{99,115},{84,116},{101,117},{86,118},{1... | collective-permute-start | bytes 1179656 | tf_op jit(solution)/shard_map/ppermute | solution.py:522
  85.2 1.4 %collective-permute-start.19 = (f32[4,24,256]{2,1,0:T(8,128)S(1)}, f32[4,24,256]{2,1,0:T(8,128)S(1)}, u32[]{:S(2)}, u32[]{:S(2)}) collective-permute-start(f32[4,24,256]{2,1,0:T(8,128)S(1)} %get-tuple-element.160), channel_id=1, source_target_pairs={{97,114},{99,116},{101,118},{103,120},{105,122},{107,124},{109,126... | collective-permute-start | bytes 294920 | tf_op jit(solution)/shard_map/ppermute | solution.py:522
  85.9 0.7 collective-permute-start.20

commit v6 on v5

--- a/solution.py
+++ b/solution.py
@@ -15,7 +15,7 @@
 W0 = (5.0 / 24.0, 1.0 / 3.0, -1.0 / 24.0)
 W1 = (-1.0 / 24.0, 1.0 / 3.0, 5.0 / 24.0)
 F32, BF16 = jnp.float32, jnp.bfloat16
-GROUPS = (((0,), (0, 0)), ((1, 2), (1, 5)), ((3, 4), (3, 4)), ((5, 6), (5, 6)), ((7,), (7, 7)))
+GROUPS = (((0,), (0, 0)), ((1, 2), (1, 1)), ((3, 4), (3, 4)), ((5, 6), (5, 6)), ((7,), (7, 7)))
 VMEM_LIMIT = 24 * 1024 * 1024
 
 
@@ -395,6 +395,12 @@
         pl.when(hosting(info, hosts) & (info[1] == host))(functools.partial(sweeps, one, two))
 
 
+def inner_kernel(z, inner):
+    info = Position()
+    for r in range(8):
+        inner[r] = jnp.where(info[0] == 0, z[ROWS - 8 + r], z[r])
+
+
 def gather(z0, za, zb, zc, z2, one, two):
     def body(xs):
         for x in xs:
@@ -422,15 +428,14 @@
 
 
 def out_kernel(
-    where, u, b0, b1, b2, share, z0, zo, zi, ab, wc, dc12, home, one, other, out, z, za, zs, spread, node, sem
+    where, u, b0, late, b1, b2, share, z0, zo, zi, ab, wc, dc12, home, other, out, z, za, zs, spread, node, sem
 ):
     info = Position()
     last = info[1] == SLICES - 1
     at_home = hosting(info, GROUPS[0][1])
     for slices, hosts in GROUPS[1:-1]:
         at_home = at_home | (hosting(info, hosts) & ((info[1] == slices[0]) | (info[1] == slices[1])))
-    first = info[1] == GROUPS[1][0][0]
-    for here, result in ((at_home, home), (first & ~at_home, one), (~at_home & ~first & ~last, other)):
+    for here, result in ((at_home, home), (~at_home & ~last, other)):
 
         @pl.when(here)
         def _():
@@ -468,7 +473,7 @@
         return copy
 
     first = info[1] == 0
-    copies = [finish(0, lambda s: jnp.where(first, u[0, s], b0[s]))]
+    copies = [finish(0, lambda s: jnp.where(first, u[0, s], b0[s] + late[s]))]
 
     @pl.when(last)
     def _():
@@ -603,10 +608,12 @@
     b1, b2 = call(base_kernel, "base", [field(SPECIES, ROWS)] * 2, n1, n2, c1, c2, pro, share)
     abx, ab = call(last_edge_kernel, "last_edge", [extended, short], outer, inner, ho, hi, abx, alias={4: 0})
 
+    forward = [(both(p), both(p + 1), SAME) for p in range(SLICES - 1)]
+    b0 = moved(b2, *forward[1:])
     ab, abx = after(ab, b1), after(abx, b1)
     result = field(3 * ROWS, CP)
     pairs = [(slices, hosts) for slices, hosts in GROUPS if len(slices) == 2]
-    short, long, back, first = [], [], [], []
+    short, long, back = [], [], []
     for slices, hosts in pairs:
         for core, host in enumerate(hosts):
             slabs = [(t, t) for t in range(core, SLABS, 2)]
@@ -615,25 +622,27 @@
             if host != slices[1]:
                 short.append((both(slices[1]), both(host), slabs))
             back.append((both(host), both(slices[0] if host == slices[1] else slices[1]), slabs))
-            if host not in slices:
-                first.append((both(host), both(slices[0]), slabs))
     short, long = moved(ab, *short), moved(abx, *long)
-    forward = [(both(p), both(p + 1), SAME) for p in range(SLICES - 1)]
     home, away, *sent = call(
         functools.partial(start_kernel, GROUPS[0][1]), "start", [result, result, coarse, eight, eight], ab, wc, dc12
     )
     for at, (slices, hosts) in enumerate(GROUPS[1:], 1):
-        z = hop(*sent, GROUPS[at - 1][1], hosts)
+        if at > 1:
+            z = hop(*sent, GROUPS[at - 1][1], hosts)
         if at == 1:
-            z = list(lax.optimization_barrier(tuple(z)))
-            b0 = moved(after(b2, z[0]), *forward)
+            zo, zm = lax.optimization_barrier(
+                (moved(sent[1], (both(0), hosts, OUTER)), moved(sent[0], (both(0), hosts, SAME)))
+            )
+            zi = moved(call(inner_kernel, "inner", eight, zm), (hosts, hosts, INNER))
+            z = [zm, zo, zi]
         elif at == 2:
             *z, b0 = lax.optimization_barrier((*z, b0))
+            late = moved(after(b2, z[0]), forward[0])
         elif at == 3:
-            *z, home, away = lax.optimization_barrier((*z, home, away))
+            *z, late, home, away = lax.optimization_barrier((*z, late, home, away))
         else:
-            other, one = moved(away, *back), moved(home, *first)
-            *z, other, one, home = lax.optimization_barrier((*z, other, one, home))
+            other = moved(away, *back)
+            *z, other, home = lax.optimization_barrier((*z, other, home))
         if len(slices) == 2:
             depth = 4 * len(GROUPS[at + 1][0])
             *sent, za, zb, zc = call(
@@ -654,7 +663,7 @@
         out_kernel,
         "out",
         field(3, SPECIES, ROWS),
-        *(species_map[:, 0], nodes, b0, b1, b2, share, *z, ab, wc, dc12, home, one, other),
+        *(species_map[:, 0], nodes, b0, late, b1, b2, share, *z, ab, wc, dc12, home, other),
         out_specs=ANY,
         scratch=[result, field(ROWS + 4, CP), field(ROWS + 8, CP), field(3, CP, ROWS), field(3, SPECIES, ROWS), pltpu.SemaphoreType.DMA((3,))],
     )

time: 120 us -> 136 us (1.13)
  the two profiles are of different devices: /device:TPU:51 before, /device:TPU:68 now
where the time goes in v6:
time: 136 us
  waiting for transfers between devices  82.5 us (61%)
  starting transfers between devices  31.9 us (23%)
  Pallas kernels  17.4 us (13%)
  local copies, waits for them, and re-layouts  1.74 us (1%)
  other arithmetic  1.5 us (1%)
    ppermute x23, waiting for transfers between devices, moved(): return lax.ppermute(value, AXES, pairs)  82.5 us
    ppermute x23, starting transfers between devices, moved(): return lax.ppermute(value, AXES, pairs)  31.9 us
    pallas_call x17, Pallas kernels, call(): pl.pallas_call(kernel, out_shape=outs, in_specs=specs, **{'out_specs': ou...  17.4 us
  transfers between devices with their start and end apart: 23, of which 5 were waited for; matrix products, arithmetic and copies ran while one was open for 0% of the time, Pallas kernels for 9%

profile of v6, /device:TPU:68, one launch (start us, length us, event | category | flops | bytes accessed | tf_op | source)
XLA Modules:
  0.0 135.6 jit_solution(12296009246183850134)
XLA Ops:
  0.0 0.7 convert_bitcast_fusion
  0.7 0.8 pad_add_fusion.raw
  1.5 0.2 prep.1
  1.7 0.0 copy-start
  1.8 1.7 %copy-done = f32[1,3,53,16,256]{4,3,2,1,0:T(8,128)S(1)} copy-done((f32[1,3,53,16,256]{4,3,2,1,0:T(8,128)S(1)}, f32[1,3,53,16,256]{4,3,2,1,0:T(8,128)}, u32[]{:S(2)}) %copy-start) | copy-done | bytes 2605080
  3.5 0.4 first.1
  3.9 2.1 %collective-permute-start = (f32[3,2,56,256]{3,2,1,0:T(8,128)S(1)}, f32[3,2,56,256]{3,2,1,0:T(8,128)S(1)}, u32[]{:S(2)}, u32[]{:S(2)}) collective-permute-start(f32[3,2,56,256]{3,2,1,0:T(8,128)S(1)} %get-tuple-element.89), channel_id=1, source_target_pairs={{1,2},{3,4},{5,6},{7,8},{9,10},{11,12},{13,14},{2,1},{4,3},{6,5},{... | collective-permute-start | bytes 1032200 | tf_op jit(solution)/shard_map/ppermute | solution.py:527
  5.9 1.7 %collective-permute-start.1 = (f32[3,2,56,256]{3,2,1,0:T(8,128)S(1)}, f32[3,2,56,256]{3,2,1,0:T(8,128)S(1)}, u32[]{:S(2)}, u32[]{:S(2)}) collective-permute-start(f32[3,2,56,256]{3,2,1,0:T(8,128)S(1)} %get-tuple-element.90), channel_id=1, source_target_pairs={{0,1},{1,0},{2,3},{3,2},{4,5},{5,4},{6,7},{7,6},{8,9},{9,8},{10,11... | collective-permute-start | bytes 1032200 | tf_op jit(solution)/shard_map/ppermute | solution.py:527
  7.6 6.3 %old.1 = (f32[16,56,256]{2,1,0:T(8,128)S(1)}, f32[16,56,256]{2,1,0:T(8,128)S(1)}, f32[16,24,256]{2,1,0:T(8,128)S(1)}, f32[16,24,256]{2,1,0:T(8,128)S(1)}, f32[16,24,256]{2,1,0:T(8,128)S(1)}) custom-call(f32[3,53,16,256]{3,2,1,0:T(8,128)S(1)} %bitcast.8, bf16[112,256]{1,0:T(8,128)(2,1)S(1)} %get-tuple-element.94.wf, ...), custom_call_target="tpu_custom_call" | custom-call | tf_op jit(solution)/shard_map/old/pallas_call | solution.py:505
  14.0 0.1 collective-permute-done.uo
  14.1 0.4 old_edge.1
  14.5 4.7 %collective-permute-start.2 = (f32[2,56,256]{2,1,0:T(8,128)S(1)}, f32[2,56,256]{2,1,0:T(8,128)S(1)}, u32[]{:S(2)}, u32[]{:S(2)}) collective-permute-start(f32[2,56,256]{2,1,0:T(8,128)S(1)} %get-tuple-element.100), channel_id=1, source_target_pairs={{1,2},{3,4},{5,6},{7,8},{9,10},{11,12},{13,14},{2,1},{4,3},{6,5},{... | collective-permute-start | bytes 344072 | tf_op jit(solution)/shard_map/ppermute | solution.py:527
  19.2 2.6 %collective-permute-start.3 = (f32[2,56,256]{2,1,0:T(8,128)S(1)}, f32[2,56,256]{2,1,0:T(8,128)S(1)}, u32[]{:S(2)}, u32[]{:S(2)}) collective-permute-start(f32[2,56,256]{2,1,0:T(8,128)S(1)} %get-tuple-element.101), channel_id=1, source_target_pairs={{0,1},{1,0},{2,3},{3,2},{4,5},{5,4},{6,7},{7,6},{8,9},{9,8},{10,11... | collective-permute-start | bytes 344072 | tf_op jit(solution)/shard_map/ppermute | solution.py:527
  21.8 3.7 %mid.1 = (f32[16,56,256]{2,1,0:T(8,128)S(1)}, f32[16,24,256]{2,1,0:T(8,128)S(1)}, f32[16,24,256]{2,1,0:T(8,128)S(1)}, f32[16,24,256]{2,1,0:T(8,128)S(1)}) custom-call(f32[16,56,256]{2,1,0:T(8,128)S(1)} %get-tuple-element.105.n1, f32[16,56,256]{2,1,0:T(8,128)S(1)} %get-tuple-element.106.s, bf16[240,256]{1,0:T(8,128)(2,1)S(1)} %get-tuple-element.107.wfr, ...), custom_call_target="tpu_custom_call" | custom-call | tf_op jit(solution)/shard_map/mid/pallas_call | solution.py:505
  25.5 0.0 collective-permute-done.2.no
  25.5 1.0 mid_edge.1
  26.5 1.9 %collective-permute-start.4 = (f32[12,24,256]{2,1,0:T(8,128)S(1)}, f32[12,24,256]{2,1,0:T(8,128)S(1)}, u32[]{:S(2)}, u32[]{:S(2)}) collective-permute-start(f32[12,24,256]{2,1,0:T(8,128)S(1)} %get-tuple-element.111.mo), channel_id=1, source_target_pairs={{1,2},{3,4},{5,6},{7,8},{9,10},{11,12},{13,14},{2,1},{4,3},{6,5},{... | collective-permute-start | bytes 884744 | tf_op jit(solution)/shard_map/ppermute | solution.py:527
  28.5 3.3 %collective-permute-start.5 = (f32[12,24,256]{2,1,0:T(8,128)S(1)}, f32[12,24,256]{2,1,0:T(8,128)S(1)}, u32[]{:S(2)}, u32[]{:S(2)}) collective-permute-start(f32[12,24,256]{2,1,0:T(8,128)S(1)} %get-tuple-element.112.mi), channel_id=1, source_target_pairs={{0,1},{1,0},{2,3},{3,2},{4,5},{5,4},{6,7},{7,6},{8,9},{9,8},{10,11... | collective-permute-start | bytes 884744 | tf_op jit(solution)/shard_map/ppermute | solution.py:527
  31.7 1.5 %base.1 = (f32[53,16,256]{2,1,0:T(8,128)S(1)}, f32[53,16,256]{2,1,0:T(8,128)S(1)}) custom-call(f32[16,56,256]{2,1,0:T(8,128)S(1)} %get-tuple-element.105.n1, f32[16,56,256]{2,1,0:T(8,128)S(1)} %get-tuple-element.115.n2, f32[16,24,256]{2,1,0:T(8,128)S(1)} %get-tuple-element.116.c1, f32[16,24,256]{2,1,0:T(8,128)S(1)} %get-tuple-element.117.c2, ...), custom_call_target="tpu_custom_call" | custom-call | tf_op jit(solution)/shard_map/base/pallas_call | solution.py:505
  33.2 2.9 %collective-permute-done.4.ho = f32[12,24,256]{2,1,0:T(8,128)S(1)} collective-permute-done((f32[12,24,256]{2,1,0:T(8,128)S(1)}, f32[12,24,256]{2,1,0:T(8,128)S(1)}, u32[]{:S(2)}, u32[]{:S(2)}) %collective-permute-start.4) | collective-permute-done | bytes 294944 | tf_op jit(solution)/shard_map/ppermute | solution.py:527
  36.1 0.0 collective-permute-done.5.hi
  36.1 0.2 last_edge.1
  36.3 0.7 collective-permute-start.10
  37.0 2.1 %collective-permute-start.9 = (f32[36,24,256]{2,1,0:T(8,128)S(1)}, f32[36,24,256]{2,1,0:T(8,128)S(1)}, u32[]{:S(2)}, u32[]{:S(2)}) collective-permute-start(f32[36,24,256]{2,1,0:T(8,128)S(1)} %get-tuple-element.121.ab), channel_id=1, source_target_pairs={{32,16},{34,18},{36,20},{38,22},{40,24},{42,26},{44,28},{46,30},{3... | collective-permute-start | bytes 2654216 | tf_op jit(solution)/shard_map/ppermute | solution.py:527
  39.1 0.7 start.1
  39.8 0.7 collective-permute-start.7
  40.5 2.8 %collective-permute-start.14 = (f32[53,16,256]{2,1,0:T(8,128)S(1)}, f32[53,16,256]{2,1,0:T(8,128)S(1)}, u32[]{:S(2)}, u32[]{:S(2)}) collective-permute-start(f32[53,16,256]{2,1,0:T(8,128)S(1)} %get-tuple-element.139.b2), channel_id=1, source_target_pairs={{16,32},{17,33},{18,34},{19,35},{20,36},{21,37},{22,38},{23,39},{2... | collective-permute-start | bytes 2605064 | tf_op jit(solution)/shard_map/ppermute | solution.py:527
  43.2 0.7 collective-permute-start.6
  43.9 0.0 collective-permute-done.7.z.z0
  44.0 0.7 collective-permute-start.8
  44.6 0.0 collective-permute-done.8.zi
  44.7 10.6 %collective-permute-done.9.short = f32[36,24,256]{2,1,0:T(8,128)S(1)} collective-permute-done((f32[36,24,256]{2,1,0:T(8,128)S(1)}, f32[36,24,256]{2,1,0:T(8,128)S(1)}, u32[]{:S(2)}, u32[]{:S(2)}) %collective-permute-start.9) | collective-permute-done | bytes 884768 | tf_op jit(solution)/shard_map/ppermute | solution.py:527
  55.3 0.7 collective-permute-start.11
  56.0 0.7 collective-permute-start.12
  56.7 0.7 collective-permute-start.13
  57.4 3.7 %collective-permute-done.14.b0 = f32[53,16,256]{2,1,0:T(8,128)S(1)} collective-permute-done((f32[53,16,256]{2,1,0:T(8,128)S(1)}, f32[53,16,256]{2,1,0:T(8,128)S(1)}, u32[]{:S(2)}, u32[]{:S(2)}) %collective-permute-start.14) | collective-permute-done | bytes 868384 | tf_op jit(solution)/shard_map/ppermute | solution.py:527
  61.1 0.7 collective-permute-start.18
  61.8 0.2 pair.4
  62.0 0.7 collective-permute-start.15
  62.7 0.7 collective-permute-start.16
  63.4 0.7 collective-permute-start.17
  64.2 0.0 copy-start.2
  64.3 1.3 collective-permute-start.22
  65.6 0.7 collective-permute-start.19
  66.3 0.7 collective-permute-start.20
  66.9 0.7 collective-permute-start.21
  67.6 65.1 %collective-permute-done.22.other = f32[48,24,256]{2,1,0:T(8,128)S(1)} collective-permute-done((f32[48,24,256]{2,1,0:T(8,128)S(1)}, f32[48,24,256]{2,1,0:T(8,128)S(1)}, u32[]{:S(2)}, u32[]{:S(2)}) %collective-permute-start.22) | collective-permute-done | bytes 1179680 | tf_op jit(solution)/shard_map/ppermute | solution.py:527
  132.8 2.6 %out.1 = f32[3,53,16,256]{3,2,1,0:T(8,128)} custom-call(s32[53]{0:T(128)S(1)} %bitcast.10, f32[3,53,16,256]{3,2,1,0:T(8,128)S(1)} %bitcast.9, f32[53,16,256]{2,1,0:T(8,128)S(1)} %collective-permute-done.14.b0, f32[53,16,256]{2,1,0:T(8,128)S(1)} %collective-permute-done.18.late, f32[53,16,256]{2,1,0:T(8,128)S(1)} %get-tuple-element.120.b1, ...), custom_call_target="tpu_custom_call" | custom-call | tf_op jit(solution)/shard_map/out/pallas_call | solution.py:505
  (23 shorter events, 0.2 us)
Async XLA Ops:
  1.7 1.7 %copy-start = (f32[1,3,53,16,256]{4,3,2,1,0:T(8,128)S(1)}, f32[1,3,53,16,256]{4,3,2,1,0:T(8,128)}, u32[]{:S(2)}) copy-start(f32[1,3,53,16,256]{4,3,2,1,0:T(8,128)} %param.8) | copy-start | bytes 7815172
  3.5 4.2 %copy-start.1 = (f32[1,3,53,16,256]{4,3,2,1,0:T(8,128)S(1)}, f32[1,3,53,16,256]{4,3,2,1,0:T(8,128)}, u32[]{:S(2)}) copy-start(f32[1,3,53,16,256]{4,3,2,1,0:T(8,128)} %param.8) | copy-start | bytes 7815172
  3.9 10.2 %collective-permute-start = (f32[3,2,56,256]{3,2,1,0:T(8,128)S(1)}, f32[3,2,56,256]{3,2,1,0:T(8,128)S(1)}, u32[]{:S(2)}, u32[]{:S(2)}) collective-permute-start(f32[3,2,56,256]{3,2,1,0:T(8,128)S(1)} %get-tuple-element.89), channel_id=1, source_target_pairs={{1,2},{3,4},{5,6},{7,8},{9,10},{11,12},{13,14},{2,1},{4,3},{6,5},{... | collective-permute-start | bytes 1032200 | tf_op jit(solution)/shard_map/ppermute | solution.py:527
  5.9 8.1 %collective-permute-start.1 = (f32[3,2,56,256]{3,2,1,0:T(8,128)S(1)}, f32[3,2,56,256]{3,2,1,0:T(8,128)S(1)}, u32[]{:S(2)}, u32[]{:S(2)}) collective-permute-start(f32[3,2,56,256]{3,2,1,0:T(8,128)S(1)} %get-tuple-element.90), channel_id=1, source_target_pairs={{0,1},{1,0},{2,3},{3,2},{4,5},{5,4},{6,7},{7,6},{8,9},{9,8},{10,11... | collective-permute-start | bytes 1032200 | tf_op jit(solution)/shard_map/ppermute | solution.py:527
  14.5 11.0 %collective-permute-start.2 = (f32[2,56,256]{2,1,0:T(8,128)S(1)}, f32[2,56,256]{2,1,0:T(8,128)S(1)}, u32[]{:S(2)}, u32[]{:S(2)}) collective-permute-start(f32[2,56,256]{2,1,0:T(8,128)S(1)} %get-tuple-element.100), channel_id=1, source_target_pairs={{1,2},{3,4},{5,6},{7,8},{9,10},{11,12},{13,14},{2,1},{4,3},{6,5},{... | collective-permute-start | bytes 344072 | tf_op jit(solution)/shard_map/ppermute | solution.py:527
  19.2 6.3 %collective-permute-start.3 = (f32[2,56,256]{2,1,0:T(8,128)S(1)}, f32[2,56,256]{2,1,0:T(8,128)S(1)}, u32[]{:S(2)}, u32[]{:S(2)}) collective-permute-start(f32[2,56,256]{2,1,0:T(8,128)S(1)} %get-tuple-element.101), channel_id=1, source_target_pairs={{0,1},{1,0},{2,3},{3,2},{4,5},{5,4},{6,7},{7,6},{8,9},{9,8},{10,11... | collective-permute-start | bytes 344072 | tf_op jit(solution)/shard_map/ppermute | solution.py:527
  26.5 9.5 %collective-permute-start.4 = (f32[12,24,256]{2,1,0:T(8,128)S(1)}, f32[12,24,256]{2,1,0:T(8,128)S(1)}, u32[]{:S(2)}, u32[]{:S(2)}) collective-permute-start(f32[12,24,256]{2,1,0:T(8,128)S(1)} %get-tuple-element.111.mo), channel_id=1, source_target_pairs={{1,2},{3,4},{5,6},{7,8},{9,10},{11,12},{13,14},{2,1},{4,3},{6,5},{... | collective-permute-start | bytes 884744 | tf_op jit(solution)/shard_map/ppermute | solution.py:527
  28.5 7.6 %collective-permute-start.5 = (f32[12,24,256]{2,1,0:T(8,128)S(1)}, f32[12,24,256]{2,1,0:T(8,128)S(1)}, u32[]{:S(2)}, u32[]{:S(2)}) collective-permute-start(f32[12,24,256]{2,1,0:T(8,128)S(1)} %get-tuple-element.112.mi), channel_id=1, source_target_pairs={{0,1},{1,0},{2,3},{3,2},{4,5},{5,4},{6,7},{7,6},{8,9},{9,8},{10,11... | collective-permute-start | bytes 884744 | tf_op jit(solution)/shard_map/ppermute | solution.py:527
  36.3 19.0 %collective-permute-start.10 = (f32[52,24,256]{2,1,0:T(8,128)S(1)}, f32[52,24,256]{2,1,0:T(8,128)S(1)}, u32[]{:S(2)}, u32[]{:S(2)}) collective-permute-start(f32[52,24,256]{2,1,0:T(8,128)S(1)} %get-tuple-element.127.mine), channel_id=1, source_target_pairs={{49,65},{51,67},{53,69},{55,71},{57,73},{59,75},{61,77},{63,79},{8... | collective-permute-start | bytes 3833864 | tf_op jit(solution)/shard_map/ppermute | solution.py:527
  37.0 18.3 %collective-permute-start.9 = (f32[36,24,256]{2,1,0:T(8,128)S(1)}, f32[36,24,256]{2,1,0:T(8,128)S(1)}, u32[]{:S(2)}, u32[]{:S(2)}) collective-permute-start(f32[36,24,256]{2,1,0:T(8,128)S(1)} %get-tuple-element.121.ab), channel_id=1, source_target_pairs={{32,16},{34,18},{36,20},{38,22},{40,24},{42,26},{44,28},{46,30},{3... | collective-permute-start | bytes 2654216 | tf_op jit(solution)/shard_map/ppermute | solution.py:527
  39.8 4.1 %collective-permute-start.7 = (f32[16,24,256]{2,1,0:T(8,128)S(1)}, f32[16,24,256]{2,1,0:T(8,128)S(1)}, u32[]{:S(2)}, u32[]{:S(2)}) collective-permute-start(f32[16,24,256]{2,1,0:T(8,128)S(1)} %get-tuple-element.123), channel_id=1, source_target_pairs={{0,16},{1,17},{2,18},{3,19},{4,20},{5,21},{6,22},{7,23},{8,24},{9,... | collective-permute-start | bytes 1179656 | tf_op jit(solution)/shard_map/ppermute | solution.py:527
  40.5 20.6 %collective-permute-start.14 = (f32[53,16,256]{2,1,0:T(8,128)S(1)}, f32[53,16,256]{2,1,0:T(8,128)S(1)}, u32[]{:S(2)}, u32[]{:S(2)}) collective-permute-start(f32[53,16,256]{2,1,0:T(8,128)S(1)} %get-tuple-element.139.b2), channel_id=1, source_target_pairs={{16,32},{17,33},{18,34},{19,35},{20,36},{21,37},{22,38},{23,39},{2... | collective-permute-start | bytes 2605064 | tf_op jit(solution)/shard_map/ppermute | solution.py:527
  43.2 0.7 collective-permute-start.6
  44.0 0.7 collective-permute-start.8
  55.3 5.8 %collective-permute-start.11 = (f32[16,24,256]{2,1,0:T(8,128)S(1)}, f32[16,24,256]{2,1,0:T(8,128)S(1)}, u32[]{:S(2)}, u32[]{:S(2)}) collective-permute-start(f32[16,24,256]{2,1,0:T(8,128)S(1)} %get-tuple-element.128.z2), channel_id=1, source_target_pairs={{16,48},{17,65},{18,50},{19,67},{20,52},{21,69},{22,54},{23,71},{2... | collective-permute-start | bytes 1179656 | tf_op jit(solution)/shard_map/ppermute | solution.py:527
  56.0 5.1 %collective-permute-start.12 = (f32[8,24,256]{2,1,0:T(8,128)S(1)}, f32[8,24,256]{2,1,0:T(8,128)S(1)}, u32[]{:S(2)}, u32[]{:S(2)}) collective-permute-start(f32[8,24,256]{2,1,0:T(8,128)S(1)} %get-tuple-element.129), channel_id=1, source_target_pairs={{17,50},{19,52},{21,54},{23,56},{25,58},{27,60},{29,62},{18,65},{2... | collective-permute-start | bytes 589832 | tf_op jit(solution)/shard_map/ppermute | solution.py:527
  56.7 4.4 %collective-permute-start.13 = (f32[8,24,256]{2,1,0:T(8,128)S(1)}, f32[8,24,256]{2,1,0:T(8,128)S(1)}, u32[]{:S(2)}, u32[]{:S(2)}) collective-permute-start(f32[8,24,256]{2,1,0:T(8,128)S(1)} %get-tuple-element.130), channel_id=1, source_target_pairs={{16,65},{17,48},{18,67},{19,50},{20,69},{21,52},{22,71},{23,54},{2... | collective-permute-start | bytes 589832 | tf_op jit(solution)/shard_map/ppermute | solution.py:527
  61.1 3.1 %collective-permute-start.18 = (f32[53,16,256]{2,1,0:T(8,128)S(1)}, f32[53,16,256]{2,1,0:T(8,128)S(1)}, u32[]{:S(2)}, u32[]{:S(2)}) collective-permute-start(f32[53,16,256]{2,1,0:T(8,128)S(1)} %get-tuple-element.139.b2), channel_id=1, source_target_pairs={{0,16},{1,17},{2,18},{3,19},{4,20},{5,21},{6,22},{7,23},{8,24},{9,... | collective-permute-start | bytes 2605064 | tf_op jit(solution)/shard_map/ppermute | solution.py:527
  62.0 2.1 %collective-permute-start.15 = (f32[16,24,256]{2,1,0:T(8,128)S(1)}, f32[16,24,256]{2,1,0:T(8,128)S(1)}, u32[]{:S(2)}, u32[]{:S(2)}) collective-permute-start(f32[16,24,256]{2,1,0:T(8,128)S(1)} %get-tuple-element.136.z2), channel_id=1, source_target_pairs={{48,80},{65,97},{50,82},{67,99},{52,84},{69,101},{54,86},{71,103},... | collective-permute-start | bytes 1179656 | tf_op jit(solution)/shard_map/ppermute | solution.py:527
  62.7 1.4 %collective-permute-start.16 = (f32[8,24,256]{2,1,0:T(8,128)S(1)}, f32[8,24,256]{2,1,0:T(8,128)S(1)}, u32[]{:S(2)}, u32[]{:S(2)}) collective-permute-start(f32[8,24,256]{2,1,0:T(8,128)S(1)} %get-tuple-element.137), channel_id=1, source_target_pairs={{65,82},{67,84},{69,86},{71,88},{73,90},{75,92},{77,94},{50,97},{5... | collective-permute-start | bytes 589832 | tf_op jit(solution)/shard_map/ppermute | solution.py:527
  63.4 0.8 collective-permute-start.17
  64.2 68.6 %copy-start.2 = (s32[53,1]{0,1:T(1,128)S(1)}, s32[53,1]{0,1:T(1,128)}, u32[]{:S(2)}) copy-start(s32[53,1]{0,1:T(1,128)} %param.15) | copy-start | bytes 640
  64.3 68.5 %collective-permute-start.22 = (f32[48,24,256]{2,1,0:T(8,128)S(1)}, f32[48,24,256]{2,1,0:T(8,128)S(1)}, u32[]{:S(2)}, u32[]{:S(2)}) collective-permute-start(f32[48,24,256]{2,1,0:T(8,128)S(1)} %get-tuple-element.164), channel_id=1, source_target_pairs={{16,32},{18,34},{20,36},{22,38},{24,40},{26,42},{28,44},{30,46},{1... | collective-permute-start | bytes 3538952 | tf_op jit(solution)/shard_map/ppermute | solution.py:527
  65.6 2.1 %collective-permute-start.19 = (f32[16,24,256]{2,1,0:T(8,128)S(1)}, f32[16,24,256]{2,1,0:T(8,128)S(1)}, u32[]{:S(2)}, u32[]{:S(2)}) collective-permute-start(f32[16,24,256]{2,1,0:T(8,128)S(1)} %get-tuple-element.156.z2), channel_id=1, source_target_pairs={{80,112},{97,113},{82,114},{99,115},{84,116},{101,117},{86,118},{1... | collective-permute-start | bytes 1179656 | tf_op jit(solution)/shard_map/ppermute | solution.py:527
  66.3 1.4 collective-permute-start.20
  66.9 0.7 collective-permute-start.21

commit v7 on v5

--- a/solution.py
+++ b/solution.py
@@ -422,7 +422,7 @@
 
 
 def out_kernel(
-    where, u, b0, b1, b2, share, z0, zo, zi, ab, wc, dc12, home, one, other, out, z, za, zs, spread, node, sem
+    where, u, b0, late, b1, b2, share, z0, zo, zi, ab, wc, dc12, home, one, other, out, z, za, zs, spread, node, sem
 ):
     info = Position()
     last = info[1] == SLICES - 1
@@ -468,7 +468,7 @@
         return copy
 
     first = info[1] == 0
-    copies = [finish(0, lambda s: jnp.where(first, u[0, s], b0[s]))]
+    copies = [finish(0, lambda s: jnp.where(first, u[0, s], b0[s] + late[s]))]
 
     @pl.when(last)
     def _():
@@ -626,11 +626,13 @@
         z = hop(*sent, GROUPS[at - 1][1], hosts)
         if at == 1:
             z = list(lax.optimization_barrier(tuple(z)))
-            b0 = moved(after(b2, z[0]), *forward)
+            b0 = moved(after(b2, z[0]), forward[2], forward[6])
+            *z, short, long = lax.optimization_barrier((*z, short, long))
+            late = moved(after(b2, z[0]), *forward[:2], *forward[3:6])
         elif at == 2:
             *z, b0 = lax.optimization_barrier((*z, b0))
         elif at == 3:
-            *z, home, away = lax.optimization_barrier((*z, home, away))
+            *z, late, home, away = lax.optimization_barrier((*z, late, home, away))
         else:
             other, one = moved(away, *back), moved(home, *first)
             *z, other, one, home = lax.optimization_barrier((*z, other, one, home))
@@ -654,7 +656,7 @@
         out_kernel,
         "out",
         field(3, SPECIES, ROWS),
-        *(species_map[:, 0], nodes, b0, b1, b2, share, *z, ab, wc, dc12, home, one, other),
+        *(species_map[:, 0], nodes, b0, late, b1, b2, share, *z, ab, wc, dc12, home, one, other),
         out_specs=ANY,
         scratch=[result, field(ROWS + 4, CP), field(ROWS + 8, CP), field(3, CP, ROWS), field(3, SPECIES, ROWS), pltpu.SemaphoreType.DMA((3,))],
     )

time: 120 us -> 120 us (level)
    ppermute x23 -> x24, starting transfers between devices: 36.9 us -> 37.6 us  [moved(): return lax.ppermute(value, AXES, pairs)]
    ppermute x23 -> x24, waiting for transfers between devices: 58.1 us -> 57.6 us  [moved(): return lax.ppermute(value, AXES, pairs)]
  transfers between devices with their start and end apart: 23 -> 24, of which waited for: 8 -> 8; matrix products, arithmetic and copies ran while one was open for 0% -> 0% of each run, Pallas kernels for 13% -> 13%
where the time goes in v7:
time: 120 us; the launch traced here: 119 us
  waiting for transfers between devices  57.6 us (48%)
  starting transfers between devices  37.6 us (31%)
  Pallas kernels  20.1 us (17%)
  local copies, waits for them, and re-layouts  1.74 us (1%)
  other arithmetic  1.5 us (1%)
    ppermute x24, waiting for transfers between devices, moved(): return lax.ppermute(value, AXES, pairs)  57.6 us
    ppermute x24, starting transfers between devices, moved(): return lax.ppermute(value, AXES, pairs)  37.6 us
    pallas_call x16, Pallas kernels, call(): pl.pallas_call(kernel, out_shape=outs, in_specs=specs, **{'out_specs': ou...  20.1 us
  transfers between devices with their start and end apart: 24, of which 8 were waited for; matrix products, arithmetic and copies ran while one was open for 0% of the time, Pallas kernels for 13%

profile of v7, /device:TPU:51, one launch (start us, length us, event | category | flops | bytes accessed | tf_op | source)
XLA Modules:
  0.0 119.1 jit_solution(12446604545864279347)
XLA Ops:
  0.0 0.7 convert_bitcast_fusion
  0.7 0.8 pad_add_fusion.raw
  1.5 0.2 prep.1
  1.7 0.0 copy-start
  1.8 1.7 %copy-done = f32[1,3,53,16,256]{4,3,2,1,0:T(8,128)S(1)} copy-done((f32[1,3,53,16,256]{4,3,2,1,0:T(8,128)S(1)}, f32[1,3,53,16,256]{4,3,2,1,0:T(8,128)}, u32[]{:S(2)}) %copy-start) | copy-done | bytes 2605080
  3.5 0.4 first.1
  3.9 4.4 %collective-permute-start = (f32[3,2,56,256]{3,2,1,0:T(8,128)S(1)}, f32[3,2,56,256]{3,2,1,0:T(8,128)S(1)}, u32[]{:S(2)}, u32[]{:S(2)}) collective-permute-start(f32[3,2,56,256]{3,2,1,0:T(8,128)S(1)} %get-tuple-element.98), channel_id=1, source_target_pairs={{1,2},{3,4},{5,6},{7,8},{9,10},{11,12},{13,14},{2,1},{4,3},{6,5},{... | collective-permute-start | bytes 1032200 | tf_op jit(solution)/shard_map/ppermute | solution.py:522
  8.3 0.1 collective-permute-start.1
  8.4 6.3 %old.1 = (f32[16,56,256]{2,1,0:T(8,128)S(1)}, f32[16,56,256]{2,1,0:T(8,128)S(1)}, f32[16,24,256]{2,1,0:T(8,128)S(1)}, f32[16,24,256]{2,1,0:T(8,128)S(1)}, f32[16,24,256]{2,1,0:T(8,128)S(1)}) custom-call(f32[3,53,16,256]{3,2,1,0:T(8,128)S(1)} %bitcast.8, bf16[112,256]{1,0:T(8,128)(2,1)S(1)} %get-tuple-element.103.wf, ...), custom_call_target="tpu_custom_call" | custom-call | tf_op jit(solution)/shard_map/old/pallas_call | solution.py:500
  14.8 2.6 %collective-permute-done.uo = f32[3,2,56,256]{3,2,1,0:T(8,128)S(1)} collective-permute-done((f32[3,2,56,256]{3,2,1,0:T(8,128)S(1)}, f32[3,2,56,256]{3,2,1,0:T(8,128)S(1)}, u32[]{:S(2)}, u32[]{:S(2)}) %collective-permute-start) | collective-permute-done | bytes 344096 | tf_op jit(solution)/shard_map/ppermute | solution.py:522
  17.4 0.4 old_edge.1
  17.8 4.6 %collective-permute-start.2 = (f32[2,56,256]{2,1,0:T(8,128)S(1)}, f32[2,56,256]{2,1,0:T(8,128)S(1)}, u32[]{:S(2)}, u32[]{:S(2)}) collective-permute-start(f32[2,56,256]{2,1,0:T(8,128)S(1)} %get-tuple-element.109), channel_id=1, source_target_pairs={{1,2},{3,4},{5,6},{7,8},{9,10},{11,12},{13,14},{2,1},{4,3},{6,5},{... | collective-permute-start | bytes 344072 | tf_op jit(solution)/shard_map/ppermute | solution.py:522
  22.4 0.7 collective-permute-start.3
  23.1 3.7 %mid.1 = (f32[16,56,256]{2,1,0:T(8,128)S(1)}, f32[16,24,256]{2,1,0:T(8,128)S(1)}, f32[16,24,256]{2,1,0:T(8,128)S(1)}, f32[16,24,256]{2,1,0:T(8,128)S(1)}) custom-call(f32[16,56,256]{2,1,0:T(8,128)S(1)} %get-tuple-element.114.n1, f32[16,56,256]{2,1,0:T(8,128)S(1)} %get-tuple-element.115.s, bf16[240,256]{1,0:T(8,128)(2,1)S(1)} %get-tuple-element.116.wfr, ...), custom_call_target="tpu_custom_call" | custom-call | tf_op jit(solution)/shard_map/mid/pallas_call | solution.py:500
  26.8 1.0 mid_edge.1
  27.8 3.8 %collective-permute-start.4 = (f32[12,24,256]{2,1,0:T(8,128)S(1)}, f32[12,24,256]{2,1,0:T(8,128)S(1)}, u32[]{:S(2)}, u32[]{:S(2)}) collective-permute-start(f32[12,24,256]{2,1,0:T(8,128)S(1)} %get-tuple-element.120.mo), channel_id=1, source_target_pairs={{1,2},{3,4},{5,6},{7,8},{9,10},{11,12},{13,14},{2,1},{4,3},{6,5},{... | collective-permute-start | bytes 884744 | tf_op jit(solution)/shard_map/ppermute | solution.py:522
  31.7 1.4 %collective-permute-start.5 = (f32[12,24,256]{2,1,0:T(8,128)S(1)}, f32[12,24,256]{2,1,0:T(8,128)S(1)}, u32[]{:S(2)}, u32[]{:S(2)}) collective-permute-start(f32[12,24,256]{2,1,0:T(8,128)S(1)} %get-tuple-element.121.mi), channel_id=1, source_target_pairs={{0,1},{1,0},{2,3},{3,2},{4,5},{5,4},{6,7},{7,6},{8,9},{9,8},{10,11... | collective-permute-start | bytes 884744 | tf_op jit(solution)/shard_map/ppermute | solution.py:522
  33.1 1.5 %base.1 = (f32[53,16,256]{2,1,0:T(8,128)S(1)}, f32[53,16,256]{2,1,0:T(8,128)S(1)}) custom-call(f32[16,56,256]{2,1,0:T(8,128)S(1)} %get-tuple-element.114.n1, f32[16,56,256]{2,1,0:T(8,128)S(1)} %get-tuple-element.124.n2, f32[16,24,256]{2,1,0:T(8,128)S(1)} %get-tuple-element.125.c1, f32[16,24,256]{2,1,0:T(8,128)S(1)} %get-tuple-element.126.c2, ...), custom_call_target="tpu_custom_call" | custom-call | tf_op jit(solution)/shard_map/base/pallas_call | solution.py:500
  34.6 5.5 %collective-permute-done.4.ho = f32[12,24,256]{2,1,0:T(8,128)S(1)} collective-permute-done((f32[12,24,256]{2,1,0:T(8,128)S(1)}, f32[12,24,256]{2,1,0:T(8,128)S(1)}, u32[]{:S(2)}, u32[]{:S(2)}) %collective-permute-start.4) | collective-permute-done | bytes 294944 | tf_op jit(solution)/shard_map/ppermute | solution.py:522
  40.1 0.2 last_edge.1
  40.3 3.6 %collective-permute-start.10 = (f32[52,24,256]{2,1,0:T(8,128)S(1)}, f32[52,24,256]{2,1,0:T(8,128)S(1)}, u32[]{:S(2)}, u32[]{:S(2)}) collective-permute-start(f32[52,24,256]{2,1,0:T(8,128)S(1)} %get-tuple-element.138.mine), channel_id=1, source_target_pairs={{17,81},{19,83},{21,85},{23,87},{25,89},{27,91},{29,93},{31,95},{4... | collective-permute-start | bytes 3833864 | tf_op jit(solution)/shard_map/ppermute | solution.py:522
  43.9 1.3 %collective-permute-start.9 = (f32[36,24,256]{2,1,0:T(8,128)S(1)}, f32[36,24,256]{2,1,0:T(8,128)S(1)}, u32[]{:S(2)}, u32[]{:S(2)}) collective-permute-start(f32[36,24,256]{2,1,0:T(8,128)S(1)} %get-tuple-element.130.ab), channel_id=1, source_target_pairs={{32,16},{34,18},{36,20},{38,22},{40,24},{42,26},{44,28},{46,30},{3... | collective-permute-start | bytes 2654216 | tf_op jit(solution)/shard_map/ppermute | solution.py:522
  45.2 1.3 %collective-permute-start.6 = (f32[16,24,256]{2,1,0:T(8,128)S(1)}, f32[16,24,256]{2,1,0:T(8,128)S(1)}, u32[]{:S(2)}, u32[]{:S(2)}) collective-permute-start(f32[16,24,256]{2,1,0:T(8,128)S(1)} %get-tuple-element.131), channel_id=1, source_target_pairs={{0,16},{1,81},{2,18},{3,83},{4,20},{5,85},{6,22},{7,87},{8,24},{9,... | collective-permute-start | bytes 1179656 | tf_op jit(solution)/shard_map/ppermute | solution.py:522
  46.5 1.3 %collective-permute-start.7 = (f32[8,24,256]{2,1,0:T(8,128)S(1)}, f32[8,24,256]{2,1,0:T(8,128)S(1)}, u32[]{:S(2)}, u32[]{:S(2)}) collective-permute-start(f32[8,24,256]{2,1,0:T(8,128)S(1)} %get-tuple-element.132), channel_id=1, source_target_pairs={{1,18},{3,20},{5,22},{7,24},{9,26},{11,28},{13,30},{2,81},{4,83},{... | collective-permute-start | bytes 589832 | tf_op jit(solution)/shard_map/ppermute | solution.py:522
  47.8 1.3 %collective-permute-start.8 = (f32[8,24,256]{2,1,0:T(8,128)S(1)}, f32[8,24,256]{2,1,0:T(8,128)S(1)}, u32[]{:S(2)}, u32[]{:S(2)}) collective-permute-start(f32[8,24,256]{2,1,0:T(8,128)S(1)} %get-tuple-element.133), channel_id=1, source_target_pairs={{0,81},{1,16},{2,83},{3,18},{4,85},{5,20},{6,87},{7,22},{8,89},{9,... | collective-permute-start | bytes 589832 | tf_op jit(solution)/shard_map/ppermute | solution.py:522
  49.1 7.4 %collective-permute-done.7.zo = f32[8,24,256]{2,1,0:T(8,128)S(1)} collective-permute-done((f32[8,24,256]{2,1,0:T(8,128)S(1)}, f32[8,24,256]{2,1,0:T(8,128)S(1)}, u32[]{:S(2)}, u32[]{:S(2)}) %collective-permute-start.7) | collective-permute-done | bytes 196640 | tf_op jit(solution)/shard_map/ppermute | solution.py:522
  56.5 3.7 %collective-permute-done.8.zi = f32[8,24,256]{2,1,0:T(8,128)S(1)} collective-permute-done((f32[8,24,256]{2,1,0:T(8,128)S(1)}, f32[8,24,256]{2,1,0:T(8,128)S(1)}, u32[]{:S(2)}, u32[]{:S(2)}) %collective-permute-start.8) | collective-permute-done | bytes 196640 | tf_op jit(solution)/shard_map/ppermute | solution.py:522
  60.1 0.7 collective-permute-start.14
  60.9 1.9 %collective-permute-start.18 = (f32[53,16,256]{2,1,0:T(8,128)S(1)}, f32[53,16,256]{2,1,0:T(8,128)S(1)}, u32[]{:S(2)}, u32[]{:S(2)}) collective-permute-start(f32[53,16,256]{2,1,0:T(8,128)S(1)} %get-tuple-element.156.b2), channel_id=1, source_target_pairs={{0,16},{1,17},{2,18},{3,19},{4,20},{5,21},{6,22},{7,23},{8,24},{9,... | collective-permute-start | bytes 2605064 | tf_op jit(solution)/shard_map/ppermute | solution.py:522
  62.8 3.4 %pair.3 = (f32[16,24,256]{2,1,0:T(8,128)S(1)}, f32[8,24,256]{2,1,0:T(8,128)S(1)}, f32[8,24,256]{2,1,0:T(8,128)S(1)}, f32[28,24,256]{2,1,0:T(8,128)S(1)}, f32[24,...) custom-call(f32[16,24,256]{2,1,0:T(8,128)S(1)} %collective-permute-done.6.z0, ...), custom_call_target="tpu_custom_call" | custom-call | tf_op jit(solution)/shard_map/pair/pallas_call | solution.py:500
  66.2 1.3 %collective-permute-start.11 = (f32[16,24,256]{2,1,0:T(8,128)S(1)}, f32[16,24,256]{2,1,0:T(8,128)S(1)}, u32[]{:S(2)}, u32[]{:S(2)}) collective-permute-start(f32[16,24,256]{2,1,0:T(8,128)S(1)} %get-tuple-element.144.z2), channel_id=1, source_target_pairs={{16,48},{81,65},{18,50},{83,67},{20,52},{85,69},{22,54},{87,71},{2... | collective-permute-start | bytes 1179656 | tf_op jit(solution)/shard_map/ppermute | solution.py:522
  67.5 1.3 %collective-permute-start.12 = (f32[8,24,256]{2,1,0:T(8,128)S(1)}, f32[8,24,256]{2,1,0:T(8,128)S(1)}, u32[]{:S(2)}, u32[]{:S(2)}) collective-permute-start(f32[8,24,256]{2,1,0:T(8,128)S(1)} %get-tuple-element.145), channel_id=1, source_target_pairs={{81,50},{83,52},{85,54},{87,56},{89,58},{91,60},{93,62},{18,65},{2... | collective-permute-start | bytes 589832 | tf_op jit(solution)/shard_map/ppermute | solution.py:522
  68.8 1.3 %collective-permute-start.13 = (f32[8,24,256]{2,1,0:T(8,128)S(1)}, f32[8,24,256]{2,1,0:T(8,128)S(1)}, u32[]{:S(2)}, u32[]{:S(2)}) collective-permute-start(f32[8,24,256]{2,1,0:T(8,128)S(1)} %get-tuple-element.146), channel_id=1, source_target_pairs={{16,65},{81,48},{18,67},{83,50},{20,69},{85,52},{22,71},{87,54},{2... | collective-permute-start | bytes 589832 | tf_op jit(solution)/shard_map/ppermute | solution.py:522
  70.1 1.3 %collective-permute-done.12.zo = f32[8,24,256]{2,1,0:T(8,128)S(1)} collective-permute-done((f32[8,24,256]{2,1,0:T(8,128)S(1)}, f32[8,24,256]{2,1,0:T(8,128)S(1)}, u32[]{:S(2)}, u32[]{:S(2)}) %collective-permute-start.12) | collective-permute-done | bytes 196640 | tf_op jit(solution)/shard_map/ppermute | solution.py:522
  71.5 2.5 %collective-permute-done.13.zi = f32[8,24,256]{2,1,0:T(8,128)S(1)} collective-permute-done((f32[8,24,256]{2,1,0:T(8,128)S(1)}, f32[8,24,256]{2,1,0:T(8,128)S(1)}, u32[]{:S(2)}, u32[]{:S(2)}) %collective-permute-start.13) | collective-permute-done | bytes 196640 | tf_op jit(solution)/shard_map/ppermute | solution.py:522
  74.0 2.4 %collective-permute-done.11.z0 = f32[16,24,256]{2,1,0:T(8,128)S(1)} collective-permute-done((f32[16,24,256]{2,1,0:T(8,128)S(1)}, f32[16,24,256]{2,1,0:T(8,128)S(1)}, u32[]{:S(2)}, u32[]{:S(2)}) %collective-permute-start.11) | collective-permute-done | bytes 393248 | tf_op jit(solution)/shard_map/ppermute | solution.py:522
  76.4 0.7 collective-permute-start.15
  77.1 0.7 collective-permute-start.16
  77.8 0.7 collective-permute-start.17
  78.5 0.2 gather.3
  78.8 0.0 copy-start.2
  78.8 1.9 %collective-permute-start.22 = (f32[48,24,256]{2,1,0:T(8,128)S(1)}, f32[48,24,256]{2,1,0:T(8,128)S(1)}, u32[]{:S(2)}, u32[]{:S(2)}) collective-permute-start(f32[48,24,256]{2,1,0:T(8,128)S(1)} %get-tuple-element.181), channel_id=1, source_target_pairs={{16,32},{18,34},{20,36},{22,38},{24,40},{26,42},{28,44},{30,46},{8... | collective-permute-start | bytes 3538952 | tf_op jit(solution)/shard_map/ppermute | solution.py:522
  80.7 1.4 %collective-permute-start.23 = (f32[48,24,256]{2,1,0:T(8,128)S(1)}, f32[48,24,256]{2,1,0:T(8,128)S(1)}, u32[]{:S(2)}, u32[]{:S(2)}) collective-permute-start(f32[48,24,256]{2,1,0:T(8,128)S(1)} %get-tuple-element.186.home), channel_id=1, source_target_pairs={{81,17},{83,19},{85,21},{87,23},{89,25},{91,27},{93,29},{95,31}} | collective-permute-start | bytes 3538952 | tf_op jit(solution)/shard_map/ppermute | solution.py:522
  82.1 0.7 collective-permute-start.19
  82.8 0.7 collective-permute-start.20
  83.5 0.7 collective-permute-start.21
  84.2 32.1 %collective-permute-done.22.other = f32[48,24,256]{2,1,0:T(8,128)S(1)} collective-permute-done((f32[48,24,256]{2,1,0:T(8,128)S(1)}, f32[48,24,256]{2,1,0:T(8,128)S(1)}, u32[]{:S(2)}, u32[]{:S(2)}) %collective-permute-start.22) | collective-permute-done | bytes 1179680 | tf_op jit(solution)/shard_map/ppermute | solution.py:522
  116.3 2.6 %out.1 = f32[3,53,16,256]{3,2,1,0:T(8,128)} custom-call(s32[53]{0:T(128)S(1)} %bitcast.10, f32[3,53,16,256]{3,2,1,0:T(8,128)S(1)} %bitcast.9, f32[53,16,256]{2,1,0:T(8,128)S(1)} %collective-permute-done.14.b0, f32[53,16,256]{2,1,0:T(8,128)S(1)} %collective-permute-done.18.late, f32[53,16,256]{2,1,0:T(8,128)S(1)} %get-tuple-element.129.b1, ...), custom_call_target="tpu_custom_call" | custom-call | tf_op jit(solution)/shard_map/out/pallas_call | solution.py:500
  (24 shorter events, 0.2 us)
Async XLA Ops:
  1.7 1.7 %copy-start = (f32[1,3,53,16,256]{4,3,2,1,0:T(8,128)S(1)}, f32[1,3,53,16,256]{4,3,2,1,0:T(8,128)}, u32[]{:S(2)}) copy-start(f32[1,3,53,16,256]{4,3,2,1,0:T(8,128)} %param.8) | copy-start | bytes 7815172
  3.5 5.0 %copy-start.1 = (f32[1,3,53,16,256]{4,3,2,1,0:T(8,128)S(1)}, f32[1,3,53,16,256]{4,3,2,1,0:T(8,128)}, u32[]{:S(2)}) copy-start(f32[1,3,53,16,256]{4,3,2,1,0:T(8,128)} %param.8) | copy-start | bytes 7815172
  3.9 13.5 %collective-permute-start = (f32[3,2,56,256]{3,2,1,0:T(8,128)S(1)}, f32[3,2,56,256]{3,2,1,0:T(8,128)S(1)}, u32[]{:S(2)}, u32[]{:S(2)}) collective-permute-start(f32[3,2,56,256]{3,2,1,0:T(8,128)S(1)} %get-tuple-element.98), channel_id=1, source_target_pairs={{1,2},{3,4},{5,6},{7,8},{9,10},{11,12},{13,14},{2,1},{4,3},{6,5},{... | collective-permute-start | bytes 1032200 | tf_op jit(solution)/shard_map/ppermute | solution.py:522
  8.3 9.1 %collective-permute-start.1 = (f32[3,2,56,256]{3,2,1,0:T(8,128)S(1)}, f32[3,2,56,256]{3,2,1,0:T(8,128)S(1)}, u32[]{:S(2)}, u32[]{:S(2)}) collective-permute-start(f32[3,2,56,256]{3,2,1,0:T(8,128)S(1)} %get-tuple-element.99), channel_id=1, source_target_pairs={{0,1},{1,0},{2,3},{3,2},{4,5},{5,4},{6,7},{7,6},{8,9},{9,8},{10,11... | collective-permute-start | bytes 1032200 | tf_op jit(solution)/shard_map/ppermute | solution.py:522
  17.8 9.0 %collective-permute-start.2 = (f32[2,56,256]{2,1,0:T(8,128)S(1)}, f32[2,56,256]{2,1,0:T(8,128)S(1)}, u32[]{:S(2)}, u32[]{:S(2)}) collective-permute-start(f32[2,56,256]{2,1,0:T(8,128)S(1)} %get-tuple-element.109), channel_id=1, source_target_pairs={{1,2},{3,4},{5,6},{7,8},{9,10},{11,12},{13,14},{2,1},{4,3},{6,5},{... | collective-permute-start | bytes 344072 | tf_op jit(solution)/shard_map/ppermute | solution.py:522
  22.4 4.4 %collective-permute-start.3 = (f32[2,56,256]{2,1,0:T(8,128)S(1)}, f32[2,56,256]{2,1,0:T(8,128)S(1)}, u32[]{:S(2)}, u32[]{:S(2)}) collective-permute-start(f32[2,56,256]{2,1,0:T(8,128)S(1)} %get-tuple-element.110), channel_id=1, source_target_pairs={{0,1},{1,0},{2,3},{3,2},{4,5},{5,4},{6,7},{7,6},{8,9},{9,8},{10,11... | collective-permute-start | bytes 344072 | tf_op jit(solution)/shard_map/ppermute | solution.py:522
  27.8 12.3 %collective-permute-start.4 = (f32[12,24,256]{2,1,0:T(8,128)S(1)}, f32[12,24,256]{2,1,0:T(8,128)S(1)}, u32[]{:S(2)}, u32[]{:S(2)}) collective-permute-start(f32[12,24,256]{2,1,0:T(8,128)S(1)} %get-tuple-element.120.mo), channel_id=1, source_target_pairs={{1,2},{3,4},{5,6},{7,8},{9,10},{11,12},{13,14},{2,1},{4,3},{6,5},{... | collective-permute-start | bytes 884744 | tf_op jit(solution)/shard_map/ppermute | solution.py:522
  31.7 8.4 %collective-permute-start.5 = (f32[12,24,256]{2,1,0:T(8,128)S(1)}, f32[12,24,256]{2,1,0:T(8,128)S(1)}, u32[]{:S(2)}, u32[]{:S(2)}) collective-permute-start(f32[12,24,256]{2,1,0:T(8,128)S(1)} %get-tuple-element.121.mi), channel_id=1, source_target_pairs={{0,1},{1,0},{2,3},{3,2},{4,5},{5,4},{6,7},{7,6},{8,9},{9,8},{10,11... | collective-permute-start | bytes 884744 | tf_op jit(solution)/shard_map/ppermute | solution.py:522
  40.3 20.6 %collective-permute-start.10 = (f32[52,24,256]{2,1,0:T(8,128)S(1)}, f32[52,24,256]{2,1,0:T(8,128)S(1)}, u32[]{:S(2)}, u32[]{:S(2)}) collective-permute-start(f32[52,24,256]{2,1,0:T(8,128)S(1)} %get-tuple-element.138.mine), channel_id=1, source_target_pairs={{17,81},{19,83},{21,85},{23,87},{25,89},{27,91},{29,93},{31,95},{4... | collective-permute-start | bytes 3833864 | tf_op jit(solution)/shard_map/ppermute | solution.py:522
  43.9 17.0 %collective-permute-start.9 = (f32[36,24,256]{2,1,0:T(8,128)S(1)}, f32[36,24,256]{2,1,0:T(8,128)S(1)}, u32[]{:S(2)}, u32[]{:S(2)}) collective-permute-start(f32[36,24,256]{2,1,0:T(8,128)S(1)} %get-tuple-element.130.ab), channel_id=1, source_target_pairs={{32,16},{34,18},{36,20},{38,22},{40,24},{42,26},{44,28},{46,30},{3... | collective-permute-start | bytes 2654216 | tf_op jit(solution)/shard_map/ppermute | solution.py:522
  45.2 15.0 %collective-permute-start.6 = (f32[16,24,256]{2,1,0:T(8,128)S(1)}, f32[16,24,256]{2,1,0:T(8,128)S(1)}, u32[]{:S(2)}, u32[]{:S(2)}) collective-permute-start(f32[16,24,256]{2,1,0:T(8,128)S(1)} %get-tuple-element.131), channel_id=1, source_target_pairs={{0,16},{1,81},{2,18},{3,83},{4,20},{5,85},{6,22},{7,87},{8,24},{9,... | collective-permute-start | bytes 1179656 | tf_op jit(solution)/shard_map/ppermute | solution.py:522
  46.5 10.0 %collective-permute-start.7 = (f32[8,24,256]{2,1,0:T(8,128)S(1)}, f32[8,24,256]{2,1,0:T(8,128)S(1)}, u32[]{:S(2)}, u32[]{:S(2)}) collective-permute-start(f32[8,24,256]{2,1,0:T(8,128)S(1)} %get-tuple-element.132), channel_id=1, source_target_pairs={{1,18},{3,20},{5,22},{7,24},{9,26},{11,28},{13,30},{2,81},{4,83},{... | collective-permute-start | bytes 589832 | tf_op jit(solution)/shard_map/ppermute | solution.py:522
  47.8 12.4 %collective-permute-start.8 = (f32[8,24,256]{2,1,0:T(8,128)S(1)}, f32[8,24,256]{2,1,0:T(8,128)S(1)}, u32[]{:S(2)}, u32[]{:S(2)}) collective-permute-start(f32[8,24,256]{2,1,0:T(8,128)S(1)} %get-tuple-element.133), channel_id=1, source_target_pairs={{0,81},{1,16},{2,83},{3,18},{4,85},{5,20},{6,87},{7,22},{8,89},{9,... | collective-permute-start | bytes 589832 | tf_op jit(solution)/shard_map/ppermute | solution.py:522
  60.1 10.0 %collective-permute-start.14 = (f32[53,16,256]{2,1,0:T(8,128)S(1)}, f32[53,16,256]{2,1,0:T(8,128)S(1)}, u32[]{:S(2)}, u32[]{:S(2)}) collective-permute-start(f32[53,16,256]{2,1,0:T(8,128)S(1)} %get-tuple-element.156.b2), channel_id=1, source_target_pairs={{32,48},{33,49},{34,50},{35,51},{36,52},{37,53},{38,54},{39,55},{4... | collective-permute-start | bytes 2605064 | tf_op jit(solution)/shard_map/ppermute | solution.py:522
  60.9 17.8 %collective-permute-start.18 = (f32[53,16,256]{2,1,0:T(8,128)S(1)}, f32[53,16,256]{2,1,0:T(8,128)S(1)}, u32[]{:S(2)}, u32[]{:S(2)}) collective-permute-start(f32[53,16,256]{2,1,0:T(8,128)S(1)} %get-tuple-element.156.b2), channel_id=1, source_target_pairs={{0,16},{1,17},{2,18},{3,19},{4,20},{5,21},{6,22},{7,23},{8,24},{9,... | collective-permute-start | bytes 2605064 | tf_op jit(solution)/shard_map/ppermute | solution.py:522
  66.2 10.2 %collective-permute-start.11 = (f32[16,24,256]{2,1,0:T(8,128)S(1)}, f32[16,24,256]{2,1,0:T(8,128)S(1)}, u32[]{:S(2)}, u32[]{:S(2)}) collective-permute-start(f32[16,24,256]{2,1,0:T(8,128)S(1)} %get-tuple-element.144.z2), channel_id=1, source_target_pairs={{16,48},{81,65},{18,50},{83,67},{20,52},{85,69},{22,54},{87,71},{2... | collective-permute-start | bytes 1179656 | tf_op jit(solution)/shard_map/ppermute | solution.py:522
  67.5 3.9 %collective-permute-start.12 = (f32[8,24,256]{2,1,0:T(8,128)S(1)}, f32[8,24,256]{2,1,0:T(8,128)S(1)}, u32[]{:S(2)}, u32[]{:S(2)}) collective-permute-start(f32[8,24,256]{2,1,0:T(8,128)S(1)} %get-tuple-element.145), channel_id=1, source_target_pairs={{81,50},{83,52},{85,54},{87,56},{89,58},{91,60},{93,62},{18,65},{2... | collective-permute-start | bytes 589832 | tf_op jit(solution)/shard_map/ppermute | solution.py:522
  68.8 5.2 %collective-permute-start.13 = (f32[8,24,256]{2,1,0:T(8,128)S(1)}, f32[8,24,256]{2,1,0:T(8,128)S(1)}, u32[]{:S(2)}, u32[]{:S(2)}) collective-permute-start(f32[8,24,256]{2,1,0:T(8,128)S(1)} %get-tuple-element.146), channel_id=1, source_target_pairs={{16,65},{81,48},{18,67},{83,50},{20,69},{85,52},{22,71},{87,54},{2... | collective-permute-start | bytes 589832 | tf_op jit(solution)/shard_map/ppermute | solution.py:522
  76.4 2.3 %collective-permute-start.15 = (f32[16,24,256]{2,1,0:T(8,128)S(1)}, f32[16,24,256]{2,1,0:T(8,128)S(1)}, u32[]{:S(2)}, u32[]{:S(2)}) collective-permute-start(f32[16,24,256]{2,1,0:T(8,128)S(1)} %get-tuple-element.153.z2), channel_id=1, source_target_pairs={{48,80},{65,97},{50,82},{67,99},{52,84},{69,101},{54,86},{71,103},... | collective-permute-start | bytes 1179656 | tf_op jit(solution)/shard_map/ppermute | solution.py:522
  77.1 1.6 %collective-permute-start.16 = (f32[8,24,256]{2,1,0:T(8,128)S(1)}, f32[8,24,256]{2,1,0:T(8,128)S(1)}, u32[]{:S(2)}, u32[]{:S(2)}) collective-permute-start(f32[8,24,256]{2,1,0:T(8,128)S(1)} %get-tuple-element.154), channel_id=1, source_target_pairs={{65,82},{67,84},{69,86},{71,88},{73,90},{75,92},{77,94},{50,97},{5... | collective-permute-start | bytes 589832 | tf_op jit(solution)/shard_map/ppermute | solution.py:522
  77.8 0.9 collective-permute-start.17
  78.8 37.5 %copy-start.2 = (s32[53,1]{0,1:T(1,128)S(1)}, s32[53,1]{0,1:T(1,128)}, u32[]{:S(2)}) copy-start(s32[53,1]{0,1:T(1,128)} %param.15) | copy-start | bytes 640
  78.8 37.5 %collective-permute-start.22 = (f32[48,24,256]{2,1,0:T(8,128)S(1)}, f32[48,24,256]{2,1,0:T(8,128)S(1)}, u32[]{:S(2)}, u32[]{:S(2)}) collective-permute-start(f32[48,24,256]{2,1,0:T(8,128)S(1)} %get-tuple-element.181), channel_id=1, source_target_pairs={{16,32},{18,34},{20,36},{22,38},{24,40},{26,42},{28,44},{30,46},{8... | collective-permute-start | bytes 3538952 | tf_op jit(solution)/shard_map/ppermute | solution.py:522
  80.7 35.5 %collective-permute-start.23 = (f32[48,24,256]{2,1,0:T(8,128)S(1)}, f32[48,24,256]{2,1,0:T(8,128)S(1)}, u32[]{:S(2)}, u32[]{:S(2)}) collective-permute-start(f32[48,24,256]{2,1,0:T(8,128)S(1)} %get-tuple-element.186.home), channel_id=1, source_target_pairs={{81,17},{83,19},{85,21},{87,23},{89,25},{91,27},{93,29},{95,31}} | collective-permute-start | bytes 3538952 | tf_op jit(solution)/shard_map/ppermute | solution.py:522
  82.1 2.1 %collective-permute-start.19 = (f32[16,24,256]{2,1,0:T(8,128)S(1)}, f32[16,24,256]{2,1,0:T(8,128)S(1)}, u32[]{:S(2)}, u32[]{:S(2)}) collective-permute-start(f32[16,24,256]{2,1,0:T(8,128)S(1)} %get-tuple-element.173.z2), channel_id=1, source_target_pairs={{80,112},{97,113},{82,114},{99,115},{84,116},{101,117},{86,118},{1... | collective-permute-start | bytes 1179656 | tf_op jit(solution)/shard_map/ppermute | solution.py:522
  82.8 1.4 %collective-permute-start.20 = (f32[4,24,256]{2,1,0:T(8,128)S(1)}, f32[4,24,256]{2,1,0:T(8,128)S(1)}, u32[]{:S(2)}, u32[]{:S(2)}) collective-permute-start(f32[4,24,256]{2,1,0:T(8,128)S(1)} %get-tuple-element.174), channel_id=1, source_target_pairs={{97,114},{99,116},{101,118},{103,120},{105,122},{107,124},{109,126... | collective-permute-start | bytes 294920 | tf_op jit(solution)/shard_map/ppermute | solution.py:522
  83.5 0.7 collective-permute-start.21

commit v8 on v6

--- a/solution.py
+++ b/solution.py
@@ -234,7 +234,7 @@
             e1[x] = (y[:CP] + y[CP:]) + dc12[...] * lap_y(c)
             n1s[x + 2], v1s[x + 2], c1s[x + 2], c1[x] = n, v, c, c
 
-    blocks(ROWS, terms)
+    blocks(ROWS, terms, 8)
 
     def laps(xs):
         for x in xs:
@@ -242,7 +242,7 @@
             r1[x] += lap_rows(v1s, x + 2) * (1.0 / 12.0)
             e1[x] += dc12[...] * lap_rows(c1s, x + 2)
 
-    blocks(ROWS, laps)
+    blocks(ROWS, laps, 8)
 
 
 def lumped_old(first, c0, e0):
@@ -427,8 +427,11 @@
     blocks(ROWS, body)
 
 
+PIECE, PIECES = 13, 4
+
+
 def out_kernel(
-    where, u, b0, late, b1, b2, share, z0, zo, zi, ab, wc, dc12, home, other, out, z, za, zs, spread, node, sem
+    where, u, b0, late, fourth, b1, b2, share, z0, zo, zi, ab, wc, dc12, home, other, out, z, za, zs, spread, node, sem
 ):
     info = Position()
     last = info[1] == SLICES - 1
@@ -466,14 +469,25 @@
         def add(s):
             node[m, s] = base(s) + spread[m, where[s]]
 
-        blocks(SPECIES, lambda at: [add(s) for s in at], 13)
+        @pl.loop(0, PIECES)
+        def _(i):
+            for k in range(PIECE):
+                add(PIECE * i + k)
+            written(m, i).start()
+
         add(SPECIES - 1)
-        copy = pltpu.make_async_copy(node.at[m], out.at[m], sem.at[m])
-        copy.start()
-        return copy
+        rest(m).start()
+
+    def written(m, i):
+        part = pl.ds(PIECE * i, PIECE)
+        return pltpu.make_async_copy(node.at[m, part], out.at[m, part], sem.at[m, i])
+
+    def rest(m):
+        part = pl.ds(PIECE * PIECES, 1)
+        return pltpu.make_async_copy(node.at[m, part], out.at[m, part], sem.at[m, PIECES])
 
     first = info[1] == 0
-    copies = [finish(0, lambda s: jnp.where(first, u[0, s], b0[s] + late[s]))]
+    finish(0, lambda s: jnp.where(first, u[0, s], b0[s] + late[s] + fourth[s]))
 
     @pl.when(last)
     def _():
@@ -486,9 +500,15 @@
 
         blocks(ROWS, body)
 
-    copies += [finish(1, lambda s: b1[s]), finish(2, lambda s: b2[s])]
-    for copy in copies:
-        copy.wait()
+    finish(1, lambda s: b1[s])
+    finish(2, lambda s: b2[s])
+    for m in range(3):
+
+        @pl.loop(0, PIECES)
+        def _(i):
+            written(m, i).wait()
+
+        rest(m).wait()
 
 
 def field(*shape):
@@ -609,7 +629,6 @@
     abx, ab = call(last_edge_kernel, "last_edge", [extended, short], outer, inner, ho, hi, abx, alias={4: 0})
 
     forward = [(both(p), both(p + 1), SAME) for p in range(SLICES - 1)]
-    b0 = moved(b2, *forward[1:])
     ab, abx = after(ab, b1), after(abx, b1)
     result = field(3 * ROWS, CP)
     pairs = [(slices, hosts) for slices, hosts in GROUPS if len(slices) == 2]
@@ -634,12 +653,15 @@
                 (moved(sent[1], (both(0), hosts, OUTER)), moved(sent[0], (both(0), hosts, SAME)))
             )
             zi = moved(call(inner_kernel, "inner", eight, zm), (hosts, hosts, INNER))
-            z = [zm, zo, zi]
+            z = list(lax.optimization_barrier((zm, zo, zi)))
+            b0 = moved(after(b2, z[2]), forward[2], *forward[4:])
+            *z, short, long = lax.optimization_barrier((*z, short, long))
+            fourth = moved(after(b2, z[0]), forward[3])
         elif at == 2:
             *z, b0 = lax.optimization_barrier((*z, b0))
-            late = moved(after(b2, z[0]), forward[0])
+            late = moved(after(b2, z[0]), *forward[:2])
         elif at == 3:
-            *z, late, home, away = lax.optimization_barrier((*z, late, home, away))
+            *z, late, fourth, home, away = lax.optimization_barrier((*z, late, fourth, home, away))
         else:
             other = moved(away, *back)
             *z, other, home = lax.optimization_barrier((*z, other, home))
@@ -663,9 +685,9 @@
         out_kernel,
         "out",
         field(3, SPECIES, ROWS),
-        *(species_map[:, 0], nodes, b0, late, b1, b2, share, *z, ab, wc, dc12, home, other),
+        *(species_map[:, 0], nodes, b0, late, fourth, b1, b2, share, *z, ab, wc, dc12, home, other),
         out_specs=ANY,
-        scratch=[result, field(ROWS + 4, CP), field(ROWS + 8, CP), field(3, CP, ROWS), field(3, SPECIES, ROWS), pltpu.SemaphoreType.DMA((3,))],
+        scratch=[result, field(ROWS + 4, CP), field(ROWS + 8, CP), field(3, CP, ROWS), field(3, SPECIES, ROWS), pltpu.SemaphoreType.DMA((3, PIECES + 1))],
     )
     return out[None]
 

time: 136 us -> 136 us (level)
  the two profiles are of different devices: /device:TPU:68 before, /device:TPU:80 now
where the time goes in v8:
time: 136 us; the launch traced here: 135 us
  waiting for transfers between devices  81.5 us (60%)
  starting transfers between devices  32.9 us (24%)
  Pallas kernels  17 us (12%)
  local copies, waits for them, and re-layouts  1.74 us (1%)
  other arithmetic  1.5 us (1%)
    ppermute x24, waiting for transfers between devices, moved(): return lax.ppermute(value, AXES, pairs)  81.5 us
    ppermute x24, starting transfers between devices, moved(): return lax.ppermute(value, AXES, pairs)  32.9 us
    pallas_call x17, Pallas kernels, call(): pl.pallas_call(kernel, out_shape=outs, in_specs=specs, **{'out_specs': ou...  17 us
  transfers between devices with their start and end apart: 24, of which 7 were waited for; matrix products, arithmetic and copies ran while one was open for 0% of the time, Pallas kernels for 9%

profile of v8, /device:TPU:80, one launch (start us, length us, event | category | flops | bytes accessed | tf_op | source)
XLA Modules:
  0.0 135.3 jit_solution(8658455739449439565)
XLA Ops:
  0.0 0.7 convert_bitcast_fusion
  0.7 0.8 pad_add_fusion.raw
  1.5 0.2 prep.1
  1.7 0.0 copy-start
  1.8 1.7 %copy-done = f32[1,3,53,16,256]{4,3,2,1,0:T(8,128)S(1)} copy-done((f32[1,3,53,16,256]{4,3,2,1,0:T(8,128)S(1)}, f32[1,3,53,16,256]{4,3,2,1,0:T(8,128)}, u32[]{:S(2)}) %copy-start) | copy-done | bytes 2605080
  3.5 0.4 first.1
  3.9 4.4 %collective-permute-start = (f32[3,2,56,256]{3,2,1,0:T(8,128)S(1)}, f32[3,2,56,256]{3,2,1,0:T(8,128)S(1)}, u32[]{:S(2)}, u32[]{:S(2)}) collective-permute-start(f32[3,2,56,256]{3,2,1,0:T(8,128)S(1)} %get-tuple-element.100), channel_id=1, source_target_pairs={{1,2},{3,4},{5,6},{7,8},{9,10},{11,12},{13,14},{2,1},{4,3},{6,5},{... | collective-permute-start | bytes 1032200 | tf_op jit(solution)/shard_map/ppermute | solution.py:547
  8.3 0.9 collective-permute-start.1
  9.2 6.3 %old.1 = (f32[16,56,256]{2,1,0:T(8,128)S(1)}, f32[16,56,256]{2,1,0:T(8,128)S(1)}, f32[16,24,256]{2,1,0:T(8,128)S(1)}, f32[16,24,256]{2,1,0:T(8,128)S(1)}, f32[16,24,256]{2,1,0:T(8,128)S(1)}) custom-call(f32[3,53,16,256]{3,2,1,0:T(8,128)S(1)} %bitcast.8, bf16[112,256]{1,0:T(8,128)(2,1)S(1)} %get-tuple-element.105.wf, ...), custom_call_target="tpu_custom_call" | custom-call | tf_op jit(solution)/shard_map/old/pallas_call | solution.py:525
  15.5 2.3 %collective-permute-done.uo = f32[3,2,56,256]{3,2,1,0:T(8,128)S(1)} collective-permute-done((f32[3,2,56,256]{3,2,1,0:T(8,128)S(1)}, f32[3,2,56,256]{3,2,1,0:T(8,128)S(1)}, u32[]{:S(2)}, u32[]{:S(2)}) %collective-permute-start) | collective-permute-done | bytes 344096 | tf_op jit(solution)/shard_map/ppermute | solution.py:547
  17.7 0.4 old_edge.1
  18.1 5.1 %collective-permute-start.2 = (f32[2,56,256]{2,1,0:T(8,128)S(1)}, f32[2,56,256]{2,1,0:T(8,128)S(1)}, u32[]{:S(2)}, u32[]{:S(2)}) collective-permute-start(f32[2,56,256]{2,1,0:T(8,128)S(1)} %get-tuple-element.111), channel_id=1, source_target_pairs={{1,2},{3,4},{5,6},{7,8},{9,10},{11,12},{13,14},{2,1},{4,3},{6,5},{... | collective-permute-start | bytes 344072 | tf_op jit(solution)/shard_map/ppermute | solution.py:547
  23.2 0.1 collective-permute-start.3
  23.3 3.3 %mid.1 = (f32[16,56,256]{2,1,0:T(8,128)S(1)}, f32[16,24,256]{2,1,0:T(8,128)S(1)}, f32[16,24,256]{2,1,0:T(8,128)S(1)}, f32[16,24,256]{2,1,0:T(8,128)S(1)}) custom-call(f32[16,56,256]{2,1,0:T(8,128)S(1)} %get-tuple-element.116.n1, f32[16,56,256]{2,1,0:T(8,128)S(1)} %get-tuple-element.117.s, bf16[240,256]{1,0:T(8,128)(2,1)S(1)} %get-tuple-element.118.wfr, ...), custom_call_target="tpu_custom_call" | custom-call | tf_op jit(solution)/shard_map/mid/pallas_call | solution.py:525
  26.6 0.3 collective-permute-done.2.no
  26.9 1.0 mid_edge.1
  27.9 5.3 %collective-permute-start.4 = (f32[12,24,256]{2,1,0:T(8,128)S(1)}, f32[12,24,256]{2,1,0:T(8,128)S(1)}, u32[]{:S(2)}, u32[]{:S(2)}) collective-permute-start(f32[12,24,256]{2,1,0:T(8,128)S(1)} %get-tuple-element.122.mo), channel_id=1, source_target_pairs={{1,2},{3,4},{5,6},{7,8},{9,10},{11,12},{13,14},{2,1},{4,3},{6,5},{... | collective-permute-start | bytes 884744 | tf_op jit(solution)/shard_map/ppermute | solution.py:547
  33.2 0.1 collective-permute-start.5
  33.3 1.5 %base.1 = (f32[53,16,256]{2,1,0:T(8,128)S(1)}, f32[53,16,256]{2,1,0:T(8,128)S(1)}) custom-call(f32[16,56,256]{2,1,0:T(8,128)S(1)} %get-tuple-element.116.n1, f32[16,56,256]{2,1,0:T(8,128)S(1)} %get-tuple-element.126.n2, f32[16,24,256]{2,1,0:T(8,128)S(1)} %get-tuple-element.127.c1, f32[16,24,256]{2,1,0:T(8,128)S(1)} %get-tuple-element.128.c2, ...), custom_call_target="tpu_custom_call" | custom-call | tf_op jit(solution)/shard_map/base/pallas_call | solution.py:525
  34.8 6.1 %collective-permute-done.4.ho = f32[12,24,256]{2,1,0:T(8,128)S(1)} collective-permute-done((f32[12,24,256]{2,1,0:T(8,128)S(1)}, f32[12,24,256]{2,1,0:T(8,128)S(1)}, u32[]{:S(2)}, u32[]{:S(2)}) %collective-permute-start.4) | collective-permute-done | bytes 294944 | tf_op jit(solution)/shard_map/ppermute | solution.py:547
  40.9 0.2 last_edge.1
  41.1 0.7 collective-permute-start.10
  41.9 0.7 start.1
  42.6 0.7 collective-permute-start.7
  43.2 2.7 %collective-permute-start.9 = (f32[36,24,256]{2,1,0:T(8,128)S(1)}, f32[36,24,256]{2,1,0:T(8,128)S(1)}, u32[]{:S(2)}, u32[]{:S(2)}) collective-permute-start(f32[36,24,256]{2,1,0:T(8,128)S(1)} %get-tuple-element.132.ab), channel_id=1, source_target_pairs={{32,16},{34,18},{36,20},{38,22},{40,24},{42,26},{44,28},{46,30},{3... | collective-permute-start | bytes 2654216 | tf_op jit(solution)/shard_map/ppermute | solution.py:547
  45.9 0.7 collective-permute-start.6
  46.6 0.0 collective-permute-done.6.zo
  46.7 0.7 collective-permute-start.8
  47.3 2.2 %collective-permute-start.14 = (f32[53,16,256]{2,1,0:T(8,128)S(1)}, f32[53,16,256]{2,1,0:T(8,128)S(1)}, u32[]{:S(2)}, u32[]{:S(2)}) collective-permute-start(f32[53,16,256]{2,1,0:T(8,128)S(1)} %get-tuple-element.160.b2), channel_id=1, source_target_pairs={{32,48},{33,49},{34,50},{35,51},{36,52},{37,53},{38,54},{39,55},{4... | collective-permute-start | bytes 2605064 | tf_op jit(solution)/shard_map/ppermute | solution.py:547
  49.6 15.0 %collective-permute-done.9.short = f32[36,24,256]{2,1,0:T(8,128)S(1)} collective-permute-done((f32[36,24,256]{2,1,0:T(8,128)S(1)}, f32[36,24,256]{2,1,0:T(8,128)S(1)}, u32[]{:S(2)}, u32[]{:S(2)}) %collective-permute-start.9) | collective-permute-done | bytes 884768 | tf_op jit(solution)/shard_map/ppermute | solution.py:547
  64.6 0.7 collective-permute-start.11
  65.3 0.7 collective-permute-start.12
  66.0 0.7 collective-permute-start.13
  66.6 0.7 collective-permute-start.19
  67.4 0.6 collective-permute-done.14.b0
  67.9 1.3 collective-permute-start.18
  69.2 0.2 pair.4
  69.5 0.7 collective-permute-start.15
  70.2 0.7 collective-permute-start.16
  70.8 0.7 collective-permute-start.17
  71.6 0.0 collective-permute-done.17.zi
  71.6 30.9 %collective-permute-done.18.late = f32[53,16,256]{2,1,0:T(8,128)S(1)} collective-permute-done((f32[53,16,256]{2,1,0:T(8,128)S(1)}, f32[53,16,256]{2,1,0:T(8,128)S(1)}, u32[]{:S(2)}, u32[]{:S(2)}) %collective-permute-start.18) | collective-permute-done | bytes 868384 | tf_op jit(solution)/shard_map/ppermute | solution.py:547
  102.5 1.4 %collective-permute-start.23 = (f32[48,24,256]{2,1,0:T(8,128)S(1)}, f32[48,24,256]{2,1,0:T(8,128)S(1)}, u32[]{:S(2)}, u32[]{:S(2)}) collective-permute-start(f32[48,24,256]{2,1,0:T(8,128)S(1)} %get-tuple-element.186), channel_id=1, source_target_pairs={{16,32},{18,34},{20,36},{22,38},{24,40},{26,42},{28,44},{30,46},{1... | collective-permute-start | bytes 3538952 | tf_op jit(solution)/shard_map/ppermute | solution.py:547
  103.9 0.7 collective-permute-start.20
  104.6 0.7 collective-permute-start.21
  105.3 0.7 collective-permute-start.22
  106.0 26.4 %collective-permute-done.23.other = f32[48,24,256]{2,1,0:T(8,128)S(1)} collective-permute-done((f32[48,24,256]{2,1,0:T(8,128)S(1)}, f32[48,24,256]{2,1,0:T(8,128)S(1)}, u32[]{:S(2)}, u32[]{:S(2)}) %collective-permute-start.23) | collective-permute-done | bytes 1179680 | tf_op jit(solution)/shard_map/ppermute | solution.py:547
  132.4 2.7 %out.1 = f32[3,53,16,256]{3,2,1,0:T(8,128)} custom-call(s32[53]{0:T(128)S(1)} %bitcast.10, f32[3,53,16,256]{3,2,1,0:T(8,128)S(1)} %bitcast.9, f32[53,16,256]{2,1,0:T(8,128)S(1)} %collective-permute-done.14.b0, f32[53,16,256]{2,1,0:T(8,128)S(1)} %collective-permute-done.18.late, f32[53,16,256]{2,1,0:T(8,128)S(1)} %collective-permute-done.19.fourth, ...), custom_call_target="tpu_custom_call" | custom-call | tf_op jit(solution)/shard_map/out/pallas_call | solution.py:525
  (25 shorter events, 0.1 us)
Async XLA Ops:
  1.7 1.7 %copy-start = (f32[1,3,53,16,256]{4,3,2,1,0:T(8,128)S(1)}, f32[1,3,53,16,256]{4,3,2,1,0:T(8,128)}, u32[]{:S(2)}) copy-start(f32[1,3,53,16,256]{4,3,2,1,0:T(8,128)} %param.8) | copy-start | bytes 7815172
  3.5 5.7 %copy-start.1 = (f32[1,3,53,16,256]{4,3,2,1,0:T(8,128)S(1)}, f32[1,3,53,16,256]{4,3,2,1,0:T(8,128)}, u32[]{:S(2)}) copy-start(f32[1,3,53,16,256]{4,3,2,1,0:T(8,128)} %param.8) | copy-start | bytes 7815172
  3.9 13.9 %collective-permute-start = (f32[3,2,56,256]{3,2,1,0:T(8,128)S(1)}, f32[3,2,56,256]{3,2,1,0:T(8,128)S(1)}, u32[]{:S(2)}, u32[]{:S(2)}) collective-permute-start(f32[3,2,56,256]{3,2,1,0:T(8,128)S(1)} %get-tuple-element.100), channel_id=1, source_target_pairs={{1,2},{3,4},{5,6},{7,8},{9,10},{11,12},{13,14},{2,1},{4,3},{6,5},{... | collective-permute-start | bytes 1032200 | tf_op jit(solution)/shard_map/ppermute | solution.py:547
  8.3 9.5 %collective-permute-start.1 = (f32[3,2,56,256]{3,2,1,0:T(8,128)S(1)}, f32[3,2,56,256]{3,2,1,0:T(8,128)S(1)}, u32[]{:S(2)}, u32[]{:S(2)}) collective-permute-start(f32[3,2,56,256]{3,2,1,0:T(8,128)S(1)} %get-tuple-element.101), channel_id=1, source_target_pairs={{0,1},{1,0},{2,3},{3,2},{4,5},{5,4},{6,7},{7,6},{8,9},{9,8},{10,11... | collective-permute-start | bytes 1032200 | tf_op jit(solution)/shard_map/ppermute | solution.py:547
  18.1 8.7 %collective-permute-start.2 = (f32[2,56,256]{2,1,0:T(8,128)S(1)}, f32[2,56,256]{2,1,0:T(8,128)S(1)}, u32[]{:S(2)}, u32[]{:S(2)}) collective-permute-start(f32[2,56,256]{2,1,0:T(8,128)S(1)} %get-tuple-element.111), channel_id=1, source_target_pairs={{1,2},{3,4},{5,6},{7,8},{9,10},{11,12},{13,14},{2,1},{4,3},{6,5},{... | collective-permute-start | bytes 344072 | tf_op jit(solution)/shard_map/ppermute | solution.py:547
  23.2 3.7 %collective-permute-start.3 = (f32[2,56,256]{2,1,0:T(8,128)S(1)}, f32[2,56,256]{2,1,0:T(8,128)S(1)}, u32[]{:S(2)}, u32[]{:S(2)}) collective-permute-start(f32[2,56,256]{2,1,0:T(8,128)S(1)} %get-tuple-element.112), channel_id=1, source_target_pairs={{0,1},{1,0},{2,3},{3,2},{4,5},{5,4},{6,7},{7,6},{8,9},{9,8},{10,11... | collective-permute-start | bytes 344072 | tf_op jit(solution)/shard_map/ppermute | solution.py:547
  27.9 13.0 %collective-permute-start.4 = (f32[12,24,256]{2,1,0:T(8,128)S(1)}, f32[12,24,256]{2,1,0:T(8,128)S(1)}, u32[]{:S(2)}, u32[]{:S(2)}) collective-permute-start(f32[12,24,256]{2,1,0:T(8,128)S(1)} %get-tuple-element.122.mo), channel_id=1, source_target_pairs={{1,2},{3,4},{5,6},{7,8},{9,10},{11,12},{13,14},{2,1},{4,3},{6,5},{... | collective-permute-start | bytes 884744 | tf_op jit(solution)/shard_map/ppermute | solution.py:547
  33.2 7.7 %collective-permute-start.5 = (f32[12,24,256]{2,1,0:T(8,128)S(1)}, f32[12,24,256]{2,1,0:T(8,128)S(1)}, u32[]{:S(2)}, u32[]{:S(2)}) collective-permute-start(f32[12,24,256]{2,1,0:T(8,128)S(1)} %get-tuple-element.123.mi), channel_id=1, source_target_pairs={{0,1},{1,0},{2,3},{3,2},{4,5},{5,4},{6,7},{7,6},{8,9},{9,8},{10,11... | collective-permute-start | bytes 884744 | tf_op jit(solution)/shard_map/ppermute | solution.py:547
  41.1 23.5 %collective-permute-start.10 = (f32[52,24,256]{2,1,0:T(8,128)S(1)}, f32[52,24,256]{2,1,0:T(8,128)S(1)}, u32[]{:S(2)}, u32[]{:S(2)}) collective-permute-start(f32[52,24,256]{2,1,0:T(8,128)S(1)} %get-tuple-element.141.mine), channel_id=1, source_target_pairs={{49,65},{51,67},{53,69},{55,71},{57,73},{59,75},{61,77},{63,79},{8... | collective-permute-start | bytes 3833864 | tf_op jit(solution)/shard_map/ppermute | solution.py:547
  42.6 4.1 %collective-permute-start.7 = (f32[16,24,256]{2,1,0:T(8,128)S(1)}, f32[16,24,256]{2,1,0:T(8,128)S(1)}, u32[]{:S(2)}, u32[]{:S(2)}) collective-permute-start(f32[16,24,256]{2,1,0:T(8,128)S(1)} %get-tuple-element.134), channel_id=1, source_target_pairs={{0,16},{1,17},{2,18},{3,19},{4,20},{5,21},{6,22},{7,23},{8,24},{9,... | collective-permute-start | bytes 1179656 | tf_op jit(solution)/shard_map/ppermute | solution.py:547
  43.2 21.4 %collective-permute-start.9 = (f32[36,24,256]{2,1,0:T(8,128)S(1)}, f32[36,24,256]{2,1,0:T(8,128)S(1)}, u32[]{:S(2)}, u32[]{:S(2)}) collective-permute-start(f32[36,24,256]{2,1,0:T(8,128)S(1)} %get-tuple-element.132.ab), channel_id=1, source_target_pairs={{32,16},{34,18},{36,20},{38,22},{40,24},{42,26},{44,28},{46,30},{3... | collective-permute-start | bytes 2654216 | tf_op jit(solution)/shard_map/ppermute | solution.py:547
  45.9 0.7 collective-permute-start.6
  46.7 0.7 collective-permute-start.8
  47.3 20.6 %collective-permute-start.14 = (f32[53,16,256]{2,1,0:T(8,128)S(1)}, f32[53,16,256]{2,1,0:T(8,128)S(1)}, u32[]{:S(2)}, u32[]{:S(2)}) collective-permute-start(f32[53,16,256]{2,1,0:T(8,128)S(1)} %get-tuple-element.160.b2), channel_id=1, source_target_pairs={{32,48},{33,49},{34,50},{35,51},{36,52},{37,53},{38,54},{39,55},{4... | collective-permute-start | bytes 2605064 | tf_op jit(solution)/shard_map/ppermute | solution.py:547
  64.6 3.3 %collective-permute-start.11 = (f32[16,24,256]{2,1,0:T(8,128)S(1)}, f32[16,24,256]{2,1,0:T(8,128)S(1)}, u32[]{:S(2)}, u32[]{:S(2)}) collective-permute-start(f32[16,24,256]{2,1,0:T(8,128)S(1)} %get-tuple-element.147.z2), channel_id=1, source_target_pairs={{16,48},{17,65},{18,50},{19,67},{20,52},{21,69},{22,54},{23,71},{2... | collective-permute-start | bytes 1179656 | tf_op jit(solution)/shard_map/ppermute | solution.py:547
  65.3 2.7 %collective-permute-start.12 = (f32[8,24,256]{2,1,0:T(8,128)S(1)}, f32[8,24,256]{2,1,0:T(8,128)S(1)}, u32[]{:S(2)}, u32[]{:S(2)}) collective-permute-start(f32[8,24,256]{2,1,0:T(8,128)S(1)} %get-tuple-element.148), channel_id=1, source_target_pairs={{17,50},{19,52},{21,54},{23,56},{25,58},{27,60},{29,62},{18,65},{2... | collective-permute-start | bytes 589832 | tf_op jit(solution)/shard_map/ppermute | solution.py:547
  66.0 2.0 %collective-permute-start.13 = (f32[8,24,256]{2,1,0:T(8,128)S(1)}, f32[8,24,256]{2,1,0:T(8,128)S(1)}, u32[]{:S(2)}, u32[]{:S(2)}) collective-permute-start(f32[8,24,256]{2,1,0:T(8,128)S(1)} %get-tuple-element.149), channel_id=1, source_target_pairs={{16,65},{17,48},{18,67},{19,50},{20,69},{21,52},{22,71},{23,54},{2... | collective-permute-start | bytes 589832 | tf_op jit(solution)/shard_map/ppermute | solution.py:547
  66.6 5.0 %collective-permute-start.19 = (f32[53,16,256]{2,1,0:T(8,128)S(1)}, f32[53,16,256]{2,1,0:T(8,128)S(1)}, u32[]{:S(2)}, u32[]{:S(2)}) collective-permute-start(f32[53,16,256]{2,1,0:T(8,128)S(1)} %get-tuple-element.160.b2), channel_id=1, source_target_pairs={{48,64},{49,65},{50,66},{51,67},{52,68},{53,69},{54,70},{55,71},{5... | collective-permute-start | bytes 2605064 | tf_op jit(solution)/shard_map/ppermute | solution.py:547
  67.9 34.6 %collective-permute-start.18 = (f32[53,16,256]{2,1,0:T(8,128)S(1)}, f32[53,16,256]{2,1,0:T(8,128)S(1)}, u32[]{:S(2)}, u32[]{:S(2)}) collective-permute-start(f32[53,16,256]{2,1,0:T(8,128)S(1)} %get-tuple-element.160.b2), channel_id=1, source_target_pairs={{0,16},{1,17},{2,18},{3,19},{4,20},{5,21},{6,22},{7,23},{8,24},{9,... | collective-permute-start | bytes 2605064 | tf_op jit(solution)/shard_map/ppermute | solution.py:547
  69.5 2.1 %collective-permute-start.15 = (f32[16,24,256]{2,1,0:T(8,128)S(1)}, f32[16,24,256]{2,1,0:T(8,128)S(1)}, u32[]{:S(2)}, u32[]{:S(2)}) collective-permute-start(f32[16,24,256]{2,1,0:T(8,128)S(1)} %get-tuple-element.156.z2), channel_id=1, source_target_pairs={{48,80},{65,97},{50,82},{67,99},{52,84},{69,101},{54,86},{71,103},... | collective-permute-start | bytes 1179656 | tf_op jit(solution)/shard_map/ppermute | solution.py:547
  70.2 1.4 %collective-permute-start.16 = (f32[8,24,256]{2,1,0:T(8,128)S(1)}, f32[8,24,256]{2,1,0:T(8,128)S(1)}, u32[]{:S(2)}, u32[]{:S(2)}) collective-permute-start(f32[8,24,256]{2,1,0:T(8,128)S(1)} %get-tuple-element.157), channel_id=1, source_target_pairs={{65,82},{67,84},{69,86},{71,88},{73,90},{75,92},{77,94},{50,97},{5... | collective-permute-start | bytes 589832 | tf_op jit(solution)/shard_map/ppermute | solution.py:547
  70.8 0.8 collective-permute-start.17
  102.5 29.9 %copy-start.2 = (s32[53,1]{0,1:T(1,128)S(1)}, s32[53,1]{0,1:T(1,128)}, u32[]{:S(2)}) copy-start(s32[53,1]{0,1:T(1,128)} %param.15) | copy-start | bytes 640
  102.5 29.9 %collective-permute-start.23 = (f32[48,24,256]{2,1,0:T(8,128)S(1)}, f32[48,24,256]{2,1,0:T(8,128)S(1)}, u32[]{:S(2)}, u32[]{:S(2)}) collective-permute-start(f32[48,24,256]{2,1,0:T(8,128)S(1)} %get-tuple-element.186), channel_id=1, source_target_pairs={{16,32},{18,34},{20,36},{22,38},{24,40},{26,42},{28,44},{30,46},{1... | collective-permute-start | bytes 3538952 | tf_op jit(solution)/shard_map/ppermute | solution.py:547
  103.9 2.1 %collective-permute-start.20 = (f32[16,24,256]{2,1,0:T(8,128)S(1)}, f32[16,24,256]{2,1,0:T(8,128)S(1)}, u32[]{:S(2)}, u32[]{:S(2)}) collective-permute-start(f32[16,24,256]{2,1,0:T(8,128)S(1)} %get-tuple-element.178.z2), channel_id=1, source_target_pairs={{80,112},{97,113},{82,114},{99,115},{84,116},{101,117},{86,118},{1... | collective-permute-start | bytes 1179656 | tf_op jit(solution)/shard_map/ppermute | solution.py:547
  104.6 1.4 collective-permute-start.21
  105.3 0.7 collective-permute-start.22

commit v9 on v7

--- a/solution.py
+++ b/solution.py
@@ -40,8 +40,12 @@
     return jnp.dot(w, x, preferred_element_type=F32)
 
 
+def two_terms(x):
+    return jnp.concatenate([x, x - x.astype(BF16).astype(F32)], axis=0).astype(BF16)
+
+
 def stacked(x, squares):
-    return split(jnp.concatenate([x, squares, zeros(16)], axis=0))
+    return split(jnp.concatenate([x, squares], axis=0))
 
 
 def lap_y(x):
@@ -61,7 +65,7 @@
 RATES, PAIRS, CRATES, CPAIRS, DIFF, CDIFF, MAP, RAW = 0, 56, 112, 136, 160, 161, 162, 168
 
 
-def prep_kernel(raw, wf, wr, wfr, lv, wc, pro, d12, dc12, share):
+def prep_kernel(raw, wf, wr, wfr, lv, wc, ws, lapm, pro, d12, dc12, share):
     row = lax.broadcasted_iota(jnp.int32, (SP, 128), 0)
     lane = lax.broadcasted_iota(jnp.int32, (SP, 128), 1)
 
@@ -92,17 +96,28 @@
     rh, rl = halves(lumped)
     dh, dl = halves(lum * diff_row)
     ch, cl = halves(coarse)
-    f = jnp.concatenate([fh, fl], axis=0).astype(BF16)
-    r = jnp.concatenate([rh, rl, lum, dh, dl, jnp.zeros((8, 128), F32)], axis=0).astype(BF16)
-    for at in (0, 128):
-        wf[:, at : at + 128] = f
-        wr[:, at : at + 128] = r
-        wfr[: 2 * SP, at : at + 128] = f
-        wfr[2 * SP :, at : at + 128] = r
+    f = jnp.concatenate([fh, fl], axis=0)
+    r = jnp.concatenate([rh, rl, lum, dh, dl, jnp.zeros((8, 128), F32)], axis=0)
+
+    def twice(w, width):
+        w = jnp.concatenate([w, jnp.zeros_like(w)], axis=1)
+        return (w + pltpu.roll(w, width, 1))[:, : 2 * width].astype(BF16)
+
+    wf[...] = twice(f, 2 * SP)
+    wr[...] = twice(r, 2 * SP)
+    wfr[: 2 * SP, :] = twice(f, 2 * SP)
+    wfr[2 * SP :, :] = twice(r, 2 * SP)
     v = jnp.concatenate([lum, dh, dl, jnp.zeros((8, 128), F32)], axis=0)
     lv[...] = (v + pltpu.roll(v, 64, 1)).astype(BF16)
     c = jnp.concatenate([ch, cl], axis=0)
-    wc[...] = (c + pltpu.roll(c, 64, 1)).astype(BF16)
+    wc[...] = twice(c, 2 * CP)
+    linear, pairs = jnp.where(lane[: 2 * CP] < CP, c, 0.0), jnp.where(lane[: 2 * CP] < CP, 0.0, c)
+    both_terms = linear + pltpu.roll(linear, CP, 1) + pltpu.roll(pairs, CP, 1) + pltpu.roll(pairs, 2 * CP, 1)
+    ws[...] = both_terms[:, : 4 * CP].astype(BF16)
+    far = lax.broadcasted_iota(jnp.int32, (COLS, COLS), 0) - lax.broadcasted_iota(jnp.int32, (COLS, COLS), 1)
+    far = jnp.abs(far)
+    far = jnp.minimum(far, COLS - far)
+    lapm[...] = jnp.where(far == 0, -60.0, jnp.where(far == 1, 16.0, jnp.where(far == 2, -1.0, 0.0))).astype(BF16)
     lane96 = lax.broadcasted_iota(jnp.int32, (SP, 96), 1)
     pro[...] = jnp.where(map_column == lane96 % 32, 1.0, 0.0).astype(BF16)
 
@@ -234,7 +249,7 @@
             e1[x] = (y[:CP] + y[CP:]) + dc12[...] * lap_y(c)
             n1s[x + 2], v1s[x + 2], c1s[x + 2], c1[x] = n, v, c, c
 
-    blocks(ROWS, terms)
+    blocks(ROWS, terms, 8)
 
     def laps(xs):
         for x in xs:
@@ -242,7 +257,7 @@
             r1[x] += lap_rows(v1s, x + 2) * (1.0 / 12.0)
             e1[x] += dc12[...] * lap_rows(c1s, x + 2)
 
-    blocks(ROWS, laps)
+    blocks(ROWS, laps, 8)
 
 
 def lumped_old(first, c0, e0):
@@ -319,15 +334,18 @@
         short[x + B0] = done[x + XB0] if x + XB0 in done else abi[x + XB0]
 
 
-def sweep(info, z, z0, add, add0, out, out0, low, rows, wc, dc12):
+def sweep(info, z, z0, add, add0, out, out0, low, rows, ws, lapm, dc12):
     size = rows // 2
 
     def body(xs):
         zr = [z[xs[0] + (low + z0 + k)] for k in range(-2, size + 2)]
+        terms = [two_terms(value) for value in zr[2:-2]]
+        laps = dot(jnp.concatenate(terms, axis=0), lapm[...])
         for k in range(size):
             x, value = xs[k] + low, zr[k + 2]
-            y = dot(wc[...], stacked(value, value * value))
-            lap = lap_y(value) + 16.0 * (zr[k + 1] + zr[k + 3]) - (zr[k] + zr[k + 4])
+            y = dot(ws[...], jnp.concatenate([terms[k], two_terms(value * value)], axis=0))
+            lap = laps[2 * CP * k : 2 * CP * k + CP] + laps[2 * CP * k + CP : 2 * CP * (k + 1)]
+            lap = lap + 16.0 * (zr[k + 1] + zr[k + 3]) - (zr[k] + zr[k + 4])
             value = value + HALF * ((y[:CP] + y[CP:]) + dc12[...] * lap) + add[x + add0]
             if low < 0:
                 inside = ((x >= 0) | (info[2] > 0)) & ((x < ROWS) | (info[2] < SLABS - 1))
@@ -357,12 +375,12 @@
     return info[1] == jnp.where(info[0] == 0, hosts[0], hosts[1])
 
 
-def start_kernel(hosts, ab, wc, dc12, result, unused, message, outer, inner):
+def start_kernel(hosts, ab, ws, lapm, dc12, result, unused, message, outer, inner):
     info = Position()
 
     @pl.when(hosting(info, hosts))
     def _():
-        sweep(info, ab, A0, ab, B0, message, 0, 0, ROWS, wc, dc12)
+        sweep(info, ab, A0, ab, B0, message, 0, 0, ROWS, ws, lapm, dc12)
         give(info, 8, outer, inner, lambda x: message[x])
 
         def body(xs):
@@ -373,20 +391,20 @@
 
 
 def pair_kernel(
-    slices, hosts, depth, z0, zo, zi, mine, short, long, wc, dc12, message, outer, inner, za, zb, zc, zs
+    slices, hosts, depth, z0, zo, zi, mine, short, long, ws, lapm, dc12, message, outer, inner, za, zb, zc, zs
 ):
     info = Position()
 
     def sweeps(one, two):
         begin(info, z0, zo, zi, 8, zs)
-        sweep(info, zs, 8, one, XA0, za, 6, -6, ROWS + 12, wc, dc12)
-        sweep(info, za, 6, one, XB0, zb, 4, -4, ROWS + 8, wc, dc12)
+        sweep(info, zs, 8, one, XA0, za, 6, -6, ROWS + 12, ws, lapm, dc12)
+        sweep(info, za, 6, one, XB0, zb, 4, -4, ROWS + 8, ws, lapm, dc12)
         if two is mine:
-            sweep(info, zb, 4, two, XA0, zc, 2, -2, ROWS + 4, wc, dc12)
-            sweep(info, zc, 2, two, XB0, message, 0, 0, ROWS, wc, dc12)
+            sweep(info, zb, 4, two, XA0, zc, 2, -2, ROWS + 4, ws, lapm, dc12)
+            sweep(info, zc, 2, two, XB0, message, 0, 0, ROWS, ws, lapm, dc12)
         else:
-            sweep(info, zb, 4, two, A0, zc, 2, -2, ROWS + 4, wc, dc12)
-            sweep(info, zc, 2, two, B0, message, 0, 0, ROWS, wc, dc12)
+            sweep(info, zb, 4, two, A0, zc, 2, -2, ROWS + 4, ws, lapm, dc12)
+            sweep(info, zc, 2, two, B0, message, 0, 0, ROWS, ws, lapm, dc12)
         give(info, depth, outer, inner, lambda x: message[x])
 
     for host in sorted(set(hosts)):
@@ -422,7 +440,7 @@
 
 
 def out_kernel(
-    where, u, b0, late, b1, b2, share, z0, zo, zi, ab, wc, dc12, home, one, other, out, z, za, zs, spread, node, sem
+    where, u, b0, late, b1, b2, share, z0, zo, zi, ab, ws, lapm, dc12, home, one, other, out, z, za, zs, spread, node, sem
 ):
     info = Position()
     last = info[1] == SLICES - 1
@@ -472,8 +490,8 @@
 
     @pl.when(last)
     def _():
-        sweep(info, zs, 4, ab, A0, za, 2, -2, ROWS + 4, wc, dc12)
-        sweep(info, za, 2, ab, B0, z.at[pl.ds(2 * ROWS, ROWS)], 0, 0, ROWS, wc, dc12)
+        sweep(info, zs, 4, ab, A0, za, 2, -2, ROWS + 4, ws, lapm, dc12)
+        sweep(info, za, 2, ab, B0, z.at[pl.ds(2 * ROWS, ROWS)], 0, 0, ROWS, ws, lapm, dc12)
 
         def body(xs):
             for x in xs:
@@ -561,10 +579,11 @@
             (MAP, species_map.reshape(1, SPECIES)),
         )
     )
-    wf, wr, wfr, lv, wc, pro, d12, dc12, share = call(
+    wf, wr, wfr, lv, wc, ws, lapm, pro, d12, dc12, share = call(
         prep_kernel,
         "prep",
-        [bf16(2 * SP, 256), bf16(128, 256), bf16(2 * SP + 128, 256), bf16(80, 128), bf16(2 * CP, 128), bf16(SP, 96)]
+        [bf16(2 * SP, 4 * SP), bf16(128, 4 * SP), bf16(2 * SP + 128, 4 * SP), bf16(80, 128), bf16(2 * CP, 4 * CP), bf16(2 * CP, 4 * CP)]
+        + [bf16(COLS, COLS), bf16(SP, 96)]
         + [field(SP), field(CP), field(CP)],
         raw,
     )
@@ -620,7 +639,7 @@
     short, long = moved(ab, *short), moved(abx, *long)
     forward = [(both(p), both(p + 1), SAME) for p in range(SLICES - 1)]
     home, away, *sent = call(
-        functools.partial(start_kernel, GROUPS[0][1]), "start", [result, result, coarse, eight, eight], ab, wc, dc12
+        functools.partial(start_kernel, GROUPS[0][1]), "start", [result, result, coarse, eight, eight], ab, ws, lapm, dc12
     )
     for at, (slices, hosts) in enumerate(GROUPS[1:], 1):
         z = hop(*sent, GROUPS[at - 1][1], hosts)
@@ -642,7 +661,7 @@
                 functools.partial(pair_kernel, slices, hosts, depth),
                 "pair",
                 [coarse, field(depth, CP), field(depth, CP), field(ROWS + 12, CP), field(ROWS + 8, CP), field(ROWS + 4, CP)],
-                *(*z, abx, short, long, wc, dc12),
+                *(*z, abx, short, long, ws, lapm, dc12),
                 scratch=[field(ROWS + 16, CP)],
             )
             home, away = call(
@@ -656,7 +675,7 @@
         out_kernel,
         "out",
         field(3, SPECIES, ROWS),
-        *(species_map[:, 0], nodes, b0, late, b1, b2, share, *z, ab, wc, dc12, home, one, other),
+        *(species_map[:, 0], nodes, b0, late, b1, b2, share, *z, ab, ws, lapm, dc12, home, one, other),
         out_specs=ANY,
         scratch=[result, field(ROWS + 4, CP), field(ROWS + 8, CP), field(3, CP, ROWS), field(3, SPECIES, ROWS), pltpu.SemaphoreType.DMA((3,))],
     )

time: 120 us -> 117 us (0.975)
  waiting for transfers between devices: 57.6 us -> 54.6 us
  Pallas kernels: 20.1 us -> 18.8 us
    ppermute x24, waiting for transfers between devices: 57.6 us -> 54.6 us  [moved(): return lax.ppermute(value, AXES, pairs)]
    pallas_call x16, Pallas kernels: 20.1 us -> 18.8 us  [call(): pl.pallas_call(kernel, out_shape=outs, in_specs=specs, **{'out_specs': ou...]
  transfers between devices with their start and end apart: 24 -> 24, of which waited for: 8 -> 9; matrix products, arithmetic and copies ran while one was open for 0% -> 0% of each run, Pallas kernels for 13% -> 12%
where the time goes in v9:
time: 117 us; the launch traced here: 115 us
  waiting for transfers between devices  54.6 us (47%)
  starting transfers between devices  38.2 us (33%)
  Pallas kernels  18.8 us (16%)
  local copies, waits for them, and re-layouts  1.74 us (1%)
  other arithmetic  1.5 us (1%)
    ppermute x24, waiting for transfers between devices, moved(): return lax.ppermute(value, AXES, pairs)  54.6 us
    ppermute x24, starting transfers between devices, moved(): return lax.ppermute(value, AXES, pairs)  38.2 us
    pallas_call x16, Pallas kernels, call(): pl.pallas_call(kernel, out_shape=outs, in_specs=specs, **{'out_specs': ou...  18.8 us
  transfers between devices with their start and end apart: 24, of which 9 were waited for; matrix products, arithmetic and copies ran while one was open for 0% of the time, Pallas kernels for 12%

profile of v9, /device:TPU:51, one launch (start us, length us, event | category | flops | bytes accessed | tf_op | source)
XLA Modules:
  0.0 115.4 jit_solution(13136331091954348315)
XLA Ops:
  0.0 0.7 convert_bitcast_fusion
  0.7 0.8 pad_add_fusion.raw
  1.5 0.4 prep.1
  1.9 0.0 copy-start
  1.9 1.7 %copy-done = f32[1,3,53,16,256]{4,3,2,1,0:T(8,128)S(1)} copy-done((f32[1,3,53,16,256]{4,3,2,1,0:T(8,128)S(1)}, f32[1,3,53,16,256]{4,3,2,1,0:T(8,128)}, u32[]{:S(2)}) %copy-start) | copy-done | bytes 2605080
  3.6 0.4 first.1
  4.0 4.4 %collective-permute-start = (f32[3,2,56,256]{3,2,1,0:T(8,128)S(1)}, f32[3,2,56,256]{3,2,1,0:T(8,128)S(1)}, u32[]{:S(2)}, u32[]{:S(2)}) collective-permute-start(f32[3,2,56,256]{3,2,1,0:T(8,128)S(1)} %get-tuple-element.100), channel_id=1, source_target_pairs={{1,2},{3,4},{5,6},{7,8},{9,10},{11,12},{13,14},{2,1},{4,3},{6,5},{... | collective-permute-start | bytes 1032200 | tf_op jit(solution)/shard_map/ppermute | solution.py:540
  8.5 0.1 collective-permute-start.1
  8.6 6.2 %old.1 = (f32[16,56,256]{2,1,0:T(8,128)S(1)}, f32[16,56,256]{2,1,0:T(8,128)S(1)}, f32[16,24,256]{2,1,0:T(8,128)S(1)}, f32[16,24,256]{2,1,0:T(8,128)S(1)}, f32[16,24,256]{2,1,0:T(8,128)S(1)}) custom-call(f32[3,53,16,256]{3,2,1,0:T(8,128)S(1)} %bitcast.8, bf16[112,224]{1,0:T(8,128)(2,1)S(1)} %get-tuple-element.105.wf, ...), custom_call_target="tpu_custom_call" | custom-call | tf_op jit(solution)/shard_map/old/pallas_call | solution.py:518
  14.8 2.7 %collective-permute-done.uo = f32[3,2,56,256]{3,2,1,0:T(8,128)S(1)} collective-permute-done((f32[3,2,56,256]{3,2,1,0:T(8,128)S(1)}, f32[3,2,56,256]{3,2,1,0:T(8,128)S(1)}, u32[]{:S(2)}, u32[]{:S(2)}) %collective-permute-start) | collective-permute-done | bytes 344096 | tf_op jit(solution)/shard_map/ppermute | solution.py:540
  17.6 0.4 old_edge.1
  17.9 4.6 %collective-permute-start.2 = (f32[2,56,256]{2,1,0:T(8,128)S(1)}, f32[2,56,256]{2,1,0:T(8,128)S(1)}, u32[]{:S(2)}, u32[]{:S(2)}) collective-permute-start(f32[2,56,256]{2,1,0:T(8,128)S(1)} %get-tuple-element.111), channel_id=1, source_target_pairs={{1,2},{3,4},{5,6},{7,8},{9,10},{11,12},{13,14},{2,1},{4,3},{6,5},{... | collective-permute-start | bytes 344072 | tf_op jit(solution)/shard_map/ppermute | solution.py:540
  22.5 0.7 collective-permute-start.3
  23.2 3.2 %mid.1 = (f32[16,56,256]{2,1,0:T(8,128)S(1)}, f32[16,24,256]{2,1,0:T(8,128)S(1)}, f32[16,24,256]{2,1,0:T(8,128)S(1)}, f32[16,24,256]{2,1,0:T(8,128)S(1)}) custom-call(f32[16,56,256]{2,1,0:T(8,128)S(1)} %get-tuple-element.116.n1, f32[16,56,256]{2,1,0:T(8,128)S(1)} %get-tuple-element.117.s, bf16[240,224]{1,0:T(8,128)(2,1)S(1)} %get-tuple-element.118.wfr, ...), custom_call_target="tpu_custom_call" | custom-call | tf_op jit(solution)/shard_map/mid/pallas_call | solution.py:518
  26.4 1.0 mid_edge.1
  27.5 4.2 %collective-permute-start.4 = (f32[12,24,256]{2,1,0:T(8,128)S(1)}, f32[12,24,256]{2,1,0:T(8,128)S(1)}, u32[]{:S(2)}, u32[]{:S(2)}) collective-permute-start(f32[12,24,256]{2,1,0:T(8,128)S(1)} %get-tuple-element.122.mo), channel_id=1, source_target_pairs={{1,2},{3,4},{5,6},{7,8},{9,10},{11,12},{13,14},{2,1},{4,3},{6,5},{... | collective-permute-start | bytes 884744 | tf_op jit(solution)/shard_map/ppermute | solution.py:540
  31.7 1.6 %collective-permute-start.5 = (f32[12,24,256]{2,1,0:T(8,128)S(1)}, f32[12,24,256]{2,1,0:T(8,128)S(1)}, u32[]{:S(2)}, u32[]{:S(2)}) collective-permute-start(f32[12,24,256]{2,1,0:T(8,128)S(1)} %get-tuple-element.123.mi), channel_id=1, source_target_pairs={{0,1},{1,0},{2,3},{3,2},{4,5},{5,4},{6,7},{7,6},{8,9},{9,8},{10,11... | collective-permute-start | bytes 884744 | tf_op jit(solution)/shard_map/ppermute | solution.py:540
  33.2 1.5 %base.1 = (f32[53,16,256]{2,1,0:T(8,128)S(1)}, f32[53,16,256]{2,1,0:T(8,128)S(1)}) custom-call(f32[16,56,256]{2,1,0:T(8,128)S(1)} %get-tuple-element.116.n1, f32[16,56,256]{2,1,0:T(8,128)S(1)} %get-tuple-element.126.n2, f32[16,24,256]{2,1,0:T(8,128)S(1)} %get-tuple-element.127.c1, f32[16,24,256]{2,1,0:T(8,128)S(1)} %get-tuple-element.128.c2, ...), custom_call_target="tpu_custom_call" | custom-call | tf_op jit(solution)/shard_map/base/pallas_call | solution.py:518
  34.7 4.4 %collective-permute-done.4.ho = f32[12,24,256]{2,1,0:T(8,128)S(1)} collective-permute-done((f32[12,24,256]{2,1,0:T(8,128)S(1)}, f32[12,24,256]{2,1,0:T(8,128)S(1)}, u32[]{:S(2)}, u32[]{:S(2)}) %collective-permute-start.4) | collective-permute-done | bytes 294944 | tf_op jit(solution)/shard_map/ppermute | solution.py:540
  39.2 0.2 last_edge.1
  39.3 3.5 %collective-permute-start.10 = (f32[52,24,256]{2,1,0:T(8,128)S(1)}, f32[52,24,256]{2,1,0:T(8,128)S(1)}, u32[]{:S(2)}, u32[]{:S(2)}) collective-permute-start(f32[52,24,256]{2,1,0:T(8,128)S(1)} %get-tuple-element.142.mine), channel_id=1, source_target_pairs={{17,81},{19,83},{21,85},{23,87},{25,89},{27,91},{29,93},{31,95},{4... | collective-permute-start | bytes 3833864 | tf_op jit(solution)/shard_map/ppermute | solution.py:540
  42.9 1.3 %collective-permute-start.9 = (f32[36,24,256]{2,1,0:T(8,128)S(1)}, f32[36,24,256]{2,1,0:T(8,128)S(1)}, u32[]{:S(2)}, u32[]{:S(2)}) collective-permute-start(f32[36,24,256]{2,1,0:T(8,128)S(1)} %get-tuple-element.132.ab), channel_id=1, source_target_pairs={{32,16},{34,18},{36,20},{38,22},{40,24},{42,26},{44,28},{46,30},{3... | collective-permute-start | bytes 2654216 | tf_op jit(solution)/shard_map/ppermute | solution.py:540
  44.2 1.3 %collective-permute-start.6 = (f32[16,24,256]{2,1,0:T(8,128)S(1)}, f32[16,24,256]{2,1,0:T(8,128)S(1)}, u32[]{:S(2)}, u32[]{:S(2)}) collective-permute-start(f32[16,24,256]{2,1,0:T(8,128)S(1)} %get-tuple-element.135), channel_id=1, source_target_pairs={{0,16},{1,81},{2,18},{3,83},{4,20},{5,85},{6,22},{7,87},{8,24},{9,... | collective-permute-start | bytes 1179656 | tf_op jit(solution)/shard_map/ppermute | solution.py:540
  45.5 1.3 %collective-permute-start.7 = (f32[8,24,256]{2,1,0:T(8,128)S(1)}, f32[8,24,256]{2,1,0:T(8,128)S(1)}, u32[]{:S(2)}, u32[]{:S(2)}) collective-permute-start(f32[8,24,256]{2,1,0:T(8,128)S(1)} %get-tuple-element.136), channel_id=1, source_target_pairs={{1,18},{3,20},{5,22},{7,24},{9,26},{11,28},{13,30},{2,81},{4,83},{... | collective-permute-start | bytes 589832 | tf_op jit(solution)/shard_map/ppermute | solution.py:540
  46.8 1.3 %collective-permute-start.8 = (f32[8,24,256]{2,1,0:T(8,128)S(1)}, f32[8,24,256]{2,1,0:T(8,128)S(1)}, u32[]{:S(2)}, u32[]{:S(2)}) collective-permute-start(f32[8,24,256]{2,1,0:T(8,128)S(1)} %get-tuple-element.137), channel_id=1, source_target_pairs={{0,81},{1,16},{2,83},{3,18},{4,85},{5,20},{6,87},{7,22},{8,89},{9,... | collective-permute-start | bytes 589832 | tf_op jit(solution)/shard_map/ppermute | solution.py:540
  48.1 7.4 %collective-permute-done.7.zo = f32[8,24,256]{2,1,0:T(8,128)S(1)} collective-permute-done((f32[8,24,256]{2,1,0:T(8,128)S(1)}, f32[8,24,256]{2,1,0:T(8,128)S(1)}, u32[]{:S(2)}, u32[]{:S(2)}) %collective-permute-start.7) | collective-permute-done | bytes 196640 | tf_op jit(solution)/shard_map/ppermute | solution.py:540
  55.5 3.7 %collective-permute-done.8.zi = f32[8,24,256]{2,1,0:T(8,128)S(1)} collective-permute-done((f32[8,24,256]{2,1,0:T(8,128)S(1)}, f32[8,24,256]{2,1,0:T(8,128)S(1)}, u32[]{:S(2)}, u32[]{:S(2)}) %collective-permute-start.8) | collective-permute-done | bytes 196640 | tf_op jit(solution)/shard_map/ppermute | solution.py:540
  59.2 0.7 collective-permute-start.14
  59.9 1.9 %collective-permute-start.18 = (f32[53,16,256]{2,1,0:T(8,128)S(1)}, f32[53,16,256]{2,1,0:T(8,128)S(1)}, u32[]{:S(2)}, u32[]{:S(2)}) collective-permute-start(f32[53,16,256]{2,1,0:T(8,128)S(1)} %get-tuple-element.160.b2), channel_id=1, source_target_pairs={{0,16},{1,17},{2,18},{3,19},{4,20},{5,21},{6,22},{7,23},{8,24},{9,... | collective-permute-start | bytes 2605064 | tf_op jit(solution)/shard_map/ppermute | solution.py:540
  61.8 2.6 %pair.3 = (f32[16,24,256]{2,1,0:T(8,128)S(1)}, f32[8,24,256]{2,1,0:T(8,128)S(1)}, f32[8,24,256]{2,1,0:T(8,128)S(1)}, f32[28,24,256]{2,1,0:T(8,128)S(1)}, f32[24,...) custom-call(f32[16,24,256]{2,1,0:T(8,128)S(1)} %collective-permute-done.6.z0, ...), custom_call_target="tpu_custom_call" | custom-call | tf_op jit(solution)/shard_map/pair/pallas_call | solution.py:518
  64.5 1.3 %collective-permute-start.11 = (f32[16,24,256]{2,1,0:T(8,128)S(1)}, f32[16,24,256]{2,1,0:T(8,128)S(1)}, u32[]{:S(2)}, u32[]{:S(2)}) collective-permute-start(f32[16,24,256]{2,1,0:T(8,128)S(1)} %get-tuple-element.148.z2), channel_id=1, source_target_pairs={{16,48},{81,65},{18,50},{83,67},{20,52},{85,69},{22,54},{87,71},{2... | collective-permute-start | bytes 1179656 | tf_op jit(solution)/shard_map/ppermute | solution.py:540
  65.8 1.3 %collective-permute-start.12 = (f32[8,24,256]{2,1,0:T(8,128)S(1)}, f32[8,24,256]{2,1,0:T(8,128)S(1)}, u32[]{:S(2)}, u32[]{:S(2)}) collective-permute-start(f32[8,24,256]{2,1,0:T(8,128)S(1)} %get-tuple-element.149), channel_id=1, source_target_pairs={{81,50},{83,52},{85,54},{87,56},{89,58},{91,60},{93,62},{18,65},{2... | collective-permute-start | bytes 589832 | tf_op jit(solution)/shard_map/ppermute | solution.py:540
  67.1 1.3 %collective-permute-start.13 = (f32[8,24,256]{2,1,0:T(8,128)S(1)}, f32[8,24,256]{2,1,0:T(8,128)S(1)}, u32[]{:S(2)}, u32[]{:S(2)}) collective-permute-start(f32[8,24,256]{2,1,0:T(8,128)S(1)} %get-tuple-element.150), channel_id=1, source_target_pairs={{16,65},{81,48},{18,67},{83,50},{20,69},{85,52},{22,71},{87,54},{2... | collective-permute-start | bytes 589832 | tf_op jit(solution)/shard_map/ppermute | solution.py:540
  68.4 1.3 %collective-permute-done.12.zo = f32[8,24,256]{2,1,0:T(8,128)S(1)} collective-permute-done((f32[8,24,256]{2,1,0:T(8,128)S(1)}, f32[8,24,256]{2,1,0:T(8,128)S(1)}, u32[]{:S(2)}, u32[]{:S(2)}) %collective-permute-start.12) | collective-permute-done | bytes 196640 | tf_op jit(solution)/shard_map/ppermute | solution.py:540
  69.7 1.7 %collective-permute-done.13.zi = f32[8,24,256]{2,1,0:T(8,128)S(1)} collective-permute-done((f32[8,24,256]{2,1,0:T(8,128)S(1)}, f32[8,24,256]{2,1,0:T(8,128)S(1)}, u32[]{:S(2)}, u32[]{:S(2)}) %collective-permute-start.13) | collective-permute-done | bytes 196640 | tf_op jit(solution)/shard_map/ppermute | solution.py:540
  71.4 1.2 %collective-permute-done.11.z0 = f32[16,24,256]{2,1,0:T(8,128)S(1)} collective-permute-done((f32[16,24,256]{2,1,0:T(8,128)S(1)}, f32[16,24,256]{2,1,0:T(8,128)S(1)}, u32[]{:S(2)}, u32[]{:S(2)}) %collective-permute-start.11) | collective-permute-done | bytes 393248 | tf_op jit(solution)/shard_map/ppermute | solution.py:540
  72.6 0.7 collective-permute-start.15
  73.3 0.7 collective-permute-start.16
  73.9 0.7 collective-permute-start.17
  74.6 0.2 gather.3
  74.9 1.5 %collective-permute-done.18.late = f32[53,16,256]{2,1,0:T(8,128)S(1)} collective-permute-done((f32[53,16,256]{2,1,0:T(8,128)S(1)}, f32[53,16,256]{2,1,0:T(8,128)S(1)}, u32[]{:S(2)}, u32[]{:S(2)}) %collective-permute-start.18) | collective-permute-done | bytes 868384 | tf_op jit(solution)/shard_map/ppermute | solution.py:540
  76.4 2.0 %collective-permute-start.22 = (f32[48,24,256]{2,1,0:T(8,128)S(1)}, f32[48,24,256]{2,1,0:T(8,128)S(1)}, u32[]{:S(2)}, u32[]{:S(2)}) collective-permute-start(f32[48,24,256]{2,1,0:T(8,128)S(1)} %get-tuple-element.185), channel_id=1, source_target_pairs={{16,32},{18,34},{20,36},{22,38},{24,40},{26,42},{28,44},{30,46},{8... | collective-permute-start | bytes 3538952 | tf_op jit(solution)/shard_map/ppermute | solution.py:540
  78.4 1.4 %collective-permute-start.23 = (f32[48,24,256]{2,1,0:T(8,128)S(1)}, f32[48,24,256]{2,1,0:T(8,128)S(1)}, u32[]{:S(2)}, u32[]{:S(2)}) collective-permute-start(f32[48,24,256]{2,1,0:T(8,128)S(1)} %get-tuple-element.190.home), channel_id=1, source_target_pairs={{81,17},{83,19},{85,21},{87,23},{89,25},{91,27},{93,29},{95,31}} | collective-permute-start | bytes 3538952 | tf_op jit(solution)/shard_map/ppermute | solution.py:540
  79.8 0.7 collective-permute-start.19
  80.5 0.7 collective-permute-start.20
  81.2 0.7 collective-permute-start.21
  81.9 30.7 %collective-permute-done.22.other = f32[48,24,256]{2,1,0:T(8,128)S(1)} collective-permute-done((f32[48,24,256]{2,1,0:T(8,128)S(1)}, f32[48,24,256]{2,1,0:T(8,128)S(1)}, u32[]{:S(2)}, u32[]{:S(2)}) %collective-permute-start.22) | collective-permute-done | bytes 1179680 | tf_op jit(solution)/shard_map/ppermute | solution.py:540
  112.6 2.6 %out.1 = f32[3,53,16,256]{3,2,1,0:T(8,128)} custom-call(s32[53]{0:T(128)S(1)} %bitcast.10, f32[3,53,16,256]{3,2,1,0:T(8,128)S(1)} %bitcast.9, f32[53,16,256]{2,1,0:T(8,128)S(1)} %collective-permute-done.14.b0, f32[53,16,256]{2,1,0:T(8,128)S(1)} %collective-permute-done.18.late, f32[53,16,256]{2,1,0:T(8,128)S(1)} %get-tuple-element.131.b1, ...), custom_call_target="tpu_custom_call" | custom-call | tf_op jit(solution)/shard_map/out/pallas_call | solution.py:518
  (24 shorter events, 0.1 us)
Async XLA Ops:
  1.9 1.7 %copy-start = (f32[1,3,53,16,256]{4,3,2,1,0:T(8,128)S(1)}, f32[1,3,53,16,256]{4,3,2,1,0:T(8,128)}, u32[]{:S(2)}) copy-start(f32[1,3,53,16,256]{4,3,2,1,0:T(8,128)} %param.8) | copy-start | bytes 7815172
  3.6 5.0 %copy-start.1 = (f32[1,3,53,16,256]{4,3,2,1,0:T(8,128)S(1)}, f32[1,3,53,16,256]{4,3,2,1,0:T(8,128)}, u32[]{:S(2)}) copy-start(f32[1,3,53,16,256]{4,3,2,1,0:T(8,128)} %param.8) | copy-start | bytes 7815172
  4.0 13.5 %collective-permute-start = (f32[3,2,56,256]{3,2,1,0:T(8,128)S(1)}, f32[3,2,56,256]{3,2,1,0:T(8,128)S(1)}, u32[]{:S(2)}, u32[]{:S(2)}) collective-permute-start(f32[3,2,56,256]{3,2,1,0:T(8,128)S(1)} %get-tuple-element.100), channel_id=1, source_target_pairs={{1,2},{3,4},{5,6},{7,8},{9,10},{11,12},{13,14},{2,1},{4,3},{6,5},{... | collective-permute-start | bytes 1032200 | tf_op jit(solution)/shard_map/ppermute | solution.py:540
  8.5 9.1 %collective-permute-start.1 = (f32[3,2,56,256]{3,2,1,0:T(8,128)S(1)}, f32[3,2,56,256]{3,2,1,0:T(8,128)S(1)}, u32[]{:S(2)}, u32[]{:S(2)}) collective-permute-start(f32[3,2,56,256]{3,2,1,0:T(8,128)S(1)} %get-tuple-element.101), channel_id=1, source_target_pairs={{0,1},{1,0},{2,3},{3,2},{4,5},{5,4},{6,7},{7,6},{8,9},{9,8},{10,11... | collective-permute-start | bytes 1032200 | tf_op jit(solution)/shard_map/ppermute | solution.py:540
  17.9 8.5 %collective-permute-start.2 = (f32[2,56,256]{2,1,0:T(8,128)S(1)}, f32[2,56,256]{2,1,0:T(8,128)S(1)}, u32[]{:S(2)}, u32[]{:S(2)}) collective-permute-start(f32[2,56,256]{2,1,0:T(8,128)S(1)} %get-tuple-element.111), channel_id=1, source_target_pairs={{1,2},{3,4},{5,6},{7,8},{9,10},{11,12},{13,14},{2,1},{4,3},{6,5},{... | collective-permute-start | bytes 344072 | tf_op jit(solution)/shard_map/ppermute | solution.py:540
  22.5 3.9 %collective-permute-start.3 = (f32[2,56,256]{2,1,0:T(8,128)S(1)}, f32[2,56,256]{2,1,0:T(8,128)S(1)}, u32[]{:S(2)}, u32[]{:S(2)}) collective-permute-start(f32[2,56,256]{2,1,0:T(8,128)S(1)} %get-tuple-element.112), channel_id=1, source_target_pairs={{0,1},{1,0},{2,3},{3,2},{4,5},{5,4},{6,7},{7,6},{8,9},{9,8},{10,11... | collective-permute-start | bytes 344072 | tf_op jit(solution)/shard_map/ppermute | solution.py:540
  27.5 11.7 %collective-permute-start.4 = (f32[12,24,256]{2,1,0:T(8,128)S(1)}, f32[12,24,256]{2,1,0:T(8,128)S(1)}, u32[]{:S(2)}, u32[]{:S(2)}) collective-permute-start(f32[12,24,256]{2,1,0:T(8,128)S(1)} %get-tuple-element.122.mo), channel_id=1, source_target_pairs={{1,2},{3,4},{5,6},{7,8},{9,10},{11,12},{13,14},{2,1},{4,3},{6,5},{... | collective-permute-start | bytes 884744 | tf_op jit(solution)/shard_map/ppermute | solution.py:540
  31.7 7.5 %collective-permute-start.5 = (f32[12,24,256]{2,1,0:T(8,128)S(1)}, f32[12,24,256]{2,1,0:T(8,128)S(1)}, u32[]{:S(2)}, u32[]{:S(2)}) collective-permute-start(f32[12,24,256]{2,1,0:T(8,128)S(1)} %get-tuple-element.123.mi), channel_id=1, source_target_pairs={{0,1},{1,0},{2,3},{3,2},{4,5},{5,4},{6,7},{7,6},{8,9},{9,8},{10,11... | collective-permute-start | bytes 884744 | tf_op jit(solution)/shard_map/ppermute | solution.py:540
  39.3 20.6 %collective-permute-start.10 = (f32[52,24,256]{2,1,0:T(8,128)S(1)}, f32[52,24,256]{2,1,0:T(8,128)S(1)}, u32[]{:S(2)}, u32[]{:S(2)}) collective-permute-start(f32[52,24,256]{2,1,0:T(8,128)S(1)} %get-tuple-element.142.mine), channel_id=1, source_target_pairs={{17,81},{19,83},{21,85},{23,87},{25,89},{27,91},{29,93},{31,95},{4... | collective-permute-start | bytes 3833864 | tf_op jit(solution)/shard_map/ppermute | solution.py:540
  42.9 17.0 %collective-permute-start.9 = (f32[36,24,256]{2,1,0:T(8,128)S(1)}, f32[36,24,256]{2,1,0:T(8,128)S(1)}, u32[]{:S(2)}, u32[]{:S(2)}) collective-permute-start(f32[36,24,256]{2,1,0:T(8,128)S(1)} %get-tuple-element.132.ab), channel_id=1, source_target_pairs={{32,16},{34,18},{36,20},{38,22},{40,24},{42,26},{44,28},{46,30},{3... | collective-permute-start | bytes 2654216 | tf_op jit(solution)/shard_map/ppermute | solution.py:540
  44.2 15.0 %collective-permute-start.6 = (f32[16,24,256]{2,1,0:T(8,128)S(1)}, f32[16,24,256]{2,1,0:T(8,128)S(1)}, u32[]{:S(2)}, u32[]{:S(2)}) collective-permute-start(f32[16,24,256]{2,1,0:T(8,128)S(1)} %get-tuple-element.135), channel_id=1, source_target_pairs={{0,16},{1,81},{2,18},{3,83},{4,20},{5,85},{6,22},{7,87},{8,24},{9,... | collective-permute-start | bytes 1179656 | tf_op jit(solution)/shard_map/ppermute | solution.py:540
  45.5 10.0 %collective-permute-start.7 = (f32[8,24,256]{2,1,0:T(8,128)S(1)}, f32[8,24,256]{2,1,0:T(8,128)S(1)}, u32[]{:S(2)}, u32[]{:S(2)}) collective-permute-start(f32[8,24,256]{2,1,0:T(8,128)S(1)} %get-tuple-element.136), channel_id=1, source_target_pairs={{1,18},{3,20},{5,22},{7,24},{9,26},{11,28},{13,30},{2,81},{4,83},{... | collective-permute-start | bytes 589832 | tf_op jit(solution)/shard_map/ppermute | solution.py:540
  46.8 12.4 %collective-permute-start.8 = (f32[8,24,256]{2,1,0:T(8,128)S(1)}, f32[8,24,256]{2,1,0:T(8,128)S(1)}, u32[]{:S(2)}, u32[]{:S(2)}) collective-permute-start(f32[8,24,256]{2,1,0:T(8,128)S(1)} %get-tuple-element.137), channel_id=1, source_target_pairs={{0,81},{1,16},{2,83},{3,18},{4,85},{5,20},{6,87},{7,22},{8,89},{9,... | collective-permute-start | bytes 589832 | tf_op jit(solution)/shard_map/ppermute | solution.py:540
  59.2 9.2 %collective-permute-start.14 = (f32[53,16,256]{2,1,0:T(8,128)S(1)}, f32[53,16,256]{2,1,0:T(8,128)S(1)}, u32[]{:S(2)}, u32[]{:S(2)}) collective-permute-start(f32[53,16,256]{2,1,0:T(8,128)S(1)} %get-tuple-element.160.b2), channel_id=1, source_target_pairs={{32,48},{33,49},{34,50},{35,51},{36,52},{37,53},{38,54},{39,55},{4... | collective-permute-start | bytes 2605064 | tf_op jit(solution)/shard_map/ppermute | solution.py:540
  59.9 16.5 %collective-permute-start.18 = (f32[53,16,256]{2,1,0:T(8,128)S(1)}, f32[53,16,256]{2,1,0:T(8,128)S(1)}, u32[]{:S(2)}, u32[]{:S(2)}) collective-permute-start(f32[53,16,256]{2,1,0:T(8,128)S(1)} %get-tuple-element.160.b2), channel_id=1, source_target_pairs={{0,16},{1,17},{2,18},{3,19},{4,20},{5,21},{6,22},{7,23},{8,24},{9,... | collective-permute-start | bytes 2605064 | tf_op jit(solution)/shard_map/ppermute | solution.py:540
  64.5 8.1 %collective-permute-start.11 = (f32[16,24,256]{2,1,0:T(8,128)S(1)}, f32[16,24,256]{2,1,0:T(8,128)S(1)}, u32[]{:S(2)}, u32[]{:S(2)}) collective-permute-start(f32[16,24,256]{2,1,0:T(8,128)S(1)} %get-tuple-element.148.z2), channel_id=1, source_target_pairs={{16,48},{81,65},{18,50},{83,67},{20,52},{85,69},{22,54},{87,71},{2... | collective-permute-start | bytes 1179656 | tf_op jit(solution)/shard_map/ppermute | solution.py:540
  65.8 3.9 %collective-permute-start.12 = (f32[8,24,256]{2,1,0:T(8,128)S(1)}, f32[8,24,256]{2,1,0:T(8,128)S(1)}, u32[]{:S(2)}, u32[]{:S(2)}) collective-permute-start(f32[8,24,256]{2,1,0:T(8,128)S(1)} %get-tuple-element.149), channel_id=1, source_target_pairs={{81,50},{83,52},{85,54},{87,56},{89,58},{91,60},{93,62},{18,65},{2... | collective-permute-start | bytes 589832 | tf_op jit(solution)/shard_map/ppermute | solution.py:540
  67.1 4.3 %collective-permute-start.13 = (f32[8,24,256]{2,1,0:T(8,128)S(1)}, f32[8,24,256]{2,1,0:T(8,128)S(1)}, u32[]{:S(2)}, u32[]{:S(2)}) collective-permute-start(f32[8,24,256]{2,1,0:T(8,128)S(1)} %get-tuple-element.150), channel_id=1, source_target_pairs={{16,65},{81,48},{18,67},{83,50},{20,69},{85,52},{22,71},{87,54},{2... | collective-permute-start | bytes 589832 | tf_op jit(solution)/shard_map/ppermute | solution.py:540
  72.6 2.3 %collective-permute-start.15 = (f32[16,24,256]{2,1,0:T(8,128)S(1)}, f32[16,24,256]{2,1,0:T(8,128)S(1)}, u32[]{:S(2)}, u32[]{:S(2)}) collective-permute-start(f32[16,24,256]{2,1,0:T(8,128)S(1)} %get-tuple-element.157.z2), channel_id=1, source_target_pairs={{48,80},{65,97},{50,82},{67,99},{52,84},{69,101},{54,86},{71,103},... | collective-permute-start | bytes 1179656 | tf_op jit(solution)/shard_map/ppermute | solution.py:540
  73.3 1.6 %collective-permute-start.16 = (f32[8,24,256]{2,1,0:T(8,128)S(1)}, f32[8,24,256]{2,1,0:T(8,128)S(1)}, u32[]{:S(2)}, u32[]{:S(2)}) collective-permute-start(f32[8,24,256]{2,1,0:T(8,128)S(1)} %get-tuple-element.158), channel_id=1, source_target_pairs={{65,82},{67,84},{69,86},{71,88},{73,90},{75,92},{77,94},{50,97},{5... | collective-permute-start | bytes 589832 | tf_op jit(solution)/shard_map/ppermute | solution.py:540
  73.9 0.9 collective-permute-start.17
  76.4 36.2 %copy-start.2 = (s32[53,1]{0,1:T(1,128)S(1)}, s32[53,1]{0,1:T(1,128)}, u32[]{:S(2)}) copy-start(s32[53,1]{0,1:T(1,128)} %param.15) | copy-start | bytes 640
  76.4 36.2 %collective-permute-start.22 = (f32[48,24,256]{2,1,0:T(8,128)S(1)}, f32[48,24,256]{2,1,0:T(8,128)S(1)}, u32[]{:S(2)}, u32[]{:S(2)}) collective-permute-start(f32[48,24,256]{2,1,0:T(8,128)S(1)} %get-tuple-element.185), channel_id=1, source_target_pairs={{16,32},{18,34},{20,36},{22,38},{24,40},{26,42},{28,44},{30,46},{8... | collective-permute-start | bytes 3538952 | tf_op jit(solution)/shard_map/ppermute | solution.py:540
  78.4 34.1 %collective-permute-start.23 = (f32[48,24,256]{2,1,0:T(8,128)S(1)}, f32[48,24,256]{2,1,0:T(8,128)S(1)}, u32[]{:S(2)}, u32[]{:S(2)}) collective-permute-start(f32[48,24,256]{2,1,0:T(8,128)S(1)} %get-tuple-element.190.home), channel_id=1, source_target_pairs={{81,17},{83,19},{85,21},{87,23},{89,25},{91,27},{93,29},{95,31}} | collective-permute-start | bytes 3538952 | tf_op jit(solution)/shard_map/ppermute | solution.py:540
  79.8 2.1 %collective-permute-start.19 = (f32[16,24,256]{2,1,0:T(8,128)S(1)}, f32[16,24,256]{2,1,0:T(8,128)S(1)}, u32[]{:S(2)}, u32[]{:S(2)}) collective-permute-start(f32[16,24,256]{2,1,0:T(8,128)S(1)} %get-tuple-element.177.z2), channel_id=1, source_target_pairs={{80,112},{97,113},{82,114},{99,115},{84,116},{101,117},{86,118},{1... | collective-permute-start | bytes 1179656 | tf_op jit(solution)/shard_map/ppermute | solution.py:540
  80.5 1.4 %collective-permute-start.20 = (f32[4,24,256]{2,1,0:T(8,128)S(1)}, f32[4,24,256]{2,1,0:T(8,128)S(1)}, u32[]{:S(2)}, u32[]{:S(2)}) collective-permute-start(f32[4,24,256]{2,1,0:T(8,128)S(1)} %get-tuple-element.178), channel_id=1, source_target_pairs={{97,114},{99,116},{101,118},{103,120},{105,122},{107,124},{109,126... | collective-permute-start | bytes 294920 | tf_op jit(solution)/shard_map/ppermute | solution.py:540
  81.2 0.7 collective-permute-start.21

commit v10 on v9

--- a/solution.py
+++ b/solution.py
@@ -204,6 +204,30 @@
 SIDES = (((0, 1), (1, 0)), ((ROWS - 1, ROWS - 2), (0, 1)))
 
 
+def packed_rows(rows):
+    return (COARSE * (rows - 1) + CP + 7) // 8 * 8
+
+
+def get(ref, r):
+    return ref[COARSE * r : COARSE * r + CP, :]
+
+
+def put(ref, r, value):
+    ref[COARSE * r : COARSE * r + CP, :] = value
+
+
+def pick_packed(info, side, outer, inner):
+    take = info[0] == side
+    return lambda r: jnp.where(take, get(outer, r), get(inner, r))
+
+
+def send_packed(info, outer, inner, tops, bottoms):
+    at_top = info[0] == 0
+    for r, (top, bottom) in enumerate(zip(tops, bottoms)):
+        put(outer, r, jnp.where(at_top, top, bottom))
+        put(inner, r, jnp.where(at_top, bottom, top))
+
+
 def pick_halo(info, side, outer, inner):
     take = info[0] == side
     return lambda *at: jnp.where(take, outer[at], inner[at])
@@ -304,7 +328,7 @@
     blocks(ROWS - 4, lambda xs: [pieces(x + 2, r1i[x + 2], e1i[x + 2]) for x in xs], ROWS - 4)
     top = [ab[x + XA0] for x in range(6)] + [ab[x + XB0] for x in range(4)] + [v2s[x + 2] for x in range(2)]
     bottom = [ab[x + XA0] for x in range(ROWS - 6, ROWS)] + [ab[x + XB0] for x in range(ROWS - 4, ROWS)]
-    send(info, outer, inner, top, bottom + [v2s[x] for x in range(ROWS, ROWS + 2)])
+    send_packed(info, outer, inner, top, bottom + [v2s[x] for x in range(ROWS, ROWS + 2)])
 
 
 def last_edge_kernel(mo, mi, ho, hi, abi, ab, short):
@@ -313,7 +337,7 @@
     done = {}
     for side, (rows, order) in enumerate(SIDES):
         inside = info[2] > 0 if side == 0 else info[2] < SLABS - 1
-        own, halo = pick_halo(info, side, mo, mi), pick_halo(info, side, ho, hi)
+        own, halo = pick_packed(info, side, mo, mi), pick_packed(info, side, ho, hi)
         fix = beside(*[halo(10 + r) for r in order])
         theirs = beside(*[own(10 + r) for r in order[::-1]])
         for i, x in enumerate(rows):
@@ -356,32 +380,31 @@
 
 
 def begin(info, z0, zo, zi, depth, zs):
-    top, bottom = pick_halo(info, 0, zo, zi), pick_halo(info, 1, zo, zi)
+    top, bottom = pick_packed(info, 0, zo, zi), pick_packed(info, 1, zo, zi)
     for r in range(depth):
         zs[r], zs[depth + ROWS + r] = top(r), bottom(r)
-
-    def body(xs):
-        for x in xs:
-            zs[depth + x] = z0[x]
-
-    blocks(ROWS, body)
-
-
-def give(info, depth, outer, inner, value):
-    send(info, outer, inner, [value(x) for x in range(depth)], [value(x) for x in range(ROWS - depth, ROWS)])
+    for x in range(ROWS):
+        zs[depth + x] = get(z0, x)
+
+
+def give(info, depth, message, packed, outer, inner):
+    for x in range(ROWS):
+        put(packed, x, message[x])
+    ends = [message[x] for x in range(depth)], [message[x] for x in range(ROWS - depth, ROWS)]
+    send_packed(info, outer, inner, *ends)
 
 
 def hosting(info, hosts):
     return info[1] == jnp.where(info[0] == 0, hosts[0], hosts[1])
 
 
-def start_kernel(hosts, ab, ws, lapm, dc12, result, unused, message, outer, inner):
+def start_kernel(hosts, ab, ws, lapm, dc12, result, unused, packed, outer, inner, message):
     info = Position()
 
     @pl.when(hosting(info, hosts))
     def _():
         sweep(info, ab, A0, ab, B0, message, 0, 0, ROWS, ws, lapm, dc12)
-        give(info, 8, outer, inner, lambda x: message[x])
+        give(info, 8, message, packed, outer, inner)
 
         def body(xs):
             for x in xs:
@@ -391,7 +414,7 @@
 
 
 def pair_kernel(
-    slices, hosts, depth, z0, zo, zi, mine, short, long, ws, lapm, dc12, message, outer, inner, za, zb, zc, zs
+    slices, hosts, depth, z0, zo, zi, mine, short, long, ws, lapm, dc12, packed, outer, inner, za, zb, zc, message, zs
 ):
     info = Position()
 
@@ -405,7 +428,7 @@
         else:
             sweep(info, zb, 4, two, A0, zc, 2, -2, ROWS + 4, ws, lapm, dc12)
             sweep(info, zc, 2, two, B0, message, 0, 0, ROWS, ws, lapm, dc12)
-        give(info, depth, outer, inner, lambda x: message[x])
+        give(info, depth, message, packed, outer, inner)
 
     for host in sorted(set(hosts)):
         one = mine if host == slices[0] else long
@@ -413,20 +436,23 @@
         pl.when(hosting(info, hosts) & (info[1] == host))(functools.partial(sweeps, one, two))
 
 
-def gather(z0, za, zb, zc, z2, one, two):
-    def body(xs):
-        for x in xs:
-            one[x], one[ROWS + x], one[2 * ROWS + x] = z0[x], za[x + 6], zb[x + 4]
-            two[x], two[ROWS + x], two[2 * ROWS + x] = zb[x + 4], zc[x + 2], z2[x]
-
-    blocks(ROWS, body)
-
-
-def gather_kernel(slices, hosts, z0, za, zb, zc, z2, home_in, away_in, home, away):
+def gather(zs, za, zb, zc, z2, one, two, away):
+    for at, result in ((0, one), (1, two)):
+        values = [lambda x: zs[x + 8], lambda x: za[x + 6], lambda x: zb[x + 4], lambda x: zc[x + 2], lambda x: z2[x]]
+        for part, value in enumerate(values[2 * at : 2 * at + 3]):
+            for x in range(ROWS):
+                if at == away:
+                    put(result, part * ROWS + x, value(x))
+                else:
+                    result[part * ROWS + x] = value(x)
+
+
+def gather_kernel(slices, hosts, zs, za, zb, zc, z2, home_in, away_in, home, away):
     info = Position()
     active, second = hosting(info, hosts), info[1] == slices[1]
-    pl.when(active & ~second)(lambda: gather(z0, za, zb, zc, z2, home, away))
-    pl.when(active & second)(lambda: gather(z0, za, zb, zc, z2, away, home))
+    pl.when(active & ~second)(lambda: gather(zs, za, zb, zc, z2, home, away, 1))
+    if slices[1] in hosts:
+        pl.when(active & second)(lambda: gather(zs, za, zb, zc, z2, away, home, 0))
 
 
 def base_kernel(n1, n2, c1, c2, pro, share, b1, b2):
@@ -448,7 +474,7 @@
     for slices, hosts in GROUPS[1:-1]:
         at_home = at_home | (hosting(info, hosts) & ((info[1] == slices[0]) | (info[1] == slices[1])))
     first = info[1] == GROUPS[1][0][0]
-    for here, result in ((at_home, home), (first & ~at_home, one), (~at_home & ~first & ~last, other)):
+    for here, result in ((at_home, home), (first & ~at_home, one)):
 
         @pl.when(here)
         def _():
@@ -459,13 +485,18 @@
 
             blocks(3 * ROWS, body)
 
+    @pl.when(~at_home & ~first & ~last)
+    def _():
+        for x in range(3 * ROWS):
+            z[x] = get(other, x)
+
     @pl.when(last)
     def _():
         begin(info, z0, zo, zi, 4, zs)
 
         def body(xs):
             for x in xs:
-                z[x] = z0[x]
+                z[x] = zs[x + 4]
 
         blocks(ROWS, body)
 
@@ -597,7 +628,7 @@
         *(nodes, wf, wr, wc, d12, dc12),
         scratch=[field(4, 3, SP), field(ROWS + 4, SP), field(ROWS + 4, SP), field(ROWS + 4, CP), field(ROWS + 4, CP)],
     )
-    two, twelve, eight = field(2, SP), field(12, CP), field(8, CP)
+    two, twelve = field(2, SP), field(packed_rows(12))
     n1, s, r0, e0, outer, inner = call(
         old_edge_kernel,
         "old_edge",
@@ -623,7 +654,8 @@
     abx, ab = call(last_edge_kernel, "last_edge", [extended, short], outer, inner, ho, hi, abx, alias={4: 0})
 
     ab, abx = after(ab, b1), after(abx, b1)
-    result = field(3 * ROWS, CP)
+    result, away_result = field(3 * ROWS, CP), field(packed_rows(3 * ROWS))
+    bulk, ends = field(packed_rows(ROWS)), field(packed_rows(8))
     pairs = [(slices, hosts) for slices, hosts in GROUPS if len(slices) == 2]
     short, long, back, first = [], [], [], []
     for slices, hosts in pairs:
@@ -639,7 +671,7 @@
     short, long = moved(ab, *short), moved(abx, *long)
     forward = [(both(p), both(p + 1), SAME) for p in range(SLICES - 1)]
     home, away, *sent = call(
-        functools.partial(start_kernel, GROUPS[0][1]), "start", [result, result, coarse, eight, eight], ab, ws, lapm, dc12
+        functools.partial(start_kernel, GROUPS[0][1]), "start", [result, away_result, bulk, ends, ends], ab, ws, lapm, dc12, scratch=[coarse]
     )
     for at, (slices, hosts) in enumerate(GROUPS[1:], 1):
         z = hop(*sent, GROUPS[at - 1][1], hosts)
@@ -657,18 +689,18 @@
             *z, other, one, home = lax.optimization_barrier((*z, other, one, home))
         if len(slices) == 2:
             depth = 4 * len(GROUPS[at + 1][0])
-            *sent, za, zb, zc = call(
+            ends = field(packed_rows(depth))
+            *sent, za, zb, zc, z2, zs = call(
                 functools.partial(pair_kernel, slices, hosts, depth),
                 "pair",
-                [coarse, field(depth, CP), field(depth, CP), field(ROWS + 12, CP), field(ROWS + 8, CP), field(ROWS + 4, CP)],
+                [bulk, ends, ends, field(ROWS + 12, CP), field(ROWS + 8, CP), field(ROWS + 4, CP), coarse, field(ROWS + 16, CP)],
                 *(*z, abx, short, long, ws, lapm, dc12),
-                scratch=[field(ROWS + 16, CP)],
             )
             home, away = call(
                 functools.partial(gather_kernel, slices, hosts),
                 "gather",
-                [result, result],
-                *(z[0], za, zb, zc, sent[0], home, away),
+                [result, away_result],
+                *(zs, za, zb, zc, z2, home, away),
                 alias={5: 0, 6: 1},
             )
     out = call(

time: 117 us -> 112 us (0.957)
  waiting for transfers between devices: 54.6 us -> 49.1 us
    ppermute x24, waiting for transfers between devices: 54.6 us -> 49.1 us  [moved(): return lax.ppermute(value, AXES, pairs)]
  transfers between devices with their start and end apart: 24 -> 24, of which waited for: 9 -> 9; matrix products, arithmetic and copies ran while one was open for 0% -> 0% of each run, Pallas kernels for 12% -> 13%
where the time goes in v10:
time: 112 us; the launch traced here: 111 us
  waiting for transfers between devices  49.1 us (44%)
  starting transfers between devices  39.2 us (35%)
  Pallas kernels  19 us (17%)
  local copies, waits for them, and re-layouts  1.74 us (2%)
  other arithmetic  1.5 us (1%)
    ppermute x24, waiting for transfers between devices, moved(): return lax.ppermute(value, AXES, pairs)  49.1 us
    ppermute x24, starting transfers between devices, moved(): return lax.ppermute(value, AXES, pairs)  39.2 us
    pallas_call x16, Pallas kernels, call(): pl.pallas_call(kernel, out_shape=outs, in_specs=specs, **{'out_specs': ou...  19 us
  transfers between devices with their start and end apart: 24, of which 9 were waited for; matrix products, arithmetic and copies ran while one was open for 0% of the time, Pallas kernels for 13%

profile of v10, /device:TPU:51, one launch (start us, length us, event | category | flops | bytes accessed | tf_op | source)
XLA Modules:
  0.0 111.0 jit_solution(7911087385832840464)
XLA Ops:
  0.0 0.7 convert_bitcast_fusion
  0.7 0.8 pad_add_fusion.raw
  1.5 0.4 prep.1
  1.9 0.0 copy-start
  1.9 1.7 %copy-done = f32[1,3,53,16,256]{4,3,2,1,0:T(8,128)S(1)} copy-done((f32[1,3,53,16,256]{4,3,2,1,0:T(8,128)S(1)}, f32[1,3,53,16,256]{4,3,2,1,0:T(8,128)}, u32[]{:S(2)}) %copy-start) | copy-done | bytes 2605080
  3.6 0.4 first.1
  4.0 4.4 %collective-permute-start = (f32[3,2,56,256]{3,2,1,0:T(8,128)S(1)}, f32[3,2,56,256]{3,2,1,0:T(8,128)S(1)}, u32[]{:S(2)}, u32[]{:S(2)}) collective-permute-start(f32[3,2,56,256]{3,2,1,0:T(8,128)S(1)} %get-tuple-element.106), channel_id=1, source_target_pairs={{1,2},{3,4},{5,6},{7,8},{9,10},{11,12},{13,14},{2,1},{4,3},{6,5},{... | collective-permute-start | bytes 1032200 | tf_op jit(solution)/shard_map/ppermute | solution.py:571
  8.5 0.1 collective-permute-start.1
  8.6 6.3 %old.1 = (f32[16,56,256]{2,1,0:T(8,128)S(1)}, f32[16,56,256]{2,1,0:T(8,128)S(1)}, f32[16,24,256]{2,1,0:T(8,128)S(1)}, f32[16,24,256]{2,1,0:T(8,128)S(1)}, f32[16,24,256]{2,1,0:T(8,128)S(1)}) custom-call(f32[3,53,16,256]{3,2,1,0:T(8,128)S(1)} %bitcast.8, bf16[112,224]{1,0:T(8,128)(2,1)S(1)} %get-tuple-element.111.wf, ...), custom_call_target="tpu_custom_call" | custom-call | tf_op jit(solution)/shard_map/old/pallas_call | solution.py:549
  14.9 2.7 %collective-permute-done.uo = f32[3,2,56,256]{3,2,1,0:T(8,128)S(1)} collective-permute-done((f32[3,2,56,256]{3,2,1,0:T(8,128)S(1)}, f32[3,2,56,256]{3,2,1,0:T(8,128)S(1)}, u32[]{:S(2)}, u32[]{:S(2)}) %collective-permute-start) | collective-permute-done | bytes 344096 | tf_op jit(solution)/shard_map/ppermute | solution.py:571
  17.6 0.4 old_edge.1
  17.9 4.6 %collective-permute-start.2 = (f32[2,56,256]{2,1,0:T(8,128)S(1)}, f32[2,56,256]{2,1,0:T(8,128)S(1)}, u32[]{:S(2)}, u32[]{:S(2)}) collective-permute-start(f32[2,56,256]{2,1,0:T(8,128)S(1)} %get-tuple-element.117), channel_id=1, source_target_pairs={{1,2},{3,4},{5,6},{7,8},{9,10},{11,12},{13,14},{2,1},{4,3},{6,5},{... | collective-permute-start | bytes 344072 | tf_op jit(solution)/shard_map/ppermute | solution.py:571
  22.5 0.7 collective-permute-start.3
  23.2 3.2 %mid.1 = (f32[16,56,256]{2,1,0:T(8,128)S(1)}, f32[16,24,256]{2,1,0:T(8,128)S(1)}, f32[16,24,256]{2,1,0:T(8,128)S(1)}, f32[16,24,256]{2,1,0:T(8,128)S(1)}) custom-call(f32[16,56,256]{2,1,0:T(8,128)S(1)} %get-tuple-element.122.n1, f32[16,56,256]{2,1,0:T(8,128)S(1)} %get-tuple-element.123.s, bf16[240,224]{1,0:T(8,128)(2,1)S(1)} %get-tuple-element.124.wfr, ...), custom_call_target="tpu_custom_call" | custom-call | tf_op jit(solution)/shard_map/mid/pallas_call | solution.py:549
  26.5 1.1 mid_edge.1
  27.5 4.2 %collective-permute-start.4 = (f32[256,256]{1,0:T(8,128)S(1)}, f32[256,256]{1,0:T(8,128)S(1)}, u32[]{:S(2)}, u32[]{:S(2)}) collective-permute-start(f32[256,256]{1,0:T(8,128)S(1)} %get-tuple-element.128.mo), channel_id=1, source_target_pairs={{1,2},{3,4},{5,6},{7,8},{9,10},{11,12},{13,14},{2,1},{4,3},{6,5},{... | collective-permute-start | bytes 786440 | tf_op jit(solution)/shard_map/ppermute | solution.py:571
  31.7 1.6 %collective-permute-start.5 = (f32[256,256]{1,0:T(8,128)S(1)}, f32[256,256]{1,0:T(8,128)S(1)}, u32[]{:S(2)}, u32[]{:S(2)}) collective-permute-start(f32[256,256]{1,0:T(8,128)S(1)} %get-tuple-element.129.mi), channel_id=1, source_target_pairs={{0,1},{1,0},{2,3},{3,2},{4,5},{5,4},{6,7},{7,6},{8,9},{9,8},{10,11... | collective-permute-start | bytes 786440 | tf_op jit(solution)/shard_map/ppermute | solution.py:571
  33.3 1.5 %base.1 = (f32[53,16,256]{2,1,0:T(8,128)S(1)}, f32[53,16,256]{2,1,0:T(8,128)S(1)}) custom-call(f32[16,56,256]{2,1,0:T(8,128)S(1)} %get-tuple-element.122.n1, f32[16,56,256]{2,1,0:T(8,128)S(1)} %get-tuple-element.132.n2, f32[16,24,256]{2,1,0:T(8,128)S(1)} %get-tuple-element.133.c1, f32[16,24,256]{2,1,0:T(8,128)S(1)} %get-tuple-element.134.c2, ...), custom_call_target="tpu_custom_call" | custom-call | tf_op jit(solution)/shard_map/base/pallas_call | solution.py:549
  34.8 3.8 %collective-permute-done.4.ho = f32[256,256]{1,0:T(8,128)S(1)} collective-permute-done((f32[256,256]{1,0:T(8,128)S(1)}, f32[256,256]{1,0:T(8,128)S(1)}, u32[]{:S(2)}, u32[]{:S(2)}) %collective-permute-start.4) | collective-permute-done | bytes 262176 | tf_op jit(solution)/shard_map/ppermute | solution.py:571
  38.5 0.2 last_edge.1
  38.8 3.5 %collective-permute-start.10 = (f32[52,24,256]{2,1,0:T(8,128)S(1)}, f32[52,24,256]{2,1,0:T(8,128)S(1)}, u32[]{:S(2)}, u32[]{:S(2)}) collective-permute-start(f32[52,24,256]{2,1,0:T(8,128)S(1)} %get-tuple-element.148.mine), channel_id=1, source_target_pairs={{17,81},{19,83},{21,85},{23,87},{25,89},{27,91},{29,93},{31,95},{4... | collective-permute-start | bytes 3833864 | tf_op jit(solution)/shard_map/ppermute | solution.py:571
  42.3 1.3 %collective-permute-start.9 = (f32[36,24,256]{2,1,0:T(8,128)S(1)}, f32[36,24,256]{2,1,0:T(8,128)S(1)}, u32[]{:S(2)}, u32[]{:S(2)}) collective-permute-start(f32[36,24,256]{2,1,0:T(8,128)S(1)} %get-tuple-element.138.ab), channel_id=1, source_target_pairs={{32,16},{34,18},{36,20},{38,22},{40,24},{42,26},{44,28},{46,30},{3... | collective-permute-start | bytes 2654216 | tf_op jit(solution)/shard_map/ppermute | solution.py:571
  43.7 1.3 %collective-permute-start.6 = (f32[344,256]{1,0:T(8,128)S(1)}, f32[344,256]{1,0:T(8,128)S(1)}, u32[]{:S(2)}, u32[]{:S(2)}) collective-permute-start(f32[344,256]{1,0:T(8,128)S(1)} %get-tuple-element.141), channel_id=1, source_target_pairs={{0,16},{1,81},{2,18},{3,83},{4,20},{5,85},{6,22},{7,87},{8,24},{9,... | collective-permute-start | bytes 1056776 | tf_op jit(solution)/shard_map/ppermute | solution.py:571
  45.0 1.3 %collective-permute-start.7 = (f32[176,256]{1,0:T(8,128)S(1)}, f32[176,256]{1,0:T(8,128)S(1)}, u32[]{:S(2)}, u32[]{:S(2)}) collective-permute-start(f32[176,256]{1,0:T(8,128)S(1)} %get-tuple-element.142), channel_id=1, source_target_pairs={{1,18},{3,20},{5,22},{7,24},{9,26},{11,28},{13,30},{2,81},{4,83},{... | collective-permute-start | bytes 540680 | tf_op jit(solution)/shard_map/ppermute | solution.py:571
  46.3 1.3 %collective-permute-start.8 = (f32[176,256]{1,0:T(8,128)S(1)}, f32[176,256]{1,0:T(8,128)S(1)}, u32[]{:S(2)}, u32[]{:S(2)}) collective-permute-start(f32[176,256]{1,0:T(8,128)S(1)} %get-tuple-element.143), channel_id=1, source_target_pairs={{0,81},{1,16},{2,83},{3,18},{4,85},{5,20},{6,87},{7,22},{8,89},{9,... | collective-permute-start | bytes 540680 | tf_op jit(solution)/shard_map/ppermute | solution.py:571
  47.6 7.0 %collective-permute-done.7.zo = f32[176,256]{1,0:T(8,128)S(1)} collective-permute-done((f32[176,256]{1,0:T(8,128)S(1)}, f32[176,256]{1,0:T(8,128)S(1)}, u32[]{:S(2)}, u32[]{:S(2)}) %collective-permute-start.7) | collective-permute-done | bytes 180256 | tf_op jit(solution)/shard_map/ppermute | solution.py:571
  54.6 2.8 %collective-permute-done.8.zi = f32[176,256]{1,0:T(8,128)S(1)} collective-permute-done((f32[176,256]{1,0:T(8,128)S(1)}, f32[176,256]{1,0:T(8,128)S(1)}, u32[]{:S(2)}, u32[]{:S(2)}) %collective-permute-start.8) | collective-permute-done | bytes 180256 | tf_op jit(solution)/shard_map/ppermute | solution.py:571
  57.4 0.7 collective-permute-start.14
  58.1 2.2 %collective-permute-start.18 = (f32[53,16,256]{2,1,0:T(8,128)S(1)}, f32[53,16,256]{2,1,0:T(8,128)S(1)}, u32[]{:S(2)}, u32[]{:S(2)}) collective-permute-start(f32[53,16,256]{2,1,0:T(8,128)S(1)} %get-tuple-element.166.b2), channel_id=1, source_target_pairs={{0,16},{1,17},{2,18},{3,19},{4,20},{5,21},{6,22},{7,23},{8,24},{9,... | collective-permute-start | bytes 2605064 | tf_op jit(solution)/shard_map/ppermute | solution.py:571
  60.3 2.7 %pair.3 = (f32[344,256]{1,0:T(8,128)S(1)}, f32[176,256]{1,0:T(8,128)S(1)}, f32[176,256]{1,0:T(8,128)S(1)}, f32[28,24,256]{2,1,0:T(8,128)S(1)}, f32[24,24,256]{2,...) custom-call(f32[344,256]{1,0:T(8,128)S(1)} %collective-permute-done.6.z0, ...), custom_call_target="tpu_custom_call" | custom-call | tf_op jit(solution)/shard_map/pair/pallas_call | solution.py:549
  63.0 1.3 %collective-permute-start.11 = (f32[344,256]{1,0:T(8,128)S(1)}, f32[344,256]{1,0:T(8,128)S(1)}, u32[]{:S(2)}, u32[]{:S(2)}) collective-permute-start(f32[344,256]{1,0:T(8,128)S(1)} %get-tuple-element.154), channel_id=1, source_target_pairs={{16,48},{81,65},{18,50},{83,67},{20,52},{85,69},{22,54},{87,71},{2... | collective-permute-start | bytes 1056776 | tf_op jit(solution)/shard_map/ppermute | solution.py:571
  64.4 1.3 %collective-permute-start.12 = (f32[176,256]{1,0:T(8,128)S(1)}, f32[176,256]{1,0:T(8,128)S(1)}, u32[]{:S(2)}, u32[]{:S(2)}) collective-permute-start(f32[176,256]{1,0:T(8,128)S(1)} %get-tuple-element.155), channel_id=1, source_target_pairs={{81,50},{83,52},{85,54},{87,56},{89,58},{91,60},{93,62},{18,65},{2... | collective-permute-start | bytes 540680 | tf_op jit(solution)/shard_map/ppermute | solution.py:571
  65.7 2.0 %collective-permute-start.13 = (f32[176,256]{1,0:T(8,128)S(1)}, f32[176,256]{1,0:T(8,128)S(1)}, u32[]{:S(2)}, u32[]{:S(2)}) collective-permute-start(f32[176,256]{1,0:T(8,128)S(1)} %get-tuple-element.156), channel_id=1, source_target_pairs={{16,65},{81,48},{18,67},{83,50},{20,69},{85,52},{22,71},{87,54},{2... | collective-permute-start | bytes 540680 | tf_op jit(solution)/shard_map/ppermute | solution.py:571
  67.7 0.4 collective-permute-done.12.zo
  68.1 2.0 %collective-permute-done.13.zi = f32[176,256]{1,0:T(8,128)S(1)} collective-permute-done((f32[176,256]{1,0:T(8,128)S(1)}, f32[176,256]{1,0:T(8,128)S(1)}, u32[]{:S(2)}, u32[]{:S(2)}) %collective-permute-start.13) | collective-permute-done | bytes 180256 | tf_op jit(solution)/shard_map/ppermute | solution.py:571
  70.1 0.4 collective-permute-done.11.z0
  70.5 0.7 collective-permute-start.15
  71.2 0.7 collective-permute-start.16
  71.9 0.7 collective-permute-start.17
  72.6 0.2 gather.3
  72.9 1.1 collective-permute-done.18.late
  73.9 1.5 %collective-permute-start.23 = (f32[48,24,256]{2,1,0:T(8,128)S(1)}, f32[48,24,256]{2,1,0:T(8,128)S(1)}, u32[]{:S(2)}, u32[]{:S(2)}) collective-permute-start(f32[48,24,256]{2,1,0:T(8,128)S(1)} %get-tuple-element.202.home), channel_id=1, source_target_pairs={{81,17},{83,19},{85,21},{87,23},{89,25},{91,27},{93,29},{95,31}} | collective-permute-start | bytes 3538952 | tf_op jit(solution)/shard_map/ppermute | solution.py:571
  75.4 1.9 %collective-permute-start.22 = (f32[1016,256]{1,0:T(8,128)S(1)}, f32[1016,256]{1,0:T(8,128)S(1)}, u32[]{:S(2)}, u32[]{:S(2)}) collective-permute-start(f32[1016,256]{1,0:T(8,128)S(1)} %get-tuple-element.197), channel_id=1, source_target_pairs={{16,32},{18,34},{20,36},{22,38},{24,40},{26,42},{28,44},{30,46},{8... | collective-permute-start | bytes 3121160 | tf_op jit(solution)/shard_map/ppermute | solution.py:571
  77.4 0.7 collective-permute-start.19
  78.1 0.7 collective-permute-start.20
  78.7 0.7 collective-permute-start.21
  79.4 28.9 %collective-permute-done.22.other = f32[1016,256]{1,0:T(8,128)S(1)} collective-permute-done((f32[1016,256]{1,0:T(8,128)S(1)}, f32[1016,256]{1,0:T(8,128)S(1)}, u32[]{:S(2)}, u32[]{:S(2)}) %collective-permute-start.22) | collective-permute-done | bytes 1040416 | tf_op jit(solution)/shard_map/ppermute | solution.py:571
  108.3 2.6 %out.1 = f32[3,53,16,256]{3,2,1,0:T(8,128)} custom-call(s32[53]{0:T(128)S(1)} %bitcast.10, f32[3,53,16,256]{3,2,1,0:T(8,128)S(1)} %bitcast.9, f32[53,16,256]{2,1,0:T(8,128)S(1)} %collective-permute-done.14.b0, f32[53,16,256]{2,1,0:T(8,128)S(1)} %collective-permute-done.18.late, f32[53,16,256]{2,1,0:T(8,128)S(1)} %get-tuple-element.137.b1, ...), custom_call_target="tpu_custom_call" | custom-call | tf_op jit(solution)/shard_map/out/pallas_call | solution.py:549
  (24 shorter events, 0.1 us)
Async XLA Ops:
  1.9 1.7 %copy-start = (f32[1,3,53,16,256]{4,3,2,1,0:T(8,128)S(1)}, f32[1,3,53,16,256]{4,3,2,1,0:T(8,128)}, u32[]{:S(2)}) copy-start(f32[1,3,53,16,256]{4,3,2,1,0:T(8,128)} %param.8) | copy-start | bytes 7815172
  3.6 5.0 %copy-start.1 = (f32[1,3,53,16,256]{4,3,2,1,0:T(8,128)S(1)}, f32[1,3,53,16,256]{4,3,2,1,0:T(8,128)}, u32[]{:S(2)}) copy-start(f32[1,3,53,16,256]{4,3,2,1,0:T(8,128)} %param.8) | copy-start | bytes 7815172
  4.0 13.5 %collective-permute-start = (f32[3,2,56,256]{3,2,1,0:T(8,128)S(1)}, f32[3,2,56,256]{3,2,1,0:T(8,128)S(1)}, u32[]{:S(2)}, u32[]{:S(2)}) collective-permute-start(f32[3,2,56,256]{3,2,1,0:T(8,128)S(1)} %get-tuple-element.106), channel_id=1, source_target_pairs={{1,2},{3,4},{5,6},{7,8},{9,10},{11,12},{13,14},{2,1},{4,3},{6,5},{... | collective-permute-start | bytes 1032200 | tf_op jit(solution)/shard_map/ppermute | solution.py:571
  8.5 9.1 %collective-permute-start.1 = (f32[3,2,56,256]{3,2,1,0:T(8,128)S(1)}, f32[3,2,56,256]{3,2,1,0:T(8,128)S(1)}, u32[]{:S(2)}, u32[]{:S(2)}) collective-permute-start(f32[3,2,56,256]{3,2,1,0:T(8,128)S(1)} %get-tuple-element.107), channel_id=1, source_target_pairs={{0,1},{1,0},{2,3},{3,2},{4,5},{5,4},{6,7},{7,6},{8,9},{9,8},{10,11... | collective-permute-start | bytes 1032200 | tf_op jit(solution)/shard_map/ppermute | solution.py:571
  17.9 8.5 %collective-permute-start.2 = (f32[2,56,256]{2,1,0:T(8,128)S(1)}, f32[2,56,256]{2,1,0:T(8,128)S(1)}, u32[]{:S(2)}, u32[]{:S(2)}) collective-permute-start(f32[2,56,256]{2,1,0:T(8,128)S(1)} %get-tuple-element.117), channel_id=1, source_target_pairs={{1,2},{3,4},{5,6},{7,8},{9,10},{11,12},{13,14},{2,1},{4,3},{6,5},{... | collective-permute-start | bytes 344072 | tf_op jit(solution)/shard_map/ppermute | solution.py:571
  22.5 3.9 %collective-permute-start.3 = (f32[2,56,256]{2,1,0:T(8,128)S(1)}, f32[2,56,256]{2,1,0:T(8,128)S(1)}, u32[]{:S(2)}, u32[]{:S(2)}) collective-permute-start(f32[2,56,256]{2,1,0:T(8,128)S(1)} %get-tuple-element.118), channel_id=1, source_target_pairs={{0,1},{1,0},{2,3},{3,2},{4,5},{5,4},{6,7},{7,6},{8,9},{9,8},{10,11... | collective-permute-start | bytes 344072 | tf_op jit(solution)/shard_map/ppermute | solution.py:571
  27.5 11.0 %collective-permute-start.4 = (f32[256,256]{1,0:T(8,128)S(1)}, f32[256,256]{1,0:T(8,128)S(1)}, u32[]{:S(2)}, u32[]{:S(2)}) collective-permute-start(f32[256,256]{1,0:T(8,128)S(1)} %get-tuple-element.128.mo), channel_id=1, source_target_pairs={{1,2},{3,4},{5,6},{7,8},{9,10},{11,12},{13,14},{2,1},{4,3},{6,5},{... | collective-permute-start | bytes 786440 | tf_op jit(solution)/shard_map/ppermute | solution.py:571
  31.7 6.8 %collective-permute-start.5 = (f32[256,256]{1,0:T(8,128)S(1)}, f32[256,256]{1,0:T(8,128)S(1)}, u32[]{:S(2)}, u32[]{:S(2)}) collective-permute-start(f32[256,256]{1,0:T(8,128)S(1)} %get-tuple-element.129.mi), channel_id=1, source_target_pairs={{0,1},{1,0},{2,3},{3,2},{4,5},{5,4},{6,7},{7,6},{8,9},{9,8},{10,11... | collective-permute-start | bytes 786440 | tf_op jit(solution)/shard_map/ppermute | solution.py:571
  38.8 19.3 %collective-permute-start.10 = (f32[52,24,256]{2,1,0:T(8,128)S(1)}, f32[52,24,256]{2,1,0:T(8,128)S(1)}, u32[]{:S(2)}, u32[]{:S(2)}) collective-permute-start(f32[52,24,256]{2,1,0:T(8,128)S(1)} %get-tuple-element.148.mine), channel_id=1, source_target_pairs={{17,81},{19,83},{21,85},{23,87},{25,89},{27,91},{29,93},{31,95},{4... | collective-permute-start | bytes 3833864 | tf_op jit(solution)/shard_map/ppermute | solution.py:571
  42.3 15.8 %collective-permute-start.9 = (f32[36,24,256]{2,1,0:T(8,128)S(1)}, f32[36,24,256]{2,1,0:T(8,128)S(1)}, u32[]{:S(2)}, u32[]{:S(2)}) collective-permute-start(f32[36,24,256]{2,1,0:T(8,128)S(1)} %get-tuple-element.138.ab), channel_id=1, source_target_pairs={{32,16},{34,18},{36,20},{38,22},{40,24},{42,26},{44,28},{46,30},{3... | collective-permute-start | bytes 2654216 | tf_op jit(solution)/shard_map/ppermute | solution.py:571
  43.7 13.7 %collective-permute-start.6 = (f32[344,256]{1,0:T(8,128)S(1)}, f32[344,256]{1,0:T(8,128)S(1)}, u32[]{:S(2)}, u32[]{:S(2)}) collective-permute-start(f32[344,256]{1,0:T(8,128)S(1)} %get-tuple-element.141), channel_id=1, source_target_pairs={{0,16},{1,81},{2,18},{3,83},{4,20},{5,85},{6,22},{7,87},{8,24},{9,... | collective-permute-start | bytes 1056776 | tf_op jit(solution)/shard_map/ppermute | solution.py:571
  45.0 9.6 %collective-permute-start.7 = (f32[176,256]{1,0:T(8,128)S(1)}, f32[176,256]{1,0:T(8,128)S(1)}, u32[]{:S(2)}, u32[]{:S(2)}) collective-permute-start(f32[176,256]{1,0:T(8,128)S(1)} %get-tuple-element.142), channel_id=1, source_target_pairs={{1,18},{3,20},{5,22},{7,24},{9,26},{11,28},{13,30},{2,81},{4,83},{... | collective-permute-start | bytes 540680 | tf_op jit(solution)/shard_map/ppermute | solution.py:571
  46.3 11.1 %collective-permute-start.8 = (f32[176,256]{1,0:T(8,128)S(1)}, f32[176,256]{1,0:T(8,128)S(1)}, u32[]{:S(2)}, u32[]{:S(2)}) collective-permute-start(f32[176,256]{1,0:T(8,128)S(1)} %get-tuple-element.143), channel_id=1, source_target_pairs={{0,81},{1,16},{2,83},{3,18},{4,85},{5,20},{6,87},{7,22},{8,89},{9,... | collective-permute-start | bytes 540680 | tf_op jit(solution)/shard_map/ppermute | solution.py:571
  57.4 10.3 %collective-permute-start.14 = (f32[53,16,256]{2,1,0:T(8,128)S(1)}, f32[53,16,256]{2,1,0:T(8,128)S(1)}, u32[]{:S(2)}, u32[]{:S(2)}) collective-permute-start(f32[53,16,256]{2,1,0:T(8,128)S(1)} %get-tuple-element.166.b2), channel_id=1, source_target_pairs={{32,48},{33,49},{34,50},{35,51},{36,52},{37,53},{38,54},{39,55},{4... | collective-permute-start | bytes 2605064 | tf_op jit(solution)/shard_map/ppermute | solution.py:571
  58.1 15.8 %collective-permute-start.18 = (f32[53,16,256]{2,1,0:T(8,128)S(1)}, f32[53,16,256]{2,1,0:T(8,128)S(1)}, u32[]{:S(2)}, u32[]{:S(2)}) collective-permute-start(f32[53,16,256]{2,1,0:T(8,128)S(1)} %get-tuple-element.166.b2), channel_id=1, source_target_pairs={{0,16},{1,17},{2,18},{3,19},{4,20},{5,21},{6,22},{7,23},{8,24},{9,... | collective-permute-start | bytes 2605064 | tf_op jit(solution)/shard_map/ppermute | solution.py:571
  63.0 7.5 %collective-permute-start.11 = (f32[344,256]{1,0:T(8,128)S(1)}, f32[344,256]{1,0:T(8,128)S(1)}, u32[]{:S(2)}, u32[]{:S(2)}) collective-permute-start(f32[344,256]{1,0:T(8,128)S(1)} %get-tuple-element.154), channel_id=1, source_target_pairs={{16,48},{81,65},{18,50},{83,67},{20,52},{85,69},{22,54},{87,71},{2... | collective-permute-start | bytes 1056776 | tf_op jit(solution)/shard_map/ppermute | solution.py:571
  64.4 3.8 %collective-permute-start.12 = (f32[176,256]{1,0:T(8,128)S(1)}, f32[176,256]{1,0:T(8,128)S(1)}, u32[]{:S(2)}, u32[]{:S(2)}) collective-permute-start(f32[176,256]{1,0:T(8,128)S(1)} %get-tuple-element.155), channel_id=1, source_target_pairs={{81,50},{83,52},{85,54},{87,56},{89,58},{91,60},{93,62},{18,65},{2... | collective-permute-start | bytes 540680 | tf_op jit(solution)/shard_map/ppermute | solution.py:571
  65.7 4.5 %collective-permute-start.13 = (f32[176,256]{1,0:T(8,128)S(1)}, f32[176,256]{1,0:T(8,128)S(1)}, u32[]{:S(2)}, u32[]{:S(2)}) collective-permute-start(f32[176,256]{1,0:T(8,128)S(1)} %get-tuple-element.156), channel_id=1, source_target_pairs={{16,65},{81,48},{18,67},{83,50},{20,69},{85,52},{22,71},{87,54},{2... | collective-permute-start | bytes 540680 | tf_op jit(solution)/shard_map/ppermute | solution.py:571
  70.5 2.3 %collective-permute-start.15 = (f32[344,256]{1,0:T(8,128)S(1)}, f32[344,256]{1,0:T(8,128)S(1)}, u32[]{:S(2)}, u32[]{:S(2)}) collective-permute-start(f32[344,256]{1,0:T(8,128)S(1)} %get-tuple-element.163), channel_id=1, source_target_pairs={{48,80},{65,97},{50,82},{67,99},{52,84},{69,101},{54,86},{71,103},... | collective-permute-start | bytes 1056776 | tf_op jit(solution)/shard_map/ppermute | solution.py:571
  71.2 1.6 %collective-permute-start.16 = (f32[176,256]{1,0:T(8,128)S(1)}, f32[176,256]{1,0:T(8,128)S(1)}, u32[]{:S(2)}, u32[]{:S(2)}) collective-permute-start(f32[176,256]{1,0:T(8,128)S(1)} %get-tuple-element.164), channel_id=1, source_target_pairs={{65,82},{67,84},{69,86},{71,88},{73,90},{75,92},{77,94},{50,97},{5... | collective-permute-start | bytes 540680 | tf_op jit(solution)/shard_map/ppermute | solution.py:571
  71.9 0.9 collective-permute-start.17
  73.9 34.4 %copy-start.2 = (s32[53,1]{0,1:T(1,128)S(1)}, s32[53,1]{0,1:T(1,128)}, u32[]{:S(2)}) copy-start(s32[53,1]{0,1:T(1,128)} %param.15) | copy-start | bytes 640
  73.9 34.4 %collective-permute-start.23 = (f32[48,24,256]{2,1,0:T(8,128)S(1)}, f32[48,24,256]{2,1,0:T(8,128)S(1)}, u32[]{:S(2)}, u32[]{:S(2)}) collective-permute-start(f32[48,24,256]{2,1,0:T(8,128)S(1)} %get-tuple-element.202.home), channel_id=1, source_target_pairs={{81,17},{83,19},{85,21},{87,23},{89,25},{91,27},{93,29},{95,31}} | collective-permute-start | bytes 3538952 | tf_op jit(solution)/shard_map/ppermute | solution.py:571
  75.4 32.9 %collective-permute-start.22 = (f32[1016,256]{1,0:T(8,128)S(1)}, f32[1016,256]{1,0:T(8,128)S(1)}, u32[]{:S(2)}, u32[]{:S(2)}) collective-permute-start(f32[1016,256]{1,0:T(8,128)S(1)} %get-tuple-element.197), channel_id=1, source_target_pairs={{16,32},{18,34},{20,36},{22,38},{24,40},{26,42},{28,44},{30,46},{8... | collective-permute-start | bytes 3121160 | tf_op jit(solution)/shard_map/ppermute | solution.py:571
  77.4 2.1 %collective-permute-start.19 = (f32[344,256]{1,0:T(8,128)S(1)}, f32[344,256]{1,0:T(8,128)S(1)}, u32[]{:S(2)}, u32[]{:S(2)}) collective-permute-start(f32[344,256]{1,0:T(8,128)S(1)} %get-tuple-element.187), channel_id=1, source_target_pairs={{80,112},{97,113},{82,114},{99,115},{84,116},{101,117},{86,118},{1... | collective-permute-start | bytes 1056776 | tf_op jit(solution)/shard_map/ppermute | solution.py:571
  78.1 1.4 %collective-permute-start.20 = (f32[88,256]{1,0:T(8,128)S(1)}, f32[88,256]{1,0:T(8,128)S(1)}, u32[]{:S(2)}, u32[]{:S(2)}) collective-permute-start(f32[88,256]{1,0:T(8,128)S(1)} %get-tuple-element.188), channel_id=1, source_target_pairs={{97,114},{99,116},{101,118},{103,120},{105,122},{107,124},{109,126... | collective-permute-start | bytes 270344 | tf_op jit(solution)/shard_map/ppermute | solution.py:571
  78.7 0.7 collective-permute-start.21

commit v11 on v10

--- a/solution.py
+++ b/solution.py
@@ -136,15 +136,20 @@
         body([size * i + k for k in range(size)])
 
 
+FIRST_ROWS = 328
+
+
 def first_kernel(u, weights_made, outer, inner):
     info = Position()
     at_top = info[0] == 0
+    for out in (outer, inner):
+        out[FIRST_ROWS - 16 :, :] = zeros(16)
     for m in range(3):
         for r in range(2):
             first, last = u[m, :, r, :], u[m, :, ROWS - 2 + r, :]
-            for out, value in ((outer, jnp.where(at_top, first, last)), (inner, jnp.where(at_top, last, first))):
-                out[m, r, SP - 8 :, :] = zeros(8)
-                out[m, r, :SPECIES, :] = value
+            at = SPECIES * (2 * m + r)
+            outer[at : at + SPECIES, :] = jnp.where(at_top, first, last)
+            inner[at : at + SPECIES, :] = jnp.where(at_top, last, first)
 
 
 def restricted(y):
@@ -244,7 +249,7 @@
     info = Position()
     for side, (rows, order) in enumerate(SIDES):
         halo = pick_halo(info, side, uo, ui)
-        us = [[halo(m, r) for m in range(3)] for r in order]
+        us = [[halo(pl.ds(SPECIES * (2 * m + r), SP)) for m in range(3)] for r in order]
         p0 = beside(*[mixed(MIX0, v) for v in us])
         ps = beside(*[mixed(MIXS, v) for v in us])
         lumped = [lumped_halo(lv, v[0]) for v in us]
@@ -273,7 +278,7 @@
             e1[x] = (y[:CP] + y[CP:]) + dc12[...] * lap_y(c)
             n1s[x + 2], v1s[x + 2], c1s[x + 2], c1[x] = n, v, c, c
 
-    blocks(ROWS, terms, 8)
+    blocks(ROWS, terms, ROWS)
 
     def laps(xs):
         for x in xs:
@@ -281,7 +286,7 @@
             r1[x] += lap_rows(v1s, x + 2) * (1.0 / 12.0)
             e1[x] += dc12[...] * lap_rows(c1s, x + 2)
 
-    blocks(ROWS, laps, 8)
+    blocks(ROWS, laps, ROWS)
 
 
 def lumped_old(first, c0, e0):
@@ -466,7 +471,7 @@
 
 
 def out_kernel(
-    where, u, b0, late, b1, b2, share, z0, zo, zi, ab, ws, lapm, dc12, home, one, other, out, z, za, zs, spread, node, sem
+    where, u, b0, late, early, b1, b2, share, z0, zo, zi, ab, ws, lapm, dc12, home, one, other, out, z, za, zs, spread, node, sem
 ):
     info = Position()
     last = info[1] == SLICES - 1
@@ -517,7 +522,7 @@
         return copy
 
     first = info[1] == 0
-    copies = [finish(0, lambda s: jnp.where(first, u[0, s], b0[s] + late[s]))]
+    copies = [finish(0, lambda s: jnp.where(first, u[0, s], b0[s] + late[s] + early[s]))]
 
     @pl.when(last)
     def _():
@@ -594,7 +599,7 @@
 def local(fine_nodes, fine_rates, fine_pairs, fine_diff, coarse_rates, coarse_pairs, coarse_diff, species_map):
     nodes = fine_nodes[0]
     fine, coarse = field(ROWS, SP), field(ROWS, CP)
-    message = field(3, 2, SP)
+    message = field(FIRST_ROWS)
     def bf16(*shape):
         return jax.ShapeDtypeStruct(shape, BF16)
 
@@ -679,11 +684,12 @@
             z = list(lax.optimization_barrier(tuple(z)))
             b0 = moved(after(b2, z[0]), forward[2], forward[6])
             *z, short, long = lax.optimization_barrier((*z, short, long))
-            late = moved(after(b2, z[0]), *forward[:2], *forward[3:6])
+            late = moved(after(b2, z[0]), *forward[3:6])
         elif at == 2:
             *z, b0 = lax.optimization_barrier((*z, b0))
+            early = moved(after(b2, z[0]), *forward[:2])
         elif at == 3:
-            *z, late, home, away = lax.optimization_barrier((*z, late, home, away))
+            *z, late, early, home, away = lax.optimization_barrier((*z, late, early, home, away))
         else:
             other, one = moved(away, *back), moved(home, *first)
             *z, other, one, home = lax.optimization_barrier((*z, other, one, home))
@@ -707,7 +713,7 @@
         out_kernel,
         "out",
         field(3, SPECIES, ROWS),
-        *(species_map[:, 0], nodes, b0, late, b1, b2, share, *z, ab, ws, lapm, dc12, home, one, other),
+        *(species_map[:, 0], nodes, b0, late, early, b1, b2, share, *z, ab, ws, lapm, dc12, home, one, other),
         out_specs=ANY,
         scratch=[result, field(ROWS + 4, CP), field(ROWS + 8, CP), field(3, CP, ROWS), field(3, SPECIES, ROWS), pltpu.SemaphoreType.DMA((3,))],
     )

time: 112 us -> 122 us (1.089)
  the two profiles are of different devices: /device:TPU:51 before, /device:TPU:77 now
where the time goes in v11:
time: 122 us; the launch traced here: 121 us
  waiting for transfers between devices  72.6 us (60%)
  starting transfers between devices  29.4 us (24%)
  Pallas kernels  15.7 us (13%)
  local copies, waits for them, and re-layouts  1.74 us (1%)
  other arithmetic  1.5 us (1%)
    ppermute x25, waiting for transfers between devices, moved(): return lax.ppermute(value, AXES, pairs)  72.6 us
    ppermute x25, starting transfers between devices, moved(): return lax.ppermute(value, AXES, pairs)  29.4 us
    pallas_call x16, Pallas kernels, call(): pl.pallas_call(kernel, out_shape=outs, in_specs=specs, **{'out_specs': ou...  15.7 us
  transfers between devices with their start and end apart: 25, of which 7 were waited for; matrix products, arithmetic and copies ran while one was open for 0% of the time, Pallas kernels for 9%

profile of v11, /device:TPU:77, one launch (start us, length us, event | category | flops | bytes accessed | tf_op | source)
XLA Modules:
  0.0 121.4 jit_solution(5568129479232248726)
XLA Ops:
  0.0 0.7 convert_bitcast_fusion
  0.7 0.8 pad_add_fusion.raw
  1.5 0.4 prep.1
  1.9 0.0 copy-start
  1.9 1.7 %copy-done = f32[1,3,53,16,256]{4,3,2,1,0:T(8,128)S(1)} copy-done((f32[1,3,53,16,256]{4,3,2,1,0:T(8,128)S(1)}, f32[1,3,53,16,256]{4,3,2,1,0:T(8,128)}, u32[]{:S(2)}) %copy-start) | copy-done | bytes 2605080
  3.6 0.4 first.1
  4.0 3.8 %collective-permute-start = (f32[328,256]{1,0:T(8,128)S(1)}, f32[328,256]{1,0:T(8,128)S(1)}, u32[]{:S(2)}, u32[]{:S(2)}) collective-permute-start(f32[328,256]{1,0:T(8,128)S(1)} %get-tuple-element.108), channel_id=1, source_target_pairs={{1,2},{3,4},{5,6},{7,8},{9,10},{11,12},{13,14},{2,1},{4,3},{6,5},{... | collective-permute-start | bytes 1007624 | tf_op jit(solution)/shard_map/ppermute | solution.py:576
  7.9 0.1 collective-permute-start.1
  8.0 6.2 %old.1 = (f32[16,56,256]{2,1,0:T(8,128)S(1)}, f32[16,56,256]{2,1,0:T(8,128)S(1)}, f32[16,24,256]{2,1,0:T(8,128)S(1)}, f32[16,24,256]{2,1,0:T(8,128)S(1)}, f32[16,24,256]{2,1,0:T(8,128)S(1)}) custom-call(f32[3,53,16,256]{3,2,1,0:T(8,128)S(1)} %bitcast.8, bf16[112,224]{1,0:T(8,128)(2,1)S(1)} %get-tuple-element.113.wf, ...), custom_call_target="tpu_custom_call" | custom-call | tf_op jit(solution)/shard_map/old/pallas_call | solution.py:554
  14.3 4.3 %collective-permute-done.uo = f32[328,256]{1,0:T(8,128)S(1)} collective-permute-done((f32[328,256]{1,0:T(8,128)S(1)}, f32[328,256]{1,0:T(8,128)S(1)}, u32[]{:S(2)}, u32[]{:S(2)}) %collective-permute-start) | collective-permute-done | bytes 335904 | tf_op jit(solution)/shard_map/ppermute | solution.py:576
  18.6 0.0 collective-permute-done.1.ui
  18.6 0.5 old_edge.1
  19.1 2.9 %collective-permute-start.2 = (f32[2,56,256]{2,1,0:T(8,128)S(1)}, f32[2,56,256]{2,1,0:T(8,128)S(1)}, u32[]{:S(2)}, u32[]{:S(2)}) collective-permute-start(f32[2,56,256]{2,1,0:T(8,128)S(1)} %get-tuple-element.119), channel_id=1, source_target_pairs={{1,2},{3,4},{5,6},{7,8},{9,10},{11,12},{13,14},{2,1},{4,3},{6,5},{... | collective-permute-start | bytes 344072 | tf_op jit(solution)/shard_map/ppermute | solution.py:576
  21.9 0.1 collective-permute-start.3
  22.0 2.6 %mid.1 = (f32[16,56,256]{2,1,0:T(8,128)S(1)}, f32[16,24,256]{2,1,0:T(8,128)S(1)}, f32[16,24,256]{2,1,0:T(8,128)S(1)}, f32[16,24,256]{2,1,0:T(8,128)S(1)}) custom-call(f32[16,56,256]{2,1,0:T(8,128)S(1)} %get-tuple-element.124.n1, f32[16,56,256]{2,1,0:T(8,128)S(1)} %get-tuple-element.125.s, bf16[240,224]{1,0:T(8,128)(2,1)S(1)} %get-tuple-element.126.wfr, ...), custom_call_target="tpu_custom_call" | custom-call | tf_op jit(solution)/shard_map/mid/pallas_call | solution.py:554
  24.6 3.4 %collective-permute-done.2.no = f32[2,56,256]{2,1,0:T(8,128)S(1)} collective-permute-done((f32[2,56,256]{2,1,0:T(8,128)S(1)}, f32[2,56,256]{2,1,0:T(8,128)S(1)}, u32[]{:S(2)}, u32[]{:S(2)}) %collective-permute-start.2) | collective-permute-done | bytes 114720 | tf_op jit(solution)/shard_map/ppermute | solution.py:576
  28.0 0.0 collective-permute-done.3.ni
  28.0 1.1 mid_edge.1
  29.1 2.7 %collective-permute-start.4 = (f32[256,256]{1,0:T(8,128)S(1)}, f32[256,256]{1,0:T(8,128)S(1)}, u32[]{:S(2)}, u32[]{:S(2)}) collective-permute-start(f32[256,256]{1,0:T(8,128)S(1)} %get-tuple-element.130.mo), channel_id=1, source_target_pairs={{1,2},{3,4},{5,6},{7,8},{9,10},{11,12},{13,14},{2,1},{4,3},{6,5},{... | collective-permute-start | bytes 786440 | tf_op jit(solution)/shard_map/ppermute | solution.py:576
  31.8 0.1 collective-permute-start.5
  31.9 1.5 %base.1 = (f32[53,16,256]{2,1,0:T(8,128)S(1)}, f32[53,16,256]{2,1,0:T(8,128)S(1)}) custom-call(f32[16,56,256]{2,1,0:T(8,128)S(1)} %get-tuple-element.124.n1, f32[16,56,256]{2,1,0:T(8,128)S(1)} %get-tuple-element.134.n2, f32[16,24,256]{2,1,0:T(8,128)S(1)} %get-tuple-element.135.c1, f32[16,24,256]{2,1,0:T(8,128)S(1)} %get-tuple-element.136.c2, ...), custom_call_target="tpu_custom_call" | custom-call | tf_op jit(solution)/shard_map/base/pallas_call | solution.py:554
  33.4 7.0 %collective-permute-done.4.ho = f32[256,256]{1,0:T(8,128)S(1)} collective-permute-done((f32[256,256]{1,0:T(8,128)S(1)}, f32[256,256]{1,0:T(8,128)S(1)}, u32[]{:S(2)}, u32[]{:S(2)}) %collective-permute-start.4) | collective-permute-done | bytes 262176 | tf_op jit(solution)/shard_map/ppermute | solution.py:576
  40.3 0.0 collective-permute-done.5.hi
  40.3 0.2 last_edge.1
  40.6 0.7 collective-permute-start.10
  41.3 5.2 %collective-permute-start.9 = (f32[36,24,256]{2,1,0:T(8,128)S(1)}, f32[36,24,256]{2,1,0:T(8,128)S(1)}, u32[]{:S(2)}, u32[]{:S(2)}) collective-permute-start(f32[36,24,256]{2,1,0:T(8,128)S(1)} %get-tuple-element.140.ab), channel_id=1, source_target_pairs={{32,16},{34,18},{36,20},{38,22},{40,24},{42,26},{44,28},{46,30},{3... | collective-permute-start | bytes 2654216 | tf_op jit(solution)/shard_map/ppermute | solution.py:576
  46.6 0.7 collective-permute-start.6
  47.3 0.7 collective-permute-start.7
  48.0 0.7 collective-permute-start.8
  48.7 1.3 %collective-permute-start.14 = (f32[53,16,256]{2,1,0:T(8,128)S(1)}, f32[53,16,256]{2,1,0:T(8,128)S(1)}, u32[]{:S(2)}, u32[]{:S(2)}) collective-permute-start(f32[53,16,256]{2,1,0:T(8,128)S(1)} %get-tuple-element.169.b2), channel_id=1, source_target_pairs={{32,48},{33,49},{34,50},{35,51},{36,52},{37,53},{38,54},{39,55},{4... | collective-permute-start | bytes 2605064 | tf_op jit(solution)/shard_map/ppermute | solution.py:576
  50.0 6.5 %collective-permute-done.9.short = f32[36,24,256]{2,1,0:T(8,128)S(1)} collective-permute-done((f32[36,24,256]{2,1,0:T(8,128)S(1)}, f32[36,24,256]{2,1,0:T(8,128)S(1)}, u32[]{:S(2)}, u32[]{:S(2)}) %collective-permute-start.9) | collective-permute-done | bytes 884768 | tf_op jit(solution)/shard_map/ppermute | solution.py:576
  56.5 0.7 collective-permute-start.11
  57.2 0.7 collective-permute-start.12
  57.9 0.7 collective-permute-start.13
  58.6 0.9 collective-permute-start.18
  59.5 6.0 %collective-permute-done.14.b0 = f32[53,16,256]{2,1,0:T(8,128)S(1)} collective-permute-done((f32[53,16,256]{2,1,0:T(8,128)S(1)}, f32[53,16,256]{2,1,0:T(8,128)S(1)}, u32[]{:S(2)}, u32[]{:S(2)}) %collective-permute-start.14) | collective-permute-done | bytes 868384 | tf_op jit(solution)/shard_map/ppermute | solution.py:576
  65.5 1.3 %collective-permute-start.19 = (f32[53,16,256]{2,1,0:T(8,128)S(1)}, f32[53,16,256]{2,1,0:T(8,128)S(1)}, u32[]{:S(2)}, u32[]{:S(2)}) collective-permute-start(f32[53,16,256]{2,1,0:T(8,128)S(1)} %get-tuple-element.169.b2), channel_id=1, source_target_pairs={{0,16},{1,17},{2,18},{3,19},{4,20},{5,21},{6,22},{7,23},{8,24},{9,... | collective-permute-start | bytes 2605064 | tf_op jit(solution)/shard_map/ppermute | solution.py:576
  66.9 0.7 collective-permute-start.15
  67.6 0.7 collective-permute-start.16
  68.2 0.7 collective-permute-start.17
  69.0 16.4 %collective-permute-done.19.early = f32[53,16,256]{2,1,0:T(8,128)S(1)} collective-permute-done((f32[53,16,256]{2,1,0:T(8,128)S(1)}, f32[53,16,256]{2,1,0:T(8,128)S(1)}, u32[]{:S(2)}, u32[]{:S(2)}) %collective-permute-start.19) | collective-permute-done | bytes 868384 | tf_op jit(solution)/shard_map/ppermute | solution.py:576
  85.4 0.9 collective-permute-start.24
  86.3 1.3 %collective-permute-start.23 = (f32[1016,256]{1,0:T(8,128)S(1)}, f32[1016,256]{1,0:T(8,128)S(1)}, u32[]{:S(2)}, u32[]{:S(2)}) collective-permute-start(f32[1016,256]{1,0:T(8,128)S(1)} %get-tuple-element.201), channel_id=1, source_target_pairs={{16,32},{18,34},{20,36},{22,38},{24,40},{26,42},{28,44},{30,46},{8... | collective-permute-start | bytes 3121160 | tf_op jit(solution)/shard_map/ppermute | solution.py:576
  87.6 0.7 collective-permute-start.20
  88.3 0.7 collective-permute-start.21
  88.9 0.7 collective-permute-start.22
  89.6 29.0 %collective-permute-done.23.other = f32[1016,256]{1,0:T(8,128)S(1)} collective-permute-done((f32[1016,256]{1,0:T(8,128)S(1)}, f32[1016,256]{1,0:T(8,128)S(1)}, u32[]{:S(2)}, u32[]{:S(2)}) %collective-permute-start.23) | collective-permute-done | bytes 1040416 | tf_op jit(solution)/shard_map/ppermute | solution.py:576
  118.6 2.6 %out.1 = f32[3,53,16,256]{3,2,1,0:T(8,128)} custom-call(s32[53]{0:T(128)S(1)} %bitcast.10, f32[3,53,16,256]{3,2,1,0:T(8,128)S(1)} %bitcast.9, f32[53,16,256]{2,1,0:T(8,128)S(1)} %collective-permute-done.14.b0, f32[53,16,256]{2,1,0:T(8,128)S(1)} %collective-permute-done.18.late, f32[53,16,256]{2,1,0:T(8,128)S(1)} %collective-permute-done.19.early, ...), custom_call_target="tpu_custom_call" | custom-call | tf_op jit(solution)/shard_map/out/pallas_call | solution.py:554
  (26 shorter events, 0.1 us)
Async XLA Ops:
  1.9 1.7 %copy-start = (f32[1,3,53,16,256]{4,3,2,1,0:T(8,128)S(1)}, f32[1,3,53,16,256]{4,3,2,1,0:T(8,128)}, u32[]{:S(2)}) copy-start(f32[1,3,53,16,256]{4,3,2,1,0:T(8,128)} %param.8) | copy-start | bytes 7815172
  3.6 4.4 %copy-start.1 = (f32[1,3,53,16,256]{4,3,2,1,0:T(8,128)S(1)}, f32[1,3,53,16,256]{4,3,2,1,0:T(8,128)}, u32[]{:S(2)}) copy-start(f32[1,3,53,16,256]{4,3,2,1,0:T(8,128)} %param.8) | copy-start | bytes 7815172
  4.0 14.5 %collective-permute-start = (f32[328,256]{1,0:T(8,128)S(1)}, f32[328,256]{1,0:T(8,128)S(1)}, u32[]{:S(2)}, u32[]{:S(2)}) collective-permute-start(f32[328,256]{1,0:T(8,128)S(1)} %get-tuple-element.108), channel_id=1, source_target_pairs={{1,2},{3,4},{5,6},{7,8},{9,10},{11,12},{13,14},{2,1},{4,3},{6,5},{... | collective-permute-start | bytes 1007624 | tf_op jit(solution)/shard_map/ppermute | solution.py:576
  7.9 10.7 %collective-permute-start.1 = (f32[328,256]{1,0:T(8,128)S(1)}, f32[328,256]{1,0:T(8,128)S(1)}, u32[]{:S(2)}, u32[]{:S(2)}) collective-permute-start(f32[328,256]{1,0:T(8,128)S(1)} %get-tuple-element.109), channel_id=1, source_target_pairs={{0,1},{1,0},{2,3},{3,2},{4,5},{5,4},{6,7},{7,6},{8,9},{9,8},{10,11... | collective-permute-start | bytes 1007624 | tf_op jit(solution)/shard_map/ppermute | solution.py:576
  19.1 8.9 %collective-permute-start.2 = (f32[2,56,256]{2,1,0:T(8,128)S(1)}, f32[2,56,256]{2,1,0:T(8,128)S(1)}, u32[]{:S(2)}, u32[]{:S(2)}) collective-permute-start(f32[2,56,256]{2,1,0:T(8,128)S(1)} %get-tuple-element.119), channel_id=1, source_target_pairs={{1,2},{3,4},{5,6},{7,8},{9,10},{11,12},{13,14},{2,1},{4,3},{6,5},{... | collective-permute-start | bytes 344072 | tf_op jit(solution)/shard_map/ppermute | solution.py:576
  21.9 6.1 %collective-permute-start.3 = (f32[2,56,256]{2,1,0:T(8,128)S(1)}, f32[2,56,256]{2,1,0:T(8,128)S(1)}, u32[]{:S(2)}, u32[]{:S(2)}) collective-permute-start(f32[2,56,256]{2,1,0:T(8,128)S(1)} %get-tuple-element.120), channel_id=1, source_target_pairs={{0,1},{1,0},{2,3},{3,2},{4,5},{5,4},{6,7},{7,6},{8,9},{9,8},{10,11... | collective-permute-start | bytes 344072 | tf_op jit(solution)/shard_map/ppermute | solution.py:576
  29.1 11.2 %collective-permute-start.4 = (f32[256,256]{1,0:T(8,128)S(1)}, f32[256,256]{1,0:T(8,128)S(1)}, u32[]{:S(2)}, u32[]{:S(2)}) collective-permute-start(f32[256,256]{1,0:T(8,128)S(1)} %get-tuple-element.130.mo), channel_id=1, source_target_pairs={{1,2},{3,4},{5,6},{7,8},{9,10},{11,12},{13,14},{2,1},{4,3},{6,5},{... | collective-permute-start | bytes 786440 | tf_op jit(solution)/shard_map/ppermute | solution.py:576
  31.8 8.6 %collective-permute-start.5 = (f32[256,256]{1,0:T(8,128)S(1)}, f32[256,256]{1,0:T(8,128)S(1)}, u32[]{:S(2)}, u32[]{:S(2)}) collective-permute-start(f32[256,256]{1,0:T(8,128)S(1)} %get-tuple-element.131.mi), channel_id=1, source_target_pairs={{0,1},{1,0},{2,3},{3,2},{4,5},{5,4},{6,7},{7,6},{8,9},{9,8},{10,11... | collective-permute-start | bytes 786440 | tf_op jit(solution)/shard_map/ppermute | solution.py:576
  40.6 16.0 %collective-permute-start.10 = (f32[52,24,256]{2,1,0:T(8,128)S(1)}, f32[52,24,256]{2,1,0:T(8,128)S(1)}, u32[]{:S(2)}, u32[]{:S(2)}) collective-permute-start(f32[52,24,256]{2,1,0:T(8,128)S(1)} %get-tuple-element.150.mine), channel_id=1, source_target_pairs={{17,81},{19,83},{21,85},{23,87},{25,89},{27,91},{29,93},{31,95},{4... | collective-permute-start | bytes 3833864 | tf_op jit(solution)/shard_map/ppermute | solution.py:576
  41.3 15.2 %collective-permute-start.9 = (f32[36,24,256]{2,1,0:T(8,128)S(1)}, f32[36,24,256]{2,1,0:T(8,128)S(1)}, u32[]{:S(2)}, u32[]{:S(2)}) collective-permute-start(f32[36,24,256]{2,1,0:T(8,128)S(1)} %get-tuple-element.140.ab), channel_id=1, source_target_pairs={{32,16},{34,18},{36,20},{38,22},{40,24},{42,26},{44,28},{46,30},{3... | collective-permute-start | bytes 2654216 | tf_op jit(solution)/shard_map/ppermute | solution.py:576
  46.6 2.1 %collective-permute-start.6 = (f32[344,256]{1,0:T(8,128)S(1)}, f32[344,256]{1,0:T(8,128)S(1)}, u32[]{:S(2)}, u32[]{:S(2)}) collective-permute-start(f32[344,256]{1,0:T(8,128)S(1)} %get-tuple-element.143), channel_id=1, source_target_pairs={{0,16},{1,81},{2,18},{3,83},{4,20},{5,85},{6,22},{7,87},{8,24},{9,... | collective-permute-start | bytes 1056776 | tf_op jit(solution)/shard_map/ppermute | solution.py:576
  47.3 1.4 %collective-permute-start.7 = (f32[176,256]{1,0:T(8,128)S(1)}, f32[176,256]{1,0:T(8,128)S(1)}, u32[]{:S(2)}, u32[]{:S(2)}) collective-permute-start(f32[176,256]{1,0:T(8,128)S(1)} %get-tuple-element.144), channel_id=1, source_target_pairs={{1,18},{3,20},{5,22},{7,24},{9,26},{11,28},{13,30},{2,81},{4,83},{... | collective-permute-start | bytes 540680 | tf_op jit(solution)/shard_map/ppermute | solution.py:576
  48.0 0.7 collective-permute-start.8
  48.7 16.8 %collective-permute-start.14 = (f32[53,16,256]{2,1,0:T(8,128)S(1)}, f32[53,16,256]{2,1,0:T(8,128)S(1)}, u32[]{:S(2)}, u32[]{:S(2)}) collective-permute-start(f32[53,16,256]{2,1,0:T(8,128)S(1)} %get-tuple-element.169.b2), channel_id=1, source_target_pairs={{32,48},{33,49},{34,50},{35,51},{36,52},{37,53},{38,54},{39,55},{4... | collective-permute-start | bytes 2605064 | tf_op jit(solution)/shard_map/ppermute | solution.py:576
  56.5 9.0 %collective-permute-start.11 = (f32[344,256]{1,0:T(8,128)S(1)}, f32[344,256]{1,0:T(8,128)S(1)}, u32[]{:S(2)}, u32[]{:S(2)}) collective-permute-start(f32[344,256]{1,0:T(8,128)S(1)} %get-tuple-element.156), channel_id=1, source_target_pairs={{16,48},{81,65},{18,50},{83,67},{20,52},{85,69},{22,54},{87,71},{2... | collective-permute-start | bytes 1056776 | tf_op jit(solution)/shard_map/ppermute | solution.py:576
  57.2 8.3 %collective-permute-start.12 = (f32[176,256]{1,0:T(8,128)S(1)}, f32[176,256]{1,0:T(8,128)S(1)}, u32[]{:S(2)}, u32[]{:S(2)}) collective-permute-start(f32[176,256]{1,0:T(8,128)S(1)} %get-tuple-element.157), channel_id=1, source_target_pairs={{81,50},{83,52},{85,54},{87,56},{89,58},{91,60},{93,62},{18,65},{2... | collective-permute-start | bytes 540680 | tf_op jit(solution)/shard_map/ppermute | solution.py:576
  57.9 7.6 %collective-permute-start.13 = (f32[176,256]{1,0:T(8,128)S(1)}, f32[176,256]{1,0:T(8,128)S(1)}, u32[]{:S(2)}, u32[]{:S(2)}) collective-permute-start(f32[176,256]{1,0:T(8,128)S(1)} %get-tuple-element.158), channel_id=1, source_target_pairs={{16,65},{81,48},{18,67},{83,50},{20,69},{85,52},{22,71},{87,54},{2... | collective-permute-start | bytes 540680 | tf_op jit(solution)/shard_map/ppermute | solution.py:576
  58.6 10.4 %collective-permute-start.18 = (f32[53,16,256]{2,1,0:T(8,128)S(1)}, f32[53,16,256]{2,1,0:T(8,128)S(1)}, u32[]{:S(2)}, u32[]{:S(2)}) collective-permute-start(f32[53,16,256]{2,1,0:T(8,128)S(1)} %get-tuple-element.169.b2), channel_id=1, source_target_pairs={{48,64},{49,65},{50,66},{51,67},{52,68},{53,69},{54,70},{55,71},{5... | collective-permute-start | bytes 2605064 | tf_op jit(solution)/shard_map/ppermute | solution.py:576
  65.5 19.9 %collective-permute-start.19 = (f32[53,16,256]{2,1,0:T(8,128)S(1)}, f32[53,16,256]{2,1,0:T(8,128)S(1)}, u32[]{:S(2)}, u32[]{:S(2)}) collective-permute-start(f32[53,16,256]{2,1,0:T(8,128)S(1)} %get-tuple-element.169.b2), channel_id=1, source_target_pairs={{0,16},{1,17},{2,18},{3,19},{4,20},{5,21},{6,22},{7,23},{8,24},{9,... | collective-permute-start | bytes 2605064 | tf_op jit(solution)/shard_map/ppermute | solution.py:576
  66.9 2.1 %collective-permute-start.15 = (f32[344,256]{1,0:T(8,128)S(1)}, f32[344,256]{1,0:T(8,128)S(1)}, u32[]{:S(2)}, u32[]{:S(2)}) collective-permute-start(f32[344,256]{1,0:T(8,128)S(1)} %get-tuple-element.165), channel_id=1, source_target_pairs={{48,80},{65,97},{50,82},{67,99},{52,84},{69,101},{54,86},{71,103},... | collective-permute-start | bytes 1056776 | tf_op jit(solution)/shard_map/ppermute | solution.py:576
  67.6 1.4 %collective-permute-start.16 = (f32[176,256]{1,0:T(8,128)S(1)}, f32[176,256]{1,0:T(8,128)S(1)}, u32[]{:S(2)}, u32[]{:S(2)}) collective-permute-start(f32[176,256]{1,0:T(8,128)S(1)} %get-tuple-element.166), channel_id=1, source_target_pairs={{65,82},{67,84},{69,86},{71,88},{73,90},{75,92},{77,94},{50,97},{5... | collective-permute-start | bytes 540680 | tf_op jit(solution)/shard_map/ppermute | solution.py:576
  68.2 0.8 collective-permute-start.17
  85.4 33.2 %copy-start.2 = (s32[53,1]{0,1:T(1,128)S(1)}, s32[53,1]{0,1:T(1,128)}, u32[]{:S(2)}) copy-start(s32[53,1]{0,1:T(1,128)} %param.15) | copy-start | bytes 640
  85.4 33.2 %collective-permute-start.24 = (f32[48,24,256]{2,1,0:T(8,128)S(1)}, f32[48,24,256]{2,1,0:T(8,128)S(1)}, u32[]{:S(2)}, u32[]{:S(2)}) collective-permute-start(f32[48,24,256]{2,1,0:T(8,128)S(1)} %get-tuple-element.206.home), channel_id=1, source_target_pairs={{81,17},{83,19},{85,21},{87,23},{89,25},{91,27},{93,29},{95,31}} | collective-permute-start | bytes 3538952 | tf_op jit(solution)/shard_map/ppermute | solution.py:576
  86.3 32.4 %collective-permute-start.23 = (f32[1016,256]{1,0:T(8,128)S(1)}, f32[1016,256]{1,0:T(8,128)S(1)}, u32[]{:S(2)}, u32[]{:S(2)}) collective-permute-start(f32[1016,256]{1,0:T(8,128)S(1)} %get-tuple-element.201), channel_id=1, source_target_pairs={{16,32},{18,34},{20,36},{22,38},{24,40},{26,42},{28,44},{30,46},{8... | collective-permute-start | bytes 3121160 | tf_op jit(solution)/shard_map/ppermute | solution.py:576
  87.6 2.1 %collective-permute-start.20 = (f32[344,256]{1,0:T(8,128)S(1)}, f32[344,256]{1,0:T(8,128)S(1)}, u32[]{:S(2)}, u32[]{:S(2)}) collective-permute-start(f32[344,256]{1,0:T(8,128)S(1)} %get-tuple-element.191), channel_id=1, source_target_pairs={{80,112},{97,113},{82,114},{99,115},{84,116},{101,117},{86,118},{1... | collective-permute-start | bytes 1056776 | tf_op jit(solution)/shard_map/ppermute | solution.py:576
  88.3 1.4 %collective-permute-start.21 = (f32[88,256]{1,0:T(8,128)S(1)}, f32[88,256]{1,0:T(8,128)S(1)}, u32[]{:S(2)}, u32[]{:S(2)}) collective-permute-start(f32[88,256]{1,0:T(8,128)S(1)} %get-tuple-element.192), channel_id=1, source_target_pairs={{97,114},{99,116},{101,118},{103,120},{105,122},{107,124},{109,126... | collective-permute-start | bytes 270344 | tf_op jit(solution)/shard_map/ppermute | solution.py:576
  88.9 0.7 collective-permute-start.22

commit v12 on v11

--- a/solution.py
+++ b/solution.py
@@ -411,11 +411,9 @@
         sweep(info, ab, A0, ab, B0, message, 0, 0, ROWS, ws, lapm, dc12)
         give(info, 8, message, packed, outer, inner)
 
-        def body(xs):
-            for x in xs:
-                result[x], result[ROWS + x], result[2 * ROWS + x] = zeros(CP), ab[x + A0], message[x]
-
-        blocks(ROWS, body)
+        for part, value in enumerate((lambda x: zeros(CP), lambda x: ab[x + A0], lambda x: message[x])):
+            for x in range(ROWS):
+                put(result, part * ROWS + x, value(x))
 
 
 def pair_kernel(
@@ -441,23 +439,20 @@
         pl.when(hosting(info, hosts) & (info[1] == host))(functools.partial(sweeps, one, two))
 
 
-def gather(zs, za, zb, zc, z2, one, two, away):
-    for at, result in ((0, one), (1, two)):
-        values = [lambda x: zs[x + 8], lambda x: za[x + 6], lambda x: zb[x + 4], lambda x: zc[x + 2], lambda x: z2[x]]
-        for part, value in enumerate(values[2 * at : 2 * at + 3]):
+def gather(zs, za, zb, zc, z2, one, two):
+    values = [lambda x: zs[x + 8], lambda x: za[x + 6], lambda x: zb[x + 4], lambda x: zc[x + 2], lambda x: z2[x]]
+    for result, parts in ((one, values[:3]), (two, values[2:])):
+        for part, value in enumerate(parts):
             for x in range(ROWS):
-                if at == away:
-                    put(result, part * ROWS + x, value(x))
-                else:
-                    result[part * ROWS + x] = value(x)
+                put(result, part * ROWS + x, value(x))
 
 
 def gather_kernel(slices, hosts, zs, za, zb, zc, z2, home_in, away_in, home, away):
     info = Position()
     active, second = hosting(info, hosts), info[1] == slices[1]
-    pl.when(active & ~second)(lambda: gather(zs, za, zb, zc, z2, home, away, 1))
+    pl.when(active & ~second)(lambda: gather(zs, za, zb, zc, z2, home, away))
     if slices[1] in hosts:
-        pl.when(active & second)(lambda: gather(zs, za, zb, zc, z2, away, home, 0))
+        pl.when(active & second)(lambda: gather(zs, za, zb, zc, z2, away, home))
 
 
 def base_kernel(n1, n2, c1, c2, pro, share, b1, b2):
@@ -471,7 +466,7 @@
 
 
 def out_kernel(
-    where, u, b0, late, early, b1, b2, share, z0, zo, zi, ab, ws, lapm, dc12, home, one, other, out, z, za, zs, spread, node, sem
+    where, u, b0, late, b1, b2, share, z0, zo, zi, ab, ws, lapm, dc12, home, one, other, out, z, za, zs, spread, node, sem
 ):
     info = Position()
     last = info[1] == SLICES - 1
@@ -479,21 +474,12 @@
     for slices, hosts in GROUPS[1:-1]:
         at_home = at_home | (hosting(info, hosts) & ((info[1] == slices[0]) | (info[1] == slices[1])))
     first = info[1] == GROUPS[1][0][0]
-    for here, result in ((at_home, home), (first & ~at_home, one)):
+    for here, result in ((at_home, home), (first & ~at_home, one), (~at_home & ~first & ~last, other)):
 
         @pl.when(here)
         def _():
-
-            def body(xs):
-                for x in xs:
-                    z[x] = result[x]
-
-            blocks(3 * ROWS, body)
-
-    @pl.when(~at_home & ~first & ~last)
-    def _():
-        for x in range(3 * ROWS):
-            z[x] = get(other, x)
+            for x in range(3 * ROWS):
+                z[x] = get(result, x)
 
     @pl.when(last)
     def _():
@@ -522,7 +508,7 @@
         return copy
 
     first = info[1] == 0
-    copies = [finish(0, lambda s: jnp.where(first, u[0, s], b0[s] + late[s] + early[s]))]
+    copies = [finish(0, lambda s: jnp.where(first, u[0, s], b0[s] + late[s]))]
 
     @pl.when(last)
     def _():
@@ -659,7 +645,7 @@
     abx, ab = call(last_edge_kernel, "last_edge", [extended, short], outer, inner, ho, hi, abx, alias={4: 0})
 
     ab, abx = after(ab, b1), after(abx, b1)
-    result, away_result = field(3 * ROWS, CP), field(packed_rows(3 * ROWS))
+    packed = field(packed_rows(3 * ROWS))
     bulk, ends = field(packed_rows(ROWS)), field(packed_rows(8))
     pairs = [(slices, hosts) for slices, hosts in GROUPS if len(slices) == 2]
     short, long, back, first = [], [], [], []
@@ -676,7 +662,7 @@
     short, long = moved(ab, *short), moved(abx, *long)
     forward = [(both(p), both(p + 1), SAME) for p in range(SLICES - 1)]
     home, away, *sent = call(
-        functools.partial(start_kernel, GROUPS[0][1]), "start", [result, away_result, bulk, ends, ends], ab, ws, lapm, dc12, scratch=[coarse]
+        functools.partial(start_kernel, GROUPS[0][1]), "start", [packed, packed, bulk, ends, ends], ab, ws, lapm, dc12, scratch=[coarse]
     )
     for at, (slices, hosts) in enumerate(GROUPS[1:], 1):
         z = hop(*sent, GROUPS[at - 1][1], hosts)
@@ -684,12 +670,11 @@
             z = list(lax.optimization_barrier(tuple(z)))
             b0 = moved(after(b2, z[0]), forward[2], forward[6])
             *z, short, long = lax.optimization_barrier((*z, short, long))
-            late = moved(after(b2, z[0]), *forward[3:6])
+            late = moved(after(b2, z[0]), *forward[:2], *forward[3:6])
         elif at == 2:
             *z, b0 = lax.optimization_barrier((*z, b0))
-            early = moved(after(b2, z[0]), *forward[:2])
         elif at == 3:
-            *z, late, early, home, away = lax.optimization_barrier((*z, late, early, home, away))
+            *z, late, home, away = lax.optimization_barrier((*z, late, home, away))
         else:
             other, one = moved(away, *back), moved(home, *first)
             *z, other, one, home = lax.optimization_barrier((*z, other, one, home))
@@ -705,7 +690,7 @@
             home, away = call(
                 functools.partial(gather_kernel, slices, hosts),
                 "gather",
-                [result, away_result],
+                [packed, packed],
                 *(zs, za, zb, zc, z2, home, away),
                 alias={5: 0, 6: 1},
             )
@@ -713,9 +698,9 @@
         out_kernel,
         "out",
         field(3, SPECIES, ROWS),
-        *(species_map[:, 0], nodes, b0, late, early, b1, b2, share, *z, ab, ws, lapm, dc12, home, one, other),
+        *(species_map[:, 0], nodes, b0, late, b1, b2, share, *z, ab, ws, lapm, dc12, home, one, other),
         out_specs=ANY,
-        scratch=[result, field(ROWS + 4, CP), field(ROWS + 8, CP), field(3, CP, ROWS), field(3, SPECIES, ROWS), pltpu.SemaphoreType.DMA((3,))],
+        scratch=[field(3 * ROWS, CP), field(ROWS + 4, CP), field(ROWS + 8, CP), field(3, CP, ROWS), field(3, SPECIES, ROWS), pltpu.SemaphoreType.DMA((3,))],
     )
     return out[None]
 

time: 122 us -> 113 us (0.926)
  the two profiles are of different devices: /device:TPU:77 before, /device:TPU:37 now
where the time goes in v12:
time: 113 us
  waiting for transfers between devices  66.5 us (59%)
  starting transfers between devices  26.6 us (24%)
  Pallas kernels  15.7 us (14%)
  local copies, waits for them, and re-layouts  1.74 us (2%)
  other arithmetic  1.5 us (1%)
    ppermute x24, waiting for transfers between devices, moved(): return lax.ppermute(value, AXES, pairs)  66.5 us
    ppermute x24, starting transfers between devices, moved(): return lax.ppermute(value, AXES, pairs)  26.6 us
    pallas_call x16, Pallas kernels, call(): pl.pallas_call(kernel, out_shape=outs, in_specs=specs, **{'out_specs': ou...  15.7 us
  transfers between devices with their start and end apart: 24, of which 6 were waited for; matrix products, arithmetic and copies ran while one was open for 0% of the time, Pallas kernels for 9%

profile of v12, /device:TPU:37, one launch (start us, length us, event | category | flops | bytes accessed | tf_op | source)
XLA Modules:
  0.0 112.7 jit_solution(8962695721285707495)
XLA Ops:
  0.0 0.7 convert_bitcast_fusion
  0.7 0.8 pad_add_fusion.raw
  1.5 0.4 prep.1
  1.9 0.0 copy-start
  1.9 1.7 %copy-done = f32[1,3,53,16,256]{4,3,2,1,0:T(8,128)S(1)} copy-done((f32[1,3,53,16,256]{4,3,2,1,0:T(8,128)S(1)}, f32[1,3,53,16,256]{4,3,2,1,0:T(8,128)}, u32[]{:S(2)}) %copy-start) | copy-done | bytes 2605080
  3.6 0.4 first.1
  4.1 3.8 %collective-permute-start = (f32[328,256]{1,0:T(8,128)S(1)}, f32[328,256]{1,0:T(8,128)S(1)}, u32[]{:S(2)}, u32[]{:S(2)}) collective-permute-start(f32[328,256]{1,0:T(8,128)S(1)} %get-tuple-element.106), channel_id=1, source_target_pairs={{1,2},{3,4},{5,6},{7,8},{9,10},{11,12},{13,14},{2,1},{4,3},{6,5},{... | collective-permute-start | bytes 1007624 | tf_op jit(solution)/shard_map/ppermute | solution.py:562
  7.9 0.1 collective-permute-start.1
  8.0 6.2 %old.1 = (f32[16,56,256]{2,1,0:T(8,128)S(1)}, f32[16,56,256]{2,1,0:T(8,128)S(1)}, f32[16,24,256]{2,1,0:T(8,128)S(1)}, f32[16,24,256]{2,1,0:T(8,128)S(1)}, f32[16,24,256]{2,1,0:T(8,128)S(1)}) custom-call(f32[3,53,16,256]{3,2,1,0:T(8,128)S(1)} %bitcast.8, bf16[112,224]{1,0:T(8,128)(2,1)S(1)} %get-tuple-element.111.wf, ...), custom_call_target="tpu_custom_call" | custom-call | tf_op jit(solution)/shard_map/old/pallas_call | solution.py:540
  14.3 4.3 %collective-permute-done.uo = f32[328,256]{1,0:T(8,128)S(1)} collective-permute-done((f32[328,256]{1,0:T(8,128)S(1)}, f32[328,256]{1,0:T(8,128)S(1)}, u32[]{:S(2)}, u32[]{:S(2)}) %collective-permute-start) | collective-permute-done | bytes 335904 | tf_op jit(solution)/shard_map/ppermute | solution.py:562
  18.6 0.0 collective-permute-done.1.ui
  18.6 0.5 old_edge.1
  19.1 2.9 %collective-permute-start.2 = (f32[2,56,256]{2,1,0:T(8,128)S(1)}, f32[2,56,256]{2,1,0:T(8,128)S(1)}, u32[]{:S(2)}, u32[]{:S(2)}) collective-permute-start(f32[2,56,256]{2,1,0:T(8,128)S(1)} %get-tuple-element.117), channel_id=1, source_target_pairs={{1,2},{3,4},{5,6},{7,8},{9,10},{11,12},{13,14},{2,1},{4,3},{6,5},{... | collective-permute-start | bytes 344072 | tf_op jit(solution)/shard_map/ppermute | solution.py:562
  21.9 0.1 collective-permute-start.3
  22.0 2.6 %mid.1 = (f32[16,56,256]{2,1,0:T(8,128)S(1)}, f32[16,24,256]{2,1,0:T(8,128)S(1)}, f32[16,24,256]{2,1,0:T(8,128)S(1)}, f32[16,24,256]{2,1,0:T(8,128)S(1)}) custom-call(f32[16,56,256]{2,1,0:T(8,128)S(1)} %get-tuple-element.122.n1, f32[16,56,256]{2,1,0:T(8,128)S(1)} %get-tuple-element.123.s, bf16[240,224]{1,0:T(8,128)(2,1)S(1)} %get-tuple-element.124.wfr, ...), custom_call_target="tpu_custom_call" | custom-call | tf_op jit(solution)/shard_map/mid/pallas_call | solution.py:540
  24.7 3.3 %collective-permute-done.2.no = f32[2,56,256]{2,1,0:T(8,128)S(1)} collective-permute-done((f32[2,56,256]{2,1,0:T(8,128)S(1)}, f32[2,56,256]{2,1,0:T(8,128)S(1)}, u32[]{:S(2)}, u32[]{:S(2)}) %collective-permute-start.2) | collective-permute-done | bytes 114720 | tf_op jit(solution)/shard_map/ppermute | solution.py:562
  28.0 1.1 mid_edge.1
  29.1 2.4 %collective-permute-start.4 = (f32[256,256]{1,0:T(8,128)S(1)}, f32[256,256]{1,0:T(8,128)S(1)}, u32[]{:S(2)}, u32[]{:S(2)}) collective-permute-start(f32[256,256]{1,0:T(8,128)S(1)} %get-tuple-element.128.mo), channel_id=1, source_target_pairs={{1,2},{3,4},{5,6},{7,8},{9,10},{11,12},{13,14},{2,1},{4,3},{6,5},{... | collective-permute-start | bytes 786440 | tf_op jit(solution)/shard_map/ppermute | solution.py:562
  31.5 0.1 collective-permute-start.5
  31.6 1.5 %base.1 = (f32[53,16,256]{2,1,0:T(8,128)S(1)}, f32[53,16,256]{2,1,0:T(8,128)S(1)}) custom-call(f32[16,56,256]{2,1,0:T(8,128)S(1)} %get-tuple-element.122.n1, f32[16,56,256]{2,1,0:T(8,128)S(1)} %get-tuple-element.132.n2, f32[16,24,256]{2,1,0:T(8,128)S(1)} %get-tuple-element.133.c1, f32[16,24,256]{2,1,0:T(8,128)S(1)} %get-tuple-element.134.c2, ...), custom_call_target="tpu_custom_call" | custom-call | tf_op jit(solution)/shard_map/base/pallas_call | solution.py:540
  33.1 7.2 %collective-permute-done.4.ho = f32[256,256]{1,0:T(8,128)S(1)} collective-permute-done((f32[256,256]{1,0:T(8,128)S(1)}, f32[256,256]{1,0:T(8,128)S(1)}, u32[]{:S(2)}, u32[]{:S(2)}) %collective-permute-start.4) | collective-permute-done | bytes 262176 | tf_op jit(solution)/shard_map/ppermute | solution.py:562
  40.3 0.0 collective-permute-done.5.hi
  40.3 0.2 last_edge.1
  40.6 2.9 %collective-permute-start.10 = (f32[52,24,256]{2,1,0:T(8,128)S(1)}, f32[52,24,256]{2,1,0:T(8,128)S(1)}, u32[]{:S(2)}, u32[]{:S(2)}) collective-permute-start(f32[52,24,256]{2,1,0:T(8,128)S(1)} %get-tuple-element.148.mine), channel_id=1, source_target_pairs={{17,81},{19,83},{21,85},{23,87},{25,89},{27,91},{29,93},{31,95},{4... | collective-permute-start | bytes 3833864 | tf_op jit(solution)/shard_map/ppermute | solution.py:562
  43.5 0.7 collective-permute-start.9
  44.2 0.7 collective-permute-start.6
  44.9 0.7 collective-permute-start.7
  45.6 0.7 collective-permute-start.8
  46.3 0.0 collective-permute-done.7.zo
  46.3 0.0 collective-permute-done.8.zi
  46.3 0.7 collective-permute-start.14
  47.1 10.5 %collective-permute-done.10.long = f32[52,24,256]{2,1,0:T(8,128)S(1)} collective-permute-done((f32[52,24,256]{2,1,0:T(8,128)S(1)}, f32[52,24,256]{2,1,0:T(8,128)S(1)}, u32[]{:S(2)}, u32[]{:S(2)}) %collective-permute-start.10) | collective-permute-done | bytes 1277984 | tf_op jit(solution)/shard_map/ppermute | solution.py:562
  57.6 2.5 %collective-permute-start.18 = (f32[53,16,256]{2,1,0:T(8,128)S(1)}, f32[53,16,256]{2,1,0:T(8,128)S(1)}, u32[]{:S(2)}, u32[]{:S(2)}) collective-permute-start(f32[53,16,256]{2,1,0:T(8,128)S(1)} %get-tuple-element.166.b2), channel_id=1, source_target_pairs={{0,16},{1,17},{2,18},{3,19},{4,20},{5,21},{6,22},{7,23},{8,24},{9,... | collective-permute-start | bytes 2605064 | tf_op jit(solution)/shard_map/ppermute | solution.py:562
  60.1 0.9 collective-permute-start.11
  61.0 0.7 collective-permute-start.12
  61.7 0.7 collective-permute-start.13
  62.4 0.0 collective-permute-done.13.zi
  62.4 0.7 collective-permute-start.15
  63.1 0.7 collective-permute-start.16
  63.8 0.7 collective-permute-start.17
  64.6 15.9 %collective-permute-done.18.late = f32[53,16,256]{2,1,0:T(8,128)S(1)} collective-permute-done((f32[53,16,256]{2,1,0:T(8,128)S(1)}, f32[53,16,256]{2,1,0:T(8,128)S(1)}, u32[]{:S(2)}, u32[]{:S(2)}) %collective-permute-start.18) | collective-permute-done | bytes 868384 | tf_op jit(solution)/shard_map/ppermute | solution.py:562
  80.4 0.8 collective-permute-start.22
  81.3 1.3 %collective-permute-start.23 = (f32[1016,256]{1,0:T(8,128)S(1)}, f32[1016,256]{1,0:T(8,128)S(1)}, u32[]{:S(2)}, u32[]{:S(2)}) collective-permute-start(f32[1016,256]{1,0:T(8,128)S(1)} %get-tuple-element.202.home), channel_id=1, source_target_pairs={{81,17},{83,19},{85,21},{87,23},{89,25},{91,27},{93,29},{95,31}} | collective-permute-start | bytes 3121160 | tf_op jit(solution)/shard_map/ppermute | solution.py:562
  82.6 0.7 collective-permute-start.19
  83.3 0.7 collective-permute-start.20
  84.0 0.7 collective-permute-start.21
  84.7 25.2 %collective-permute-done.23.one = f32[1016,256]{1,0:T(8,128)S(1)} collective-permute-done((f32[1016,256]{1,0:T(8,128)S(1)}, f32[1016,256]{1,0:T(8,128)S(1)}, u32[]{:S(2)}, u32[]{:S(2)}) %collective-permute-start.23) | collective-permute-done | bytes 1040416 | tf_op jit(solution)/shard_map/ppermute | solution.py:562
  109.9 2.6 %out.1 = f32[3,53,16,256]{3,2,1,0:T(8,128)} custom-call(s32[53]{0:T(128)S(1)} %bitcast.10, f32[3,53,16,256]{3,2,1,0:T(8,128)S(1)} %bitcast.9, f32[53,16,256]{2,1,0:T(8,128)S(1)} %collective-permute-done.14.b0, f32[53,16,256]{2,1,0:T(8,128)S(1)} %collective-permute-done.18.late, f32[53,16,256]{2,1,0:T(8,128)S(1)} %get-tuple-element.137.b1, ...), custom_call_target="tpu_custom_call" | custom-call | tf_op jit(solution)/shard_map/out/pallas_call | solution.py:540
  (24 shorter events, 0.2 us)
Async XLA Ops:
  1.9 1.7 %copy-start = (f32[1,3,53,16,256]{4,3,2,1,0:T(8,128)S(1)}, f32[1,3,53,16,256]{4,3,2,1,0:T(8,128)}, u32[]{:S(2)}) copy-start(f32[1,3,53,16,256]{4,3,2,1,0:T(8,128)} %param.8) | copy-start | bytes 7815172
  3.6 4.4 %copy-start.1 = (f32[1,3,53,16,256]{4,3,2,1,0:T(8,128)S(1)}, f32[1,3,53,16,256]{4,3,2,1,0:T(8,128)}, u32[]{:S(2)}) copy-start(f32[1,3,53,16,256]{4,3,2,1,0:T(8,128)} %param.8) | copy-start | bytes 7815172
  4.1 14.5 %collective-permute-start = (f32[328,256]{1,0:T(8,128)S(1)}, f32[328,256]{1,0:T(8,128)S(1)}, u32[]{:S(2)}, u32[]{:S(2)}) collective-permute-start(f32[328,256]{1,0:T(8,128)S(1)} %get-tuple-element.106), channel_id=1, source_target_pairs={{1,2},{3,4},{5,6},{7,8},{9,10},{11,12},{13,14},{2,1},{4,3},{6,5},{... | collective-permute-start | bytes 1007624 | tf_op jit(solution)/shard_map/ppermute | solution.py:562
  7.9 10.7 %collective-permute-start.1 = (f32[328,256]{1,0:T(8,128)S(1)}, f32[328,256]{1,0:T(8,128)S(1)}, u32[]{:S(2)}, u32[]{:S(2)}) collective-permute-start(f32[328,256]{1,0:T(8,128)S(1)} %get-tuple-element.107), channel_id=1, source_target_pairs={{0,1},{1,0},{2,3},{3,2},{4,5},{5,4},{6,7},{7,6},{8,9},{9,8},{10,11... | collective-permute-start | bytes 1007624 | tf_op jit(solution)/shard_map/ppermute | solution.py:562
  19.1 9.0 %collective-permute-start.2 = (f32[2,56,256]{2,1,0:T(8,128)S(1)}, f32[2,56,256]{2,1,0:T(8,128)S(1)}, u32[]{:S(2)}, u32[]{:S(2)}) collective-permute-start(f32[2,56,256]{2,1,0:T(8,128)S(1)} %get-tuple-element.117), channel_id=1, source_target_pairs={{1,2},{3,4},{5,6},{7,8},{9,10},{11,12},{13,14},{2,1},{4,3},{6,5},{... | collective-permute-start | bytes 344072 | tf_op jit(solution)/shard_map/ppermute | solution.py:562
  21.9 6.1 %collective-permute-start.3 = (f32[2,56,256]{2,1,0:T(8,128)S(1)}, f32[2,56,256]{2,1,0:T(8,128)S(1)}, u32[]{:S(2)}, u32[]{:S(2)}) collective-permute-start(f32[2,56,256]{2,1,0:T(8,128)S(1)} %get-tuple-element.118), channel_id=1, source_target_pairs={{0,1},{1,0},{2,3},{3,2},{4,5},{5,4},{6,7},{7,6},{8,9},{9,8},{10,11... | collective-permute-start | bytes 344072 | tf_op jit(solution)/shard_map/ppermute | solution.py:562
  29.1 11.2 %collective-permute-start.4 = (f32[256,256]{1,0:T(8,128)S(1)}, f32[256,256]{1,0:T(8,128)S(1)}, u32[]{:S(2)}, u32[]{:S(2)}) collective-permute-start(f32[256,256]{1,0:T(8,128)S(1)} %get-tuple-element.128.mo), channel_id=1, source_target_pairs={{1,2},{3,4},{5,6},{7,8},{9,10},{11,12},{13,14},{2,1},{4,3},{6,5},{... | collective-permute-start | bytes 786440 | tf_op jit(solution)/shard_map/ppermute | solution.py:562
  31.5 8.8 %collective-permute-start.5 = (f32[256,256]{1,0:T(8,128)S(1)}, f32[256,256]{1,0:T(8,128)S(1)}, u32[]{:S(2)}, u32[]{:S(2)}) collective-permute-start(f32[256,256]{1,0:T(8,128)S(1)} %get-tuple-element.129.mi), channel_id=1, source_target_pairs={{0,1},{1,0},{2,3},{3,2},{4,5},{5,4},{6,7},{7,6},{8,9},{9,8},{10,11... | collective-permute-start | bytes 786440 | tf_op jit(solution)/shard_map/ppermute | solution.py:562
  40.6 17.0 %collective-permute-start.10 = (f32[52,24,256]{2,1,0:T(8,128)S(1)}, f32[52,24,256]{2,1,0:T(8,128)S(1)}, u32[]{:S(2)}, u32[]{:S(2)}) collective-permute-start(f32[52,24,256]{2,1,0:T(8,128)S(1)} %get-tuple-element.148.mine), channel_id=1, source_target_pairs={{17,81},{19,83},{21,85},{23,87},{25,89},{27,91},{29,93},{31,95},{4... | collective-permute-start | bytes 3833864 | tf_op jit(solution)/shard_map/ppermute | solution.py:562
  43.5 3.6 %collective-permute-start.9 = (f32[36,24,256]{2,1,0:T(8,128)S(1)}, f32[36,24,256]{2,1,0:T(8,128)S(1)}, u32[]{:S(2)}, u32[]{:S(2)}) collective-permute-start(f32[36,24,256]{2,1,0:T(8,128)S(1)} %get-tuple-element.138.ab), channel_id=1, source_target_pairs={{32,16},{34,18},{36,20},{38,22},{40,24},{42,26},{44,28},{46,30},{3... | collective-permute-start | bytes 2654216 | tf_op jit(solution)/shard_map/ppermute | solution.py:562
  44.2 2.1 %collective-permute-start.6 = (f32[344,256]{1,0:T(8,128)S(1)}, f32[344,256]{1,0:T(8,128)S(1)}, u32[]{:S(2)}, u32[]{:S(2)}) collective-permute-start(f32[344,256]{1,0:T(8,128)S(1)} %get-tuple-element.141), channel_id=1, source_target_pairs={{0,16},{1,81},{2,18},{3,83},{4,20},{5,85},{6,22},{7,87},{8,24},{9,... | collective-permute-start | bytes 1056776 | tf_op jit(solution)/shard_map/ppermute | solution.py:562
  44.9 1.4 %collective-permute-start.7 = (f32[176,256]{1,0:T(8,128)S(1)}, f32[176,256]{1,0:T(8,128)S(1)}, u32[]{:S(2)}, u32[]{:S(2)}) collective-permute-start(f32[176,256]{1,0:T(8,128)S(1)} %get-tuple-element.142), channel_id=1, source_target_pairs={{1,18},{3,20},{5,22},{7,24},{9,26},{11,28},{13,30},{2,81},{4,83},{... | collective-permute-start | bytes 540680 | tf_op jit(solution)/shard_map/ppermute | solution.py:562
  45.6 0.7 collective-permute-start.8
  46.3 16.0 %collective-permute-start.14 = (f32[53,16,256]{2,1,0:T(8,128)S(1)}, f32[53,16,256]{2,1,0:T(8,128)S(1)}, u32[]{:S(2)}, u32[]{:S(2)}) collective-permute-start(f32[53,16,256]{2,1,0:T(8,128)S(1)} %get-tuple-element.166.b2), channel_id=1, source_target_pairs={{32,48},{33,49},{34,50},{35,51},{36,52},{37,53},{38,54},{39,55},{4... | collective-permute-start | bytes 2605064 | tf_op jit(solution)/shard_map/ppermute | solution.py:562
  57.6 22.8 %collective-permute-start.18 = (f32[53,16,256]{2,1,0:T(8,128)S(1)}, f32[53,16,256]{2,1,0:T(8,128)S(1)}, u32[]{:S(2)}, u32[]{:S(2)}) collective-permute-start(f32[53,16,256]{2,1,0:T(8,128)S(1)} %get-tuple-element.166.b2), channel_id=1, source_target_pairs={{0,16},{1,17},{2,18},{3,19},{4,20},{5,21},{6,22},{7,23},{8,24},{9,... | collective-permute-start | bytes 2605064 | tf_op jit(solution)/shard_map/ppermute | solution.py:562
  60.1 2.3 %collective-permute-start.11 = (f32[344,256]{1,0:T(8,128)S(1)}, f32[344,256]{1,0:T(8,128)S(1)}, u32[]{:S(2)}, u32[]{:S(2)}) collective-permute-start(f32[344,256]{1,0:T(8,128)S(1)} %get-tuple-element.154), channel_id=1, source_target_pairs={{16,48},{81,65},{18,50},{83,67},{20,52},{85,69},{22,54},{87,71},{2... | collective-permute-start | bytes 1056776 | tf_op jit(solution)/shard_map/ppermute | solution.py:562
  61.0 1.4 %collective-permute-start.12 = (f32[176,256]{1,0:T(8,128)S(1)}, f32[176,256]{1,0:T(8,128)S(1)}, u32[]{:S(2)}, u32[]{:S(2)}) collective-permute-start(f32[176,256]{1,0:T(8,128)S(1)} %get-tuple-element.155), channel_id=1, source_target_pairs={{81,50},{83,52},{85,54},{87,56},{89,58},{91,60},{93,62},{18,65},{2... | collective-permute-start | bytes 540680 | tf_op jit(solution)/shard_map/ppermute | solution.py:562
  61.7 0.7 collective-permute-start.13
  62.4 2.1 %collective-permute-start.15 = (f32[344,256]{1,0:T(8,128)S(1)}, f32[344,256]{1,0:T(8,128)S(1)}, u32[]{:S(2)}, u32[]{:S(2)}) collective-permute-start(f32[344,256]{1,0:T(8,128)S(1)} %get-tuple-element.163), channel_id=1, source_target_pairs={{48,80},{65,97},{50,82},{67,99},{52,84},{69,101},{54,86},{71,103},... | collective-permute-start | bytes 1056776 | tf_op jit(solution)/shard_map/ppermute | solution.py:562
  63.1 1.4 %collective-permute-start.16 = (f32[176,256]{1,0:T(8,128)S(1)}, f32[176,256]{1,0:T(8,128)S(1)}, u32[]{:S(2)}, u32[]{:S(2)}) collective-permute-start(f32[176,256]{1,0:T(8,128)S(1)} %get-tuple-element.164), channel_id=1, source_target_pairs={{65,82},{67,84},{69,86},{71,88},{73,90},{75,92},{77,94},{50,97},{5... | collective-permute-start | bytes 540680 | tf_op jit(solution)/shard_map/ppermute | solution.py:562
  63.8 0.8 collective-permute-start.17
  80.4 29.5 %copy-start.2 = (s32[53,1]{0,1:T(1,128)S(1)}, s32[53,1]{0,1:T(1,128)}, u32[]{:S(2)}) copy-start(s32[53,1]{0,1:T(1,128)} %param.15) | copy-start | bytes 640
  80.4 4.2 %collective-permute-start.22 = (f32[1016,256]{1,0:T(8,128)S(1)}, f32[1016,256]{1,0:T(8,128)S(1)}, u32[]{:S(2)}, u32[]{:S(2)}) collective-permute-start(f32[1016,256]{1,0:T(8,128)S(1)} %get-tuple-element.197), channel_id=1, source_target_pairs={{16,32},{18,34},{20,36},{22,38},{24,40},{26,42},{28,44},{30,46},{8... | collective-permute-start | bytes 3121160 | tf_op jit(solution)/shard_map/ppermute | solution.py:562
  81.3 28.6 %collective-permute-start.23 = (f32[1016,256]{1,0:T(8,128)S(1)}, f32[1016,256]{1,0:T(8,128)S(1)}, u32[]{:S(2)}, u32[]{:S(2)}) collective-permute-start(f32[1016,256]{1,0:T(8,128)S(1)} %get-tuple-element.202.home), channel_id=1, source_target_pairs={{81,17},{83,19},{85,21},{87,23},{89,25},{91,27},{93,29},{95,31}} | collective-permute-start | bytes 3121160 | tf_op jit(solution)/shard_map/ppermute | solution.py:562
  82.6 2.1 %collective-permute-start.19 = (f32[344,256]{1,0:T(8,128)S(1)}, f32[344,256]{1,0:T(8,128)S(1)}, u32[]{:S(2)}, u32[]{:S(2)}) collective-permute-start(f32[344,256]{1,0:T(8,128)S(1)} %get-tuple-element.187), channel_id=1, source_target_pairs={{80,112},{97,113},{82,114},{99,115},{84,116},{101,117},{86,118},{1... | collective-permute-start | bytes 1056776 | tf_op jit(solution)/shard_map/ppermute | solution.py:562
  83.3 1.4 %collective-permute-start.20 = (f32[88,256]{1,0:T(8,128)S(1)}, f32[88,256]{1,0:T(8,128)S(1)}, u32[]{:S(2)}, u32[]{:S(2)}) collective-permute-start(f32[88,256]{1,0:T(8,128)S(1)} %get-tuple-element.188), channel_id=1, source_target_pairs={{97,114},{99,116},{101,118},{103,120},{105,122},{107,124},{109,126... | collective-permute-start | bytes 270344 | tf_op jit(solution)/shard_map/ppermute | solution.py:562
  84.0 0.7 collective-permute-start.21

commit v13 on v11

--- a/solution.py
+++ b/solution.py
@@ -471,7 +471,7 @@
 
 
 def out_kernel(
-    where, u, b0, late, early, b1, b2, share, z0, zo, zi, ab, ws, lapm, dc12, home, one, other, out, z, za, zs, spread, node, sem
+    where, u, b0, late, b1, b2, share, z0, zo, zi, ab, ws, lapm, dc12, home, one, other, out, z, za, zs, spread, node, sem
 ):
     info = Position()
     last = info[1] == SLICES - 1
@@ -522,7 +522,7 @@
         return copy
 
     first = info[1] == 0
-    copies = [finish(0, lambda s: jnp.where(first, u[0, s], b0[s] + late[s] + early[s]))]
+    copies = [finish(0, lambda s: jnp.where(first, u[0, s], b0[s] + late[s]))]
 
     @pl.when(last)
     def _():
@@ -684,12 +684,11 @@
             z = list(lax.optimization_barrier(tuple(z)))
             b0 = moved(after(b2, z[0]), forward[2], forward[6])
             *z, short, long = lax.optimization_barrier((*z, short, long))
-            late = moved(after(b2, z[0]), *forward[3:6])
+            late = moved(after(b2, z[0]), *forward[:2], *forward[3:6])
         elif at == 2:
             *z, b0 = lax.optimization_barrier((*z, b0))
-            early = moved(after(b2, z[0]), *forward[:2])
         elif at == 3:
-            *z, late, early, home, away = lax.optimization_barrier((*z, late, early, home, away))
+            *z, late, home, away = lax.optimization_barrier((*z, late, home, away))
         else:
             other, one = moved(away, *back), moved(home, *first)
             *z, other, one, home = lax.optimization_barrier((*z, other, one, home))
@@ -713,7 +712,7 @@
         out_kernel,
         "out",
         field(3, SPECIES, ROWS),
-        *(species_map[:, 0], nodes, b0, late, early, b1, b2, share, *z, ab, ws, lapm, dc12, home, one, other),
+        *(species_map[:, 0], nodes, b0, late, b1, b2, share, *z, ab, ws, lapm, dc12, home, one, other),
         out_specs=ANY,
         scratch=[result, field(ROWS + 4, CP), field(ROWS + 8, CP), field(3, CP, ROWS), field(3, SPECIES, ROWS), pltpu.SemaphoreType.DMA((3,))],
     )

time: 122 us -> 114 us (0.934)
  the two profiles are of different devices: /device:TPU:77 before, /device:TPU:69 now
where the time goes in v13:
time: 114 us; the launch traced here: 113 us
  waiting for transfers between devices  65.1 us (57%)
  starting transfers between devices  28.5 us (25%)
  Pallas kernels  15.7 us (14%)
  local copies, waits for them, and re-layouts  1.74 us (2%)
  other arithmetic  1.5 us (1%)
    ppermute x24, waiting for transfers between devices, moved(): return lax.ppermute(value, AXES, pairs)  65.1 us
    ppermute x24, starting transfers between devices, moved(): return lax.ppermute(value, AXES, pairs)  28.5 us
    pallas_call x16, Pallas kernels, call(): pl.pallas_call(kernel, out_shape=outs, in_specs=specs, **{'out_specs': ou...  15.7 us
  transfers between devices with their start and end apart: 24, of which 7 were waited for; matrix products, arithmetic and copies ran while one was open for 0% of the time, Pallas kernels for 9%

profile of v13, /device:TPU:69, one launch (start us, length us, event | category | flops | bytes accessed | tf_op | source)
XLA Modules:
  0.0 113.0 jit_solution(8472031317212278052)
XLA Ops:
  0.0 0.7 convert_bitcast_fusion
  0.7 0.8 pad_add_fusion.raw
  1.5 0.4 prep.1
  1.9 0.0 copy-start
  1.9 1.7 %copy-done = f32[1,3,53,16,256]{4,3,2,1,0:T(8,128)S(1)} copy-done((f32[1,3,53,16,256]{4,3,2,1,0:T(8,128)S(1)}, f32[1,3,53,16,256]{4,3,2,1,0:T(8,128)}, u32[]{:S(2)}) %copy-start) | copy-done | bytes 2605080
  3.6 0.4 first.1
  4.0 3.8 %collective-permute-start = (f32[328,256]{1,0:T(8,128)S(1)}, f32[328,256]{1,0:T(8,128)S(1)}, u32[]{:S(2)}, u32[]{:S(2)}) collective-permute-start(f32[328,256]{1,0:T(8,128)S(1)} %get-tuple-element.106), channel_id=1, source_target_pairs={{1,2},{3,4},{5,6},{7,8},{9,10},{11,12},{13,14},{2,1},{4,3},{6,5},{... | collective-permute-start | bytes 1007624 | tf_op jit(solution)/shard_map/ppermute | solution.py:576
  7.9 0.1 collective-permute-start.1
  8.0 6.3 %old.1 = (f32[16,56,256]{2,1,0:T(8,128)S(1)}, f32[16,56,256]{2,1,0:T(8,128)S(1)}, f32[16,24,256]{2,1,0:T(8,128)S(1)}, f32[16,24,256]{2,1,0:T(8,128)S(1)}, f32[16,24,256]{2,1,0:T(8,128)S(1)}) custom-call(f32[3,53,16,256]{3,2,1,0:T(8,128)S(1)} %bitcast.8, bf16[112,224]{1,0:T(8,128)(2,1)S(1)} %get-tuple-element.111.wf, ...), custom_call_target="tpu_custom_call" | custom-call | tf_op jit(solution)/shard_map/old/pallas_call | solution.py:554
  14.3 4.3 %collective-permute-done.uo = f32[328,256]{1,0:T(8,128)S(1)} collective-permute-done((f32[328,256]{1,0:T(8,128)S(1)}, f32[328,256]{1,0:T(8,128)S(1)}, u32[]{:S(2)}, u32[]{:S(2)}) %collective-permute-start) | collective-permute-done | bytes 335904 | tf_op jit(solution)/shard_map/ppermute | solution.py:576
  18.6 0.0 collective-permute-done.1.ui
  18.6 0.5 old_edge.1
  19.1 2.9 %collective-permute-start.2 = (f32[2,56,256]{2,1,0:T(8,128)S(1)}, f32[2,56,256]{2,1,0:T(8,128)S(1)}, u32[]{:S(2)}, u32[]{:S(2)}) collective-permute-start(f32[2,56,256]{2,1,0:T(8,128)S(1)} %get-tuple-element.117), channel_id=1, source_target_pairs={{1,2},{3,4},{5,6},{7,8},{9,10},{11,12},{13,14},{2,1},{4,3},{6,5},{... | collective-permute-start | bytes 344072 | tf_op jit(solution)/shard_map/ppermute | solution.py:576
  21.9 0.1 collective-permute-start.3
  22.0 2.6 %mid.1 = (f32[16,56,256]{2,1,0:T(8,128)S(1)}, f32[16,24,256]{2,1,0:T(8,128)S(1)}, f32[16,24,256]{2,1,0:T(8,128)S(1)}, f32[16,24,256]{2,1,0:T(8,128)S(1)}) custom-call(f32[16,56,256]{2,1,0:T(8,128)S(1)} %get-tuple-element.122.n1, f32[16,56,256]{2,1,0:T(8,128)S(1)} %get-tuple-element.123.s, bf16[240,224]{1,0:T(8,128)(2,1)S(1)} %get-tuple-element.124.wfr, ...), custom_call_target="tpu_custom_call" | custom-call | tf_op jit(solution)/shard_map/mid/pallas_call | solution.py:554
  24.7 3.4 %collective-permute-done.2.no = f32[2,56,256]{2,1,0:T(8,128)S(1)} collective-permute-done((f32[2,56,256]{2,1,0:T(8,128)S(1)}, f32[2,56,256]{2,1,0:T(8,128)S(1)}, u32[]{:S(2)}, u32[]{:S(2)}) %collective-permute-start.2) | collective-permute-done | bytes 114720 | tf_op jit(solution)/shard_map/ppermute | solution.py:576
  28.0 1.1 mid_edge.1
  29.1 2.4 %collective-permute-start.4 = (f32[256,256]{1,0:T(8,128)S(1)}, f32[256,256]{1,0:T(8,128)S(1)}, u32[]{:S(2)}, u32[]{:S(2)}) collective-permute-start(f32[256,256]{1,0:T(8,128)S(1)} %get-tuple-element.128.mo), channel_id=1, source_target_pairs={{1,2},{3,4},{5,6},{7,8},{9,10},{11,12},{13,14},{2,1},{4,3},{6,5},{... | collective-permute-start | bytes 786440 | tf_op jit(solution)/shard_map/ppermute | solution.py:576
  31.6 0.1 collective-permute-start.5
  31.6 1.5 %base.1 = (f32[53,16,256]{2,1,0:T(8,128)S(1)}, f32[53,16,256]{2,1,0:T(8,128)S(1)}) custom-call(f32[16,56,256]{2,1,0:T(8,128)S(1)} %get-tuple-element.122.n1, f32[16,56,256]{2,1,0:T(8,128)S(1)} %get-tuple-element.132.n2, f32[16,24,256]{2,1,0:T(8,128)S(1)} %get-tuple-element.133.c1, f32[16,24,256]{2,1,0:T(8,128)S(1)} %get-tuple-element.134.c2, ...), custom_call_target="tpu_custom_call" | custom-call | tf_op jit(solution)/shard_map/base/pallas_call | solution.py:554
  33.1 7.2 %collective-permute-done.4.ho = f32[256,256]{1,0:T(8,128)S(1)} collective-permute-done((f32[256,256]{1,0:T(8,128)S(1)}, f32[256,256]{1,0:T(8,128)S(1)}, u32[]{:S(2)}, u32[]{:S(2)}) %collective-permute-start.4) | collective-permute-done | bytes 262176 | tf_op jit(solution)/shard_map/ppermute | solution.py:576
  40.3 0.2 last_edge.1
  40.6 0.7 collective-permute-start.10
  41.3 5.2 %collective-permute-start.9 = (f32[36,24,256]{2,1,0:T(8,128)S(1)}, f32[36,24,256]{2,1,0:T(8,128)S(1)}, u32[]{:S(2)}, u32[]{:S(2)}) collective-permute-start(f32[36,24,256]{2,1,0:T(8,128)S(1)} %get-tuple-element.138.ab), channel_id=1, source_target_pairs={{32,16},{34,18},{36,20},{38,22},{40,24},{42,26},{44,28},{46,30},{3... | collective-permute-start | bytes 2654216 | tf_op jit(solution)/shard_map/ppermute | solution.py:576
  46.6 0.7 collective-permute-start.6
  47.3 0.7 collective-permute-start.7
  48.0 0.7 collective-permute-start.8
  48.7 0.0 collective-permute-done.8.zi
  48.7 0.0 collective-permute-done.6.z0
  48.7 1.3 %collective-permute-start.14 = (f32[53,16,256]{2,1,0:T(8,128)S(1)}, f32[53,16,256]{2,1,0:T(8,128)S(1)}, u32[]{:S(2)}, u32[]{:S(2)}) collective-permute-start(f32[53,16,256]{2,1,0:T(8,128)S(1)} %get-tuple-element.166.b2), channel_id=1, source_target_pairs={{32,48},{33,49},{34,50},{35,51},{36,52},{37,53},{38,54},{39,55},{4... | collective-permute-start | bytes 2605064 | tf_op jit(solution)/shard_map/ppermute | solution.py:576
  50.0 6.5 %collective-permute-done.9.short = f32[36,24,256]{2,1,0:T(8,128)S(1)} collective-permute-done((f32[36,24,256]{2,1,0:T(8,128)S(1)}, f32[36,24,256]{2,1,0:T(8,128)S(1)}, u32[]{:S(2)}, u32[]{:S(2)}) %collective-permute-start.9) | collective-permute-done | bytes 884768 | tf_op jit(solution)/shard_map/ppermute | solution.py:576
  56.5 1.3 %collective-permute-start.18 = (f32[53,16,256]{2,1,0:T(8,128)S(1)}, f32[53,16,256]{2,1,0:T(8,128)S(1)}, u32[]{:S(2)}, u32[]{:S(2)}) collective-permute-start(f32[53,16,256]{2,1,0:T(8,128)S(1)} %get-tuple-element.166.b2), channel_id=1, source_target_pairs={{0,16},{1,17},{2,18},{3,19},{4,20},{5,21},{6,22},{7,23},{8,24},{9,... | collective-permute-start | bytes 2605064 | tf_op jit(solution)/shard_map/ppermute | solution.py:576
  57.9 0.7 collective-permute-start.11
  58.6 0.9 collective-permute-start.12
  59.4 0.7 collective-permute-start.13
  60.1 2.6 %collective-permute-done.14.b0 = f32[53,16,256]{2,1,0:T(8,128)S(1)} collective-permute-done((f32[53,16,256]{2,1,0:T(8,128)S(1)}, f32[53,16,256]{2,1,0:T(8,128)S(1)}, u32[]{:S(2)}, u32[]{:S(2)}) %collective-permute-start.14) | collective-permute-done | bytes 868384 | tf_op jit(solution)/shard_map/ppermute | solution.py:576
  62.7 0.0 collective-permute-done.12.zo
  62.7 0.7 collective-permute-start.15
  63.4 0.7 collective-permute-start.16
  64.1 0.7 collective-permute-start.17
  64.9 14.2 %collective-permute-done.18.late = f32[53,16,256]{2,1,0:T(8,128)S(1)} collective-permute-done((f32[53,16,256]{2,1,0:T(8,128)S(1)}, f32[53,16,256]{2,1,0:T(8,128)S(1)}, u32[]{:S(2)}, u32[]{:S(2)}) %collective-permute-start.18) | collective-permute-done | bytes 868384 | tf_op jit(solution)/shard_map/ppermute | solution.py:576
  79.0 0.9 collective-permute-start.23
  79.9 1.3 %collective-permute-start.22 = (f32[1016,256]{1,0:T(8,128)S(1)}, f32[1016,256]{1,0:T(8,128)S(1)}, u32[]{:S(2)}, u32[]{:S(2)}) collective-permute-start(f32[1016,256]{1,0:T(8,128)S(1)} %get-tuple-element.197), channel_id=1, source_target_pairs={{16,32},{18,34},{20,36},{22,38},{24,40},{26,42},{28,44},{30,46},{8... | collective-permute-start | bytes 3121160 | tf_op jit(solution)/shard_map/ppermute | solution.py:576
  81.2 0.7 collective-permute-start.19
  81.9 0.7 collective-permute-start.20
  82.6 0.7 collective-permute-start.21
  83.3 27.0 %collective-permute-done.22.other = f32[1016,256]{1,0:T(8,128)S(1)} collective-permute-done((f32[1016,256]{1,0:T(8,128)S(1)}, f32[1016,256]{1,0:T(8,128)S(1)}, u32[]{:S(2)}, u32[]{:S(2)}) %collective-permute-start.22) | collective-permute-done | bytes 1040416 | tf_op jit(solution)/shard_map/ppermute | solution.py:576
  110.3 2.6 %out.1 = f32[3,53,16,256]{3,2,1,0:T(8,128)} custom-call(s32[53]{0:T(128)S(1)} %bitcast.10, f32[3,53,16,256]{3,2,1,0:T(8,128)S(1)} %bitcast.9, f32[53,16,256]{2,1,0:T(8,128)S(1)} %collective-permute-done.14.b0, f32[53,16,256]{2,1,0:T(8,128)S(1)} %collective-permute-done.18.late, f32[53,16,256]{2,1,0:T(8,128)S(1)} %get-tuple-element.137.b1, ...), custom_call_target="tpu_custom_call" | custom-call | tf_op jit(solution)/shard_map/out/pallas_call | solution.py:554
  (24 shorter events, 0.2 us)
Async XLA Ops:
  1.9 1.7 %copy-start = (f32[1,3,53,16,256]{4,3,2,1,0:T(8,128)S(1)}, f32[1,3,53,16,256]{4,3,2,1,0:T(8,128)}, u32[]{:S(2)}) copy-start(f32[1,3,53,16,256]{4,3,2,1,0:T(8,128)} %param.8) | copy-start | bytes 7815172
  3.6 4.4 %copy-start.1 = (f32[1,3,53,16,256]{4,3,2,1,0:T(8,128)S(1)}, f32[1,3,53,16,256]{4,3,2,1,0:T(8,128)}, u32[]{:S(2)}) copy-start(f32[1,3,53,16,256]{4,3,2,1,0:T(8,128)} %param.8) | copy-start | bytes 7815172
  4.0 14.5 %collective-permute-start = (f32[328,256]{1,0:T(8,128)S(1)}, f32[328,256]{1,0:T(8,128)S(1)}, u32[]{:S(2)}, u32[]{:S(2)}) collective-permute-start(f32[328,256]{1,0:T(8,128)S(1)} %get-tuple-element.106), channel_id=1, source_target_pairs={{1,2},{3,4},{5,6},{7,8},{9,10},{11,12},{13,14},{2,1},{4,3},{6,5},{... | collective-permute-start | bytes 1007624 | tf_op jit(solution)/shard_map/ppermute | solution.py:576
  7.9 10.7 %collective-permute-start.1 = (f32[328,256]{1,0:T(8,128)S(1)}, f32[328,256]{1,0:T(8,128)S(1)}, u32[]{:S(2)}, u32[]{:S(2)}) collective-permute-start(f32[328,256]{1,0:T(8,128)S(1)} %get-tuple-element.107), channel_id=1, source_target_pairs={{0,1},{1,0},{2,3},{3,2},{4,5},{5,4},{6,7},{7,6},{8,9},{9,8},{10,11... | collective-permute-start | bytes 1007624 | tf_op jit(solution)/shard_map/ppermute | solution.py:576
  19.1 8.9 %collective-permute-start.2 = (f32[2,56,256]{2,1,0:T(8,128)S(1)}, f32[2,56,256]{2,1,0:T(8,128)S(1)}, u32[]{:S(2)}, u32[]{:S(2)}) collective-permute-start(f32[2,56,256]{2,1,0:T(8,128)S(1)} %get-tuple-element.117), channel_id=1, source_target_pairs={{1,2},{3,4},{5,6},{7,8},{9,10},{11,12},{13,14},{2,1},{4,3},{6,5},{... | collective-permute-start | bytes 344072 | tf_op jit(solution)/shard_map/ppermute | solution.py:576
  21.9 6.1 %collective-permute-start.3 = (f32[2,56,256]{2,1,0:T(8,128)S(1)}, f32[2,56,256]{2,1,0:T(8,128)S(1)}, u32[]{:S(2)}, u32[]{:S(2)}) collective-permute-start(f32[2,56,256]{2,1,0:T(8,128)S(1)} %get-tuple-element.118), channel_id=1, source_target_pairs={{0,1},{1,0},{2,3},{3,2},{4,5},{5,4},{6,7},{7,6},{8,9},{9,8},{10,11... | collective-permute-start | bytes 344072 | tf_op jit(solution)/shard_map/ppermute | solution.py:576
  29.1 11.2 %collective-permute-start.4 = (f32[256,256]{1,0:T(8,128)S(1)}, f32[256,256]{1,0:T(8,128)S(1)}, u32[]{:S(2)}, u32[]{:S(2)}) collective-permute-start(f32[256,256]{1,0:T(8,128)S(1)} %get-tuple-element.128.mo), channel_id=1, source_target_pairs={{1,2},{3,4},{5,6},{7,8},{9,10},{11,12},{13,14},{2,1},{4,3},{6,5},{... | collective-permute-start | bytes 786440 | tf_op jit(solution)/shard_map/ppermute | solution.py:576
  31.6 8.8 %collective-permute-start.5 = (f32[256,256]{1,0:T(8,128)S(1)}, f32[256,256]{1,0:T(8,128)S(1)}, u32[]{:S(2)}, u32[]{:S(2)}) collective-permute-start(f32[256,256]{1,0:T(8,128)S(1)} %get-tuple-element.129.mi), channel_id=1, source_target_pairs={{0,1},{1,0},{2,3},{3,2},{4,5},{5,4},{6,7},{7,6},{8,9},{9,8},{10,11... | collective-permute-start | bytes 786440 | tf_op jit(solution)/shard_map/ppermute | solution.py:576
  40.6 16.0 %collective-permute-start.10 = (f32[52,24,256]{2,1,0:T(8,128)S(1)}, f32[52,24,256]{2,1,0:T(8,128)S(1)}, u32[]{:S(2)}, u32[]{:S(2)}) collective-permute-start(f32[52,24,256]{2,1,0:T(8,128)S(1)} %get-tuple-element.148.mine), channel_id=1, source_target_pairs={{17,81},{19,83},{21,85},{23,87},{25,89},{27,91},{29,93},{31,95},{4... | collective-permute-start | bytes 3833864 | tf_op jit(solution)/shard_map/ppermute | solution.py:576
  41.3 15.2 %collective-permute-start.9 = (f32[36,24,256]{2,1,0:T(8,128)S(1)}, f32[36,24,256]{2,1,0:T(8,128)S(1)}, u32[]{:S(2)}, u32[]{:S(2)}) collective-permute-start(f32[36,24,256]{2,1,0:T(8,128)S(1)} %get-tuple-element.138.ab), channel_id=1, source_target_pairs={{32,16},{34,18},{36,20},{38,22},{40,24},{42,26},{44,28},{46,30},{3... | collective-permute-start | bytes 2654216 | tf_op jit(solution)/shard_map/ppermute | solution.py:576
  46.6 2.1 %collective-permute-start.6 = (f32[344,256]{1,0:T(8,128)S(1)}, f32[344,256]{1,0:T(8,128)S(1)}, u32[]{:S(2)}, u32[]{:S(2)}) collective-permute-start(f32[344,256]{1,0:T(8,128)S(1)} %get-tuple-element.141), channel_id=1, source_target_pairs={{0,16},{1,81},{2,18},{3,83},{4,20},{5,85},{6,22},{7,87},{8,24},{9,... | collective-permute-start | bytes 1056776 | tf_op jit(solution)/shard_map/ppermute | solution.py:576
  47.3 1.4 %collective-permute-start.7 = (f32[176,256]{1,0:T(8,128)S(1)}, f32[176,256]{1,0:T(8,128)S(1)}, u32[]{:S(2)}, u32[]{:S(2)}) collective-permute-start(f32[176,256]{1,0:T(8,128)S(1)} %get-tuple-element.142), channel_id=1, source_target_pairs={{1,18},{3,20},{5,22},{7,24},{9,26},{11,28},{13,30},{2,81},{4,83},{... | collective-permute-start | bytes 540680 | tf_op jit(solution)/shard_map/ppermute | solution.py:576
  48.0 0.7 collective-permute-start.8
  48.7 14.0 %collective-permute-start.14 = (f32[53,16,256]{2,1,0:T(8,128)S(1)}, f32[53,16,256]{2,1,0:T(8,128)S(1)}, u32[]{:S(2)}, u32[]{:S(2)}) collective-permute-start(f32[53,16,256]{2,1,0:T(8,128)S(1)} %get-tuple-element.166.b2), channel_id=1, source_target_pairs={{32,48},{33,49},{34,50},{35,51},{36,52},{37,53},{38,54},{39,55},{4... | collective-permute-start | bytes 2605064 | tf_op jit(solution)/shard_map/ppermute | solution.py:576
  56.5 22.5 %collective-permute-start.18 = (f32[53,16,256]{2,1,0:T(8,128)S(1)}, f32[53,16,256]{2,1,0:T(8,128)S(1)}, u32[]{:S(2)}, u32[]{:S(2)}) collective-permute-start(f32[53,16,256]{2,1,0:T(8,128)S(1)} %get-tuple-element.166.b2), channel_id=1, source_target_pairs={{0,16},{1,17},{2,18},{3,19},{4,20},{5,21},{6,22},{7,23},{8,24},{9,... | collective-permute-start | bytes 2605064 | tf_op jit(solution)/shard_map/ppermute | solution.py:576
  57.9 4.8 %collective-permute-start.11 = (f32[344,256]{1,0:T(8,128)S(1)}, f32[344,256]{1,0:T(8,128)S(1)}, u32[]{:S(2)}, u32[]{:S(2)}) collective-permute-start(f32[344,256]{1,0:T(8,128)S(1)} %get-tuple-element.154), channel_id=1, source_target_pairs={{16,48},{81,65},{18,50},{83,67},{20,52},{85,69},{22,54},{87,71},{2... | collective-permute-start | bytes 1056776 | tf_op jit(solution)/shard_map/ppermute | solution.py:576
  58.6 4.1 %collective-permute-start.12 = (f32[176,256]{1,0:T(8,128)S(1)}, f32[176,256]{1,0:T(8,128)S(1)}, u32[]{:S(2)}, u32[]{:S(2)}) collective-permute-start(f32[176,256]{1,0:T(8,128)S(1)} %get-tuple-element.155), channel_id=1, source_target_pairs={{81,50},{83,52},{85,54},{87,56},{89,58},{91,60},{93,62},{18,65},{2... | collective-permute-start | bytes 540680 | tf_op jit(solution)/shard_map/ppermute | solution.py:576
  59.4 3.3 %collective-permute-start.13 = (f32[176,256]{1,0:T(8,128)S(1)}, f32[176,256]{1,0:T(8,128)S(1)}, u32[]{:S(2)}, u32[]{:S(2)}) collective-permute-start(f32[176,256]{1,0:T(8,128)S(1)} %get-tuple-element.156), channel_id=1, source_target_pairs={{16,65},{81,48},{18,67},{83,50},{20,69},{85,52},{22,71},{87,54},{2... | collective-permute-start | bytes 540680 | tf_op jit(solution)/shard_map/ppermute | solution.py:576
  62.7 2.1 %collective-permute-start.15 = (f32[344,256]{1,0:T(8,128)S(1)}, f32[344,256]{1,0:T(8,128)S(1)}, u32[]{:S(2)}, u32[]{:S(2)}) collective-permute-start(f32[344,256]{1,0:T(8,128)S(1)} %get-tuple-element.163), channel_id=1, source_target_pairs={{48,80},{65,97},{50,82},{67,99},{52,84},{69,101},{54,86},{71,103},... | collective-permute-start | bytes 1056776 | tf_op jit(solution)/shard_map/ppermute | solution.py:576
  63.4 1.4 %collective-permute-start.16 = (f32[176,256]{1,0:T(8,128)S(1)}, f32[176,256]{1,0:T(8,128)S(1)}, u32[]{:S(2)}, u32[]{:S(2)}) collective-permute-start(f32[176,256]{1,0:T(8,128)S(1)} %get-tuple-element.164), channel_id=1, source_target_pairs={{65,82},{67,84},{69,86},{71,88},{73,90},{75,92},{77,94},{50,97},{5... | collective-permute-start | bytes 540680 | tf_op jit(solution)/shard_map/ppermute | solution.py:576
  64.1 0.8 collective-permute-start.17
  79.0 31.3 %copy-start.2 = (s32[53,1]{0,1:T(1,128)S(1)}, s32[53,1]{0,1:T(1,128)}, u32[]{:S(2)}) copy-start(s32[53,1]{0,1:T(1,128)} %param.15) | copy-start | bytes 640
  79.0 31.3 %collective-permute-start.23 = (f32[48,24,256]{2,1,0:T(8,128)S(1)}, f32[48,24,256]{2,1,0:T(8,128)S(1)}, u32[]{:S(2)}, u32[]{:S(2)}) collective-permute-start(f32[48,24,256]{2,1,0:T(8,128)S(1)} %get-tuple-element.202.home), channel_id=1, source_target_pairs={{81,17},{83,19},{85,21},{87,23},{89,25},{91,27},{93,29},{95,31}} | collective-permute-start | bytes 3538952 | tf_op jit(solution)/shard_map/ppermute | solution.py:576
  79.9 30.4 %collective-permute-start.22 = (f32[1016,256]{1,0:T(8,128)S(1)}, f32[1016,256]{1,0:T(8,128)S(1)}, u32[]{:S(2)}, u32[]{:S(2)}) collective-permute-start(f32[1016,256]{1,0:T(8,128)S(1)} %get-tuple-element.197), channel_id=1, source_target_pairs={{16,32},{18,34},{20,36},{22,38},{24,40},{26,42},{28,44},{30,46},{8... | collective-permute-start | bytes 3121160 | tf_op jit(solution)/shard_map/ppermute | solution.py:576
  81.2 2.1 %collective-permute-start.19 = (f32[344,256]{1,0:T(8,128)S(1)}, f32[344,256]{1,0:T(8,128)S(1)}, u32[]{:S(2)}, u32[]{:S(2)}) collective-permute-start(f32[344,256]{1,0:T(8,128)S(1)} %get-tuple-element.187), channel_id=1, source_target_pairs={{80,112},{97,113},{82,114},{99,115},{84,116},{101,117},{86,118},{1... | collective-permute-start | bytes 1056776 | tf_op jit(solution)/shard_map/ppermute | solution.py:576
  81.9 1.4 %collective-permute-start.20 = (f32[88,256]{1,0:T(8,128)S(1)}, f32[88,256]{1,0:T(8,128)S(1)}, u32[]{:S(2)}, u32[]{:S(2)}) collective-permute-start(f32[88,256]{1,0:T(8,128)S(1)} %get-tuple-element.188), channel_id=1, source_target_pairs={{97,114},{99,116},{101,118},{103,120},{105,122},{107,124},{109,126... | collective-permute-start | bytes 270344 | tf_op jit(solution)/shard_map/ppermute | solution.py:576
  82.6 0.7 collective-permute-start.21
